TPU v7x, 32 devices: a whole 2x2x4 slice. The times are simulated.
32 devices in a mesh: segment: 2 (over x), ctx: 8 (over z, y), tp: 2 (over core).
Axes of the slice: x: 2, y: 2, z: 4, core: 2. Of those that a mesh axis runs over, the one named last changes fastest.
Arguments:
- patch_feats: bfloat16 [768, 1152], P('ctx', 'segment'), may hold values from -6 to 6
- proj_weight: bfloat16 [1152, 3584], P('segment', 'tp'), may hold values from -0.1875 to 0.1875
- text_embed: bfloat16 [2048, 3584], P('ctx', 'tp'), may hold values from -6 to 6
- frame_start: int32 [8], replicated, may hold values from 0 to 1952, as said below
- gain: float32 [2, 3584], P('segment'), may hold values from 0.5 to 4
- q_weight: bfloat16 [2, 3584, 2048], P('segment', None, 'tp'), may hold values from -1 to 1
- kv_weight: bfloat16 [2, 3584, 1024], P('segment', None, 'tp'), may hold values from -1 to 1
- out_weight: bfloat16 [2, 2048, 3584], P('segment', 'tp'), may hold values from -0.125 to 0.125
Outputs:
- hidden: bfloat16 [2, 2048, 3584], P('segment', 'ctx', 'tp')
Inputs may be any that keep to these rules, and one draw needn't show every extreme that they name: Frames are in order: frame f's 96 positions start at frame_start[f] and end at or before frame_start[f + 1]; the last frame's positions end the sequence of 2048 positions.
All inputs are finite; a program needn't handle non-finite values.
Results may differ from a plain program's by a relative error of at most 0.035.
Values may be sent and summed in bfloat16 or wider, within the bound.
No kernel may reach another device: no remote copies, remote signals or barrier semaphores. Data moves between devices by JAX's collectives and lax.ppermute only.
A program may use at most 128 MiB of HBM per device.

v0:
```python
import math

import jax
import jax.numpy as jnp
from jax import lax
from jax.sharding import PartitionSpec as P

HEADS = 16
KV_HEADS = 4
HDIM = 128
FRAME_TOK = 96


NEG_LARGE = -1e30
EPSILON = 1e-06
ROPE_BASE = 1000000.0


def shifted(value, axis, steps):
    count = lax.axis_size(axis)
    leading, last = (max(0, -steps), min(count, count - steps))
    return lax.ppermute(value, axis, [(source, source + steps) for source in range(leading, last)])


def rotate(values, positions):
    head_size = values.shape[-1]
    half_size = head_size // 2
    freqs = jnp.exp(
        -math.log(ROPE_BASE) * jnp.arange(half_size, dtype=jnp.float32) * 2.0 / head_size
    )
    angles = positions.astype(jnp.float32)[:, None] * freqs[None, :]
    cosine = jnp.cos(angles)[:, None, :]
    sine = jnp.sin(angles)[:, None, :]
    first_half = values[..., :half_size]
    second_half = values[..., half_size:]
    return jnp.concatenate(
        [first_half * cosine - second_half * sine, second_half * cosine + first_half * sine],
        axis=-1,
    )


def frame_rows(frame_start, positions):
    frame_count = frame_start.shape[0]
    starts = frame_start[None, :]
    column = positions[:, None]
    inside = (column >= starts) & (column < starts + FRAME_TOK)
    offsets = jnp.arange(frame_count, dtype=jnp.int32)[None, :] * FRAME_TOK + column - starts
    row_index = jnp.sum(jnp.where(inside, offsets, 0), axis=1)
    is_frame = jnp.any(inside, axis=1)
    return (row_index, is_frame)


def embed_rows(frame_embed, text_rows, frame_start, positions):
    row_index, is_frame = frame_rows(frame_start, positions)
    picked = jnp.take(frame_embed, row_index, axis=0)
    return jnp.where(is_frame[:, None], picked, text_rows)


def attend(running, query_block, query_at, key_block, value_block, key_at, per_kv):
    row_max, row_sum, accum = running
    key_full = jnp.repeat(key_block, per_kv, axis=1)
    value_full = jnp.repeat(value_block, per_kv, axis=1)
    scores = jnp.einsum(
        "qhd,khd->hqk", query_block, key_full, preferred_element_type=jnp.float32
    ) * (1.0 / math.sqrt(query_block.shape[-1]))
    causal = key_at[None, None, :] <= query_at[None, :, None]
    scores = jnp.where(causal, scores, NEG_LARGE)
    row_top = jnp.maximum(row_max, jnp.max(scores, axis=-1))
    weights = jnp.where(causal, jnp.exp(scores - row_top[..., None]), 0.0).astype(jnp.bfloat16)
    rescale = jnp.exp(row_max - row_top)
    row_sum = row_sum * rescale + jnp.sum(weights.astype(jnp.float32), axis=-1)
    accum = accum * rescale[..., None] + jnp.einsum(
        "hqk,khd->hqd", weights, value_full, preferred_element_type=jnp.float32
    )
    return (row_top, row_sum, accum)


def section_apply(hidden, gain_row, q_matrix, kv_matrix, out_matrix, query_pos, tp_index):
    tok_rows = hidden.shape[0]
    half_rows = tok_rows // 2
    wide = hidden.astype(jnp.float32)
    normed = (
        wide
        * lax.rsqrt(jnp.mean(wide * wide, axis=-1, keepdims=True) + EPSILON)
        * gain_row[None, :]
    ).astype(jnp.bfloat16)
    local_heads = HEADS // lax.axis_size("tp")
    group_size = HEADS // KV_HEADS
    kv_local = max(1, local_heads // group_size)
    per_kv = local_heads // kv_local
    queries = jnp.dot(normed, q_matrix, preferred_element_type=jnp.float32).reshape(
        tok_rows, local_heads, HDIM
    )
    queries = rotate(queries, query_pos).astype(jnp.bfloat16)
    kv_proj = jnp.dot(normed, kv_matrix, preferred_element_type=jnp.float32)
    kv_count = kv_proj.shape[1] // HDIM
    kv_proj = kv_proj.reshape(tok_rows, kv_count, HDIM)
    head_ids = tp_index * kv_count + jnp.arange(kv_count, dtype=jnp.int32)
    kv_proj = jnp.where((head_ids < KV_HEADS)[None, :, None], rotate(kv_proj, query_pos), kv_proj)
    kv_proj = kv_proj.astype(jnp.bfloat16).reshape(tok_rows, kv_count * HDIM)
    kv_all = lax.all_gather(kv_proj, "tp", axis=1, tiled=True)
    first_kv = tp_index * local_heads // group_size
    keys = lax.dynamic_slice_in_dim(kv_all, first_kv * HDIM, kv_local * HDIM, 1)
    values = lax.dynamic_slice_in_dim(kv_all, (KV_HEADS + first_kv) * HDIM, kv_local * HDIM, 1)
    query_halves = queries.reshape(2, half_rows, local_heads, HDIM)
    pos_halves = query_pos.reshape(2, half_rows)
    empty = (
        jnp.full((local_heads, half_rows), NEG_LARGE, jnp.float32),
        jnp.zeros((local_heads, half_rows), jnp.float32),
        jnp.zeros((local_heads, half_rows, HDIM), jnp.float32),
    )
    running = (empty, empty)
    key_piece = lax.all_gather(keys, "ctx", axis=0, tiled=True)
    value_piece = lax.all_gather(values, "ctx", axis=0, tiled=True)
    count_rows = key_piece.shape[0]
    block_count = count_rows // half_rows
    key_positions = jnp.arange(count_rows, dtype=jnp.int32).reshape(block_count, half_rows)
    key_blocks = key_piece.reshape(block_count, half_rows, kv_local, HDIM)
    value_blocks = value_piece.reshape(block_count, half_rows, kv_local, HDIM)
    updated = []
    for query_half in range(2):
        query_block = query_halves[query_half]
        query_at = pos_halves[query_half]
        latest = jnp.max(query_at)

        def block_step(
            current, block_inputs, query_block=query_block, query_at=query_at, latest=latest
        ):
            key_block, value_block, key_at = block_inputs
            fresh = lax.cond(
                jnp.min(key_at) > latest,
                lambda kept_state: kept_state,
                lambda kept_state: attend(
                    kept_state, query_block, query_at, key_block, value_block, key_at, per_kv
                ),
                current,
            )
            return (fresh, None)

        final_state, _ = lax.scan(
            block_step, running[query_half], (key_blocks, value_blocks, key_positions)
        )
        updated.append(final_state)
    folded = (updated[0], updated[1])
    attended = jnp.stack(
        [folded[0][2] / folded[0][1][..., None], folded[1][2] / folded[1][1][..., None]]
    )
    attended = (
        jnp.transpose(attended, (0, 2, 1, 3))
        .reshape(tok_rows, local_heads * HDIM)
        .astype(jnp.bfloat16)
    )
    partial_value = jnp.dot(attended, out_matrix, preferred_element_type=jnp.float32)
    return (wide + lax.psum(partial_value.astype(jnp.bfloat16), "tp").astype(jnp.float32)).astype(
        jnp.bfloat16
    )


def per_device(
    patch_feats, proj_weight, text_embed, frame_start, gain, q_weight, kv_weight, out_weight
):
    tok_rows = text_embed.shape[0]
    share_cols = text_embed.shape[1]
    ctx_count = lax.axis_size("ctx")
    segment_count = lax.axis_size("segment")
    ctx_index = lax.axis_index("ctx")
    tp_index = lax.axis_index("tp")
    segment_index = lax.axis_index("segment")
    projected = lax.psum(
        jnp.dot(patch_feats, proj_weight, preferred_element_type=jnp.float32), "segment"
    )
    frame_embed = jax.nn.gelu(projected, approximate=False).astype(jnp.bfloat16)
    plain_index = ctx_index * tok_rows + jnp.arange(tok_rows, dtype=jnp.int32)
    spread_frames = lax.all_to_all(frame_embed, "ctx", split_axis=1, concat_axis=0, tiled=True)
    every_index = jnp.arange(ctx_count * tok_rows, dtype=jnp.int32)
    blank_rows = jnp.zeros((ctx_count * tok_rows, spread_frames.shape[1]), jnp.bfloat16)
    placed = embed_rows(spread_frames, blank_rows, frame_start, every_index)
    delivered = lax.all_to_all(placed, "ctx", split_axis=0, concat_axis=1, tiled=True)
    unused_rows, is_frame = frame_rows(frame_start, plain_index)
    embedded = jnp.where(is_frame[:, None], delivered, text_embed)
    hidden = lax.all_gather(embedded, "tp", axis=1, tiled=True)
    collected = jnp.zeros_like(embedded)
    for tick_index in range(segment_count):
        result = section_apply(
            hidden, gain[0], q_weight[0], kv_weight[0], out_weight[0], plain_index, tp_index
        )
        own_cols = lax.dynamic_slice_in_dim(result, tp_index * share_cols, share_cols, 1)
        collected = jnp.where(segment_index == tick_index, own_cols, collected)
        if tick_index + 1 < segment_count:
            hidden = shifted(result, "segment", 1)
    return collected[None]


def solution(mesh):
    return jax.shard_map(
        per_device,
        mesh=mesh,
        in_specs=(
            P("ctx", "segment"),
            P("segment", "tp"),
            P("ctx", "tp"),
            P(),
            P("segment", None),
            P("segment", None, "tp"),
            P("segment", None, "tp"),
            P("segment", "tp", None),
        ),
        out_specs=P("segment", "ctx", "tp"),
        check_vma=False,
    )
```

profile of v0, /device:TPU:19, one launch (start us, length us, event | category | flops | bytes accessed | tf_op | source)
XLA Modules:
  0.0 656.5 jit_solution(17410955307516009316)
XLA Ops:
  12.6 30.3 %all-reduce.4.cloned.1.call-done = f32[96,1792]{1,0:T(8,128)} async-done(((f32[96,1792]{1,0:T(8,128)}), f32[96,1792]{1,0:T(8,128)}) %all-reduce.4.cloned.1.call-update) | async-done | bytes 688144 | tf_op jit(solution)/shard_map/psum | solution.py:169
  46.8 5.5 all-to-all-start
  52.3 9.6 %all-to-all-done = bf16[96,8,224]{2,0,1:T(8,128)(2,1)S(1)} async-done(((bf16[96,8,224]{2,0,1:T(8,128)(2,1)}), bf16[96,8,224]{2,0,1:T(8,128)(2,1)S(1)}, u32[]{:S(2)}, u32[]{:S(2)}) %all-to-all-start) | async-done | bytes 344096 | tf_op jit(solution)/shard_map/all_to_all | solution.py:174
  61.9 7.5 %gather_fusion = bf16[2048,224]{1,0:T(8,128)(2,1)S(1)} fusion(bf16[768,224]{1,0:T(8,128)(2,1)S(1)} %bitcast.150, s32[2048]{0:T(1024)S(1)} %broadcast_clamp_fusion), kind=kCustom, calls=%fused_computation | custom fusion | bytes 1843200 | tf_op jit(solution)/shard_map/jit(_take)/gather | solution.py:55
  71.0 5.6 all-to-all-start.1
  76.7 19.6 %all-to-all-done.1 = bf16[8,256,224]{1,2,0:T(8,128)(2,1)S(1)} async-done(((bf16[8,256,224]{1,2,0:T(8,128)(2,1)}), bf16[8,256,224]{1,2,0:T(8,128)(2,1)S(1)}, u32[]{:S(2)}, u32[]{:S(2)}) %all-to-all-start.1) | async-done | bytes 917536 | tf_op jit(solution)/shard_map/all_to_all | solution.py:178
  99.3 5.9 copy.102
  105.6 6.9 %all-gather.6.cloned.1.call-done = bf16[256,3584]{1,0:T(8,128)(2,1)} async-done(((bf16[256,1792]{1,0:T(8,128)(2,1)}), bf16[256,3584]{1,0:T(8,128)(2,1)}) %all-gather.6.cloned.1.call-update) | async-done | bytes 1835024 | tf_op jit(solution)/shard_map/all_gather | solution.py:181
  122.3 10.2 %copy.103 = bf16[1024,3584]{1,0:T(8,128)(2,1)} copy(bf16[1024,3584]{0,1:T(8,128)(2,1)} %bitcast.159) | data formatting | bytes 14680064 | tf_op jit(solution)/shard_map/dot_general | solution.py:91
  133.1 5.3 fusion.29
  139.1 21.3 %all-gather.8.cloned.1.call-done = bf16[2048,256]{0,1:T(8,128)(2,1)} async-done(((bf16[256,256]{0,1:T(8,128)(2,1)}), bf16[2048,256]{0,1:T(8,128)(2,1)}) %all-gather.8.cloned.1.call-update) | async-done | bytes 1048592 | tf_op jit(solution)/shard_map/all_gather | solution.py:113
  163.4 37.3 %all-gather.10.cloned.1.call-done = bf16[2048,256]{0,1:T(8,128)(2,1)} async-done(((bf16[256,256]{0,1:T(8,128)(2,1)}), bf16[2048,256]{0,1:T(8,128)(2,1)}) %all-gather.10.cloned.1.call-update) | async-done | bytes 1048592 | tf_op jit(solution)/shard_map/all_gather | solution.py:114
  203.8 49.4 %while.56 = (s32[]{:T(128)}, f32[8,128]{1,0:T(8,128)S(1)}, f32[8,128]{1,0:T(8,128)S(1)}, f32[8,128,128]{2,1,0:T(8,128)S(1)}, s32[16,128]{1,0:T(8,128)S(1)}, /*in...) while((s32[]{:T(128)}, f32[8,128]{1,0:T(8,128)S(1)}, ...), condition=%wide.region_12.13_spmd, body=%wide.region_6.12_spmd.sunk | while | flops 68831360 | bytes 4458751 | solution.py:140
  253.3 52.3 %while.57 = (s32[]{:T(128)}, f32[8,128]{1,0:T(8,128)S(1)}, f32[8,128]{1,0:T(8,128)S(1)}, f32[8,128,128]{2,1,0:T(8,128)S(1)}, s32[16,128]{1,0:T(8,128)S(1)}, /*in...) while((s32[]{:T(128)}, f32[8,128]{1,0:T(8,128)S(1)}, ...), condition=%wide.region_20.21_spmd, body=%wide.region_14.20_spmd.sunk | while | flops 68831360 | bytes 4458751 | solution.py:140
  306.5 6.6 fusion.16
  313.1 45.2 %all-reduce.6.cloned.1.call-done = bf16[256,3584]{1,0:T(8,128)(2,1)} async-done(((bf16[256,3584]{1,0:T(8,128)(2,1)}), bf16[256,3584]{1,0:T(8,128)(2,1)}) %all-reduce.6.cloned.1.call-update) | async-done | bytes 1835024 | tf_op jit(solution)/shard_map/psum | solution.py:154
  361.7 42.0 %collective-permute-done = bf16[256,3584]{1,0:T(8,128)(2,1)S(1)} collective-permute-done((bf16[256,3584]{1,0:T(8,128)(2,1)S(1)}, bf16[256,3584]{1,0:T(8,128)(2,1)S(1)}, u32[]{:S(2)}, u32[]{:S(2)}) %collective-permute-start) | collective-permute-done | bytes 1835040 | tf_op jit(solution)/shard_map/ppermute | solution.py:22
  410.2 5.3 fusion.33
  416.1 32.2 %all-gather.12.cloned.1.call-done = bf16[2048,256]{0,1:T(8,128)(2,1)} async-done(((bf16[256,256]{0,1:T(8,128)(2,1)}), bf16[2048,256]{0,1:T(8,128)(2,1)}) %all-gather.12.cloned.1.call-update) | async-done | bytes 1048592 | tf_op jit(solution)/shard_map/all_gather | solution.py:113
  451.3 37.7 %all-gather.14.cloned.1.call-done = bf16[2048,256]{0,1:T(8,128)(2,1)} async-done(((bf16[256,256]{0,1:T(8,128)(2,1)}), bf16[2048,256]{0,1:T(8,128)(2,1)}) %all-gather.14.cloned.1.call-update) | async-done | bytes 1048592 | tf_op jit(solution)/shard_map/all_gather | solution.py:114
  492.1 49.4 %while.58 = (s32[]{:T(128)}, f32[8,128]{1,0:T(8,128)S(1)}, f32[8,128]{1,0:T(8,128)S(1)}, f32[8,128,128]{2,1,0:T(8,128)S(1)}, s32[16,128]{1,0:T(8,128)S(1)}, /*in...) while((s32[]{:T(128)}, f32[8,128]{1,0:T(8,128)S(1)}, ...), condition=%wide.region_29.30_spmd, body=%wide.region_23.29_spmd.sunk | while | flops 68831360 | bytes 4458751 | solution.py:140
  541.6 52.3 %while.59 = (s32[]{:T(128)}, f32[8,128]{1,0:T(8,128)S(1)}, f32[8,128]{1,0:T(8,128)S(1)}, f32[8,128,128]{2,1,0:T(8,128)S(1)}, s32[16,128]{1,0:T(8,128)S(1)}, /*in...) while((s32[]{:T(128)}, f32[8,128]{1,0:T(8,128)S(1)}, ...), condition=%wide.region_36.37_spmd, body=%wide.region_30.36_spmd.sunk | while | flops 68831360 | bytes 4458751 | solution.py:140
  594.7 6.4 fusion.19
  605.1 41.3 %all-reduce.8.cloned.1.call-done = bf16[256,3584]{1,0:T(8,128)(2,1)} async-done(((bf16[256,3584]{1,0:T(8,128)(2,1)}), bf16[256,3584]{1,0:T(8,128)(2,1)}) %all-reduce.8.cloned.1.call-update) | async-done | bytes 1835024 | tf_op jit(solution)/shard_map/psum | solution.py:154
  (673 shorter events, 247.3 us)
Async XLA Ops:
  6.5 1.6 copy-start
  6.5 36.3 %all-reduce.4.cloned.1.call-start = ((), (), s32[]{:S(2)}) async-start(), calls=%async_computation.2 | async-start | bytes 1376256 | tf_op jit(solution)/shard_map/psum | solution.py:169
  46.8 15.1 %all-to-all-start = ((bf16[96,8,224]{2,0,1:T(8,128)(2,1)}), bf16[96,8,224]{2,0,1:T(8,128)(2,1)S(1)}, u32[]{:S(2)}, u32[]{:S(2)}) async-start(bf16[96,8,224]{2,0,1:T(8,128)(2,1)} %copy.77), calls=%async_computation | async-start | bytes 786432 | tf_op jit(solution)/shard_map/all_to_all | solution.py:174
  69.4 7.2 %copy-start.8 = (s32[8]{0:T(128)S(1)}, s32[8]{0:T(128)}, u32[]{:S(2)}) copy-start(s32[8]{0:T(128)} %param.27) | copy-start | bytes 100
  71.0 25.3 %all-to-all-start.1 = ((bf16[8,256,224]{1,2,0:T(8,128)(2,1)}), bf16[8,256,224]{1,2,0:T(8,128)(2,1)S(1)}, u32[]{:S(2)}, u32[]{:S(2)}) async-start(bf16[8,256,224]{1,2,0:T(8,128)(2,1)} %select_select_fusion), calls=%async_computation.1 | async-start | bytes 1835008 | tf_op jit(solution)/shard_map/all_to_all | solution.py:178
  76.6 36.0 %all-gather.6.cloned.1.call-start = ((), (), s32[]{:S(2)}) async-start(), calls=%async_computation.3 | async-start | bytes 2752512 | tf_op jit(solution)/shard_map/all_gather | solution.py:181
  99.2 61.2 %all-gather.8.cloned.1.call-start = ((), (), s32[]{:S(2)}) async-start(), calls=%async_computation.4 | async-start | bytes 1179648 | tf_op jit(solution)/shard_map/all_gather | solution.py:113
  99.3 5.9 copy-start.7
  121.4 79.3 %all-gather.10.cloned.1.call-start = ((), (), s32[]{:S(2)}) async-start(), calls=%async_computation.5 | async-start | bytes 1179648 | tf_op jit(solution)/shard_map/all_gather | solution.py:114
  122.0 236.3 %all-reduce.6.cloned.1.call-start = ((), (), s32[]{:S(2)}) async-start(), calls=%async_computation.6 | async-start | bytes 3670016 | tf_op jit(solution)/shard_map/psum | solution.py:154
  122.2 10.9 %copy-start.2 = (bf16[256,3584]{1,0:T(8,128)(2,1)S(1)}, bf16[256,3584]{1,0:T(8,128)(2,1)}, u32[]{:S(2)}) copy-start(bf16[256,3584]{1,0:T(8,128)(2,1)} %all-gather.6.cloned.1.call-done) | copy-start | bytes 5505028
  306.5 51.8 %copy-start.3 = (bf16[256,3584]{1,0:T(8,128)(2,1)S(1)}, bf16[256,3584]{1,0:T(8,128)(2,1)}, u32[]{:S(2)}) copy-start(bf16[256,3584]{1,0:T(8,128)(2,1)} %all-gather.6.cloned.1.call-done) | copy-start | bytes 5505028
  313.1 135.2 %all-gather.12.cloned.1.call-start = ((), (), s32[]{:S(2)}) async-start(), calls=%async_computation.7 | async-start | bytes 1179648 | tf_op jit(solution)/shard_map/all_gather | solution.py:113
  358.3 45.9 %copy-start.6 = (bf16[512,3584]{1,0:T(8,128)(2,1)S(1)}, bf16[512,3584]{1,0:T(8,128)(2,1)}, u32[]{:S(2)}) copy-start(bf16[512,3584]{1,0:T(8,128)(2,1)} %copy.102) | copy-start | bytes 11010052
  360.4 45.0 %copy-start.5 = (bf16[256,3584]{1,0:T(8,128)(2,1)}, bf16[256,3584]{1,0:T(8,128)(2,1)S(1)}, u32[]{:S(2)}) copy-start(bf16[256,3584]{1,0:T(8,128)(2,1)S(1)} %fusion.25) | copy-start | bytes 5505028
  360.4 43.3 %collective-permute-start = (bf16[256,3584]{1,0:T(8,128)(2,1)S(1)}, bf16[256,3584]{1,0:T(8,128)(2,1)S(1)}, u32[]{:S(2)}, u32[]{:S(2)}) collective-permute-start(bf16[256,3584]{1,0:T(8,128)(2,1)S(1)} %fusion.25), channel_id=1, source_target_pairs={{0,16},{1,17},{2,18},{3,19},{4,20},{5,21},{6,22},{7,23},{8,24},{9,... | collective-permute-start | bytes 5505032 | tf_op jit(solution)/shard_map/ppermute | solution.py:22
  403.7 6.5 copy-start.4
  409.2 79.8 %all-gather.14.cloned.1.call-start = ((), (), s32[]{:S(2)}) async-start(), calls=%async_computation.8 | async-start | bytes 1179648 | tf_op jit(solution)/shard_map/all_gather | solution.py:114
  409.9 236.4 %all-reduce.8.cloned.1.call-start = ((), (), s32[]{:S(2)}) async-start(), calls=%async_computation.9 | async-start | bytes 3670016 | tf_op jit(solution)/shard_map/psum | solution.py:154
  601.2 48.5 %copy-start.1 = (bf16[576,1792]{1,0:T(8,128)(2,1)S(1)}, bf16[576,1792]{1,0:T(8,128)(2,1)}, u32[]{:S(2)}) copy-start(bf16[576,1792]{1,0:T(8,128)(2,1)} %param.25) | copy-start | bytes 6193156
Sparse Core Ops, SparseCore 0:
  10.5 32.3 all-reduce.3
  99.3 13.1 all-gather.5
  121.6 38.7 all-gather.7
  162.3 38.4 all-gather.9
  313.2 45.0 all-reduce.5
  409.3 38.9 all-gather.11
  450.5 38.4 all-gather.13
  601.3 45.0 all-reduce.7
where the time goes:
time: 663 us; the launch traced here: 656 us
  waiting for transfers between devices  325 us (49%)
  loops' own time  89.9 us (14%)
  local copies, waits for them, and re-layouts  79.6 us (12%)
  other arithmetic  71.4 us (11%)
  matrix products  59 us (9%)
  between operations  14 us (2%)
  starting transfers between devices  13 us (2%)
    psum x2, waiting for transfers between devices, section_apply(): lax.psum(partial_value.astype(jnp.bfloat16), 'tp').astype(jnp.float32)  86.5 us
    another operation x4, loops' own time, section_apply(): lax.scan(block_step, running[query_half], (key_blocks, value_blocks, key_...  86.2 us
    all_gather x2, waiting for transfers between devices, section_apply(): value_piece = lax.all_gather(values, 'ctx', axis=0, tiled=True)  75 us
    all_gather x2, waiting for transfers between devices, section_apply(): key_piece = lax.all_gather(keys, 'ctx', axis=0, tiled=True)  53.5 us
    ppermute x1, waiting for transfers between devices, shifted(): lax.ppermute(value, axis, [(source, source + steps) for source in range(l...  42 us
    reduce_min x64, other arithmetic, block_step(): jnp.min(key_at) > latest  40.9 us
    squeeze x38, local copies, waits for them, and re-layouts, section_apply(): lax.scan(block_step, running[query_half], (key_blocks, value_blocks, key_...  33.8 us
    psum x1, waiting for transfers between devices, per_device(): lax.psum(jnp.dot(patch_feats, proj_weight, preferred_element_type=jnp.flo...  30.3 us
  transfers between devices with their start and end apart: 11, of which 11 were waited for; matrix products, arithmetic and copies ran while one was open for 6% of the time, Pallas kernels for 0%

commit v1 on v0

v1 whole, which is shorter than its diff:
```python
import math

import jax
import jax.numpy as jnp
from jax import lax
from jax.experimental import pallas as pl
from jax.experimental.pallas import tpu as pltpu
from jax.sharding import Mesh
from jax.sharding import PartitionSpec as P

HEADS = 16
KV_HEADS = 4
HDIM = 128
FRAME_TOK = 96

EPSILON = 1e-06
ROPE_BASE = 1000000.0
NEG_LARGE = -1e30
MIB = 1 << 20
F32 = jnp.float32
BF16 = jnp.bfloat16
CTX = ("grp", "mem")


def params(mib):
    return pltpu.CompilerParams(vmem_limit_bytes=mib * MIB)


def swap(value):
    return lax.ppermute(value, "tp", [(0, 1), (1, 0)])


def rope_tables(positions):
    half = HDIM // 2
    freqs = jnp.exp(-math.log(ROPE_BASE) * jnp.arange(half, dtype=F32) * 2.0 / HDIM)
    angles = positions.astype(F32)[:, None] * freqs[None, :]
    cosine, sine = jnp.cos(angles), jnp.sin(angles)
    return (
        jnp.concatenate([cosine, cosine], axis=1),
        jnp.concatenate([-sine, sine], axis=1),
    )


def place_kernel(idx_own, idx_oth, pf_own, pf_oth, w_ref, wide_ref, sent_ref, placed):
    @pl.when(pl.program_id(0) == 0)
    def _():
        rows, count = idx_own.shape[0], pf_own.shape[0]
        at = lax.broadcasted_iota(jnp.int32, (rows, count), 1)
        hot_own = jnp.where(at == idx_own[...], 1.0, 0.0).astype(BF16)
        hot_oth = jnp.where(at == idx_oth[...], 1.0, 0.0).astype(BF16)
        picked = jnp.dot(hot_own, pf_own[...], preferred_element_type=F32)
        picked += jnp.dot(hot_oth, pf_oth[...], preferred_element_type=F32)
        placed[...] = picked.astype(BF16)

    term = jnp.dot(placed[...], w_ref[...], preferred_element_type=F32)
    wide_ref[...] = term
    sent_ref[...] = term.astype(BF16)


def project_placed(idx_own, idx_oth, pf_own, pf_oth, proj_weight):
    rows, (depth, cols) = idx_own.shape[0], proj_weight.shape
    block = 256
    whole = lambda i: (0, 0)
    return pl.pallas_call(
        place_kernel,
        grid=(cols // block,),
        in_specs=[
            pl.BlockSpec(idx_own.shape, whole),
            pl.BlockSpec(idx_oth.shape, whole),
            pl.BlockSpec(pf_own.shape, whole),
            pl.BlockSpec(pf_oth.shape, whole),
            pl.BlockSpec((depth, block), lambda i: (0, i)),
        ],
        out_specs=[pl.BlockSpec((rows, block), lambda i: (0, i))] * 2,
        out_shape=[
            jax.ShapeDtypeStruct((rows, cols), F32),
            jax.ShapeDtypeStruct((rows, cols), BF16),
        ],
        scratch_shapes=[pltpu.VMEM((rows, depth), BF16)],
        compiler_params=params(32),
    )(idx_own, idx_oth, pf_own, pf_oth, proj_weight)


def rope(values, cosine, sine):
    return values * cosine + pltpu.roll(values, HDIM // 2, 1) * sine


def kv_kernel(tp_ref, own, oth, gain, w_ref, cos_ref, sin_ref, normed_ref, kv_ref, scratch):
    half = own.shape[1]

    @pl.when(pl.program_id(0) == 0)
    def _():
        t = tp_ref[0]
        own_at = pl.multiple_of(t * half, 128)
        oth_at = pl.multiple_of((1 - t) * half, 128)

        def chunk(c, carry):
            rows = pl.ds(pl.multiple_of(c * 32, 32), 32)
            a = own[rows, :].astype(F32)
            b = oth[rows, :].astype(F32)
            total = jnp.sum(a * a, axis=1, keepdims=True) + jnp.sum(b * b, axis=1, keepdims=True)
            scale = lax.rsqrt(total * (1.0 / (2 * half)) + EPSILON)
            scratch[rows, pl.ds(own_at, half)] = (
                a * scale * gain[:, pl.ds(own_at, half)]
            ).astype(BF16)
            scratch[rows, pl.ds(oth_at, half)] = (
                b * scale * gain[:, pl.ds(oth_at, half)]
            ).astype(BF16)
            return carry

        lax.fori_loop(0, own.shape[0] // 32, chunk, 0)
        normed_ref[...] = scratch[...]

    wide = jnp.dot(scratch[...], w_ref[...], preferred_element_type=F32)
    for h in range(wide.shape[1] // HDIM):
        head = rope(wide[:, h * HDIM : (h + 1) * HDIM], cos_ref[...], sin_ref[...]).astype(BF16)
        for g in range(kv_ref.shape[0]):
            kv_ref[g, h] = head


def keyvals(tp_index, own, oth, gain, kv_weight, cosine, sine, groups):
    rows, half = own.shape
    depth, cols = kv_weight.shape
    block = 256
    whole = lambda i, t: (0, 0)
    per = block // HDIM
    return pl.pallas_call(
        kv_kernel,
        grid_spec=pltpu.PrefetchScalarGridSpec(
            num_scalar_prefetch=1,
            grid=(cols // block,),
            in_specs=[
                pl.BlockSpec(own.shape, whole),
                pl.BlockSpec(oth.shape, whole),
                pl.BlockSpec(gain.shape, whole),
                pl.BlockSpec((depth, block), lambda i, t: (0, i)),
                pl.BlockSpec(cosine.shape, whole),
                pl.BlockSpec(sine.shape, whole),
            ],
            out_specs=[
                pl.BlockSpec((rows, depth), whole),
                pl.BlockSpec((groups, per, rows, HDIM), lambda i, t: (0, i, 0, 0)),
            ],
            scratch_shapes=[pltpu.VMEM((rows, depth), BF16)],
        ),
        out_shape=[
            jax.ShapeDtypeStruct((rows, depth), BF16),
            jax.ShapeDtypeStruct((groups, cols // HDIM, rows, HDIM), BF16),
        ],
        compiler_params=params(32),
    )(tp_index, own, oth, gain, kv_weight, cosine, sine)


def q_kernel(tp_ref, normed, w_ref, cos_ref, sin_ref, q_ref):
    wide = jnp.dot(normed[...], w_ref[...], preferred_element_type=F32)
    for h in range(wide.shape[1] // HDIM):
        at = slice(h * HDIM, (h + 1) * HDIM)
        q_ref[0, 0, :, at] = rope(wide[:, at], cos_ref[...], sin_ref[...]).astype(BF16)


def queries_of(tp_index, normed, q_weight, cosine, sine):
    rows, depth = normed.shape
    cols = q_weight.shape[1]
    block = 2 * HDIM
    pairs = cols // block
    whole = lambda i, t: (0, 0)
    half = pairs // 2

    def column(i, t):
        kept = 1 - i // half
        core = jnp.where(kept == 1, t[0], 1 - t[0])
        return (0, 2 * (i % half) + core)

    return pl.pallas_call(
        q_kernel,
        grid_spec=pltpu.PrefetchScalarGridSpec(
            num_scalar_prefetch=1,
            grid=(pairs,),
            in_specs=[
                pl.BlockSpec(normed.shape, whole),
                pl.BlockSpec((depth, block), column),
                pl.BlockSpec(cosine.shape, whole),
                pl.BlockSpec(sine.shape, whole),
            ],
            out_specs=pl.BlockSpec(
                (1, 1, rows, block), lambda i, t: (i // half, i % half, 0, 0)
            ),
        ),
        out_shape=jax.ShapeDtypeStruct((2, half, rows, block), BF16),
        compiler_params=params(32),
    )(tp_index, normed, q_weight, cosine, sine)


BQ = 256
BK = 512


def attend_kernel(at_ref, q_ref, own, oth, o_ref, keys, vals):
    step = pl.program_id(0)

    @pl.when(step == 0)
    def _():
        vals[:, HDIM:] = jnp.ones((vals.shape[0], HDIM), BF16)

        @pl.when(at_ref[1] == 0)
        def _():
            keys[...] = own[...]
            vals[:, :HDIM] = oth[...]

        @pl.when(at_ref[1] == 1)
        def _():
            keys[...] = oth[...]
            vals[:, :HDIM] = own[...]

    row0 = at_ref[0] + step * BQ
    factor = math.log2(math.e) / math.sqrt(HDIM)
    heads = q_ref.shape[1] // HDIM
    q = [q_ref[:, h * HDIM : (h + 1) * HDIM] for h in range(heads)]

    def block(b, carry, masked):
        at = pl.ds(pl.multiple_of(b * BK, BK), BK)
        k, v = keys[at, :], vals[at, :]
        fresh = []
        for h in range(heads):
            top, acc = carry[h]
            s = lax.dot_general(q[h], k, (((1,), (1,)), ((), ())), preferred_element_type=F32)
            if masked:
                qa = row0 + lax.broadcasted_iota(jnp.int32, s.shape, 0)
                ka = b * BK + lax.broadcasted_iota(jnp.int32, s.shape, 1)
                s = jnp.where(ka <= qa, s, NEG_LARGE)
            new = jnp.maximum(top, jnp.max(s, axis=1, keepdims=True))
            p = jnp.exp2((s - new) * factor).astype(BF16)
            alpha = jnp.exp2((top - new) * factor)
            acc = acc * alpha + jnp.dot(p, v, preferred_element_type=F32)
            fresh.append((new, acc))
        return tuple(fresh)

    start = tuple(
        (jnp.full((BQ, 1), NEG_LARGE, F32), jnp.zeros((BQ, 2 * HDIM), F32)) for _ in range(heads)
    )
    full = row0 // BK
    state = lax.fori_loop(0, full, lambda b, c: block(b, c, False), start)
    state = block(full, state, True)
    for h in range(heads):
        acc = state[h][1]
        o_ref[:, h * HDIM : (h + 1) * HDIM] = (acc[:, :HDIM] / acc[:, HDIM:]).astype(BF16)


def attend(at, q, own, oth):
    rows, cols = q.shape
    whole = lambda i, t: (0, 0)
    return pl.pallas_call(
        attend_kernel,
        grid_spec=pltpu.PrefetchScalarGridSpec(
            num_scalar_prefetch=1,
            grid=(rows // BQ,),
            in_specs=[
                pl.BlockSpec((BQ, cols), lambda i, t: (i, 0)),
                pl.BlockSpec(own.shape, whole),
                pl.BlockSpec(oth.shape, whole),
            ],
            out_specs=pl.BlockSpec((BQ, cols), lambda i, t: (i, 0)),
            scratch_shapes=[
                pltpu.VMEM(own.shape, BF16),
                pltpu.VMEM((own.shape[0], 2 * HDIM), BF16),
            ],
        ),
        out_shape=jax.ShapeDtypeStruct((rows, cols), BF16),
        compiler_params=params(32),
    )(at, q, own, oth)


def out_kernel(tp_ref, a_own, a_oth, w_own, w_oth, h_ref, o_ref, near, far):
    pair = 2 * HDIM

    @pl.when(pl.program_id(0) == 0)
    def _():
        t = tp_ref[0]
        for jj in range(2):
            mine = pl.multiple_of((2 * jj + t) * pair, pair)
            theirs = pl.multiple_of((2 * jj + 1 - t) * pair, pair)
            near[:, pl.ds(mine, pair)] = a_own[2 * t + jj]
            near[:, pl.ds(theirs, pair)] = a_oth[2 * t + jj]
            far[:, pl.ds(mine, pair)] = a_own[2 * (1 - t) + jj]
            far[:, pl.ds(theirs, pair)] = a_oth[2 * (1 - t) + jj]

    first = jnp.dot(near[...], w_own[...], preferred_element_type=F32)
    second = jnp.dot(far[...], w_oth[...], preferred_element_type=F32)
    o_ref[...] = (h_ref[...].astype(F32) + (first + second)).astype(BF16)


def project_out(tp_index, a_own, a_oth, w_own, w_oth, h):
    rows, cols = h.shape
    depth = w_own.shape[0]
    block = 256
    steps = cols // block
    three = lambda i, t: (0, 0, 0)
    return pl.pallas_call(
        out_kernel,
        grid_spec=pltpu.PrefetchScalarGridSpec(
            num_scalar_prefetch=1,
            grid=(steps,),
            in_specs=[
                pl.BlockSpec(a_own.shape, three),
                pl.BlockSpec(a_oth.shape, three),
                pl.BlockSpec((depth, block), lambda i, t: (0, t[0] * steps + i)),
                pl.BlockSpec((depth, block), lambda i, t: (0, i)),
                pl.BlockSpec((rows, block), lambda i, t: (0, i)),
            ],
            out_specs=pl.BlockSpec((rows, block), lambda i, t: (0, i)),
            scratch_shapes=[pltpu.VMEM((rows, depth), BF16)] * 2,
        ),
        out_shape=jax.ShapeDtypeStruct((rows, cols), BF16),
        compiler_params=params(32),
    )(tp_index, a_own, a_oth, w_own, w_oth, h)


def per_device(
    patch_feats, proj_weight, text_embed, frame_start, gain, q_weight, kv_weight, out_weight
):
    rows, cols = text_embed.shape
    groups, members = lax.axis_size("grp"), lax.axis_size("mem")
    count = groups * members
    t = lax.axis_index("tp")
    segment = lax.axis_index("segment")
    group = lax.axis_index("grp")
    ctx = group * members + lax.axis_index("mem")
    tp_index = t.reshape(1).astype(jnp.int32)
    q_weight, kv_weight, out_weight = q_weight[0], kv_weight[0], out_weight[0]

    w_oth = swap(lax.dynamic_slice_in_dim(out_weight, (1 - t) * cols, cols, 1))

    positions = ctx * rows + jnp.arange(rows, dtype=jnp.int32)
    cosine, sine = rope_tables(positions)
    kv_cos = jnp.where(t == 0, cosine, 1.0)
    kv_sin = jnp.where(t == 0, sine, 0.0)

    part = patch_feats.shape[0] // 2
    mine = lax.dynamic_slice_in_dim(patch_feats, t * part, part, 0)
    spread = jnp.broadcast_to(mine[None], (count, *mine.shape))
    pf_own = lax.all_to_all(spread, CTX, split_axis=0, concat_axis=0, tiled=True)
    pf_own = pf_own.reshape(count * part, -1)
    pf_oth = swap(pf_own)
    offset = positions[:, None] - frame_start[None, :]
    inside = (offset >= 0) & (offset < FRAME_TOK)
    is_frame = jnp.any(inside, axis=1)
    frames = jnp.arange(frame_start.shape[0], dtype=jnp.int32)[None, :]

    def index_of(core):
        local = offset - core * part
        here = inside & (local >= 0) & (local < part)
        return jnp.max(jnp.where(here, frames * part + local, -1), axis=1, keepdims=True)

    wide, sent = project_placed(index_of(t), index_of(1 - t), pf_own, pf_oth, proj_weight)
    came = lax.ppermute(sent, "segment", [(1, 0)])
    frame_embed = jax.nn.gelu(wide + came.astype(F32), approximate=False).astype(BF16)
    h = jnp.where(is_frame[:, None], frame_embed, text_embed)

    results = []
    for tick in range(lax.axis_size("segment")):
        if tick:
            h = lax.ppermute(h, "segment", [(tick - 1, tick)])
        h_oth = swap(h)
        normed, kv = keyvals(tp_index, h, h_oth, gain, kv_weight, kv_cos, kv_sin, groups)
        kv = kv.reshape(count, rows, HDIM)
        kv = lax.all_to_all(kv, CTX, split_axis=0, concat_axis=0, tiled=True)
        kv_own = kv.reshape(count * rows, HDIM)
        kv_oth = swap(kv_own)
        q = queries_of(tp_index, normed, q_weight, cosine, sine)
        kept, given = q[0], swap(q[1])
        pairs = jnp.where(
            t == 0, jnp.concatenate([kept, given], 0), jnp.concatenate([given, kept], 0)
        )
        pairs = lax.all_to_all(pairs, "mem", split_axis=0, concat_axis=0, tiled=True)
        at = jnp.stack([group * members * rows, t]).astype(jnp.int32)
        attended = attend(at, pairs.reshape(members * rows, 2 * HDIM), kv_own, kv_oth)
        attended = attended.reshape(members, rows, 2 * HDIM)
        a_own = lax.all_to_all(attended, "mem", split_axis=0, concat_axis=0, tiled=True)
        a_oth = swap(a_own)
        h = project_out(tp_index, a_own, a_oth, out_weight, w_oth, h)
        results.append(h)
    out = results[0]
    for tick in range(1, len(results)):
        out = jnp.where(segment == tick, results[tick], out)
    return out[None]


def solution(mesh):
    segments, ctx, tp = mesh.devices.shape
    split = Mesh(
        mesh.devices.reshape(segments, ctx // KV_HEADS, KV_HEADS, tp),
        ("segment", "grp", "mem", "tp"),
    )
    return jax.shard_map(
        per_device,
        mesh=split,
        in_specs=(
            P(CTX, "segment"),
            P("segment", "tp"),
            P(CTX, "tp"),
            P(),
            P("segment", None),
            P("segment", None, "tp"),
            P("segment", None, "tp"),
            P("segment", "tp", None),
        ),
        out_specs=P("segment", CTX, "tp"),
        check_vma=False,
    )
```

time: 663 us -> 233 us (0.35)
  waiting for transfers between devices: 325 us -> 64.1 us
  loops' own time: 89.9 us -> 0 us
  other arithmetic: 71.4 us -> 10.7 us
  matrix products: 59 us -> 0 us
  Pallas kernels: 0 us -> 57.2 us
  local copies, waits for them, and re-layouts: 79.6 us -> 28 us
  blocking collectives: 5.02 us -> 38.3 us
  starting transfers between devices: 13 us -> 33 us
  between operations: 14 us -> 0.23 us
    all_gather x5 -> x0, waiting for transfers between devices: 135 us -> none  [the longest x2 75 us: section_apply(): value_piece = lax.all_gather(values, 'ctx', axis=0, tiled=True)]
    psum x3 -> x0, waiting for transfers between devices: 117 us -> none  [the longest x2 86.5 us: section_apply(): lax.psum(partial_value.astype(jnp.bfloat16), 'tp').astype(jnp.float32)]
    another operation x68 -> x0, loops' own time: 89.9 us -> none  [the longest x4 86.2 us: section_apply(): lax.scan(block_step, running[query_half], (key_blocks, value_blocks, key_...]
    dot_general x83 -> x0, matrix products: 59 us -> none  [the longest x38 16.4 us: attend(): jnp.einsum('hqk,khd->hqd', weights, value_full, preferred_element_type=jn...]
    pallas_call x0 -> x9, Pallas kernels: none -> 57.2 us  [the longest x2 24.9 us: attend(): pl.pallas_call(attend_kernel, grid_spec=pltpu.PrefetchScalarGridSpec(num_...]
    reduce_min x64 -> x0, other arithmetic: 40.9 us -> none  [block_step(): jnp.min(key_at) > latest]
    all_to_all x0 -> x3, blocking collectives: none -> 38.3 us  [the longest x2 21.1 us: per_device(): lax.all_to_all(attended, 'mem', split_axis=0, concat_axis=0, tiled=True)]
    squeeze x38 -> x2, local copies, waits for them, and re-layouts: 33.8 us -> 0.07 us  [per_device(): kept, given = (q[0], swap(q[1]))]
  transfers between devices with their start and end apart: 11 -> 16, of which waited for: 11 -> 12; matrix products, arithmetic and copies ran while one was open for 6% -> 4% of each run, Pallas kernels for 0% -> 10%
where the time goes in v1:
time: 233 us; the launch traced here: 232 us
  waiting for transfers between devices  64.1 us (28%)
  Pallas kernels  57.2 us (25%)
  blocking collectives  38.3 us (16%)
  starting transfers between devices  33 us (14%)
  local copies, waits for them, and re-layouts  28 us (12%)
  other arithmetic  10.7 us (5%)
    pallas_call x2, Pallas kernels, attend(): pl.pallas_call(attend_kernel, grid_spec=pltpu.PrefetchScalarGridSpec(num_...  24.9 us
    unnamed x42, local copies, waits for them, and re-layouts  23.5 us
    ppermute x1, waiting for transfers between devices, per_device(): h = lax.ppermute(h, 'segment', [(tick - 1, tick)])  22.4 us
    all_to_all x2, blocking collectives, per_device(): lax.all_to_all(attended, 'mem', split_axis=0, concat_axis=0, tiled=True)  21.1 us
    ppermute x1, waiting for transfers between devices, per_device(): came = lax.ppermute(sent, 'segment', [(1, 0)])  18.6 us
    all_to_all x1, blocking collectives, per_device(): lax.all_to_all(spread, CTX, split_axis=0, concat_axis=0, tiled=True)  17.2 us
    all_to_all x2, waiting for transfers between devices, per_device(): lax.all_to_all(pairs, 'mem', split_axis=0, concat_axis=0, tiled=True)  13.1 us
    pallas_call x2, Pallas kernels, project_out(): pl.pallas_call(out_kernel, grid_spec=pltpu.PrefetchScalarGridSpec(num_sca...  12.8 us
  transfers between devices with their start and end apart: 16, of which 12 were waited for; matrix products, arithmetic and copies ran while one was open for 4% of the time, Pallas kernels for 10%

profile of v1, /device:TPU:19, one launch (start us, length us, event | category | flops | bytes accessed | tf_op | source)
XLA Modules:
  0.0 231.6 jit_solution(1501057596854470951)
XLA Ops:
  1.0 17.2 %all_to_all.35 = bf16[8,48,576]{2,1,0:T(8,128)(2,1)S(1)} all-to-all(bf16[8,48,576]{2,1,0:T(8,128)(2,1)S(1)} %broadcast_in_dim.45), channel_id=1, replica_groups=mesh['segment'=2,'grp'=2,'mem'=4,'tp'=2] {'grp','mem'}, dimensions={0} | all-to-all | bytes 884736 | tf_op jit(solution)/shard_map/all_to_all | solution.py:341
  22.7 4.4 %shard_map.82 = (f32[256,1792]{1,0:T(8,128)S(1)}, bf16[256,1792]{1,0:T(8,128)(2,1)}) custom-call(s32[256,1]{1,0:T(8,128)S(1)} %copy.11.idx_own, s32[256,1]{1,0:T(8,128)S(1)} %copy.12.idx_oth, bf16[384,576]{1,0:T(8,128)(2,1)S(1)} %bitcast.43, bf16[384,576]{1,0:T(8,128)(2,1)S(1)} %collective-permute-done.pf_oth, bf16[576,1792]{1,0:T(8,128)(2,1)S(1)} %copy-done.7), custom_call_target="tpu_custom_call" | custom-call | tf_op jit(solution)/shard_map/pallas_call | solution.py:64
  27.1 3.1 %collective-permute-start.1 = (bf16[256,1792]{1,0:T(8,128)(2,1)}, bf16[256,1792]{1,0:T(8,128)(2,1)}, u32[]{:S(2)}, u32[]{:S(2)}) collective-permute-start(bf16[256,1792]{1,0:T(8,128)(2,1)} %get-tuple-element.12), channel_id=1, source_target_pairs={{16,0},{17,1},{18,2},{19,3},{20,4},{21,5},{22,6},{23,7},{24,8},{25... | collective-permute-start | bytes 2752520 | tf_op jit(solution)/shard_map/ppermute | solution.py:355
  30.3 18.6 %collective-permute-done.1 = bf16[256,1792]{1,0:T(8,128)(2,1)} collective-permute-done((bf16[256,1792]{1,0:T(8,128)(2,1)}, bf16[256,1792]{1,0:T(8,128)(2,1)}, u32[]{:S(2)}, u32[]{:S(2)}) %collective-permute-start.1) | collective-permute-done | bytes 917536 | tf_op jit(solution)/shard_map/ppermute | solution.py:355
  48.9 5.6 %fusion.10.own.h_ref = bf16[256,1792]{1,0:T(8,128)(2,1)S(1)} fusion(bf16[256,1792]{1,0:T(8,128)(2,1)} %param.10, f32[256,1792]{1,0:T(8,128)S(1)} %get-tuple-element.11, bf16[256,1792]{1,0:T(8,128)(2,1)} %collective-permute-done.1, pred[256]{0:T(512)(128)(4,1)S(1)} %fusion.27), kind=kLoop, calls=%fused_computation.22 | loop fusion | flops 31195136 | bytes 4587776 | tf_op jit(solution)/shard_map/jit(_where)/select_n | solution.py:357
  55.8 4.1 %dynamic-slice_bitcast_fusion = bf16[1024,1792]{1,0:T(8,128)(2,1)} fusion(bf16[1,1024,3584]{2,1,0:T(8,128)(2,1)} %param.15, s32[]{:T(128)S(6)} %select_n.59), kind=kLoop, calls=%fused_computation | loop fusion | bytes 7340036 | tf_op jit(solution)/shard_map/dynamic_slice | solution.py:331
  65.5 3.2 %shard_map.83 = (bf16[256,3584]{1,0:T(8,128)(2,1)S(1)}, bf16[2,4,256,128]{3,2,1,0:T(8,128)(2,1)S(1)}) custom-call(s32[1]{0:T(128)} %bitcast.tp_ref, bf16[256,1792]{1,0:T(8,128)(2,1)S(1)} %fusion.10.own.h_ref, bf16[256,1792]{1,0:T(8,128)(2,1)S(1)} %copy-done.17, f32[1,3584]{1,0:T(1,128)S(1)} %copy-done.19, bf16[3584,512]{1,0:T(8,128)(2,1)S(1)} %bitcast.32, ...), custom_call_target="tpu_custom_call" | custom-call | tf_op jit(solution)/shard_map/pallas_call | solution.py:127
  69.6 4.9 %all-to-all-start.2 = ((bf16[8,256,128]{2,1,0:T(8,128)(2,1)}), bf16[8,256,128]{2,1,0:T(8,128)(2,1)S(1)}, u32[]{:S(2)}, u32[]{:S(2)}) async-start(bf16[8,256,128]{2,1,0:T(8,128)(2,1)} %bitcast.44), calls=%async_computation.2 | async-start | bytes 1048576 | tf_op jit(solution)/shard_map/all_to_all | solution.py:366
  78.5 3.9 %shard_map.84 = bf16[2,2,256,256]{3,2,1,0:T(8,128)(2,1)S(1)} custom-call(s32[1]{0:T(128)} %bitcast.tp_ref, bf16[256,3584]{1,0:T(8,128)(2,1)S(1)} %get-tuple-element.13.normed, bf16[3584,1024]{1,0:T(8,128)(2,1)S(1)} %bitcast.30, f32[256,128]{1,0:T(8,128)S(1)} %copy-done.10, f32[256,128]{1,0:T(8,128)S(1)} %get-tuple-element.20.sin_ref), custom_call_target="tpu_custom_call" | custom-call | tf_op jit(solution)/shard_map/pallas_call | solution.py:174
  86.9 3.9 %all-to-all-start.1 = ((bf16[4,256,256]{2,1,0:T(8,128)(2,1)}), bf16[4,256,256]{2,1,0:T(8,128)(2,1)S(1)}, u32[]{:S(2)}, u32[]{:S(2)}) async-start(bf16[4,256,256]{2,1,0:T(8,128)(2,1)} %maximum_select_fusion), calls=%async_computation.1 | async-start | bytes 1048576 | tf_op jit(solution)/shard_map/all_to_all | solution.py:374
  91.6 6.5 %all-to-all-done.1 = bf16[4,256,256]{2,1,0:T(8,128)(2,1)S(1)} async-done(((bf16[4,256,256]{2,1,0:T(8,128)(2,1)}), bf16[4,256,256]{2,1,0:T(8,128)(2,1)S(1)}, u32[]{:S(2)}, u32[]{:S(2)}) %all-to-all-start.1) | async-done | bytes 524320 | tf_op jit(solution)/shard_map/all_to_all | solution.py:374
  98.1 12.5 %shard_map.85 = bf16[1024,256]{1,0:T(8,128)(2,1)S(1)} custom-call(s32[2]{0:T(128)S(1)} %pad_add_fusion.at_ref, bf16[1024,256]{1,0:T(8,128)(2,1)S(1)} %bitcast.38, bf16[2048,128]{1,0:T(8,128)(2,1)S(1)} %bitcast.35, bf16[2048,128]{1,0:T(8,128)(2,1)S(1)} %collective-permute-done.4.oth), custom_call_target="tpu_custom_call" | custom-call | tf_op jit(solution)/shard_map/pallas_call | solution.py:252
  110.6 10.6 %all_to_all.36.a_own = bf16[4,256,256]{2,1,0:T(8,128)(2,1)S(1)} all-to-all(bf16[4,256,256]{2,1,0:T(8,128)(2,1)S(1)} %bitcast.41), channel_id=1, replica_groups=mesh['segment'=2,'grp'=2,'mem'=4,'tp'=2] {'mem'}, dimensions={0} | all-to-all | bytes 1048576 | tf_op jit(solution)/shard_map/all_to_all | solution.py:378
  128.0 6.5 %shard_map.86 = bf16[256,1792]{1,0:T(8,128)(2,1)S(1)} custom-call(s32[1]{0:T(128)} %bitcast.tp_ref, bf16[4,256,256]{2,1,0:T(8,128)(2,1)S(1)} %all_to_all.36.a_own, bf16[4,256,256]{2,1,0:T(8,128)(2,1)S(1)} %collective-permute-done.5.a_oth, bf16[1024,3584]{1,0:T(8,128)(2,1)S(1)} %bitcast.28, bf16[1024,1792]{1,0:T(8,128)(2,1)} %collective-permute-done.6.w_oth, ...), custom_call_target="tpu_custom_call" | custom-call | tf_op jit(solution)/shard_map/pallas_call | solution.py:298
  136.0 22.4 %collective-permute-done.7.own.h_ref = bf16[256,1792]{1,0:T(8,128)(2,1)S(1)} collective-permute-done((bf16[256,1792]{1,0:T(8,128)(2,1)S(1)}, bf16[256,1792]{1,0:T(8,128)(2,1)S(1)}, u32[]{:S(2)}, u32[]{:S(2)}) %collective-permute-start.7) | collective-permute-done | bytes 917536 | tf_op jit(solution)/shard_map/ppermute | solution.py:362
  161.6 3.9 %shard_map.87 = (bf16[256,3584]{1,0:T(8,128)(2,1)S(1)}, bf16[2,4,256,128]{3,2,1,0:T(8,128)(2,1)}) custom-call(s32[1]{0:T(128)} %bitcast.tp_ref, bf16[256,1792]{1,0:T(8,128)(2,1)S(1)} %collective-permute-done.7.own.h_ref, bf16[256,1792]{1,0:T(8,128)(2,1)S(1)} %collective-permute-done.8.oth, f32[1,3584]{1,0:T(1,128)S(1)} %copy-done.19, ...), custom_call_target="tpu_custom_call" | custom-call | tf_op jit(solution)/shard_map/pallas_call | solution.py:127
  166.7 4.0 %all-to-all-start.5 = ((bf16[8,256,128]{2,1,0:T(8,128)(2,1)}), bf16[8,256,128]{2,1,0:T(8,128)(2,1)S(1)}, u32[]{:S(2)}, u32[]{:S(2)}) async-start(bf16[8,256,128]{2,1,0:T(8,128)(2,1)} %bitcast.18), calls=%async_computation.5 | async-start | bytes 1048576 | tf_op jit(solution)/shard_map/all_to_all | solution.py:366
  170.7 3.1 %copy-done.4 = bf16[1,3584,1024]{2,1,0:T(8,128)(2,1)S(1)} copy-done((bf16[1,3584,1024]{2,1,0:T(8,128)(2,1)S(1)}, bf16[1,3584,1024]{2,1,0:T(8,128)(2,1)}, u32[]{:S(2)}) %copy-start.4) | copy-done | bytes 7340056
  175.3 3.9 %shard_map.88 = bf16[2,2,256,256]{3,2,1,0:T(8,128)(2,1)S(1)} custom-call(s32[1]{0:T(128)} %bitcast.tp_ref, bf16[256,3584]{1,0:T(8,128)(2,1)S(1)} %copy-done.9, bf16[3584,1024]{1,0:T(8,128)(2,1)S(1)} %bitcast.31, f32[256,128]{1,0:T(8,128)S(1)} %copy-done.11, f32[256,128]{1,0:T(8,128)S(1)} %get-tuple-element.20.sin_ref), custom_call_target="tpu_custom_call" | custom-call | tf_op jit(solution)/shard_map/pallas_call | solution.py:174
  183.1 3.9 %all-to-all-start.4 = ((bf16[4,256,256]{2,1,0:T(8,128)(2,1)}), bf16[4,256,256]{2,1,0:T(8,128)(2,1)S(1)}, u32[]{:S(2)}, u32[]{:S(2)}) async-start(bf16[4,256,256]{2,1,0:T(8,128)(2,1)} %maximum_select_fusion.1), calls=%async_computation.4 | async-start | bytes 1048576 | tf_op jit(solution)/shard_map/all_to_all | solution.py:374
  187.7 6.6 %all-to-all-done.4 = bf16[4,256,256]{2,1,0:T(8,128)(2,1)S(1)} async-done(((bf16[4,256,256]{2,1,0:T(8,128)(2,1)}), bf16[4,256,256]{2,1,0:T(8,128)(2,1)S(1)}, u32[]{:S(2)}, u32[]{:S(2)}) %all-to-all-start.4) | async-done | bytes 524320 | tf_op jit(solution)/shard_map/all_to_all | solution.py:374
  194.3 12.5 %shard_map.89 = bf16[1024,256]{1,0:T(8,128)(2,1)S(1)} custom-call(s32[2]{0:T(128)S(1)} %pad_add_fusion.at_ref, bf16[1024,256]{1,0:T(8,128)(2,1)S(1)} %bitcast.39, bf16[2048,128]{1,0:T(8,128)(2,1)S(1)} %bitcast.37, bf16[2048,128]{1,0:T(8,128)(2,1)S(1)} %collective-permute-done.10.oth), custom_call_target="tpu_custom_call" | custom-call | tf_op jit(solution)/shard_map/pallas_call | solution.py:252
  206.8 10.6 %all_to_all.37.a_own = bf16[4,256,256]{2,1,0:T(8,128)(2,1)S(1)} all-to-all(bf16[4,256,256]{2,1,0:T(8,128)(2,1)S(1)} %bitcast.40), channel_id=1, replica_groups=mesh['segment'=2,'grp'=2,'mem'=4,'tp'=2] {'mem'}, dimensions={0} | all-to-all | bytes 1048576 | tf_op jit(solution)/shard_map/all_to_all | solution.py:378
  224.2 6.3 %shard_map.90 = bf16[256,1792]{1,0:T(8,128)(2,1)S(1)} custom-call(s32[1]{0:T(128)} %bitcast.tp_ref, bf16[4,256,256]{2,1,0:T(8,128)(2,1)S(1)} %all_to_all.37.a_own, bf16[4,256,256]{2,1,0:T(8,128)(2,1)S(1)} %collective-permute-done.11.a_oth, bf16[1024,3584]{1,0:T(8,128)(2,1)S(1)} %bitcast.29, bf16[1024,1792]{1,0:T(8,128)(2,1)} %collective-permute-done.6.w_oth, ...), custom_call_target="tpu_custom_call" | custom-call | tf_op jit(solution)/shard_map/pallas_call | solution.py:298
  (83 shorter events, 49.2 us)
Async XLA Ops:
  18.2 12.1 %copy-start.20 = (s32[8]{0:T(128)S(1)}, s32[8]{0:T(128)}, u32[]{:S(2)}) copy-start(s32[8]{0:T(128)} %param.11) | copy-start | bytes 100
  18.2 2.9 %collective-permute-start = (bf16[384,576]{1,0:T(8,128)(2,1)S(1)}, bf16[384,576]{1,0:T(8,128)(2,1)S(1)}, u32[]{:S(2)}, u32[]{:S(2)}) collective-permute-start(bf16[384,576]{1,0:T(8,128)(2,1)S(1)} %bitcast.42), channel_id=1, source_target_pairs={{0,1},{1,0},{2,3},{3,2},{4,5},{5,4},{6,7},{7,6},{8,9},{9,8},{10,11... | collective-permute-start | bytes 1327112 | tf_op jit(solution)/shard_map/ppermute | solution.py:30
  27.1 21.8 %collective-permute-start.1 = (bf16[256,1792]{1,0:T(8,128)(2,1)}, bf16[256,1792]{1,0:T(8,128)(2,1)}, u32[]{:S(2)}, u32[]{:S(2)}) collective-permute-start(bf16[256,1792]{1,0:T(8,128)(2,1)} %get-tuple-element.12), channel_id=1, source_target_pairs={{16,0},{17,1},{18,2},{19,3},{20,4},{21,5},{22,6},{23,7},{24,8},{25... | collective-permute-start | bytes 2752520 | tf_op jit(solution)/shard_map/ppermute | solution.py:355
  54.5 7.8 %copy-start.19 = (f32[1,3584]{1,0:T(1,128)S(1)}, f32[1,3584]{1,0:T(1,128)}, u32[]{:S(2)}) copy-start(f32[1,3584]{1,0:T(1,128)} %gain.3) | copy-start | bytes 43012
  54.5 6.8 %collective-permute-start.2 = (bf16[256,1792]{1,0:T(8,128)(2,1)S(1)}, bf16[256,1792]{1,0:T(8,128)(2,1)S(1)}, u32[]{:S(2)}, u32[]{:S(2)}) collective-permute-start(bf16[256,1792]{1,0:T(8,128)(2,1)S(1)} %fusion.10.own.h_ref), channel_id=1, source_target_pairs={{0,1},{1,0},{2,3},{3,2},{4,5},{5,4},{6,7},{7,6},{8,9},{9,8},{10,11... | collective-permute-start | bytes 2752520 | tf_op jit(solution)/shard_map/ppermute | solution.py:30
  59.9 63.5 %collective-permute-start.6 = (bf16[1024,1792]{1,0:T(8,128)(2,1)}, bf16[1024,1792]{1,0:T(8,128)(2,1)}, u32[]{:S(2)}, u32[]{:S(2)}) collective-permute-start(bf16[1024,1792]{1,0:T(8,128)(2,1)} %dynamic-slice_bitcast_fusion), channel_id=1, source_target_pairs={{0,1},{1,0},{2,3},{3,2},{4,5},{5,4},{6,7},{7,6},{8,9},{9,8},{10,11... | collective-permute-start | bytes 11010056 | tf_op jit(solution)/shard_map/ppermute | solution.py:30
  61.2 7.5 %copy-start.14 = (f32[256,128]{1,0:T(8,128)}, f32[256,128]{1,0:T(8,128)S(1)}, u32[]{:S(2)}) copy-start(f32[256,128]{1,0:T(8,128)S(1)} %get-tuple-element.26.cos_ref) | copy-start | bytes 393220
  61.3 7.4 %copy-start.12 = (f32[256,128]{1,0:T(8,128)}, f32[256,128]{1,0:T(8,128)S(1)}, u32[]{:S(2)}) copy-start(f32[256,128]{1,0:T(8,128)S(1)} %get-tuple-element.19.sin_ref) | copy-start | bytes 393220
  69.6 17.3 %all-to-all-start.2 = ((bf16[8,256,128]{2,1,0:T(8,128)(2,1)}), bf16[8,256,128]{2,1,0:T(8,128)(2,1)S(1)}, u32[]{:S(2)}, u32[]{:S(2)}) async-start(bf16[8,256,128]{2,1,0:T(8,128)(2,1)} %bitcast.44), calls=%async_computation.2 | async-start | bytes 1048576 | tf_op jit(solution)/shard_map/all_to_all | solution.py:366
  82.5 2.2 collective-permute-start.3
  86.9 11.2 %all-to-all-start.1 = ((bf16[4,256,256]{2,1,0:T(8,128)(2,1)}), bf16[4,256,256]{2,1,0:T(8,128)(2,1)S(1)}, u32[]{:S(2)}, u32[]{:S(2)}) async-start(bf16[4,256,256]{2,1,0:T(8,128)(2,1)} %maximum_select_fusion), calls=%async_computation.1 | async-start | bytes 1048576 | tf_op jit(solution)/shard_map/all_to_all | solution.py:374
  90.8 7.4 %collective-permute-start.4 = (bf16[2048,128]{1,0:T(8,128)(2,1)S(1)}, bf16[2048,128]{1,0:T(8,128)(2,1)S(1)}, u32[]{:S(2)}, u32[]{:S(2)}) collective-permute-start(bf16[2048,128]{1,0:T(8,128)(2,1)S(1)} %bitcast.34), channel_id=1, source_target_pairs={{0,1},{1,0},{2,3},{3,2},{4,5},{5,4},{6,7},{7,6},{8,9},{9,8},{10,11... | collective-permute-start | bytes 1572872 | tf_op jit(solution)/shard_map/ppermute | solution.py:30
  121.2 3.8 %collective-permute-start.5 = (bf16[4,256,256]{2,1,0:T(8,128)(2,1)S(1)}, bf16[4,256,256]{2,1,0:T(8,128)(2,1)S(1)}, u32[]{:S(2)}, u32[]{:S(2)}) collective-permute-start(bf16[4,256,256]{2,1,0:T(8,128)(2,1)S(1)} %all_to_all.36.a_own), channel_id=1, source_target_pairs={{0,1},{1,0},{2,3},{3,2},{4,5},{5,4},{6,7},{7,6},{8,9},{9,8},{10,11... | collective-permute-start | bytes 1572872 | tf_op jit(solution)/shard_map/ppermute | solution.py:30
  128.0 33.5 %copy-start.6 = (bf16[1,3584,512]{2,1,0:T(8,128)(2,1)S(1)}, bf16[1,3584,512]{2,1,0:T(8,128)(2,1)}, u32[]{:S(2)}) copy-start(bf16[1,3584,512]{2,1,0:T(8,128)(2,1)} %param.14) | copy-start | bytes 11010052
  128.0 33.5 %copy-start.13 = (f32[256,128]{1,0:T(8,128)S(1)}, f32[256,128]{1,0:T(8,128)}, u32[]{:S(2)}) copy-start(f32[256,128]{1,0:T(8,128)} %copy-done.12) | copy-start | bytes 393220
  128.0 33.5 %copy-start.15 = (f32[256,128]{1,0:T(8,128)S(1)}, f32[256,128]{1,0:T(8,128)}, u32[]{:S(2)}) copy-start(f32[256,128]{1,0:T(8,128)} %copy-done.14) | copy-start | bytes 393220
  134.5 36.2 %copy-start.11 = (f32[256,128]{1,0:T(8,128)S(1)}, f32[256,128]{1,0:T(8,128)}, u32[]{:S(2)}) copy-start(f32[256,128]{1,0:T(8,128)} %get-tuple-element.25.cos_ref) | copy-start | bytes 393220
  134.5 23.8 %collective-permute-start.7 = (bf16[256,1792]{1,0:T(8,128)(2,1)S(1)}, bf16[256,1792]{1,0:T(8,128)(2,1)S(1)}, u32[]{:S(2)}, u32[]{:S(2)}) collective-permute-start(bf16[256,1792]{1,0:T(8,128)(2,1)S(1)} %shard_map.86), channel_id=1, source_target_pairs={{0,16},{1,17},{2,18},{3,19},{4,20},{5,21},{6,22},{7,23},{8,24},{9,... | collective-permute-start | bytes 2752520 | tf_op jit(solution)/shard_map/ppermute | solution.py:362
  158.4 3.2 %collective-permute-start.8 = (bf16[256,1792]{1,0:T(8,128)(2,1)S(1)}, bf16[256,1792]{1,0:T(8,128)(2,1)S(1)}, u32[]{:S(2)}, u32[]{:S(2)}) collective-permute-start(bf16[256,1792]{1,0:T(8,128)(2,1)S(1)} %collective-permute-done.7.own.h_ref), channel_id=1, source_target_pairs={{0,1},{1,0},{2,3},{3,2},{4,5},{5,4},{6,7},{7,6},{8,9},{9,8},{10,11... | collective-permute-start | bytes 2752520 | tf_op jit(solution)/shard_map/ppermute | solution.py:30
  166.7 16.4 %all-to-all-start.5 = ((bf16[8,256,128]{2,1,0:T(8,128)(2,1)}), bf16[8,256,128]{2,1,0:T(8,128)(2,1)S(1)}, u32[]{:S(2)}, u32[]{:S(2)}) async-start(bf16[8,256,128]{2,1,0:T(8,128)(2,1)} %bitcast.18), calls=%async_computation.5 | async-start | bytes 1048576 | tf_op jit(solution)/shard_map/all_to_all | solution.py:366
  179.3 2.2 collective-permute-start.9
  183.1 11.2 %all-to-all-start.4 = ((bf16[4,256,256]{2,1,0:T(8,128)(2,1)}), bf16[4,256,256]{2,1,0:T(8,128)(2,1)S(1)}, u32[]{:S(2)}, u32[]{:S(2)}) async-start(bf16[4,256,256]{2,1,0:T(8,128)(2,1)} %maximum_select_fusion.1), calls=%async_computation.4 | async-start | bytes 1048576 | tf_op jit(solution)/shard_map/all_to_all | solution.py:374
  186.9 7.4 %collective-permute-start.10 = (bf16[2048,128]{1,0:T(8,128)(2,1)S(1)}, bf16[2048,128]{1,0:T(8,128)(2,1)S(1)}, u32[]{:S(2)}, u32[]{:S(2)}) collective-permute-start(bf16[2048,128]{1,0:T(8,128)(2,1)S(1)} %bitcast.36), channel_id=1, source_target_pairs={{0,1},{1,0},{2,3},{3,2},{4,5},{5,4},{6,7},{7,6},{8,9},{9,8},{10,11... | collective-permute-start | bytes 1572872 | tf_op jit(solution)/shard_map/ppermute | solution.py:30
  217.3 3.8 %collective-permute-start.11 = (bf16[4,256,256]{2,1,0:T(8,128)(2,1)S(1)}, bf16[4,256,256]{2,1,0:T(8,128)(2,1)S(1)}, u32[]{:S(2)}, u32[]{:S(2)}) collective-permute-start(bf16[4,256,256]{2,1,0:T(8,128)(2,1)S(1)} %all_to_all.37.a_own), channel_id=1, source_target_pairs={{0,1},{1,0},{2,3},{3,2},{4,5},{5,4},{6,7},{7,6},{8,9},{9,8},{10,11... | collective-permute-start | bytes 1572872 | tf_op jit(solution)/shard_map/ppermute | solution.py:30
  (13 other events, 23.5 us)

commit v2 on v1

--- a/solution.py
+++ b/solution.py
@@ -1,3 +1,4 @@
+import functools
 import math
 
 import jax
@@ -79,6 +80,31 @@
         scratch_shapes=[pltpu.VMEM((rows, depth), BF16)],
         compiler_params=params(32),
     )(idx_own, idx_oth, pf_own, pf_oth, proj_weight)
+
+
+def project_kernel(x_ref, w_ref, wide_ref, sent_ref):
+    term = jnp.dot(x_ref[...], w_ref[...], preferred_element_type=F32)
+    wide_ref[...] = term
+    sent_ref[...] = term.astype(BF16)
+
+
+def project(values, proj_weight):
+    rows, (depth, cols) = values.shape[0], proj_weight.shape
+    block = 256
+    return pl.pallas_call(
+        project_kernel,
+        grid=(cols // block,),
+        in_specs=[
+            pl.BlockSpec((rows, depth), lambda i: (0, 0)),
+            pl.BlockSpec((depth, block), lambda i: (0, i)),
+        ],
+        out_specs=[pl.BlockSpec((rows, block), lambda i: (0, i))] * 2,
+        out_shape=[
+            jax.ShapeDtypeStruct((rows, cols), F32),
+            jax.ShapeDtypeStruct((rows, cols), BF16),
+        ],
+        compiler_params=params(32),
+    )(values, proj_weight)
 
 
 def rope(values, cosine, sine):
@@ -155,7 +181,7 @@
     wide = jnp.dot(normed[...], w_ref[...], preferred_element_type=F32)
     for h in range(wide.shape[1] // HDIM):
         at = slice(h * HDIM, (h + 1) * HDIM)
-        q_ref[0, 0, :, at] = rope(wide[:, at], cos_ref[...], sin_ref[...]).astype(BF16)
+        q_ref[0, 0, h] = rope(wide[:, at], cos_ref[...], sin_ref[...]).astype(BF16)
 
 
 def queries_of(tp_index, normed, q_weight, cosine, sine):
@@ -183,106 +209,153 @@
                 pl.BlockSpec(sine.shape, whole),
             ],
             out_specs=pl.BlockSpec(
-                (1, 1, rows, block), lambda i, t: (i // half, i % half, 0, 0)
+                (1, 1, 2, rows, HDIM), lambda i, t: (i // half, i % half, 0, 0, 0)
             ),
         ),
-        out_shape=jax.ShapeDtypeStruct((2, half, rows, block), BF16),
+        out_shape=jax.ShapeDtypeStruct((2, half, 2, rows, HDIM), BF16),
         compiler_params=params(32),
     )(tp_index, normed, q_weight, cosine, sine)
 
 
-BQ = 256
 BK = 512
-
-
-def attend_kernel(at_ref, q_ref, own, oth, o_ref, keys, vals):
-    step = pl.program_id(0)
-
-    @pl.when(step == 0)
+PAD = 128
+
+
+def place(target, lanes, start, block):
+    window = FRAME_TOK + 16
+    first = pl.multiple_of((start // 16) * 16, 16)
+    shift = start - first
+    r = lax.broadcasted_iota(jnp.int32, (window, FRAME_TOK), 0)
+    c = lax.broadcasted_iota(jnp.int32, (window, FRAME_TOK), 1)
+    hot = jnp.where(r - c == shift, 1.0, 0.0).astype(BF16)
+    moved = jnp.dot(hot, block, preferred_element_type=F32)
+    row = lax.broadcasted_iota(jnp.int32, moved.shape, 0)
+    inside = (row >= shift) & (row < shift + FRAME_TOK)
+    at = pl.ds(first, window)
+    kept = target[at, lanes].astype(F32)
+    target[at, lanes] = jnp.where(inside, moved, kept).astype(BF16)
+
+
+def attend_kernel(frames, at_ref, q_ref, own, oth, o_ref, keys, vals, qs):
+    members, heads, rows, _ = q_ref.shape
+    count = own.shape[0]
+    base, core = at_ref[0], at_ref[1]
+    every, low = slice(None), slice(0, HDIM)
+    vals[:, HDIM:] = jnp.ones((vals.shape[0], HDIM), BF16)
+
+    def fill(k_from, v_from):
+        for c in range(count):
+            keys[c * rows : (c + 1) * rows, :] = k_from[c, :rows, :]
+            vals[c * rows : (c + 1) * rows, :HDIM] = v_from[c, :rows, :]
+        if frames:
+
+            def one(f, carry):
+                start = at_ref[2 + f]
+                place(keys, every, start, k_from[f, rows : rows + FRAME_TOK, :])
+                place(vals, low, start, v_from[f, rows : rows + FRAME_TOK, :])
+                return carry
+
+            lax.fori_loop(0, frames, one, 0)
+
+    @pl.when(core == 0)
     def _():
-        vals[:, HDIM:] = jnp.ones((vals.shape[0], HDIM), BF16)
-
-        @pl.when(at_ref[1] == 0)
-        def _():
-            keys[...] = own[...]
-            vals[:, :HDIM] = oth[...]
-
-        @pl.when(at_ref[1] == 1)
-        def _():
-            keys[...] = oth[...]
-            vals[:, :HDIM] = own[...]
-
-    row0 = at_ref[0] + step * BQ
-    factor = math.log2(math.e) / math.sqrt(HDIM)
-    heads = q_ref.shape[1] // HDIM
-    q = [q_ref[:, h * HDIM : (h + 1) * HDIM] for h in range(heads)]
-
-    def block(b, carry, masked):
+        fill(own, oth)
+
+    @pl.when(core == 1)
+    def _():
+        fill(oth, own)
+
+    for h in range(heads):
+        for c in range(members):
+            qs[h, PAD + c * rows : PAD + (c + 1) * rows, :] = q_ref[c, h]
+    if frames:
+
+        def one(f, carry):
+            start = at_ref[2 + f] - base
+
+            @pl.when((start > -FRAME_TOK) & (start < members * rows))
+            def _():
+                for h in range(heads):
+                    lower = rows + (1 + h) * FRAME_TOK
+                    block = own[f, lower : lower + FRAME_TOK, :]
+                    place(qs.at[h], every, start + PAD, block)
+
+            return carry
+
+        lax.fori_loop(0, frames, one, 0)
+
+    chains = [(h, c) for c in range(members) for h in range(heads)]
+
+    def update(state, h, c, b, masked):
+        top, acc = state
         at = pl.ds(pl.multiple_of(b * BK, BK), BK)
-        k, v = keys[at, :], vals[at, :]
-        fresh = []
-        for h in range(heads):
-            top, acc = carry[h]
-            s = lax.dot_general(q[h], k, (((1,), (1,)), ((), ())), preferred_element_type=F32)
-            if masked:
-                qa = row0 + lax.broadcasted_iota(jnp.int32, s.shape, 0)
-                ka = b * BK + lax.broadcasted_iota(jnp.int32, s.shape, 1)
-                s = jnp.where(ka <= qa, s, NEG_LARGE)
-            new = jnp.maximum(top, jnp.max(s, axis=1, keepdims=True))
-            p = jnp.exp2((s - new) * factor).astype(BF16)
-            alpha = jnp.exp2((top - new) * factor)
-            acc = acc * alpha + jnp.dot(p, v, preferred_element_type=F32)
-            fresh.append((new, acc))
-        return tuple(fresh)
+        q = qs[h, PAD + c * rows : PAD + (c + 1) * rows, :]
+        s = lax.dot_general(q, keys[at, :], (((1,), (1,)), ((), ())), preferred_element_type=F32)
+        if masked:
+            qa = base + c * rows + lax.broadcasted_iota(jnp.int32, s.shape, 0)
+            ka = b * BK + lax.broadcasted_iota(jnp.int32, s.shape, 1)
+            s = jnp.where(ka <= qa, s, NEG_LARGE)
+        new = jnp.maximum(top, jnp.max(s, axis=1, keepdims=True))
+        p = jnp.exp2(s - new).astype(BF16)
+        acc = acc * jnp.exp2(top - new) + jnp.dot(p, vals[at, :], preferred_element_type=F32)
+        return (new, acc)
 
     start = tuple(
-        (jnp.full((BQ, 1), NEG_LARGE, F32), jnp.zeros((BQ, 2 * HDIM), F32)) for _ in range(heads)
+        (jnp.full((rows, 1), NEG_LARGE, F32), jnp.zeros((rows, 2 * HDIM), F32)) for _ in chains
     )
-    full = row0 // BK
-    state = lax.fori_loop(0, full, lambda b, c: block(b, c, False), start)
-    state = block(full, state, True)
-    for h in range(heads):
-        acc = state[h][1]
-        o_ref[:, h * HDIM : (h + 1) * HDIM] = (acc[:, :HDIM] / acc[:, HDIM:]).astype(BF16)
-
-
-def attend(at, q, own, oth):
-    rows, cols = q.shape
-    whole = lambda i, t: (0, 0)
+    full = base // BK
+    step = lambda b, state: tuple(
+        update(state[i], h, c, b, False) for i, (h, c) in enumerate(chains)
+    )
+    state = list(lax.fori_loop(0, full, step, start))
+    for e in range(members * rows // BK):
+        for i, (h, c) in enumerate(chains):
+            if (c + 1) * rows > e * BK:
+                state[i] = update(state[i], h, c, full + e, c * rows < (e + 1) * BK)
+    for i, (h, c) in enumerate(chains):
+        acc = state[i][1]
+        o_ref[c, h] = (acc[:, :HDIM] / acc[:, HDIM:]).astype(BF16)
+
+
+def attend(at, q, own, oth, frames):
+    members, heads, rows, _ = q.shape
+    span = own.shape[0] * rows
+    whole = lambda i, t: (0, 0, 0)
+    four = lambda i, t: (0, 0, 0, 0)
     return pl.pallas_call(
-        attend_kernel,
+        functools.partial(attend_kernel, frames),
         grid_spec=pltpu.PrefetchScalarGridSpec(
             num_scalar_prefetch=1,
-            grid=(rows // BQ,),
+            grid=(1,),
             in_specs=[
-                pl.BlockSpec((BQ, cols), lambda i, t: (i, 0)),
+                pl.BlockSpec(q.shape, four),
                 pl.BlockSpec(own.shape, whole),
                 pl.BlockSpec(oth.shape, whole),
             ],
-            out_specs=pl.BlockSpec((BQ, cols), lambda i, t: (i, 0)),
+            out_specs=pl.BlockSpec(q.shape, four),
             scratch_shapes=[
-                pltpu.VMEM(own.shape, BF16),
-                pltpu.VMEM((own.shape[0], 2 * HDIM), BF16),
+                pltpu.VMEM((span + PAD, HDIM), BF16),
+                pltpu.VMEM((span + PAD, 2 * HDIM), BF16),
+                pltpu.VMEM((heads, members * rows + 2 * PAD, HDIM), BF16),
             ],
         ),
-        out_shape=jax.ShapeDtypeStruct((rows, cols), BF16),
-        compiler_params=params(32),
+        out_shape=jax.ShapeDtypeStruct(q.shape, BF16),
+        compiler_params=params(40),
     )(at, q, own, oth)
 
 
 def out_kernel(tp_ref, a_own, a_oth, w_own, w_oth, h_ref, o_ref, near, far):
-    pair = 2 * HDIM
-
     @pl.when(pl.program_id(0) == 0)
     def _():
         t = tp_ref[0]
         for jj in range(2):
-            mine = pl.multiple_of((2 * jj + t) * pair, pair)
-            theirs = pl.multiple_of((2 * jj + 1 - t) * pair, pair)
-            near[:, pl.ds(mine, pair)] = a_own[2 * t + jj]
-            near[:, pl.ds(theirs, pair)] = a_oth[2 * t + jj]
-            far[:, pl.ds(mine, pair)] = a_own[2 * (1 - t) + jj]
-            far[:, pl.ds(theirs, pair)] = a_oth[2 * (1 - t) + jj]
+            for h in range(2):
+                mine = pl.multiple_of((2 * (2 * jj + t) + h) * HDIM, HDIM)
+                theirs = pl.multiple_of((2 * (2 * jj + 1 - t) + h) * HDIM, HDIM)
+                near[:, pl.ds(mine, HDIM)] = a_own[2 * t + jj, h]
+                near[:, pl.ds(theirs, HDIM)] = a_oth[2 * t + jj, h]
+                far[:, pl.ds(mine, HDIM)] = a_own[2 * (1 - t) + jj, h]
+                far[:, pl.ds(theirs, HDIM)] = a_oth[2 * (1 - t) + jj, h]
 
     first = jnp.dot(near[...], w_own[...], preferred_element_type=F32)
     second = jnp.dot(far[...], w_oth[...], preferred_element_type=F32)
@@ -294,17 +367,17 @@
     depth = w_own.shape[0]
     block = 256
     steps = cols // block
-    three = lambda i, t: (0, 0, 0)
+    four = lambda i, t: (0, 0, 0, 0)
     return pl.pallas_call(
         out_kernel,
         grid_spec=pltpu.PrefetchScalarGridSpec(
             num_scalar_prefetch=1,
             grid=(steps,),
             in_specs=[
-                pl.BlockSpec(a_own.shape, three),
-                pl.BlockSpec(a_oth.shape, three),
+                pl.BlockSpec(a_own.shape, four),
+                pl.BlockSpec(a_oth.shape, four),
                 pl.BlockSpec((depth, block), lambda i, t: (0, t[0] * steps + i)),
-                pl.BlockSpec((depth, block), lambda i, t: (0, i)),
+                pl.BlockSpec((depth, block), lambda i, t: (0, t[0] * steps + i)),
                 pl.BlockSpec((rows, block), lambda i, t: (0, i)),
             ],
             out_specs=pl.BlockSpec((rows, block), lambda i, t: (0, i)),
@@ -328,19 +401,50 @@
     tp_index = t.reshape(1).astype(jnp.int32)
     q_weight, kv_weight, out_weight = q_weight[0], kv_weight[0], out_weight[0]
 
-    w_oth = swap(lax.dynamic_slice_in_dim(out_weight, (1 - t) * cols, cols, 1))
-
     positions = ctx * rows + jnp.arange(rows, dtype=jnp.int32)
-    cosine, sine = rope_tables(positions)
-    kv_cos = jnp.where(t == 0, cosine, 1.0)
-    kv_sin = jnp.where(t == 0, sine, 0.0)
+    frame_at = lax.dynamic_index_in_dim(frame_start, ctx, 0, keepdims=False)
+    factor = math.log2(math.e) / math.sqrt(HDIM)
+
+    def tables(at):
+        cosine, sine = rope_tables(at)
+        plain = t != 0
+        kv_tables = (jnp.where(plain, 1.0, cosine), jnp.where(plain, 0.0, sine))
+        return kv_tables, (cosine * factor, sine * factor)
+
+    text_kv, text_q = tables(positions)
+    frame_kv, frame_q = tables(frame_at + jnp.arange(FRAME_TOK, dtype=jnp.int32))
 
     part = patch_feats.shape[0] // 2
     mine = lax.dynamic_slice_in_dim(patch_feats, t * part, part, 0)
     spread = jnp.broadcast_to(mine[None], (count, *mine.shape))
     pf_own = lax.all_to_all(spread, CTX, split_axis=0, concat_axis=0, tiled=True)
+
+    def joined(wide, sent):
+        came = lax.ppermute(sent, "segment", [(1, 0)])
+        return jax.nn.gelu(wide + came.astype(F32), approximate=False).astype(BF16)
+
+    def by_member(q):
+        kept, given = q[0], swap(q[1])
+        first = jnp.where(t == 0, kept, given)
+        second = jnp.where(t == 0, given, kept)
+        return jnp.concatenate([first, second], 0)
+
+    frame_embed = joined(*project(patch_feats, proj_weight))
+
+    normed, kv = keyvals(tp_index, text_embed, swap(text_embed), gain, kv_weight, *text_kv, 1)
+    q = by_member(queries_of(tp_index, normed, q_weight, *text_q))
+    f_normed, f_kv = keyvals(tp_index, frame_embed, swap(frame_embed), gain, kv_weight, *frame_kv, 1)
+    f_q = by_member(queries_of(tp_index, f_normed, q_weight, *frame_q))
+    message = jnp.concatenate([kv[0], f_kv[0], f_q[:, 0], f_q[:, 1]], axis=1)
+    message = jnp.broadcast_to(message[None], (groups, *message.shape))
+    message = message.reshape(count, *message.shape[2:])
+
+    pf_own, q = lax.optimization_barrier((pf_own, q))
+    q = lax.all_to_all(q, "mem", split_axis=0, concat_axis=0, tiled=True)
+    q, message = lax.optimization_barrier((q, message))
+    message = lax.all_to_all(message, CTX, split_axis=0, concat_axis=0, tiled=True)
+
     pf_own = pf_own.reshape(count * part, -1)
-    pf_oth = swap(pf_own)
     offset = positions[:, None] - frame_start[None, :]
     inside = (offset >= 0) & (offset < FRAME_TOK)
     is_frame = jnp.any(inside, axis=1)
@@ -351,33 +455,29 @@
         here = inside & (local >= 0) & (local < part)
         return jnp.max(jnp.where(here, frames * part + local, -1), axis=1, keepdims=True)
 
-    wide, sent = project_placed(index_of(t), index_of(1 - t), pf_own, pf_oth, proj_weight)
-    came = lax.ppermute(sent, "segment", [(1, 0)])
-    frame_embed = jax.nn.gelu(wide + came.astype(F32), approximate=False).astype(BF16)
-    h = jnp.where(is_frame[:, None], frame_embed, text_embed)
-
+    placed = joined(
+        *project_placed(index_of(t), index_of(1 - t), pf_own, swap(pf_own), proj_weight)
+    )
+    h = jnp.where(is_frame[:, None], placed, text_embed)
+    w_oth = swap(out_weight)
+
+    base = jnp.stack([group * members * rows, t]).astype(jnp.int32)
     results = []
     for tick in range(lax.axis_size("segment")):
-        if tick:
+        if tick == 0:
+            at = jnp.concatenate([base, frame_start])
+            kv_oth = swap(message[:, : rows + FRAME_TOK])
+            attended = attend(at, q, message, kv_oth, frame_start.shape[0])
+        else:
             h = lax.ppermute(h, "segment", [(tick - 1, tick)])
-        h_oth = swap(h)
-        normed, kv = keyvals(tp_index, h, h_oth, gain, kv_weight, kv_cos, kv_sin, groups)
-        kv = kv.reshape(count, rows, HDIM)
-        kv = lax.all_to_all(kv, CTX, split_axis=0, concat_axis=0, tiled=True)
-        kv_own = kv.reshape(count * rows, HDIM)
-        kv_oth = swap(kv_own)
-        q = queries_of(tp_index, normed, q_weight, cosine, sine)
-        kept, given = q[0], swap(q[1])
-        pairs = jnp.where(
-            t == 0, jnp.concatenate([kept, given], 0), jnp.concatenate([given, kept], 0)
-        )
-        pairs = lax.all_to_all(pairs, "mem", split_axis=0, concat_axis=0, tiled=True)
-        at = jnp.stack([group * members * rows, t]).astype(jnp.int32)
-        attended = attend(at, pairs.reshape(members * rows, 2 * HDIM), kv_own, kv_oth)
-        attended = attended.reshape(members, rows, 2 * HDIM)
+            normed, kv = keyvals(tp_index, h, swap(h), gain, kv_weight, *text_kv, groups)
+            kv = kv.reshape(count, rows, HDIM)
+            kv = lax.all_to_all(kv, CTX, split_axis=0, concat_axis=0, tiled=True)
+            q = by_member(queries_of(tp_index, normed, q_weight, *text_q))
+            q = lax.all_to_all(q, "mem", split_axis=0, concat_axis=0, tiled=True)
+            attended = attend(base, q, kv, swap(kv), 0)
         a_own = lax.all_to_all(attended, "mem", split_axis=0, concat_axis=0, tiled=True)
-        a_oth = swap(a_own)
-        h = project_out(tp_index, a_own, a_oth, out_weight, w_oth, h)
+        h = project_out(tp_index, a_own, swap(a_own), out_weight, w_oth, h)
         results.append(h)
     out = results[0]
     for tick in range(1, len(results)):

time: 233 us -> 239 us (1.026)
  waiting for transfers between devices: 64.1 us -> 52.1 us
  starting transfers between devices: 33 us -> 41.1 us
  other arithmetic: 10.7 us -> 15.2 us
  blocking collectives: 38.3 us -> 41.6 us
  Pallas kernels: 57.2 us -> 60.1 us
    ppermute x1 -> x2, waiting for transfers between devices: 18.6 us -> 2.36 us  [joined(): came = lax.ppermute(sent, 'segment', [(1, 0)])]
    all_to_all x1, blocking collectives: 17.2 us -> 31 us  [per_device(): lax.all_to_all(message, CTX, split_axis=0, concat_axis=0, tiled=True)]
    all_to_all x2 -> x1, blocking collectives: 21.1 us -> 10.6 us  [per_device(): lax.all_to_all(attended, 'mem', split_axis=0, concat_axis=0, tiled=True)]
    all_to_all x2 -> x4, starting transfers between devices: 7.71 us -> 16.5 us  [the longest x2 7.33 us: per_device(): q = lax.all_to_all(q, 'mem', split_axis=0, concat_axis=0, tiled=True)]
    all_to_all x2 -> x4, waiting for transfers between devices: 13.1 us -> 19.6 us  [the longest x2 12.2 us: per_device(): q = lax.all_to_all(q, 'mem', split_axis=0, concat_axis=0, tiled=True)]
    ppermute x1 -> x2, starting transfers between devices: 3.1 us -> 8.09 us  [joined(): came = lax.ppermute(sent, 'segment', [(1, 0)])]
    all_to_all x2 -> x1, starting transfers between devices: 8.93 us -> 4.54 us  [per_device(): kv = lax.all_to_all(kv, CTX, split_axis=0, concat_axis=0, tiled=True)]
    dynamic_slice x1, local copies, waits for them, and re-layouts: 4.07 us -> 0.6 us  [per_device(): frame_at = lax.dynamic_index_in_dim(frame_start, ctx, 0, keepdims=False)]
  transfers between devices with their start and end apart: 16 -> 20, of which waited for: 12 -> 11; matrix products, arithmetic and copies ran while one was open for 4% -> 7% of each run, Pallas kernels for 10% -> 15%
where the time goes in v2:
time: 239 us; the launch traced here: 238 us
  Pallas kernels  60.1 us (25%)
  waiting for transfers between devices  52.1 us (22%)
  blocking collectives  41.6 us (17%)
  starting transfers between devices  41.1 us (17%)
  local copies, waits for them, and re-layouts  27.3 us (11%)
  other arithmetic  15.2 us (6%)
    all_to_all x1, blocking collectives, per_device(): lax.all_to_all(message, CTX, split_axis=0, concat_axis=0, tiled=True)  31 us
    ppermute x1, waiting for transfers between devices, per_device(): h = lax.ppermute(h, 'segment', [(tick - 1, tick)])  22.6 us
    unnamed x52, local copies, waits for them, and re-layouts  22.3 us
    pallas_call x2, Pallas kernels, attend(): pl.pallas_call(functools.partial(attend_kernel, frames), grid_spec=pltpu....  20.2 us
    pallas_call x2, Pallas kernels, project_out(): pl.pallas_call(out_kernel, grid_spec=pltpu.PrefetchScalarGridSpec(num_sca...  13.2 us
    all_to_all x2, waiting for transfers between devices, per_device(): q = lax.all_to_all(q, 'mem', split_axis=0, concat_axis=0, tiled=True)  12.2 us
    pallas_call x3, Pallas kernels, queries_of(): pl.pallas_call(q_kernel, grid_spec=pltpu.PrefetchScalarGridSpec(num_scala...  11.1 us
    ppermute x12, starting transfers between devices, swap(): return lax.ppermute(value, 'tp', [(0, 1), (1, 0)])  10.7 us
  transfers between devices with their start and end apart: 20, of which 11 were waited for; matrix products, arithmetic and copies ran while one was open for 7% of the time, Pallas kernels for 15%

profile of v2, /device:TPU:19, one launch (start us, length us, event | category | flops | bytes accessed | tf_op | source)
XLA Modules:
  0.0 237.8 jit_solution(4396857753163985811)
XLA Ops:
  1.7 5.7 %all-to-all-start = ((bf16[8,48,576]{2,1,0:T(8,128)(2,1)}), bf16[8,48,576]{2,1,0:T(8,128)(2,1)}, u32[]{:S(2)}, u32[]{:S(2)}) async-start(bf16[8,48,576]{2,1,0:T(8,128)(2,1)} %broadcast_in_dim.56), calls=%async_computation | async-start | bytes 983040 | tf_op jit(solution)/shard_map/all_to_all | solution.py:420
  28.0 3.2 %shard_map.82 = (bf16[256,3584]{1,0:T(8,128)(2,1)S(1)}, bf16[1,4,256,128]{3,2,1,0:T(8,128)(2,1)S(1)}) custom-call(s32[1]{0:T(128)} %bitcast.tp_ref, bf16[256,1792]{1,0:T(8,128)(2,1)S(1)} %copy-done.9, bf16[256,1792]{1,0:T(8,128)(2,1)S(1)} %collective-permute-done.oth, f32[1,3584]{1,0:T(1,128)S(1)} %copy-done.24, bf16[3584,512]{1,0:T(8,128)(2,1)S(1)} %bitcast.46, ...), custom_call_target="tpu_custom_call" | custom-call | tf_op jit(solution)/shard_map/pallas_call | solution.py:153
  31.2 4.0 %shard_map.83 = bf16[2,2,2,256,128]{4,3,2,1,0:T(8,128)(2,1)S(1)} custom-call(s32[1]{0:T(128)} %bitcast.tp_ref, bf16[256,3584]{1,0:T(8,128)(2,1)S(1)} %get-tuple-element.19.normed, bf16[3584,1024]{1,0:T(8,128)(2,1)S(1)} %bitcast.43, f32[256,128]{1,0:T(8,128)S(1)} %get-tuple-element.45.cos_ref, f32[256,128]{1,0:T(8,128)S(1)} %get-tuple-element.58.sin_ref), custom_call_target="tpu_custom_call" | custom-call | tf_op jit(solution)/shard_map/pallas_call | solution.py:200
  37.6 3.1 %shard_map.86 = bf16[2,2,2,96,128]{4,3,2,1,0:T(8,128)(2,1)S(1)} custom-call(s32[1]{0:T(128)} %bitcast.tp_ref, bf16[96,3584]{1,0:T(8,128)(2,1)S(1)} %get-tuple-element.25.normed, bf16[3584,1024]{1,0:T(8,128)(2,1)S(1)} %bitcast.44, f32[96,128]{1,0:T(8,128)S(1)} %get-tuple-element.49.cos_ref, f32[96,128]{1,0:T(8,128)S(1)} %get-tuple-element.60.sin_ref), custom_call_target="tpu_custom_call" | custom-call | tf_op jit(solution)/shard_map/pallas_call | solution.py:200
  41.6 3.5 %all-to-all-start.1 = ((bf16[4,2,256,128]{3,2,1,0:T(8,128)(2,1)}), bf16[4,2,256,128]{3,2,1,0:T(8,128)(2,1)S(1)}, u32[]{:S(2)}, u32[]{:S(2)}) async-start(bf16[4,2,256,128]{3,2,1,0:T(8,128)(2,1)} %pad_maximum_fusion.1), calls=%async_computation.1 | async-start | bytes 1048576 | tf_op jit(solution)/shard_map/all_to_all | solution.py:443
  46.9 5.7 %all-to-all-done.1.q_ref = bf16[4,2,256,128]{3,2,1,0:T(8,128)(2,1)S(1)} async-done(((bf16[4,2,256,128]{3,2,1,0:T(8,128)(2,1)}), bf16[4,2,256,128]{3,2,1,0:T(8,128)(2,1)S(1)}, u32[]{:S(2)}, u32[]{:S(2)}) %all-to-all-start.1) | async-done | bytes 524320 | tf_op jit(solution)/shard_map/all_to_all | solution.py:443
  53.4 31.0 %all_to_all.35.own = bf16[8,544,128]{2,1,0:T(8,128)(2,1)S(1)} all-to-all(bf16[8,544,128]{2,1,0:T(8,128)(2,1)S(1)} %bitcast.55), channel_id=1, replica_groups=mesh['segment'=2,'grp'=2,'mem'=4,'tp'=2] {'grp','mem'}, dimensions={0} | all-to-all | bytes 2228224 | tf_op jit(solution)/shard_map/all_to_all | solution.py:445
  91.2 5.6 %shard_map.88 = (f32[256,1792]{1,0:T(8,128)S(1)}, bf16[256,1792]{1,0:T(8,128)(2,1)}) custom-call(s32[256,1]{1,0:T(8,128)S(1)} %copy-done.20, s32[256,1]{1,0:T(8,128)S(1)} %copy-done.21, bf16[384,576]{1,0:T(8,128)(2,1)} %bitcast.17.pf_own, bf16[384,576]{1,0:T(8,128)(2,1)} %collective-permute-done.8.pf_oth, bf16[576,1792]{1,0:T(8,128)(2,1)S(1)} %copy-done.8), custom_call_target="tpu_custom_call" | custom-call | tf_op jit(solution)/shard_map/pallas_call | solution.py:65
  98.0 5.2 %collective-permute-start.9 = (bf16[256,1792]{1,0:T(8,128)(2,1)}, bf16[256,1792]{1,0:T(8,128)(2,1)}, u32[]{:S(2)}, u32[]{:S(2)}) collective-permute-start(bf16[256,1792]{1,0:T(8,128)(2,1)} %get-tuple-element.30), channel_id=1, source_target_pairs={{16,0},{17,1},{18,2},{19,3},{20,4},{21,5},{22,6},{23,7},{24,8},{25... | collective-permute-start | bytes 2752520 | tf_op jit(solution)/shard_map/ppermute | solution.py:423
  104.4 12.1 %shard_map.87 = bf16[4,2,256,128]{3,2,1,0:T(8,128)(2,1)} custom-call(s32[10]{0:T(128)S(1)} %pad_add_fusion.1.at_ref, bf16[4,2,256,128]{3,2,1,0:T(8,128)(2,1)S(1)} %copy-done.12, bf16[8,544,128]{2,1,0:T(8,128)(2,1)S(1)} %all_to_all.35.own, bf16[8,352,128]{2,1,0:T(8,128)(2,1)} %collective-permute-done.5.oth), custom_call_target="tpu_custom_call" | custom-call | tf_op jit(solution)/shard_map/pallas_call | solution.py:325
  116.6 3.5 %all-to-all-start.3 = ((bf16[4,2,256,128]{3,2,1,0:T(8,128)(2,1)}), bf16[4,2,256,128]{3,2,1,0:T(8,128)(2,1)S(1)}, u32[]{:S(2)}, u32[]{:S(2)}) async-start(bf16[4,2,256,128]{3,2,1,0:T(8,128)(2,1)} %shard_map.87), calls=%async_computation.3 | async-start | bytes 1048576 | tf_op jit(solution)/shard_map/all_to_all | solution.py:479
  120.1 7.4 %all-to-all-done.3.a_own = bf16[4,2,256,128]{3,2,1,0:T(8,128)(2,1)S(1)} async-done(((bf16[4,2,256,128]{3,2,1,0:T(8,128)(2,1)}), bf16[4,2,256,128]{3,2,1,0:T(8,128)(2,1)S(1)}, u32[]{:S(2)}, u32[]{:S(2)}) %all-to-all-start.3) | async-done | bytes 524320 | tf_op jit(solution)/shard_map/all_to_all | solution.py:479
  129.0 5.7 %fusion.10.h_ref = bf16[256,1792]{1,0:T(8,128)(2,1)S(1)} fusion(bf16[256,1792]{1,0:T(8,128)(2,1)S(1)} %copy-done.10, f32[256,1792]{1,0:T(8,128)} %copy-done.15, bf16[256,1792]{1,0:T(8,128)(2,1)} %collective-permute-done.9, pred[256]{0:T(512)(128)(4,1)S(1)} %fusion.45), kind=kLoop, calls=%fused_computation.22 | loop fusion | flops 31195136 | bytes 4587776 | tf_op jit(solution)/shard_map/jit(_where)/select_n | solution.py:461
  137.8 6.7 %shard_map.89 = bf16[256,1792]{1,0:T(8,128)(2,1)S(1)} custom-call(s32[1]{0:T(128)} %bitcast.tp_ref, bf16[4,2,256,128]{3,2,1,0:T(8,128)(2,1)S(1)} %all-to-all-done.3.a_own, bf16[4,2,256,128]{3,2,1,0:T(8,128)(2,1)S(1)} %collective-permute-done.6.a_oth, bf16[1024,3584]{1,0:T(8,128)(2,1)S(1)} %bitcast.50, bf16[1024,3584]{1,0:T(8,128)(2,1)} %collective-permute-done.7.w_oth, ...), custom_call_target="tpu_custom_call" | custom-call | tf_op jit(solution)/shard_map/pallas_call | solution.py:371
  145.8 22.6 %collective-permute-done.10.own.h_ref = bf16[256,1792]{1,0:T(8,128)(2,1)S(1)} collective-permute-done((bf16[256,1792]{1,0:T(8,128)(2,1)S(1)}, bf16[256,1792]{1,0:T(8,128)(2,1)S(1)}, u32[]{:S(2)}, u32[]{:S(2)}) %collective-permute-start.10) | collective-permute-done | bytes 917536 | tf_op jit(solution)/shard_map/ppermute | solution.py:472
  171.3 3.2 %shard_map.90 = (bf16[256,3584]{1,0:T(8,128)(2,1)S(1)}, bf16[2,4,256,128]{3,2,1,0:T(8,128)(2,1)S(1)}) custom-call(s32[1]{0:T(128)} %bitcast.tp_ref, bf16[256,1792]{1,0:T(8,128)(2,1)S(1)} %collective-permute-done.10.own.h_ref, bf16[256,1792]{1,0:T(8,128)(2,1)S(1)} %collective-permute-done.11.oth, f32[1,3584]{1,0:T(1,128)S(1)} %copy-done.24, ...), custom_call_target="tpu_custom_call" | custom-call | tf_op jit(solution)/shard_map/pallas_call | solution.py:153
  176.6 4.5 %all-to-all-start.5 = ((bf16[8,256,128]{2,1,0:T(8,128)(2,1)}), bf16[8,256,128]{2,1,0:T(8,128)(2,1)S(1)}, u32[]{:S(2)}, u32[]{:S(2)}) async-start(bf16[8,256,128]{2,1,0:T(8,128)(2,1)} %bitcast.52), calls=%async_computation.5 | async-start | bytes 1048576 | tf_op jit(solution)/shard_map/all_to_all | solution.py:475
  181.1 3.1 %copy-done.1 = bf16[1,3584,1024]{2,1,0:T(8,128)(2,1)S(1)} copy-done((bf16[1,3584,1024]{2,1,0:T(8,128)(2,1)S(1)}, bf16[1,3584,1024]{2,1,0:T(8,128)(2,1)}, u32[]{:S(2)}) %copy-start.1) | copy-done | bytes 7340056
  185.7 3.9 %shard_map.91 = bf16[2,2,2,256,128]{4,3,2,1,0:T(8,128)(2,1)S(1)} custom-call(s32[1]{0:T(128)} %bitcast.tp_ref, bf16[256,3584]{1,0:T(8,128)(2,1)S(1)} %copy-done.14, bf16[3584,1024]{1,0:T(8,128)(2,1)S(1)} %bitcast.45, f32[256,128]{1,0:T(8,128)S(1)} %get-tuple-element.45.cos_ref, f32[256,128]{1,0:T(8,128)S(1)} %get-tuple-element.58.sin_ref), custom_call_target="tpu_custom_call" | custom-call | tf_op jit(solution)/shard_map/pallas_call | solution.py:200
  193.5 3.9 %all-to-all-start.4 = ((bf16[4,2,256,128]{3,2,1,0:T(8,128)(2,1)}), bf16[4,2,256,128]{3,2,1,0:T(8,128)(2,1)S(1)}, u32[]{:S(2)}, u32[]{:S(2)}) async-start(bf16[4,2,256,128]{3,2,1,0:T(8,128)(2,1)} %pad_maximum_fusion.2), calls=%async_computation.4 | async-start | bytes 1048576 | tf_op jit(solution)/shard_map/all_to_all | solution.py:477
  198.2 6.5 %all-to-all-done.4.q_ref = bf16[4,2,256,128]{3,2,1,0:T(8,128)(2,1)S(1)} async-done(((bf16[4,2,256,128]{3,2,1,0:T(8,128)(2,1)}), bf16[4,2,256,128]{3,2,1,0:T(8,128)(2,1)S(1)}, u32[]{:S(2)}, u32[]{:S(2)}) %all-to-all-start.4) | async-done | bytes 524320 | tf_op jit(solution)/shard_map/all_to_all | solution.py:477
  204.7 8.1 %shard_map.92 = bf16[4,2,256,128]{3,2,1,0:T(8,128)(2,1)S(1)} custom-call(s32[2]{0:T(128)S(1)} %pad_add_fusion.at_ref, bf16[4,2,256,128]{3,2,1,0:T(8,128)(2,1)S(1)} %all-to-all-done.4.q_ref, bf16[8,256,128]{2,1,0:T(8,128)(2,1)S(1)} %all-to-all-done.5.own, bf16[8,256,128]{2,1,0:T(8,128)(2,1)S(1)} %collective-permute-done.13.oth), custom_call_target="tpu_custom_call" | custom-call | tf_op jit(solution)/shard_map/pallas_call | solution.py:325
  212.8 10.6 %all_to_all.36.a_own = bf16[4,2,256,128]{3,2,1,0:T(8,128)(2,1)S(1)} all-to-all(bf16[4,2,256,128]{3,2,1,0:T(8,128)(2,1)S(1)} %shard_map.92), channel_id=1, replica_groups=mesh['segment'=2,'grp'=2,'mem'=4,'tp'=2] {'mem'}, dimensions={0} | all-to-all | bytes 1048576 | tf_op jit(solution)/shard_map/all_to_all | solution.py:479
  230.2 6.5 %shard_map.93 = bf16[256,1792]{1,0:T(8,128)(2,1)S(1)} custom-call(s32[1]{0:T(128)} %bitcast.tp_ref, bf16[4,2,256,128]{3,2,1,0:T(8,128)(2,1)S(1)} %all_to_all.36.a_own, bf16[4,2,256,128]{3,2,1,0:T(8,128)(2,1)S(1)} %collective-permute-done.14.a_oth, bf16[1024,3584]{1,0:T(8,128)(2,1)S(1)} %bitcast.51, bf16[1024,3584]{1,0:T(8,128)(2,1)} %collective-permute-done.7.w_oth, ...), custom_call_target="tpu_custom_call" | custom-call | tf_op jit(solution)/shard_map/pallas_call | solution.py:371
  (115 shorter events, 62.2 us)
Async XLA Ops:
  1.7 39.9 %all-to-all-start = ((bf16[8,48,576]{2,1,0:T(8,128)(2,1)}), bf16[8,48,576]{2,1,0:T(8,128)(2,1)}, u32[]{:S(2)}, u32[]{:S(2)}) async-start(bf16[8,48,576]{2,1,0:T(8,128)(2,1)} %broadcast_in_dim.56), calls=%async_computation | async-start | bytes 983040 | tf_op jit(solution)/shard_map/all_to_all | solution.py:420
  7.5 18.5 %collective-permute-start = (bf16[256,1792]{1,0:T(8,128)(2,1)}, bf16[256,1792]{1,0:T(8,128)(2,1)S(1)}, u32[]{:S(2)}, u32[]{:S(2)}) collective-permute-start(bf16[256,1792]{1,0:T(8,128)(2,1)} %own.1), channel_id=1, source_target_pairs={{0,1},{1,0},{2,3},{3,2},{4,5},{5,4},{6,7},{7,6},{8,9},{9,8},{10,11... | collective-permute-start | bytes 2752520 | tf_op jit(solution)/shard_map/ppermute | solution.py:31
  12.9 9.6 %collective-permute-start.2 = (bf16[96,1792]{1,0:T(8,128)(2,1)S(1)}, bf16[96,1792]{1,0:T(8,128)(2,1)}, u32[]{:S(2)}, u32[]{:S(2)}) collective-permute-start(bf16[96,1792]{1,0:T(8,128)(2,1)S(1)} %get-tuple-element.23), channel_id=1, source_target_pairs={{16,0},{17,1},{18,2},{19,3},{20,4},{21,5},{22,6},{23,7},{24,8},{25... | collective-permute-start | bytes 1032200 | tf_op jit(solution)/shard_map/ppermute | solution.py:423
  15.8 118.9 %collective-permute-start.7 = (bf16[1024,3584]{1,0:T(8,128)(2,1)}, bf16[1024,3584]{1,0:T(8,128)(2,1)}, u32[]{:S(2)}, u32[]{:S(2)}) collective-permute-start(bf16[1024,3584]{1,0:T(8,128)(2,1)} %bitcast.49), channel_id=1, source_target_pairs={{0,1},{1,0},{2,3},{3,2},{4,5},{5,4},{6,7},{7,6},{8,9},{9,8},{10,11... | collective-permute-start | bytes 22020104 | tf_op jit(solution)/shard_map/ppermute | solution.py:31
  25.1 10.6 %collective-permute-start.3 = (bf16[96,1792]{1,0:T(8,128)(2,1)S(1)}, bf16[96,1792]{1,0:T(8,128)(2,1)S(1)}, u32[]{:S(2)}, u32[]{:S(2)}) collective-permute-start(bf16[96,1792]{1,0:T(8,128)(2,1)S(1)} %fusion.13.own), channel_id=1, source_target_pairs={{0,1},{1,0},{2,3},{3,2},{4,5},{5,4},{6,7},{7,6},{8,9},{9,8},{10,11... | collective-permute-start | bytes 1032200 | tf_op jit(solution)/shard_map/ppermute | solution.py:31
  35.2 5.5 %collective-permute-start.1 = (bf16[2,2,256,128]{3,2,1,0:T(8,128)(2,1)S(1)}, bf16[2,2,256,128]{3,2,1,0:T(8,128)(2,1)S(1)}, u32[]{:S(2)}, u32[]{:S(2)}) collective-permute-start(bf16[2,2,256,128]{3,2,1,0:T(8,128)(2,1)S(1)} %slice_bitcast_fusion.2), channel_id=1, source_target_pairs={{0,1},{1,0},{2,3},{3,2},{4,5},{5,4},{6,7},{7,6},{8,9},{9,8},{10,11... | collective-permute-start | bytes 786440 | tf_op jit(solution)/shard_map/ppermute | solution.py:31
  41.6 10.9 %all-to-all-start.1 = ((bf16[4,2,256,128]{3,2,1,0:T(8,128)(2,1)}), bf16[4,2,256,128]{3,2,1,0:T(8,128)(2,1)S(1)}, u32[]{:S(2)}, u32[]{:S(2)}) async-start(bf16[4,2,256,128]{3,2,1,0:T(8,128)(2,1)} %pad_maximum_fusion.1), calls=%async_computation.1 | async-start | bytes 1048576 | tf_op jit(solution)/shard_map/all_to_all | solution.py:443
  45.1 1.6 collective-permute-start.4
  53.4 36.0 %copy-start.8 = (bf16[576,1792]{1,0:T(8,128)(2,1)S(1)}, bf16[576,1792]{1,0:T(8,128)(2,1)}, u32[]{:S(2)}) copy-start(bf16[576,1792]{1,0:T(8,128)(2,1)} %w_ref.3) | copy-start | bytes 6193156
  85.3 18.0 %collective-permute-start.5 = (bf16[8,352,128]{2,1,0:T(8,128)(2,1)}, bf16[8,352,128]{2,1,0:T(8,128)(2,1)}, u32[]{:S(2)}, u32[]{:S(2)}) collective-permute-start(bf16[8,352,128]{2,1,0:T(8,128)(2,1)} %slice.42), channel_id=1, source_target_pairs={{0,1},{1,0},{2,3},{3,2},{4,5},{5,4},{6,7},{7,6},{8,9},{9,8},{10,11... | collective-permute-start | bytes 2162696 | tf_op jit(solution)/shard_map/ppermute | solution.py:31
  86.5 2.9 %collective-permute-start.8 = (bf16[384,576]{1,0:T(8,128)(2,1)}, bf16[384,576]{1,0:T(8,128)(2,1)}, u32[]{:S(2)}, u32[]{:S(2)}) collective-permute-start(bf16[384,576]{1,0:T(8,128)(2,1)} %bitcast.17.pf_own), channel_id=1, source_target_pairs={{0,1},{1,0},{2,3},{3,2},{4,5},{5,4},{6,7},{7,6},{8,9},{9,8},{10,11... | collective-permute-start | bytes 1327112 | tf_op jit(solution)/shard_map/ppermute | solution.py:31
  98.0 30.9 %collective-permute-start.9 = (bf16[256,1792]{1,0:T(8,128)(2,1)}, bf16[256,1792]{1,0:T(8,128)(2,1)}, u32[]{:S(2)}, u32[]{:S(2)}) collective-permute-start(bf16[256,1792]{1,0:T(8,128)(2,1)} %get-tuple-element.30), channel_id=1, source_target_pairs={{16,0},{17,1},{18,2},{19,3},{20,4},{21,5},{22,6},{23,7},{24,8},{25... | collective-permute-start | bytes 2752520 | tf_op jit(solution)/shard_map/ppermute | solution.py:423
  116.6 10.9 %all-to-all-start.3 = ((bf16[4,2,256,128]{3,2,1,0:T(8,128)(2,1)}), bf16[4,2,256,128]{3,2,1,0:T(8,128)(2,1)S(1)}, u32[]{:S(2)}, u32[]{:S(2)}) async-start(bf16[4,2,256,128]{3,2,1,0:T(8,128)(2,1)} %shard_map.87), calls=%async_computation.3 | async-start | bytes 1048576 | tf_op jit(solution)/shard_map/all_to_all | solution.py:479
  127.5 7.2 %collective-permute-start.6 = (bf16[4,2,256,128]{3,2,1,0:T(8,128)(2,1)S(1)}, bf16[4,2,256,128]{3,2,1,0:T(8,128)(2,1)S(1)}, u32[]{:S(2)}, u32[]{:S(2)}) collective-permute-start(bf16[4,2,256,128]{3,2,1,0:T(8,128)(2,1)S(1)} %all-to-all-done.3.a_own), channel_id=1, source_target_pairs={{0,1},{1,0},{2,3},{3,2},{4,5},{5,4},{6,7},{7,6},{8,9},{9,8},{10,11... | collective-permute-start | bytes 1572872 | tf_op jit(solution)/shard_map/ppermute | solution.py:31
  129.0 42.3 %copy-start.17 = (f32[256,128]{1,0:T(8,128)S(1)}, f32[256,128]{1,0:T(8,128)}, u32[]{:S(2)}) copy-start(f32[256,128]{1,0:T(8,128)} %copy-done.16) | copy-start | bytes 393220
  129.0 42.3 %copy-start.19 = (f32[256,128]{1,0:T(8,128)S(1)}, f32[256,128]{1,0:T(8,128)}, u32[]{:S(2)}) copy-start(f32[256,128]{1,0:T(8,128)} %copy-done.18) | copy-start | bytes 393220
  137.8 33.5 %copy-start.4 = (bf16[1,3584,512]{2,1,0:T(8,128)(2,1)S(1)}, bf16[1,3584,512]{2,1,0:T(8,128)(2,1)}, u32[]{:S(2)}) copy-start(bf16[1,3584,512]{2,1,0:T(8,128)(2,1)} %param.14) | copy-start | bytes 11010052
  144.5 23.9 %collective-permute-start.10 = (bf16[256,1792]{1,0:T(8,128)(2,1)S(1)}, bf16[256,1792]{1,0:T(8,128)(2,1)S(1)}, u32[]{:S(2)}, u32[]{:S(2)}) collective-permute-start(bf16[256,1792]{1,0:T(8,128)(2,1)S(1)} %shard_map.89), channel_id=1, source_target_pairs={{0,16},{1,17},{2,18},{3,19},{4,20},{5,21},{6,22},{7,23},{8,24},{9,... | collective-permute-start | bytes 2752520 | tf_op jit(solution)/shard_map/ppermute | solution.py:472
  168.3 2.9 %collective-permute-start.11 = (bf16[256,1792]{1,0:T(8,128)(2,1)S(1)}, bf16[256,1792]{1,0:T(8,128)(2,1)S(1)}, u32[]{:S(2)}, u32[]{:S(2)}) collective-permute-start(bf16[256,1792]{1,0:T(8,128)(2,1)S(1)} %collective-permute-done.10.own.h_ref), channel_id=1, source_target_pairs={{0,1},{1,0},{2,3},{3,2},{4,5},{5,4},{6,7},{7,6},{8,9},{9,8},{10,11... | collective-permute-start | bytes 2752520 | tf_op jit(solution)/shard_map/ppermute | solution.py:31
  176.6 16.9 %all-to-all-start.5 = ((bf16[8,256,128]{2,1,0:T(8,128)(2,1)}), bf16[8,256,128]{2,1,0:T(8,128)(2,1)S(1)}, u32[]{:S(2)}, u32[]{:S(2)}) async-start(bf16[8,256,128]{2,1,0:T(8,128)(2,1)} %bitcast.52), calls=%async_computation.5 | async-start | bytes 1048576 | tf_op jit(solution)/shard_map/all_to_all | solution.py:475
  189.7 2.2 collective-permute-start.12
  193.5 11.2 %all-to-all-start.4 = ((bf16[4,2,256,128]{3,2,1,0:T(8,128)(2,1)}), bf16[4,2,256,128]{3,2,1,0:T(8,128)(2,1)S(1)}, u32[]{:S(2)}, u32[]{:S(2)}) async-start(bf16[4,2,256,128]{3,2,1,0:T(8,128)(2,1)} %pad_maximum_fusion.2), calls=%async_computation.4 | async-start | bytes 1048576 | tf_op jit(solution)/shard_map/all_to_all | solution.py:477
  197.4 7.4 %collective-permute-start.13 = (bf16[8,256,128]{2,1,0:T(8,128)(2,1)S(1)}, bf16[8,256,128]{2,1,0:T(8,128)(2,1)S(1)}, u32[]{:S(2)}, u32[]{:S(2)}) collective-permute-start(bf16[8,256,128]{2,1,0:T(8,128)(2,1)S(1)} %all-to-all-done.5.own), channel_id=1, source_target_pairs={{0,1},{1,0},{2,3},{3,2},{4,5},{5,4},{6,7},{7,6},{8,9},{9,8},{10,11... | collective-permute-start | bytes 1572872 | tf_op jit(solution)/shard_map/ppermute | solution.py:31
  223.4 3.8 %collective-permute-start.14 = (bf16[4,2,256,128]{3,2,1,0:T(8,128)(2,1)S(1)}, bf16[4,2,256,128]{3,2,1,0:T(8,128)(2,1)S(1)}, u32[]{:S(2)}, u32[]{:S(2)}) collective-permute-start(bf16[4,2,256,128]{3,2,1,0:T(8,128)(2,1)S(1)} %all_to_all.36.a_own), channel_id=1, source_target_pairs={{0,1},{1,0},{2,3},{3,2},{4,5},{5,4},{6,7},{7,6},{8,9},{9,8},{10,11... | collective-permute-start | bytes 1572872 | tf_op jit(solution)/shard_map/ppermute | solution.py:31
  (22 other events, 133.2 us)

commit v3 on v2

--- a/solution.py
+++ b/solution.py
@@ -21,10 +21,16 @@
 F32 = jnp.float32
 BF16 = jnp.bfloat16
 CTX = ("grp", "mem")
+ANY = pl.BlockSpec(memory_space=pl.ANY)
+SMEM = pl.BlockSpec(memory_space=pltpu.SMEM)
+VMEM = pl.BlockSpec(memory_space=pltpu.VMEM)
 
 
 def params(mib):
     return pltpu.CompilerParams(vmem_limit_bytes=mib * MIB)
+
+
+LITTLE = pl.CostEstimate(flops=1, bytes_accessed=1, transcendentals=0)
 
 
 def swap(value):
@@ -42,7 +48,7 @@
     )
 
 
-def place_kernel(idx_own, idx_oth, pf_own, pf_oth, w_ref, wide_ref, sent_ref, placed):
+def place_kernel(after, idx_own, idx_oth, pf_own, pf_oth, w_ref, wide_ref, upper, lower, placed):
     @pl.when(pl.program_id(0) == 0)
     def _():
         rows, count = idx_own.shape[0], pf_own.shape[0]
@@ -55,56 +61,98 @@
 
     term = jnp.dot(placed[...], w_ref[...], preferred_element_type=F32)
     wide_ref[...] = term
-    sent_ref[...] = term.astype(BF16)
-
-
-def project_placed(idx_own, idx_oth, pf_own, pf_oth, proj_weight):
+    half = upper.shape[0]
+    upper[...] = term[:half].astype(BF16)
+    lower[...] = term[half:].astype(BF16)
+
+
+def project_placed(after, idx_own, idx_oth, pf_own, pf_oth, proj_weight):
     rows, (depth, cols) = idx_own.shape[0], proj_weight.shape
-    block = 256
+    block = cols // 2
     whole = lambda i: (0, 0)
     return pl.pallas_call(
         place_kernel,
         grid=(cols // block,),
         in_specs=[
+            ANY,
             pl.BlockSpec(idx_own.shape, whole),
             pl.BlockSpec(idx_oth.shape, whole),
             pl.BlockSpec(pf_own.shape, whole),
             pl.BlockSpec(pf_oth.shape, whole),
             pl.BlockSpec((depth, block), lambda i: (0, i)),
         ],
-        out_specs=[pl.BlockSpec((rows, block), lambda i: (0, i))] * 2,
+        out_specs=[
+            pl.BlockSpec((rows, block), lambda i: (0, i)),
+            *[pl.BlockSpec((rows // 2, block), lambda i: (0, i))] * 2,
+        ],
+        out_shape=[
+            jax.ShapeDtypeStruct((rows, cols), F32),
+            *[jax.ShapeDtypeStruct((rows // 2, cols), BF16)] * 2,
+        ],
+        scratch_shapes=[pltpu.VMEM((rows, depth), BF16)],
+        cost_estimate=LITTLE,
+        compiler_params=params(56),
+    )(after, idx_own, idx_oth, pf_own, pf_oth, proj_weight)
+
+
+def project_kernel(tp_ref, x_ref, w_ref, wide_ref, sent_ref, spread_ref):
+    @pl.when(pl.program_id(0) == 0)
+    def _():
+        part = spread_ref.shape[1]
+        mine = x_ref[pl.ds(pl.multiple_of(tp_ref[0] * part, part), part), :]
+        for c in range(spread_ref.shape[0]):
+            spread_ref[c] = mine
+
+    term = jnp.dot(x_ref[...], w_ref[...], preferred_element_type=F32)
+    wide_ref[...] = term
+    sent_ref[...] = term.astype(BF16)
+
+
+def project(tp_index, values, proj_weight, count):
+    rows, (depth, cols) = values.shape[0], proj_weight.shape
+    block = cols // 2
+    part = rows // 2
+    return pl.pallas_call(
+        project_kernel,
+        grid_spec=pltpu.PrefetchScalarGridSpec(
+            num_scalar_prefetch=1,
+            grid=(cols // block,),
+            in_specs=[
+                pl.BlockSpec((rows, depth), lambda i, t: (0, 0)),
+                pl.BlockSpec((depth, block), lambda i, t: (0, i)),
+            ],
+            out_specs=[
+                pl.BlockSpec((rows, block), lambda i, t: (0, i)),
+                pl.BlockSpec((rows, block), lambda i, t: (0, i)),
+                pl.BlockSpec((count, part, depth), lambda i, t: (0, 0, 0)),
+            ],
+        ),
         out_shape=[
             jax.ShapeDtypeStruct((rows, cols), F32),
             jax.ShapeDtypeStruct((rows, cols), BF16),
+            jax.ShapeDtypeStruct((count, part, depth), BF16),
         ],
-        scratch_shapes=[pltpu.VMEM((rows, depth), BF16)],
-        compiler_params=params(32),
-    )(idx_own, idx_oth, pf_own, pf_oth, proj_weight)
-
-
-def project_kernel(x_ref, w_ref, wide_ref, sent_ref):
-    term = jnp.dot(x_ref[...], w_ref[...], preferred_element_type=F32)
-    wide_ref[...] = term
-    sent_ref[...] = term.astype(BF16)
-
-
-def project(values, proj_weight):
-    rows, (depth, cols) = values.shape[0], proj_weight.shape
-    block = 256
-    return pl.pallas_call(
-        project_kernel,
-        grid=(cols // block,),
+        compiler_params=params(56),
+    )(tp_index, values, proj_weight)
+
+
+def gelu_kernel(after, wide_ref, came_ref, o_ref):
+    total = wide_ref[...] + came_ref[...].astype(F32)
+    o_ref[...] = (0.5 * total * (1.0 + lax.erf(total * math.sqrt(0.5)))).astype(BF16)
+
+
+def gelu_sum(after, wide, came):
+    return pl.pallas_call(
+        gelu_kernel,
         in_specs=[
-            pl.BlockSpec((rows, depth), lambda i: (0, 0)),
-            pl.BlockSpec((depth, block), lambda i: (0, i)),
+            pl.BlockSpec(memory_space=pl.ANY),
+            pl.BlockSpec(memory_space=pltpu.VMEM),
+            pl.BlockSpec(memory_space=pltpu.VMEM),
         ],
-        out_specs=[pl.BlockSpec((rows, block), lambda i: (0, i))] * 2,
-        out_shape=[
-            jax.ShapeDtypeStruct((rows, cols), F32),
-            jax.ShapeDtypeStruct((rows, cols), BF16),
-        ],
-        compiler_params=params(32),
-    )(values, proj_weight)
+        out_specs=pl.BlockSpec(memory_space=pltpu.VMEM),
+        out_shape=jax.ShapeDtypeStruct(wide.shape, BF16),
+        compiler_params=params(16),
+    )(after, wide, came)
 
 
 def rope(values, cosine, sine):
@@ -173,55 +221,152 @@
             jax.ShapeDtypeStruct((rows, depth), BF16),
             jax.ShapeDtypeStruct((groups, cols // HDIM, rows, HDIM), BF16),
         ],
-        compiler_params=params(32),
+        compiler_params=params(56),
     )(tp_index, own, oth, gain, kv_weight, cosine, sine)
 
 
-def q_kernel(tp_ref, normed, w_ref, cos_ref, sin_ref, q_ref):
+def q_kernel(tp_ref, *refs):
+    normed, w_ref, cos_ref, sin_ref, kept_ref, given_ref = refs[-6:]
     wide = jnp.dot(normed[...], w_ref[...], preferred_element_type=F32)
-    for h in range(wide.shape[1] // HDIM):
-        at = slice(h * HDIM, (h + 1) * HDIM)
-        q_ref[0, 0, h] = rope(wide[:, at], cos_ref[...], sin_ref[...]).astype(BF16)
-
-
-def queries_of(tp_index, normed, q_weight, cosine, sine):
+    first = tp_ref[0] == 0
+    for h in range(2):
+        heads = []
+        for u in range(2):
+            lower = (2 * u + h) * HDIM
+            heads.append(rope(wide[:, lower : lower + HDIM], cos_ref[...], sin_ref[...]))
+        kept_ref[0, h] = jnp.where(first, heads[0], heads[1]).astype(BF16)
+        given_ref[0, h] = jnp.where(first, heads[1], heads[0]).astype(BF16)
+
+
+def queries_of(tp_index, normed, q_weight, cosine, sine, *after):
     rows, depth = normed.shape
     cols = q_weight.shape[1]
-    block = 2 * HDIM
-    pairs = cols // block
+    block = 4 * HDIM
+    steps = cols // block
     whole = lambda i, t: (0, 0)
-    half = pairs // 2
-
-    def column(i, t):
-        kept = 1 - i // half
-        core = jnp.where(kept == 1, t[0], 1 - t[0])
-        return (0, 2 * (i % half) + core)
-
     return pl.pallas_call(
         q_kernel,
         grid_spec=pltpu.PrefetchScalarGridSpec(
             num_scalar_prefetch=1,
-            grid=(pairs,),
+            grid=(steps,),
             in_specs=[
+                *[ANY] * len(after),
                 pl.BlockSpec(normed.shape, whole),
-                pl.BlockSpec((depth, block), column),
+                pl.BlockSpec((depth, block), lambda i, t: (0, i)),
                 pl.BlockSpec(cosine.shape, whole),
                 pl.BlockSpec(sine.shape, whole),
             ],
-            out_specs=pl.BlockSpec(
-                (1, 1, 2, rows, HDIM), lambda i, t: (i // half, i % half, 0, 0, 0)
-            ),
+            out_specs=[pl.BlockSpec((1, 2, rows, HDIM), lambda i, t: (i, 0, 0, 0))] * 2,
         ),
-        out_shape=jax.ShapeDtypeStruct((2, half, 2, rows, HDIM), BF16),
+        out_shape=[jax.ShapeDtypeStruct((steps, 2, rows, HDIM), BF16)] * 2,
+        cost_estimate=LITTLE,
+        compiler_params=params(56),
+    )(tp_index, *after, normed, q_weight, cosine, sine)
+
+
+def route_kernel(at_ref, kept, given, *outs):
+    core, me = at_ref[1], at_ref[2]
+    for d, out in enumerate(outs):
+        to = jnp.bitwise_xor(me, d)
+        mine = jnp.right_shift(to, 1) == core
+        low = jnp.bitwise_and(to, 1)
+
+        @pl.when(mine)
+        def _():
+            out[...] = kept[low]
+
+        @pl.when(jnp.logical_not(mine))
+        def _():
+            out[...] = given[low]
+
+
+def route(at, kept, given):
+    return pl.pallas_call(
+        route_kernel,
+        in_specs=[SMEM, VMEM, VMEM],
+        out_specs=[VMEM] * KV_HEADS,
+        out_shape=[jax.ShapeDtypeStruct(kept.shape[1:], BF16)] * KV_HEADS,
+        cost_estimate=LITTLE,
+        compiler_params=params(16),
+    )(at, kept, given)
+
+
+def pack_kernel(at_ref, after, kv, f_kv, f_kept, f_given, out):
+    rows, more = kv.shape[2], f_kv.shape[2]
+    for g in range(out.shape[0]):
+        for j in range(KV_HEADS):
+            out[g, j, :rows] = kv[0, j]
+            out[g, j, rows : rows + more] = f_kv[0, j]
+
+    def heads(first, second):
+        for g in range(out.shape[0]):
+            for j in range(KV_HEADS):
+                source = (first if j < 2 else second)[j % 2]
+                for h in range(2):
+                    lower = rows + (1 + h) * more
+                    out[g, j, lower : lower + more] = source[h]
+
+    @pl.when(at_ref[1] == 0)
+    def _():
+        heads(f_kept, f_given)
+
+    @pl.when(at_ref[1] == 1)
+    def _():
+        heads(f_given, f_kept)
+
+
+def pack(at, after, kv, f_kv, f_kept, f_given, groups):
+    rows = kv.shape[2] + 3 * f_kv.shape[2]
+    return pl.pallas_call(
+        pack_kernel,
+        in_specs=[SMEM, ANY, VMEM, VMEM, VMEM, VMEM],
+        out_specs=VMEM,
+        out_shape=jax.ShapeDtypeStruct((groups, KV_HEADS, rows, HDIM), BF16),
         compiler_params=params(32),
-    )(tp_index, normed, q_weight, cosine, sine)
+    )(at, after, kv, f_kv, f_kept, f_given)
+
+
+def gate_kernel(*refs):
+    pass
+
+
+def gate(value, *after):
+    return pl.pallas_call(
+        gate_kernel,
+        in_specs=[ANY] * (1 + len(after)),
+        out_specs=ANY,
+        out_shape=jax.ShapeDtypeStruct(value.shape, value.dtype),
+        input_output_aliases={0: 0},
+        compiler_params=params(16),
+    )(value, *after)
+
+
+def half_kernel(tp_ref, after, w_ref, o_ref):
+    o_ref[...] = w_ref[...]
+
+
+def other_columns(tp_index, after, weight):
+    depth, cols = weight.shape
+    block = depth // 2
+    return pl.pallas_call(
+        half_kernel,
+        grid_spec=pltpu.PrefetchScalarGridSpec(
+            num_scalar_prefetch=1,
+            grid=(2,),
+            in_specs=[ANY, pl.BlockSpec((block, cols // 2), lambda i, t: (i, 1 - t[0]))],
+            out_specs=pl.BlockSpec((block, cols // 2), lambda i, t: (i, 0)),
+        ),
+        out_shape=jax.ShapeDtypeStruct((depth, cols // 2), BF16),
+        cost_estimate=LITTLE,
+        compiler_params=params(56),
+    )(tp_index, after, weight)
 
 
 BK = 512
 PAD = 128
 
 
-def place(target, lanes, start, block):
+def shifted_rows(start, block):
     window = FRAME_TOK + 16
     first = pl.multiple_of((start // 16) * 16, 16)
     shift = start - first
@@ -229,18 +374,23 @@
     c = lax.broadcasted_iota(jnp.int32, (window, FRAME_TOK), 1)
     hot = jnp.where(r - c == shift, 1.0, 0.0).astype(BF16)
     moved = jnp.dot(hot, block, preferred_element_type=F32)
-    row = lax.broadcasted_iota(jnp.int32, moved.shape, 0)
+    row = lax.broadcasted_iota(jnp.int32, (window, HDIM), 0)
     inside = (row >= shift) & (row < shift + FRAME_TOK)
-    at = pl.ds(first, window)
+    return pl.ds(first, window), inside, moved
+
+
+def merge(target, at, lanes, inside, moved):
     kept = target[at, lanes].astype(F32)
     target[at, lanes] = jnp.where(inside, moved, kept).astype(BF16)
 
 
-def attend_kernel(frames, at_ref, q_ref, own, oth, o_ref, keys, vals, qs):
-    members, heads, rows, _ = q_ref.shape
+def attend_kernel(frames, skip, at_ref, *refs):
+    refs = refs[skip:]
+    pieces, (own, oth, o_ref, keys, vals, qs) = refs[:-6], refs[-6:]
+    members, heads, rows, _ = o_ref.shape
     count = own.shape[0]
-    base, core = at_ref[0], at_ref[1]
-    every, low = slice(None), slice(0, HDIM)
+    base, core, me = at_ref[0], at_ref[1], at_ref[2]
+    every, low, high = slice(None), slice(0, HDIM), slice(HDIM, 2 * HDIM)
     vals[:, HDIM:] = jnp.ones((vals.shape[0], HDIM), BF16)
 
     def fill(k_from, v_from):
@@ -250,12 +400,14 @@
         if frames:
 
             def one(f, carry):
-                start = at_ref[2 + f]
-                place(keys, every, start, k_from[f, rows : rows + FRAME_TOK, :])
-                place(vals, low, start, v_from[f, rows : rows + FRAME_TOK, :])
+                lines = slice(rows, rows + FRAME_TOK)
+                both = jnp.concatenate([k_from[f, lines, :], v_from[f, lines, :]], axis=1)
+                at, inside, moved = shifted_rows(at_ref[3 + f], both)
+                merge(keys, at, every, inside, moved[:, low])
+                merge(vals, at, low, inside, moved[:, high])
                 return carry
 
-            lax.fori_loop(0, frames, one, 0)
+            lax.fori_loop(0, frames, one, 0, unroll=8 if frames % 8 == 0 else 1)
 
     @pl.when(core == 0)
     def _():
@@ -266,23 +418,26 @@
         fill(oth, own)
 
     for h in range(heads):
-        for c in range(members):
-            qs[h, PAD + c * rows : PAD + (c + 1) * rows, :] = q_ref[c, h]
+        for d in range(members):
+            slot = jnp.bitwise_xor(me, d)
+            qs[h, pl.ds(pl.multiple_of(PAD + slot * rows, PAD), rows), :] = pieces[d][h]
     if frames:
 
         def one(f, carry):
-            start = at_ref[2 + f] - base
-
-            @pl.when((start > -FRAME_TOK) & (start < members * rows))
-            def _():
-                for h in range(heads):
-                    lower = rows + (1 + h) * FRAME_TOK
-                    block = own[f, lower : lower + FRAME_TOK, :]
-                    place(qs.at[h], every, start + PAD, block)
-
+            start = at_ref[3 + f] - base
+            here = (start > -FRAME_TOK) & (start < members * rows)
+            start = jnp.where(here, start + PAD, members * rows + 2 * PAD)
+            lower = rows + FRAME_TOK
+            both = jnp.concatenate(
+                [own[f, lower + h * FRAME_TOK : lower + (h + 1) * FRAME_TOK, :] for h in range(2)],
+                axis=1,
+            )
+            at, inside, moved = shifted_rows(start, both)
+            merge(qs.at[0], at, every, inside, moved[:, low])
+            merge(qs.at[1], at, every, inside, moved[:, high])
             return carry
 
-        lax.fori_loop(0, frames, one, 0)
+        lax.fori_loop(0, frames, one, 0, unroll=8 if frames % 8 == 0 else 1)
 
     chains = [(h, c) for c in range(members) for h in range(heads)]
 
@@ -317,34 +472,37 @@
         o_ref[c, h] = (acc[:, :HDIM] / acc[:, HDIM:]).astype(BF16)
 
 
-def attend(at, q, own, oth, frames):
-    members, heads, rows, _ = q.shape
+def attend(at, pieces, own, oth, frames, *after):
+    heads, rows, _ = pieces[0].shape[-3:]
+    members = KV_HEADS
     span = own.shape[0] * rows
-    whole = lambda i, t: (0, 0, 0)
-    four = lambda i, t: (0, 0, 0, 0)
-    return pl.pallas_call(
-        functools.partial(attend_kernel, frames),
+    zeros = lambda value: pl.BlockSpec(value.shape, lambda i, t: (0,) * value.ndim)
+    shape = (members, heads, rows, HDIM)
+    return pl.pallas_call(
+        functools.partial(attend_kernel, frames, len(after)),
         grid_spec=pltpu.PrefetchScalarGridSpec(
             num_scalar_prefetch=1,
             grid=(1,),
             in_specs=[
-                pl.BlockSpec(q.shape, four),
-                pl.BlockSpec(own.shape, whole),
-                pl.BlockSpec(oth.shape, whole),
-            ],
-            out_specs=pl.BlockSpec(q.shape, four),
+                *[ANY] * len(after),
+                *[zeros(value) for value in (*pieces, own, oth)],
+            ],
+            out_specs=pl.BlockSpec(shape, lambda i, t: (0, 0, 0, 0)),
             scratch_shapes=[
                 pltpu.VMEM((span + PAD, HDIM), BF16),
                 pltpu.VMEM((span + PAD, 2 * HDIM), BF16),
-                pltpu.VMEM((heads, members * rows + 2 * PAD, HDIM), BF16),
+                pltpu.VMEM((heads, members * rows + 3 * PAD, HDIM), BF16),
             ],
         ),
-        out_shape=jax.ShapeDtypeStruct(q.shape, BF16),
+        out_shape=jax.ShapeDtypeStruct(shape, BF16),
         compiler_params=params(40),
-    )(at, q, own, oth)
-
-
-def out_kernel(tp_ref, a_own, a_oth, w_own, w_oth, h_ref, o_ref, near, far):
+    )(at, *after, *pieces, own, oth)
+
+
+def out_kernel(placing, tp_ref, a_own, a_oth, w_own, w_oth, *refs):
+    near, far = refs[-2:]
+    o_ref = refs[-3]
+
     @pl.when(pl.program_id(0) == 0)
     def _():
         t = tp_ref[0]
@@ -357,35 +515,49 @@
                 far[:, pl.ds(mine, HDIM)] = a_own[2 * (1 - t) + jj, h]
                 far[:, pl.ds(theirs, HDIM)] = a_oth[2 * (1 - t) + jj, h]
 
+    if placing:
+        text, wide, upper, lower, is_frame = refs[:5]
+        came = jnp.concatenate([upper[...], lower[...]], axis=0)
+        total = wide[...] + came.astype(F32)
+        gelu = 0.5 * total * (1.0 + lax.erf(total * math.sqrt(0.5)))
+        h = jnp.where(is_frame[...] > 0, gelu.astype(BF16).astype(F32), text[...].astype(F32))
+    else:
+        h = refs[0][...].astype(F32)
     first = jnp.dot(near[...], w_own[...], preferred_element_type=F32)
     second = jnp.dot(far[...], w_oth[...], preferred_element_type=F32)
-    o_ref[...] = (h_ref[...].astype(F32) + (first + second)).astype(BF16)
-
-
-def project_out(tp_index, a_own, a_oth, w_own, w_oth, h):
-    rows, cols = h.shape
+    o_ref[...] = (h + (first + second)).astype(BF16)
+
+
+def project_out(tp_index, a_own, a_oth, w_own, w_oth, *residual):
+    rows, cols = residual[0].shape
     depth = w_own.shape[0]
-    block = 256
-    steps = cols // block
+    steps = 2
+    block = cols // steps
     four = lambda i, t: (0, 0, 0, 0)
-    return pl.pallas_call(
-        out_kernel,
+    mine = lambda i, t: (0, t[0] * steps + i)
+    return pl.pallas_call(
+        functools.partial(out_kernel, len(residual) > 1),
         grid_spec=pltpu.PrefetchScalarGridSpec(
             num_scalar_prefetch=1,
             grid=(steps,),
             in_specs=[
                 pl.BlockSpec(a_own.shape, four),
                 pl.BlockSpec(a_oth.shape, four),
-                pl.BlockSpec((depth, block), lambda i, t: (0, t[0] * steps + i)),
-                pl.BlockSpec((depth, block), lambda i, t: (0, t[0] * steps + i)),
-                pl.BlockSpec((rows, block), lambda i, t: (0, i)),
+                pl.BlockSpec((depth, block), mine),
+                pl.BlockSpec((depth, block), lambda i, t: (0, i)),
+                *[
+                    pl.BlockSpec((value.shape[0], block), lambda i, t: (0, i))
+                    if value.shape[1] == cols
+                    else pl.BlockSpec(value.shape, lambda i, t: (0, 0))
+                    for value in residual
+                ],
             ],
             out_specs=pl.BlockSpec((rows, block), lambda i, t: (0, i)),
             scratch_shapes=[pltpu.VMEM((rows, depth), BF16)] * 2,
         ),
         out_shape=jax.ShapeDtypeStruct((rows, cols), BF16),
-        compiler_params=params(32),
-    )(tp_index, a_own, a_oth, w_own, w_oth, h)
+        compiler_params=params(56),
+    )(tp_index, a_own, a_oth, w_own, w_oth, *residual)
 
 
 def per_device(
@@ -414,40 +586,37 @@
     text_kv, text_q = tables(positions)
     frame_kv, frame_q = tables(frame_at + jnp.arange(FRAME_TOK, dtype=jnp.int32))
 
-    part = patch_feats.shape[0] // 2
-    mine = lax.dynamic_slice_in_dim(patch_feats, t * part, part, 0)
-    spread = jnp.broadcast_to(mine[None], (count, *mine.shape))
+    me = lax.axis_index("mem")
+
+    def from_vision(sent):
+        return lax.ppermute(sent, "segment", [(1, 0)])
+
+    base = jnp.stack([group * members * rows, t, me]).astype(jnp.int32)
+
+    def spread_heads(kept, given):
+        pieces = route(base, kept, swap(given))
+        return [pieces[0]] + [
+            lax.ppermute(pieces[d], "mem", [(i, i ^ d) for i in range(KV_HEADS)])
+            for d in range(1, KV_HEADS)
+        ]
+
+    wide, sent, spread = project(tp_index, patch_feats, proj_weight, count)
+    came = from_vision(sent)
     pf_own = lax.all_to_all(spread, CTX, split_axis=0, concat_axis=0, tiled=True)
 
-    def joined(wide, sent):
-        came = lax.ppermute(sent, "segment", [(1, 0)])
-        return jax.nn.gelu(wide + came.astype(F32), approximate=False).astype(BF16)
-
-    def by_member(q):
-        kept, given = q[0], swap(q[1])
-        first = jnp.where(t == 0, kept, given)
-        second = jnp.where(t == 0, given, kept)
-        return jnp.concatenate([first, second], 0)
-
-    frame_embed = joined(*project(patch_feats, proj_weight))
-
     normed, kv = keyvals(tp_index, text_embed, swap(text_embed), gain, kv_weight, *text_kv, 1)
-    q = by_member(queries_of(tp_index, normed, q_weight, *text_q))
+    frame_embed = gelu_sum(kv, wide, came)
     f_normed, f_kv = keyvals(tp_index, frame_embed, swap(frame_embed), gain, kv_weight, *frame_kv, 1)
-    f_q = by_member(queries_of(tp_index, f_normed, q_weight, *frame_q))
-    message = jnp.concatenate([kv[0], f_kv[0], f_q[:, 0], f_q[:, 1]], axis=1)
-    message = jnp.broadcast_to(message[None], (groups, *message.shape))
-    message = message.reshape(count, *message.shape[2:])
-
-    pf_own, q = lax.optimization_barrier((pf_own, q))
-    q = lax.all_to_all(q, "mem", split_axis=0, concat_axis=0, tiled=True)
-    q, message = lax.optimization_barrier((q, message))
+    f_kept, f_given = queries_of(tp_index, f_normed, q_weight, *frame_q)
+    packed = pack(base, pf_own, kv, f_kv, f_kept, swap(f_given), groups)
+    message = packed.reshape(count, *packed.shape[2:])
     message = lax.all_to_all(message, CTX, split_axis=0, concat_axis=0, tiled=True)
 
+    part = pf_own.shape[1]
     pf_own = pf_own.reshape(count * part, -1)
     offset = positions[:, None] - frame_start[None, :]
     inside = (offset >= 0) & (offset < FRAME_TOK)
-    is_frame = jnp.any(inside, axis=1)
+    is_frame = jnp.any(inside, axis=1, keepdims=True).astype(jnp.int32)
     frames = jnp.arange(frame_start.shape[0], dtype=jnp.int32)[None, :]
 
     def index_of(core):
@@ -455,29 +624,31 @@
         here = inside & (local >= 0) & (local < part)
         return jnp.max(jnp.where(here, frames * part + local, -1), axis=1, keepdims=True)
 
-    placed = joined(
-        *project_placed(index_of(t), index_of(1 - t), pf_own, swap(pf_own), proj_weight)
+    wide, *sent = project_placed(
+        packed, index_of(t), index_of(1 - t), pf_own, swap(pf_own), proj_weight
     )
-    h = jnp.where(is_frame[:, None], placed, text_embed)
-    w_oth = swap(out_weight)
-
-    base = jnp.stack([group * members * rows, t]).astype(jnp.int32)
+    placed = [from_vision(half) for half in sent]
+    pieces = spread_heads(*queries_of(tp_index, normed, q_weight, *text_q, *sent))
     results = []
     for tick in range(lax.axis_size("segment")):
         if tick == 0:
             at = jnp.concatenate([base, frame_start])
-            kv_oth = swap(message[:, : rows + FRAME_TOK])
-            attended = attend(at, q, message, kv_oth, frame_start.shape[0])
+            message = gate(message, *placed, *pieces[1:])
+            w_given = other_columns(tp_index, sent[0], out_weight)
+            w_oth = swap(w_given)
+            attended = attend(at, pieces, message, swap(message), frame_start.shape[0], w_given)
+            residual = (text_embed, wide, *placed, is_frame)
         else:
             h = lax.ppermute(h, "segment", [(tick - 1, tick)])
             normed, kv = keyvals(tp_index, h, swap(h), gain, kv_weight, *text_kv, groups)
             kv = kv.reshape(count, rows, HDIM)
             kv = lax.all_to_all(kv, CTX, split_axis=0, concat_axis=0, tiled=True)
-            q = by_member(queries_of(tp_index, normed, q_weight, *text_q))
-            q = lax.all_to_all(q, "mem", split_axis=0, concat_axis=0, tiled=True)
-            attended = attend(base, q, kv, swap(kv), 0)
+            pieces = spread_heads(*queries_of(tp_index, normed, q_weight, *text_q))
+            kv = gate(kv, *pieces[1:])
+            attended = attend(base, pieces, kv, swap(kv), 0)
+            residual = (h,)
         a_own = lax.all_to_all(attended, "mem", split_axis=0, concat_axis=0, tiled=True)
-        h = project_out(tp_index, a_own, swap(a_own), out_weight, w_oth, h)
+        h = project_out(tp_index, a_own, swap(a_own), out_weight, w_oth, *residual)
         results.append(h)
     out = results[0]
     for tick in range(1, len(results)):

time: 239 us -> 212 us (0.89)
  blocking collectives: 41.6 us -> 21.1 us
  Pallas kernels: 60.1 us -> 78.2 us
  local copies, waits for them, and re-layouts: 27.3 us -> 13.8 us
  other arithmetic: 15.2 us -> 6.41 us
    all_to_all x1 -> x0, blocking collectives: 31 us -> none  [per_device(): lax.all_to_all(message, CTX, split_axis=0, concat_axis=0, tiled=True)]
    all_to_all x3 -> x1, waiting for transfers between devices: 19.6 us -> 0.01 us  [per_device(): lax.all_to_all(message, CTX, split_axis=0, concat_axis=0, tiled=True)]
    ppermute x2 -> x9, waiting for transfers between devices: 2.36 us -> 18.5 us  [the longest x6 11.3 us: spread_heads(): lax.ppermute(pieces[d], 'mem', [(i, i ^ d) for i in range(KV_HEADS)])]
    unnamed x52 -> x50, local copies, waits for them, and re-layouts: 22.3 us -> 10.8 us
    all_to_all x1 -> x2, blocking collectives: 10.6 us -> 21.1 us  [per_device(): lax.all_to_all(attended, 'mem', split_axis=0, concat_axis=0, tiled=True)]
    pallas_call x3, Pallas kernels: 8.31 us -> 16.1 us  [keyvals(): pl.pallas_call(kv_kernel, grid_spec=pltpu.PrefetchScalarGridSpec(num_scal...]
    select_n x4 -> x0, other arithmetic: 5.83 us -> none  [the longest x1 5.7 us: per_device(): h = jnp.where(is_frame[:, None], placed, text_embed)]
    pallas_call x3, Pallas kernels: 11.1 us -> 16.7 us  [queries_of(): pl.pallas_call(q_kernel, grid_spec=pltpu.PrefetchScalarGridSpec(num_scala...]
  transfers between devices with their start and end apart: 20 -> 25, of which waited for: 11 -> 15; matrix products, arithmetic and copies ran while one was open for 7% -> 3% of each run, Pallas kernels for 15% -> 23%
where the time goes in v3:
time: 212 us; the launch traced here: 211 us
  Pallas kernels  78.2 us (37%)
  waiting for transfers between devices  52 us (25%)
  starting transfers between devices  39.6 us (19%)
  blocking collectives  21.1 us (10%)
  local copies, waits for them, and re-layouts  13.8 us (7%)
  other arithmetic  6.41 us (3%)
    ppermute x1, waiting for transfers between devices, per_device(): h = lax.ppermute(h, 'segment', [(tick - 1, tick)])  22.6 us
    all_to_all x2, blocking collectives, per_device(): lax.all_to_all(attended, 'mem', split_axis=0, concat_axis=0, tiled=True)  21.1 us
    pallas_call x2, Pallas kernels, attend(): pl.pallas_call(functools.partial(attend_kernel, frames, len(after)), grid...  17.5 us
    pallas_call x3, Pallas kernels, queries_of(): pl.pallas_call(q_kernel, grid_spec=pltpu.PrefetchScalarGridSpec(num_scala...  16.7 us
    pallas_call x3, Pallas kernels, keyvals(): pl.pallas_call(kv_kernel, grid_spec=pltpu.PrefetchScalarGridSpec(num_scal...  16.1 us
    pallas_call x2, Pallas kernels, project_out(): pl.pallas_call(functools.partial(out_kernel, len(residual) > 1), grid_spe...  14 us
    ppermute x6, waiting for transfers between devices, spread_heads(): lax.ppermute(pieces[d], 'mem', [(i, i ^ d) for i in range(KV_HEADS)])  11.3 us
    ppermute x12, starting transfers between devices, swap(): return lax.ppermute(value, 'tp', [(0, 1), (1, 0)])  11.3 us
  transfers between devices with their start and end apart: 25, of which 15 were waited for; matrix products, arithmetic and copies ran while one was open for 3% of the time, Pallas kernels for 23%

profile of v3, /device:TPU:19, one launch (start us, length us, event | category | flops | bytes accessed | tf_op | source)
XLA Modules:
  0.0 211.4 jit_solution(7335283530772141203)
XLA Ops:
  0.7 2.8 %shard_map.82 = (f32[96,1792]{1,0:T(8,128)}, bf16[96,1792]{1,0:T(8,128)(2,1)}, bf16[8,48,576]{2,1,0:T(8,128)(2,1)}) custom-call(s32[1]{0:T(128)} %bitcast.tp_ref, bf16[96,576]{1,0:T(8,128)(2,1)} %x_ref.1, bf16[576,1792]{1,0:T(8,128)(2,1)} %w_ref.3), custom_call_target="tpu_custom_call" | custom-call | tf_op jit(solution)/shard_map/pallas_call | solution.py:115
  5.7 5.6 %all-to-all-start = ((bf16[8,48,576]{2,1,0:T(8,128)(2,1)}), bf16[8,48,576]{2,1,0:T(8,128)(2,1)S(1)}, u32[]{:S(2)}, u32[]{:S(2)}) async-start(bf16[8,48,576]{2,1,0:T(8,128)(2,1)} %get-tuple-element.31), calls=%async_computation | async-start | bytes 983040 | tf_op jit(solution)/shard_map/all_to_all | solution.py:605
  15.6 6.1 %shard_map.83 = (bf16[256,3584]{1,0:T(8,128)(2,1)}, bf16[1,4,256,128]{3,2,1,0:T(8,128)(2,1)}) custom-call(s32[1]{0:T(128)} %bitcast.tp_ref, bf16[256,1792]{1,0:T(8,128)(2,1)} %refs_0_.1, bf16[256,1792]{1,0:T(8,128)(2,1)} %copy-done.17, f32[1,3584]{1,0:T(1,128)} %gain.5, bf16[3584,512]{1,0:T(8,128)(2,1)} %bitcast.23, f32[256,128]{1,0:T(8,128)} %get-tuple-element.62.cos_ref, ...), custom_call_target="tpu_custom_call" | custom-call | tf_op jit(solution)/shard_map/pallas_call | solution.py:201
  25.8 3.9 %shard_map.85 = (bf16[96,3584]{1,0:T(8,128)(2,1)}, bf16[1,4,96,128]{3,2,1,0:T(8,128)(2,1)}) custom-call(s32[1]{0:T(128)} %bitcast.tp_ref, bf16[96,1792]{1,0:T(8,128)(2,1)} %copy-done.4, bf16[96,1792]{1,0:T(8,128)(2,1)} %copy-done.23, f32[1,3584]{1,0:T(1,128)} %gain.5, bf16[3584,512]{1,0:T(8,128)(2,1)} %bitcast.24, f32[96,128]{1,0:T(8,128)} %get-tuple-element.66.cos_ref, ...), custom_call_target="tpu_custom_call" | custom-call | tf_op jit(solution)/shard_map/pallas_call | solution.py:201
  29.7 4.9 %shard_map.86 = (bf16[2,2,96,128]{3,2,1,0:T(8,128)(2,1)}, bf16[2,2,96,128]{3,2,1,0:T(8,128)(2,1)}) custom-call(s32[1]{0:T(128)} %bitcast.tp_ref, bf16[96,3584]{1,0:T(8,128)(2,1)} %get-tuple-element.36.refs_0_, bf16[3584,1024]{1,0:T(8,128)(2,1)} %bitcast.20, f32[96,128]{1,0:T(8,128)} %get-tuple-element.65.refs_2_, f32[96,128]{1,0:T(8,128)} %get-tuple-element.76.refs_3_), custom_call_target="tpu_custom_call" | custom-call | flops 1 | bytes 1 | tf_op jit(solution)/shard_map/pallas_call | solution.py:247
  38.8 5.4 %all-to-all-start.1 = ((bf16[8,544,128]{2,1,0:T(8,128)(2,1)}), bf16[8,544,128]{2,1,0:T(8,128)(2,1)S(1)}, u32[]{:S(2)}, u32[]{:S(2)}) async-start(bf16[8,544,128]{2,1,0:T(8,128)(2,1)} %bitcast.10), calls=%async_computation.1 | async-start | bytes 2228224 | tf_op jit(solution)/shard_map/all_to_all | solution.py:613
  47.7 4.4 %shard_map.88 = (f32[256,1792]{1,0:T(8,128)}, bf16[128,1792]{1,0:T(8,128)(2,1)}, bf16[128,1792]{1,0:T(8,128)(2,1)}) custom-call(bf16[2,4,544,128]{3,2,1,0:T(8,128)(2,1)} %shard_map.87.after, s32[256,1]{1,0:T(8,128)} %copy.14.idx_own, s32[256,1]{1,0:T(8,128)} %copy.15.idx_oth, bf16[384,576]{1,0:T(8,128)(2,1)} %bitcast.16, bf16[384,576]{1,0:T(8,128)(2,1)} %copy-done.21, ...), custom_call_target="tpu_custom_call" | custom-call | flops 1 | bytes 1 | tf_op jit(solution)/shard_map/pallas_call | solution.py:73
  52.1 3.4 %shard_map.89.refs_0_ = bf16[1024,1792]{1,0:T(8,128)(2,1)} custom-call(s32[1]{0:T(128)} %bitcast.tp_ref, bf16[128,1792]{1,0:T(8,128)(2,1)} %get-tuple-element.39.after.refs_0_, bf16[1024,3584]{1,0:T(8,128)(2,1)} %bitcast.17), custom_call_target="tpu_custom_call" | custom-call | flops 1 | bytes 1 | tf_op jit(solution)/shard_map/pallas_call | solution.py:351
  55.7 5.9 %shard_map.90 = (bf16[2,2,256,128]{3,2,1,0:T(8,128)(2,1)}, bf16[2,2,256,128]{3,2,1,0:T(8,128)(2,1)}) custom-call(s32[1]{0:T(128)} %bitcast.tp_ref, bf16[128,1792]{1,0:T(8,128)(2,1)} %get-tuple-element.39.after.refs_0_, bf16[128,1792]{1,0:T(8,128)(2,1)} %get-tuple-element.40.refs_1_, bf16[256,3584]{1,0:T(8,128)(2,1)} %get-tuple-element.41.refs_2_, ...), custom_call_target="tpu_custom_call" | custom-call | flops 1 | bytes 1 | tf_op jit(solution)/shard_map/pallas_call | solution.py:247
  68.6 2.6 %collective-permute-done.6.refs_3_.refs_2_ = bf16[2,256,128]{2,1,0:T(8,128)(2,1)S(1)} collective-permute-done((bf16[2,256,128]{2,1,0:T(8,128)(2,1)S(1)}, bf16[2,256,128]{2,1,0:T(8,128)(2,1)S(1)}, u32[]{:S(2)}, u32[]{:S(2)}) %collective-permute-start.6) | collective-permute-done | bytes 131104 | tf_op jit(solution)/shard_map/ppermute | solution.py:599
  73.3 2.6 %collective-permute-done.8.refs_5_.refs_4_ = bf16[2,256,128]{2,1,0:T(8,128)(2,1)S(1)} collective-permute-done((bf16[2,256,128]{2,1,0:T(8,128)(2,1)S(1)}, bf16[2,256,128]{2,1,0:T(8,128)(2,1)S(1)}, u32[]{:S(2)}, u32[]{:S(2)}) %collective-permute-start.8) | collective-permute-done | bytes 131104 | tf_op jit(solution)/shard_map/ppermute | solution.py:599
  75.9 7.2 %collective-permute-done.9.refs_1_.refs_2_ = bf16[128,1792]{1,0:T(8,128)(2,1)S(1)} collective-permute-done((bf16[128,1792]{1,0:T(8,128)(2,1)S(1)}, bf16[128,1792]{1,0:T(8,128)(2,1)S(1)}, u32[]{:S(2)}, u32[]{:S(2)}) %collective-permute-start.9) | collective-permute-done | bytes 458784 | tf_op jit(solution)/shard_map/ppermute | solution.py:592
  83.9 2.3 %collective-permute-done.11.refs_6_ = bf16[8,544,128]{2,1,0:T(8,128)(2,1)S(1)} collective-permute-done((bf16[8,544,128]{2,1,0:T(8,128)(2,1)S(1)}, bf16[8,544,128]{2,1,0:T(8,128)(2,1)S(1)}, u32[]{:S(2)}, u32[]{:S(2)}) %collective-permute-start.11) | collective-permute-done | bytes 1114144 | tf_op jit(solution)/shard_map/ppermute | solution.py:37
  88.2 9.0 %shard_map.93 = bf16[4,2,256,128]{3,2,1,0:T(8,128)(2,1)S(1)} custom-call(s32[11]{0:T(128)S(1)} %pad_add_fusion.1.at_ref, bf16[1024,1792]{1,0:T(8,128)(2,1)S(1)} %copy-done, bf16[2,256,128]{2,1,0:T(8,128)(2,1)S(1)} %get-tuple-element.44.refs_1_, bf16[2,256,128]{2,1,0:T(8,128)(2,1)S(1)} %collective-permute-done.6.refs_3_.refs_2_, ...), custom_call_target="tpu_custom_call" | custom-call | tf_op jit(solution)/shard_map/pallas_call | solution.py:481
  97.3 10.6 %all_to_all.25.a_own = bf16[4,2,256,128]{3,2,1,0:T(8,128)(2,1)S(1)} all-to-all(bf16[4,2,256,128]{3,2,1,0:T(8,128)(2,1)S(1)} %shard_map.93), channel_id=1, replica_groups=mesh['segment'=2,'grp'=2,'mem'=4,'tp'=2] {'mem'}, dimensions={0} | all-to-all | bytes 1048576 | tf_op jit(solution)/shard_map/all_to_all | solution.py:650
  112.3 7.4 %shard_map.94 = bf16[256,1792]{1,0:T(8,128)(2,1)} custom-call(s32[1]{0:T(128)} %bitcast.tp_ref, bf16[4,2,256,128]{3,2,1,0:T(8,128)(2,1)} %copy-done.14, bf16[4,2,256,128]{3,2,1,0:T(8,128)(2,1)} %copy-done.19, bf16[1024,3584]{1,0:T(8,128)(2,1)} %bitcast.18, bf16[1024,1792]{1,0:T(8,128)(2,1)} %collective-permute-done.13.w_oth, bf16[256,1792]{1,0:T(8,128)(2,1)} %refs_0_.1, ...), custom_call_target="tpu_custom_call" | custom-call | tf_op jit(solution)/shard_map/pallas_call | solution.py:538
  121.0 22.6 %collective-permute-done.14.own.refs_0_ = bf16[256,1792]{1,0:T(8,128)(2,1)S(1)} collective-permute-done((bf16[256,1792]{1,0:T(8,128)(2,1)}, bf16[256,1792]{1,0:T(8,128)(2,1)S(1)}, u32[]{:S(2)}, u32[]{:S(2)}) %collective-permute-start.14) | collective-permute-done | bytes 917536 | tf_op jit(solution)/shard_map/ppermute | solution.py:642
  147.7 6.1 %shard_map.95 = (bf16[256,3584]{1,0:T(8,128)(2,1)}, bf16[2,4,256,128]{3,2,1,0:T(8,128)(2,1)}) custom-call(s32[1]{0:T(128)} %bitcast.tp_ref, bf16[256,1792]{1,0:T(8,128)(2,1)} %copy-done.12, bf16[256,1792]{1,0:T(8,128)(2,1)} %copy-done.18, f32[1,3584]{1,0:T(1,128)} %gain.5, bf16[3584,512]{1,0:T(8,128)(2,1)} %bitcast.25, ...), custom_call_target="tpu_custom_call" | custom-call | tf_op jit(solution)/shard_map/pallas_call | solution.py:201
  153.8 4.0 %all-to-all-start.3 = ((bf16[8,256,128]{2,1,0:T(8,128)(2,1)}), bf16[8,256,128]{2,1,0:T(8,128)(2,1)S(1)}, u32[]{:S(2)}, u32[]{:S(2)}) async-start(bf16[8,256,128]{2,1,0:T(8,128)(2,1)} %bitcast.26), calls=%async_computation.3 | async-start | bytes 1048576 | tf_op jit(solution)/shard_map/all_to_all | solution.py:645
  157.8 5.8 %shard_map.96 = (bf16[2,2,256,128]{3,2,1,0:T(8,128)(2,1)}, bf16[2,2,256,128]{3,2,1,0:T(8,128)(2,1)}) custom-call(s32[1]{0:T(128)} %bitcast.tp_ref, bf16[256,3584]{1,0:T(8,128)(2,1)} %get-tuple-element.49.refs_0_, bf16[3584,1024]{1,0:T(8,128)(2,1)} %bitcast.22, f32[256,128]{1,0:T(8,128)} %get-tuple-element.61.refs_4_.refs_2_, ...), custom_call_target="tpu_custom_call" | custom-call | flops 1 | bytes 1 | tf_op jit(solution)/shard_map/pallas_call | solution.py:247
  173.2 3.2 %collective-permute-done.19.refs_3_ = bf16[2,256,128]{2,1,0:T(8,128)(2,1)S(1)} collective-permute-done((bf16[2,256,128]{2,1,0:T(8,128)(2,1)S(1)}, bf16[2,256,128]{2,1,0:T(8,128)(2,1)S(1)}, u32[]{:S(2)}, u32[]{:S(2)}) %collective-permute-start.19) | collective-permute-done | bytes 131104 | tf_op jit(solution)/shard_map/ppermute | solution.py:599
  179.1 8.5 %shard_map.99 = bf16[4,2,256,128]{3,2,1,0:T(8,128)(2,1)S(1)} custom-call(s32[3]{0:T(128)S(1)} %pad_add_fusion.at_ref, bf16[2,256,128]{2,1,0:T(8,128)(2,1)S(1)} %get-tuple-element.52.refs_0_, bf16[2,256,128]{2,1,0:T(8,128)(2,1)S(1)} %collective-permute-done.17.refs_1_, bf16[2,256,128]{2,1,0:T(8,128)(2,1)S(1)} %collective-permute-done.18.refs_2_, ...), custom_call_target="tpu_custom_call" | custom-call | tf_op jit(solution)/shard_map/pallas_call | solution.py:481
  187.5 10.6 %all_to_all.26.a_own = bf16[4,2,256,128]{3,2,1,0:T(8,128)(2,1)S(1)} all-to-all(bf16[4,2,256,128]{3,2,1,0:T(8,128)(2,1)S(1)} %shard_map.99), channel_id=1, replica_groups=mesh['segment'=2,'grp'=2,'mem'=4,'tp'=2] {'mem'}, dimensions={0} | all-to-all | bytes 1048576 | tf_op jit(solution)/shard_map/all_to_all | solution.py:650
  202.5 6.6 %shard_map.100 = bf16[256,1792]{1,0:T(8,128)(2,1)} custom-call(s32[1]{0:T(128)} %bitcast.tp_ref, bf16[4,2,256,128]{3,2,1,0:T(8,128)(2,1)} %copy-done.15, bf16[4,2,256,128]{3,2,1,0:T(8,128)(2,1)} %copy-done.20, bf16[1024,3584]{1,0:T(8,128)(2,1)} %bitcast.19, bf16[1024,1792]{1,0:T(8,128)(2,1)} %collective-permute-done.13.w_oth, bf16[256,1792]{1,0:T(8,128)(2,1)} %copy-done.12), custom_call_target="tpu_custom_call" | custom-call | tf_op jit(solution)/shard_map/pallas_call | solution.py:538
  (116 shorter events, 59.4 us)
Async XLA Ops:
  0.0 14.7 %collective-permute-start = (bf16[256,1792]{1,0:T(8,128)(2,1)}, bf16[256,1792]{1,0:T(8,128)(2,1)S(1)}, u32[]{:S(2)}, u32[]{:S(2)}) collective-permute-start(bf16[256,1792]{1,0:T(8,128)(2,1)} %refs_0_.1), channel_id=1, source_target_pairs={{0,1},{1,0},{2,3},{3,2},{4,5},{5,4},{6,7},{7,6},{8,9},{9,8},{10,11... | collective-permute-start | bytes 2752520 | tf_op jit(solution)/shard_map/ppermute | solution.py:37
  3.5 18.3 %collective-permute-start.1 = (bf16[96,1792]{1,0:T(8,128)(2,1)}, bf16[96,1792]{1,0:T(8,128)(2,1)S(1)}, u32[]{:S(2)}, u32[]{:S(2)}) collective-permute-start(bf16[96,1792]{1,0:T(8,128)(2,1)} %get-tuple-element.34), channel_id=1, source_target_pairs={{16,0},{17,1},{18,2},{19,3},{20,4},{21,5},{22,6},{23,7},{24,8},{25... | collective-permute-start | bytes 1032200 | tf_op jit(solution)/shard_map/ppermute | solution.py:592
  5.7 29.4 %all-to-all-start = ((bf16[8,48,576]{2,1,0:T(8,128)(2,1)}), bf16[8,48,576]{2,1,0:T(8,128)(2,1)S(1)}, u32[]{:S(2)}, u32[]{:S(2)}) async-start(bf16[8,48,576]{2,1,0:T(8,128)(2,1)} %get-tuple-element.31), calls=%async_computation | async-start | bytes 983040 | tf_op jit(solution)/shard_map/all_to_all | solution.py:605
  22.9 2.2 %collective-permute-start.2 = (bf16[96,1792]{1,0:T(8,128)(2,1)S(1)}, bf16[96,1792]{1,0:T(8,128)(2,1)S(1)}, u32[]{:S(2)}, u32[]{:S(2)}) collective-permute-start(bf16[96,1792]{1,0:T(8,128)(2,1)S(1)} %shard_map.84.own), channel_id=1, source_target_pairs={{0,1},{1,0},{2,3},{3,2},{4,5},{5,4},{6,7},{7,6},{8,9},{9,8},{10,11... | collective-permute-start | bytes 1032200 | tf_op jit(solution)/shard_map/ppermute | solution.py:37
  38.8 44.3 %all-to-all-start.1 = ((bf16[8,544,128]{2,1,0:T(8,128)(2,1)}), bf16[8,544,128]{2,1,0:T(8,128)(2,1)S(1)}, u32[]{:S(2)}, u32[]{:S(2)}) async-start(bf16[8,544,128]{2,1,0:T(8,128)(2,1)} %bitcast.10), calls=%async_computation.1 | async-start | bytes 2228224 | tf_op jit(solution)/shard_map/all_to_all | solution.py:613
  44.3 2.6 %collective-permute-start.4 = (bf16[384,576]{1,0:T(8,128)(2,1)S(1)}, bf16[384,576]{1,0:T(8,128)(2,1)S(1)}, u32[]{:S(2)}, u32[]{:S(2)}) collective-permute-start(bf16[384,576]{1,0:T(8,128)(2,1)S(1)} %bitcast.15), channel_id=1, source_target_pairs={{0,1},{1,0},{2,3},{3,2},{4,5},{5,4},{6,7},{7,6},{8,9},{9,8},{10,11... | collective-permute-start | bytes 1327112 | tf_op jit(solution)/shard_map/ppermute | solution.py:37
  55.5 55.3 %collective-permute-start.13 = (bf16[1024,1792]{1,0:T(8,128)(2,1)}, bf16[1024,1792]{1,0:T(8,128)(2,1)}, u32[]{:S(2)}, u32[]{:S(2)}) collective-permute-start(bf16[1024,1792]{1,0:T(8,128)(2,1)} %shard_map.89.refs_0_), channel_id=1, source_target_pairs={{0,1},{1,0},{2,3},{3,2},{4,5},{5,4},{6,7},{7,6},{8,9},{9,8},{10,11... | collective-permute-start | bytes 11010056 | tf_op jit(solution)/shard_map/ppermute | solution.py:37
  61.6 3.0 %collective-permute-start.5 = (bf16[2,2,256,128]{3,2,1,0:T(8,128)(2,1)}, bf16[2,2,256,128]{3,2,1,0:T(8,128)(2,1)S(1)}, u32[]{:S(2)}, u32[]{:S(2)}) collective-permute-start(bf16[2,2,256,128]{3,2,1,0:T(8,128)(2,1)} %get-tuple-element.43), channel_id=1, source_target_pairs={{0,1},{1,0},{2,3},{3,2},{4,5},{5,4},{6,7},{7,6},{8,9},{9,8},{10,11... | collective-permute-start | bytes 786440 | tf_op jit(solution)/shard_map/ppermute | solution.py:37
  61.9 14.0 %collective-permute-start.10 = (bf16[128,1792]{1,0:T(8,128)(2,1)S(1)}, bf16[128,1792]{1,0:T(8,128)(2,1)S(1)}, u32[]{:S(2)}, u32[]{:S(2)}) collective-permute-start(bf16[128,1792]{1,0:T(8,128)(2,1)S(1)} %copy-done.22), channel_id=1, source_target_pairs={{16,0},{17,1},{18,2},{19,3},{20,4},{21,5},{22,6},{23,7},{24,8},{25... | collective-permute-start | bytes 1376264 | tf_op jit(solution)/shard_map/ppermute | solution.py:592
  63.3 19.9 %collective-permute-start.9 = (bf16[128,1792]{1,0:T(8,128)(2,1)S(1)}, bf16[128,1792]{1,0:T(8,128)(2,1)S(1)}, u32[]{:S(2)}, u32[]{:S(2)}) collective-permute-start(bf16[128,1792]{1,0:T(8,128)(2,1)S(1)} %copy-done.16), channel_id=1, source_target_pairs={{16,0},{17,1},{18,2},{19,3},{20,4},{21,5},{22,6},{23,7},{24,8},{25... | collective-permute-start | bytes 1376264 | tf_op jit(solution)/shard_map/ppermute | solution.py:592
  66.2 5.0 %collective-permute-start.6 = (bf16[2,256,128]{2,1,0:T(8,128)(2,1)S(1)}, bf16[2,256,128]{2,1,0:T(8,128)(2,1)S(1)}, u32[]{:S(2)}, u32[]{:S(2)}) collective-permute-start(bf16[2,256,128]{2,1,0:T(8,128)(2,1)S(1)} %get-tuple-element.45), channel_id=1, source_target_pairs={{0,2},{2,0},{4,6},{6,4},{1,3},{3,1},{5,7},{7,5},{8,10},{10,8},{12,... | collective-permute-start | bytes 393224 | tf_op jit(solution)/shard_map/ppermute | solution.py:599
  67.4 5.8 %collective-permute-start.7 = (bf16[2,256,128]{2,1,0:T(8,128)(2,1)S(1)}, bf16[2,256,128]{2,1,0:T(8,128)(2,1)S(1)}, u32[]{:S(2)}, u32[]{:S(2)}) collective-permute-start(bf16[2,256,128]{2,1,0:T(8,128)(2,1)S(1)} %get-tuple-element.46), channel_id=1, source_target_pairs={{0,4},{2,6},{4,0},{6,2},{1,5},{3,7},{5,1},{7,3},{8,12},{10,14},{12... | collective-permute-start | bytes 393224 | tf_op jit(solution)/shard_map/ppermute | solution.py:599
  71.2 4.7 %collective-permute-start.8 = (bf16[2,256,128]{2,1,0:T(8,128)(2,1)S(1)}, bf16[2,256,128]{2,1,0:T(8,128)(2,1)S(1)}, u32[]{:S(2)}, u32[]{:S(2)}) collective-permute-start(bf16[2,256,128]{2,1,0:T(8,128)(2,1)S(1)} %get-tuple-element.47), channel_id=1, source_target_pairs={{0,6},{2,4},{4,2},{6,0},{1,7},{3,5},{5,3},{7,1},{8,14},{10,12},{12... | collective-permute-start | bytes 393224 | tf_op jit(solution)/shard_map/ppermute | solution.py:599
  83.1 3.0 %collective-permute-start.11 = (bf16[8,544,128]{2,1,0:T(8,128)(2,1)S(1)}, bf16[8,544,128]{2,1,0:T(8,128)(2,1)S(1)}, u32[]{:S(2)}, u32[]{:S(2)}) collective-permute-start(bf16[8,544,128]{2,1,0:T(8,128)(2,1)S(1)} %shard_map.92.refs_5_), channel_id=1, source_target_pairs={{0,1},{1,0},{2,3},{3,2},{4,5},{5,4},{6,7},{7,6},{8,9},{9,8},{10,11... | collective-permute-start | bytes 3342344 | tf_op jit(solution)/shard_map/ppermute | solution.py:37
  107.8 3.6 %collective-permute-start.12 = (bf16[4,2,256,128]{3,2,1,0:T(8,128)(2,1)S(1)}, bf16[4,2,256,128]{3,2,1,0:T(8,128)(2,1)S(1)}, u32[]{:S(2)}, u32[]{:S(2)}) collective-permute-start(bf16[4,2,256,128]{3,2,1,0:T(8,128)(2,1)S(1)} %all_to_all.25.a_own), channel_id=1, source_target_pairs={{0,1},{1,0},{2,3},{3,2},{4,5},{5,4},{6,7},{7,6},{8,9},{9,8},{10,11... | collective-permute-start | bytes 1572872 | tf_op jit(solution)/shard_map/ppermute | solution.py:37
  119.7 23.9 %collective-permute-start.14 = (bf16[256,1792]{1,0:T(8,128)(2,1)}, bf16[256,1792]{1,0:T(8,128)(2,1)S(1)}, u32[]{:S(2)}, u32[]{:S(2)}) collective-permute-start(bf16[256,1792]{1,0:T(8,128)(2,1)} %shard_map.94), channel_id=1, source_target_pairs={{0,16},{1,17},{2,18},{3,19},{4,20},{5,21},{6,22},{7,23},{8,24},{9,... | collective-permute-start | bytes 2752520 | tf_op jit(solution)/shard_map/ppermute | solution.py:642
  143.6 3.2 %collective-permute-start.15 = (bf16[256,1792]{1,0:T(8,128)(2,1)S(1)}, bf16[256,1792]{1,0:T(8,128)(2,1)S(1)}, u32[]{:S(2)}, u32[]{:S(2)}) collective-permute-start(bf16[256,1792]{1,0:T(8,128)(2,1)S(1)} %collective-permute-done.14.own.refs_0_), channel_id=1, source_target_pairs={{0,1},{1,0},{2,3},{3,2},{4,5},{5,4},{6,7},{7,6},{8,9},{9,8},{10,11... | collective-permute-start | bytes 2752520 | tf_op jit(solution)/shard_map/ppermute | solution.py:37
  153.8 22.6 %all-to-all-start.3 = ((bf16[8,256,128]{2,1,0:T(8,128)(2,1)}), bf16[8,256,128]{2,1,0:T(8,128)(2,1)S(1)}, u32[]{:S(2)}, u32[]{:S(2)}) async-start(bf16[8,256,128]{2,1,0:T(8,128)(2,1)} %bitcast.26), calls=%async_computation.3 | async-start | bytes 1048576 | tf_op jit(solution)/shard_map/all_to_all | solution.py:645
  163.7 2.3 %collective-permute-start.16 = (bf16[2,2,256,128]{3,2,1,0:T(8,128)(2,1)}, bf16[2,2,256,128]{3,2,1,0:T(8,128)(2,1)S(1)}, u32[]{:S(2)}, u32[]{:S(2)}) collective-permute-start(bf16[2,2,256,128]{3,2,1,0:T(8,128)(2,1)} %get-tuple-element.51), channel_id=1, source_target_pairs={{0,1},{1,0},{2,3},{3,2},{4,5},{5,4},{6,7},{7,6},{8,9},{9,8},{10,11... | collective-permute-start | bytes 786440 | tf_op jit(solution)/shard_map/ppermute | solution.py:37
  167.5 4.8 %collective-permute-start.17 = (bf16[2,256,128]{2,1,0:T(8,128)(2,1)S(1)}, bf16[2,256,128]{2,1,0:T(8,128)(2,1)S(1)}, u32[]{:S(2)}, u32[]{:S(2)}) collective-permute-start(bf16[2,256,128]{2,1,0:T(8,128)(2,1)S(1)} %get-tuple-element.53), channel_id=1, source_target_pairs={{0,2},{2,0},{4,6},{6,4},{1,3},{3,1},{5,7},{7,5},{8,10},{10,8},{12,... | collective-permute-start | bytes 393224 | tf_op jit(solution)/shard_map/ppermute | solution.py:599
  168.8 4.4 %collective-permute-start.18 = (bf16[2,256,128]{2,1,0:T(8,128)(2,1)S(1)}, bf16[2,256,128]{2,1,0:T(8,128)(2,1)S(1)}, u32[]{:S(2)}, u32[]{:S(2)}) collective-permute-start(bf16[2,256,128]{2,1,0:T(8,128)(2,1)S(1)} %get-tuple-element.54), channel_id=1, source_target_pairs={{0,4},{2,6},{4,0},{6,2},{1,5},{3,7},{5,1},{7,3},{8,12},{10,14},{12... | collective-permute-start | bytes 393224 | tf_op jit(solution)/shard_map/ppermute | solution.py:599
  170.0 6.4 %collective-permute-start.19 = (bf16[2,256,128]{2,1,0:T(8,128)(2,1)S(1)}, bf16[2,256,128]{2,1,0:T(8,128)(2,1)S(1)}, u32[]{:S(2)}, u32[]{:S(2)}) collective-permute-start(bf16[2,256,128]{2,1,0:T(8,128)(2,1)S(1)} %get-tuple-element.55), channel_id=1, source_target_pairs={{0,6},{2,4},{4,2},{6,0},{1,7},{3,5},{5,3},{7,1},{8,14},{10,12},{12... | collective-permute-start | bytes 393224 | tf_op jit(solution)/shard_map/ppermute | solution.py:599
  176.4 2.7 %collective-permute-start.20 = (bf16[8,256,128]{2,1,0:T(8,128)(2,1)S(1)}, bf16[8,256,128]{2,1,0:T(8,128)(2,1)S(1)}, u32[]{:S(2)}, u32[]{:S(2)}) collective-permute-start(bf16[8,256,128]{2,1,0:T(8,128)(2,1)S(1)} %shard_map.98.refs_4_), channel_id=1, source_target_pairs={{0,1},{1,0},{2,3},{3,2},{4,5},{5,4},{6,7},{7,6},{8,9},{9,8},{10,11... | collective-permute-start | bytes 1572872 | tf_op jit(solution)/shard_map/ppermute | solution.py:37
  198.1 3.6 %collective-permute-start.21 = (bf16[4,2,256,128]{3,2,1,0:T(8,128)(2,1)S(1)}, bf16[4,2,256,128]{3,2,1,0:T(8,128)(2,1)S(1)}, u32[]{:S(2)}, u32[]{:S(2)}) collective-permute-start(bf16[4,2,256,128]{3,2,1,0:T(8,128)(2,1)S(1)} %all_to_all.26.a_own), channel_id=1, source_target_pairs={{0,1},{1,0},{2,3},{3,2},{4,5},{5,4},{6,7},{7,6},{8,9},{9,8},{10,11... | collective-permute-start | bytes 1572872 | tf_op jit(solution)/shard_map/ppermute | solution.py:37
  (26 other events, 122.7 us)

commit v4 on v3

--- a/solution.py
+++ b/solution.py
@@ -136,93 +136,142 @@
     )(tp_index, values, proj_weight)
 
 
-def gelu_kernel(after, wide_ref, came_ref, o_ref):
+def gelu_kernel(*refs):
+    wide_ref, came_ref, o_ref = refs[-3:]
     total = wide_ref[...] + came_ref[...].astype(F32)
     o_ref[...] = (0.5 * total * (1.0 + lax.erf(total * math.sqrt(0.5)))).astype(BF16)
 
 
-def gelu_sum(after, wide, came):
+def gelu_sum(wide, came, *after):
     return pl.pallas_call(
         gelu_kernel,
-        in_specs=[
-            pl.BlockSpec(memory_space=pl.ANY),
-            pl.BlockSpec(memory_space=pltpu.VMEM),
-            pl.BlockSpec(memory_space=pltpu.VMEM),
-        ],
-        out_specs=pl.BlockSpec(memory_space=pltpu.VMEM),
+        in_specs=[*[ANY] * len(after), VMEM, VMEM],
+        out_specs=VMEM,
         out_shape=jax.ShapeDtypeStruct(wide.shape, BF16),
         compiler_params=params(16),
-    )(after, wide, came)
+    )(*after, wide, came)
 
 
 def rope(values, cosine, sine):
     return values * cosine + pltpu.roll(values, HDIM // 2, 1) * sine
 
 
-def kv_kernel(tp_ref, own, oth, gain, w_ref, cos_ref, sin_ref, normed_ref, kv_ref, scratch):
-    half = own.shape[1]
-
-    @pl.when(pl.program_id(0) == 0)
-    def _():
-        t = tp_ref[0]
-        own_at = pl.multiple_of(t * half, 128)
-        oth_at = pl.multiple_of((1 - t) * half, 128)
-
-        def chunk(c, carry):
-            rows = pl.ds(pl.multiple_of(c * 32, 32), 32)
-            a = own[rows, :].astype(F32)
-            b = oth[rows, :].astype(F32)
-            total = jnp.sum(a * a, axis=1, keepdims=True) + jnp.sum(b * b, axis=1, keepdims=True)
-            scale = lax.rsqrt(total * (1.0 / (2 * half)) + EPSILON)
-            scratch[rows, pl.ds(own_at, half)] = (
-                a * scale * gain[:, pl.ds(own_at, half)]
-            ).astype(BF16)
-            scratch[rows, pl.ds(oth_at, half)] = (
-                b * scale * gain[:, pl.ds(oth_at, half)]
-            ).astype(BF16)
-            return carry
-
-        lax.fori_loop(0, own.shape[0] // 32, chunk, 0)
-        normed_ref[...] = scratch[...]
-
-    wide = jnp.dot(scratch[...], w_ref[...], preferred_element_type=F32)
+def norm_rows(t, own, oth, gain, scratch, first_row):
+    rows, width = own[0].shape
+    half = width * len(own)
+    places = []
+    for refs, core in ((own, t), (oth, 1 - t)):
+        for i, ref in enumerate(refs):
+            places.append((ref, pl.ds(pl.multiple_of(core * half + i * width, HDIM), width)))
+
+    def chunk(c, carry):
+        at = pl.ds(pl.multiple_of(c * 32, 32), 32)
+        to = pl.ds(pl.multiple_of(first_row + c * 32, 32), 32)
+        values = [ref[at, :].astype(F32) for ref, _ in places]
+        total = sum(jnp.sum(v * v, axis=1, keepdims=True) for v in values)
+        scale = lax.rsqrt(total * (1.0 / (2 * half)) + EPSILON)
+        for v, (_, lanes) in zip(values, places):
+            scratch[to, lanes] = (v * scale * gain[:, lanes]).astype(BF16)
+        return carry
+
+    lax.fori_loop(0, rows // 32, chunk, 0)
+
+
+def kv_kernel(pieces, tp_ref, *refs):
+    own, oth, refs = refs[:pieces], refs[pieces : 2 * pieces], refs[2 * pieces :]
+    gain, w_hbm, cos_ref, sin_ref, normed, kv_ref, w_ref, sem = refs
+    rows = normed.shape[0]
+    copy = pltpu.make_async_copy(w_hbm, w_ref, sem)
+    copy.start()
+    norm_rows(tp_ref[0], own, oth, gain, normed, 0)
+    copy.wait()
+    wide = jnp.dot(normed[...], w_ref[...], preferred_element_type=F32)
     for h in range(wide.shape[1] // HDIM):
-        head = rope(wide[:, h * HDIM : (h + 1) * HDIM], cos_ref[...], sin_ref[...]).astype(BF16)
+        head = rope(wide[:, h * HDIM : (h + 1) * HDIM], cos_ref[:rows, :], sin_ref[:rows, :])
+        head = head.astype(BF16)
         for g in range(kv_ref.shape[0]):
             kv_ref[g, h] = head
 
 
 def keyvals(tp_index, own, oth, gain, kv_weight, cosine, sine, groups):
-    rows, half = own.shape
+    rows = own[0].shape[0]
     depth, cols = kv_weight.shape
-    block = 256
-    whole = lambda i, t: (0, 0)
-    per = block // HDIM
-    return pl.pallas_call(
-        kv_kernel,
-        grid_spec=pltpu.PrefetchScalarGridSpec(
-            num_scalar_prefetch=1,
-            grid=(cols // block,),
-            in_specs=[
-                pl.BlockSpec(own.shape, whole),
-                pl.BlockSpec(oth.shape, whole),
-                pl.BlockSpec(gain.shape, whole),
-                pl.BlockSpec((depth, block), lambda i, t: (0, i)),
-                pl.BlockSpec(cosine.shape, whole),
-                pl.BlockSpec(sine.shape, whole),
-            ],
-            out_specs=[
-                pl.BlockSpec((rows, depth), whole),
-                pl.BlockSpec((groups, per, rows, HDIM), lambda i, t: (0, i, 0, 0)),
-            ],
-            scratch_shapes=[pltpu.VMEM((rows, depth), BF16)],
-        ),
+    return pl.pallas_call(
+        functools.partial(kv_kernel, len(own)),
+        in_specs=[SMEM, *[VMEM] * (len(own) + len(oth) + 1), ANY, VMEM, VMEM],
+        out_specs=[VMEM, VMEM],
         out_shape=[
             jax.ShapeDtypeStruct((rows, depth), BF16),
             jax.ShapeDtypeStruct((groups, cols // HDIM, rows, HDIM), BF16),
         ],
+        scratch_shapes=[pltpu.VMEM(kv_weight.shape, BF16), pltpu.SemaphoreType.DMA],
         compiler_params=params(56),
-    )(tp_index, own, oth, gain, kv_weight, cosine, sine)
+    )(tp_index, *own, *oth, gain, kv_weight, cosine, sine)
+
+
+def qkv_kernel(tp_ref, *refs):
+    ins, outs, scratch = refs[:11], refs[11:16], refs[16:]
+    t_own, t_oth, f_own, f_oth, gain, kv_hbm, q_hbm, kv_cos, kv_sin, q_cos, q_sin = ins
+    packed, kept, given, f_kept, f_given = outs
+    normed, kv_w, q_w, sems = scratch
+    rows, more = t_own.shape[0], f_own.shape[0]
+    steps, block = q_w.shape[0], q_w.shape[2]
+    copies = [pltpu.make_async_copy(kv_hbm, kv_w, sems.at[0])]
+    for i in range(steps):
+        source = q_hbm.at[:, i * block : (i + 1) * block]
+        copies.append(pltpu.make_async_copy(source, q_w.at[i], sems.at[1 + i]))
+    for copy in copies:
+        copy.start()
+    t = tp_ref[0]
+    norm_rows(t, [t_own], [t_oth], gain, normed, 0)
+    norm_rows(t, [f_own], [f_oth], gain, normed, rows)
+    copies[0].wait()
+    wide = jnp.dot(normed[...], kv_w[...], preferred_element_type=F32)
+    for j in range(KV_HEADS):
+        head = rope(wide[:, j * HDIM : (j + 1) * HDIM], kv_cos[...], kv_sin[...]).astype(BF16)
+        for g in range(packed.shape[0]):
+            packed[g, j, : rows + more] = head
+    first = t == 0
+    for i in range(steps):
+        copies[1 + i].wait()
+        wide = jnp.dot(normed[...], q_w[i], preferred_element_type=F32)
+        for h in range(2):
+            heads = []
+            for u in range(2):
+                lower = (2 * u + h) * HDIM
+                heads.append(rope(wide[:, lower : lower + HDIM], q_cos[...], q_sin[...]))
+            for here, text, frame in ((first, kept, f_kept), (t == 1, given, f_given)):
+                head = jnp.where(here, heads[0], heads[1]).astype(BF16)
+                text[i, h] = head[:rows]
+                frame[i, h] = head[rows:]
+
+
+def qkv(tp_index, t_own, t_oth, f_own, f_oth, gain, kv_weight, q_weight, kv_tables, q_tables, groups):
+    rows, more = t_own.shape[0], f_own.shape[0]
+    depth, cols = q_weight.shape
+    block = 4 * HDIM
+    steps = cols // block
+    text = jax.ShapeDtypeStruct((steps, 2, rows, HDIM), BF16)
+    frame = jax.ShapeDtypeStruct((steps, 2, more, HDIM), BF16)
+    return pl.pallas_call(
+        qkv_kernel,
+        in_specs=[SMEM, *[VMEM] * 5, ANY, ANY, *[VMEM] * 4],
+        out_specs=[VMEM] * 5,
+        out_shape=[
+            jax.ShapeDtypeStruct((groups, KV_HEADS, rows + 3 * more, HDIM), BF16),
+            text,
+            text,
+            frame,
+            frame,
+        ],
+        scratch_shapes=[
+            pltpu.VMEM((rows + more, depth), BF16),
+            pltpu.VMEM(kv_weight.shape, BF16),
+            pltpu.VMEM((steps, depth, block), BF16),
+            pltpu.SemaphoreType.DMA((1 + steps,)),
+        ],
+        compiler_params=params(60),
+    )(tp_index, t_own, t_oth, f_own, f_oth, gain, kv_weight, q_weight, *kv_tables, *q_tables)
 
 
 def q_kernel(tp_ref, *refs):
@@ -253,8 +302,8 @@
                 *[ANY] * len(after),
                 pl.BlockSpec(normed.shape, whole),
                 pl.BlockSpec((depth, block), lambda i, t: (0, i)),
-                pl.BlockSpec(cosine.shape, whole),
-                pl.BlockSpec(sine.shape, whole),
+                pl.BlockSpec((rows, HDIM), whole),
+                pl.BlockSpec((rows, HDIM), whole),
             ],
             out_specs=[pl.BlockSpec((1, 2, rows, HDIM), lambda i, t: (i, 0, 0, 0))] * 2,
         ),
@@ -264,7 +313,8 @@
     )(tp_index, *after, normed, q_weight, cosine, sine)
 
 
-def route_kernel(at_ref, kept, given, *outs):
+def route_kernel(skip, at_ref, *refs):
+    kept, given, *outs = refs[skip:]
     core, me = at_ref[1], at_ref[2]
     for d, out in enumerate(outs):
         to = jnp.bitwise_xor(me, d)
@@ -280,31 +330,33 @@
             out[...] = given[low]
 
 
-def route(at, kept, given):
-    return pl.pallas_call(
-        route_kernel,
-        in_specs=[SMEM, VMEM, VMEM],
+def route(at, kept, given, *after):
+    return pl.pallas_call(
+        functools.partial(route_kernel, len(after)),
+        in_specs=[SMEM, *[ANY] * len(after), VMEM, VMEM],
         out_specs=[VMEM] * KV_HEADS,
         out_shape=[jax.ShapeDtypeStruct(kept.shape[1:], BF16)] * KV_HEADS,
         cost_estimate=LITTLE,
         compiler_params=params(16),
-    )(at, kept, given)
-
-
-def pack_kernel(at_ref, after, kv, f_kv, f_kept, f_given, out):
-    rows, more = kv.shape[2], f_kv.shape[2]
-    for g in range(out.shape[0]):
-        for j in range(KV_HEADS):
-            out[g, j, :rows] = kv[0, j]
-            out[g, j, rows : rows + more] = f_kv[0, j]
+    )(at, *after, kept, given)
+
+
+def pack_kernel(at_ref, after, packed, f_kept, f_given, out, sems):
+    more = f_kept.shape[2]
+    rows = out.shape[2] - 2 * more
 
     def heads(first, second):
+        copies = []
         for g in range(out.shape[0]):
             for j in range(KV_HEADS):
-                source = (first if j < 2 else second)[j % 2]
                 for h in range(2):
-                    lower = rows + (1 + h) * more
-                    out[g, j, lower : lower + more] = source[h]
+                    source = (first if j < 2 else second).at[j % 2, h]
+                    target = out.at[g, j, rows + h * more : rows + (h + 1) * more]
+                    copies.append(pltpu.make_async_copy(source, target, sems.at[len(copies)]))
+        for copy in copies:
+            copy.start()
+        for copy in copies:
+            copy.wait()
 
     @pl.when(at_ref[1] == 0)
     def _():
@@ -315,15 +367,16 @@
         heads(f_given, f_kept)
 
 
-def pack(at, after, kv, f_kv, f_kept, f_given, groups):
-    rows = kv.shape[2] + 3 * f_kv.shape[2]
+def pack(at, after, packed, f_kept, f_given):
     return pl.pallas_call(
         pack_kernel,
-        in_specs=[SMEM, ANY, VMEM, VMEM, VMEM, VMEM],
-        out_specs=VMEM,
-        out_shape=jax.ShapeDtypeStruct((groups, KV_HEADS, rows, HDIM), BF16),
-        compiler_params=params(32),
-    )(at, after, kv, f_kv, f_kept, f_given)
+        in_specs=[SMEM, ANY, ANY, VMEM, VMEM],
+        out_specs=ANY,
+        out_shape=jax.ShapeDtypeStruct(packed.shape, BF16),
+        scratch_shapes=[pltpu.SemaphoreType.DMA((2 * KV_HEADS * packed.shape[0],))],
+        input_output_aliases={2: 0},
+        compiler_params=params(16),
+    )(at, after, packed, f_kept, f_given)
 
 
 def gate_kernel(*refs):
@@ -402,7 +455,7 @@
             def one(f, carry):
                 lines = slice(rows, rows + FRAME_TOK)
                 both = jnp.concatenate([k_from[f, lines, :], v_from[f, lines, :]], axis=1)
-                at, inside, moved = shifted_rows(at_ref[3 + f], both)
+                at, inside, moved = shifted_rows(at_ref[4 + f], both)
                 merge(keys, at, every, inside, moved[:, low])
                 merge(vals, at, low, inside, moved[:, high])
                 return carry
@@ -424,7 +477,7 @@
     if frames:
 
         def one(f, carry):
-            start = at_ref[3 + f] - base
+            start = at_ref[4 + f] - base
             here = (start > -FRAME_TOK) & (start < members * rows)
             start = jnp.where(here, start + PAD, members * rows + 2 * PAD)
             lower = rows + FRAME_TOK
@@ -499,65 +552,91 @@
     )(at, *after, *pieces, own, oth)
 
 
-def out_kernel(placing, tp_ref, a_own, a_oth, w_own, w_oth, *refs):
-    near, far = refs[-2:]
-    o_ref = refs[-3]
-
-    @pl.when(pl.program_id(0) == 0)
-    def _():
-        t = tp_ref[0]
-        for jj in range(2):
-            for h in range(2):
-                mine = pl.multiple_of((2 * (2 * jj + t) + h) * HDIM, HDIM)
-                theirs = pl.multiple_of((2 * (2 * jj + 1 - t) + h) * HDIM, HDIM)
-                near[:, pl.ds(mine, HDIM)] = a_own[2 * t + jj, h]
-                near[:, pl.ds(theirs, HDIM)] = a_oth[2 * t + jj, h]
-                far[:, pl.ds(mine, HDIM)] = a_own[2 * (1 - t) + jj, h]
-                far[:, pl.ds(theirs, HDIM)] = a_oth[2 * (1 - t) + jj, h]
-
+def out_kernel(placing, width, chunk, at_ref, a_own, a_oth, w_own, w_oth, *refs):
+    *residual, o_ref, near, far, own_w, oth_w, sems = refs
+    core, segment = at_ref[1], at_ref[3]
+    half = o_ref.shape[-1]
+    lanes = [slice(c, min(c + width, half)) for c in range(0, half, width)]
+    start = pl.multiple_of(core * w_oth.shape[1], HDIM) + chunk * half
+    copies = []
+    for i, at in enumerate(lanes):
+        size = at.stop - at.start
+        mine = w_own.at[:, pl.ds(pl.multiple_of(start + at.start, HDIM), size)]
+        theirs = w_oth.at[:, chunk * half + at.start : chunk * half + at.stop]
+        copies.append(
+            (
+                pltpu.make_async_copy(mine, own_w.at[:, at], sems.at[0, i]),
+                pltpu.make_async_copy(theirs, oth_w.at[:, at], sems.at[1, i]),
+            )
+        )
+    for pair in copies:
+        for copy in pair:
+            copy.start()
+    for jj in range(2):
+        for h in range(2):
+            mine = pl.multiple_of((2 * (2 * jj + core) + h) * HDIM, HDIM)
+            theirs = pl.multiple_of((2 * (2 * jj + 1 - core) + h) * HDIM, HDIM)
+            near[:, pl.ds(mine, HDIM)] = a_own[2 * core + jj, h]
+            near[:, pl.ds(theirs, HDIM)] = a_oth[2 * core + jj, h]
+            far[:, pl.ds(mine, HDIM)] = a_own[2 * (1 - core) + jj, h]
+            far[:, pl.ds(theirs, HDIM)] = a_oth[2 * (1 - core) + jj, h]
     if placing:
-        text, wide, upper, lower, is_frame = refs[:5]
-        came = jnp.concatenate([upper[...], lower[...]], axis=0)
-        total = wide[...] + came.astype(F32)
-        gelu = 0.5 * total * (1.0 + lax.erf(total * math.sqrt(0.5)))
-        h = jnp.where(is_frame[...] > 0, gelu.astype(BF16).astype(F32), text[...].astype(F32))
-    else:
-        h = refs[0][...].astype(F32)
-    first = jnp.dot(near[...], w_own[...], preferred_element_type=F32)
-    second = jnp.dot(far[...], w_oth[...], preferred_element_type=F32)
-    o_ref[...] = (h + (first + second)).astype(BF16)
-
-
-def project_out(tp_index, a_own, a_oth, w_own, w_oth, *residual):
-    rows, cols = residual[0].shape
-    depth = w_own.shape[0]
-    steps = 2
-    block = cols // steps
-    four = lambda i, t: (0, 0, 0, 0)
-    mine = lambda i, t: (0, t[0] * steps + i)
-    return pl.pallas_call(
-        functools.partial(out_kernel, len(residual) > 1),
-        grid_spec=pltpu.PrefetchScalarGridSpec(
-            num_scalar_prefetch=1,
-            grid=(steps,),
-            in_specs=[
-                pl.BlockSpec(a_own.shape, four),
-                pl.BlockSpec(a_oth.shape, four),
-                pl.BlockSpec((depth, block), mine),
-                pl.BlockSpec((depth, block), lambda i, t: (0, i)),
-                *[
-                    pl.BlockSpec((value.shape[0], block), lambda i, t: (0, i))
-                    if value.shape[1] == cols
-                    else pl.BlockSpec(value.shape, lambda i, t: (0, 0))
-                    for value in residual
-                ],
-            ],
-            out_specs=pl.BlockSpec((rows, block), lambda i, t: (0, i)),
-            scratch_shapes=[pltpu.VMEM((rows, depth), BF16)] * 2,
-        ),
-        out_shape=jax.ShapeDtypeStruct((rows, cols), BF16),
+        text, wide, upper, lower, idx_own, idx_oth = residual
+        is_frame = jnp.maximum(idx_own[...], idx_oth[...]) >= 0
+        rows = upper.shape[0]
+        for r, came in enumerate((upper, lower)):
+            at = slice(r * rows, (r + 1) * rows)
+            total = wide[at, :] + came[...].astype(F32)
+            gelu = 0.5 * total * (1.0 + lax.erf(total * math.sqrt(0.5)))
+            o_ref[at, :] = jnp.where(is_frame[at], gelu, text[at, :].astype(F32)).astype(BF16)
+    for i, at in enumerate(lanes):
+        for copy in copies[i]:
+            copy.wait()
+        term = jnp.dot(near[...], own_w[:, at], preferred_element_type=F32)
+        term += jnp.dot(far[...], oth_w[:, at], preferred_element_type=F32)
+        if placing:
+            o_ref[:, at] = (o_ref[:, at].astype(F32) + term).astype(BF16)
+        else:
+            pieces = len(residual) // 2
+            step = half // pieces
+            for p in range(pieces):
+                low, high = max(at.start, p * step), min(at.stop, (p + 1) * step)
+                if low < high:
+                    inner = slice(low - p * step, high - p * step)
+                    h = residual[p][:, inner].astype(F32)
+                    h = (h + term[:, low - at.start : high - at.start]).astype(BF16)
+                    first = residual[pieces + p][:, inner]
+                    o_ref[0, :, low:high] = jnp.where(segment == 0, first, h)
+
+
+def project_out(at, a_own, a_oth, w_own, w_oth, residual, placing, chunk, chunks):
+    rows = a_own.shape[2]
+    depth, cols = w_oth.shape
+    width = cols // chunks
+    shape = (rows, width) if placing else (1, rows, width)
+    whole = lambda i: (0, 0)
+    part = lambda i: (0, chunk)
+    specs = [
+        pl.BlockSpec((value.shape[0], width), part)
+        if value.shape[1] == cols
+        else pl.BlockSpec(value.shape, whole)
+        for value in residual
+    ]
+    four = pl.BlockSpec(a_own.shape, lambda i: (0, 0, 0, 0))
+    block = 4 * HDIM
+    return pl.pallas_call(
+        functools.partial(out_kernel, placing, block, chunk),
+        grid=(1,),
+        in_specs=[SMEM, four, four, ANY, ANY, *specs],
+        out_specs=pl.BlockSpec(shape, lambda i: (0,) * len(shape)),
+        out_shape=jax.ShapeDtypeStruct(shape, BF16),
+        scratch_shapes=[
+            *[pltpu.VMEM((rows, depth), BF16)] * 2,
+            *[pltpu.VMEM((depth, width), BF16)] * 2,
+            pltpu.SemaphoreType.DMA((2, -(-width // block))),
+        ],
         compiler_params=params(56),
-    )(tp_index, a_own, a_oth, w_own, w_oth, *residual)
+    )(at, a_own, a_oth, w_own, w_oth, *residual)
 
 
 def per_device(
@@ -583,40 +662,25 @@
         kv_tables = (jnp.where(plain, 1.0, cosine), jnp.where(plain, 0.0, sine))
         return kv_tables, (cosine * factor, sine * factor)
 
-    text_kv, text_q = tables(positions)
-    frame_kv, frame_q = tables(frame_at + jnp.arange(FRAME_TOK, dtype=jnp.int32))
-
+    frame_rows = frame_at + jnp.arange(FRAME_TOK, dtype=jnp.int32)
+    kv_tables, q_tables = tables(jnp.concatenate([positions, frame_rows]))
     me = lax.axis_index("mem")
 
     def from_vision(sent):
         return lax.ppermute(sent, "segment", [(1, 0)])
 
-    base = jnp.stack([group * members * rows, t, me]).astype(jnp.int32)
-
-    def spread_heads(kept, given):
-        pieces = route(base, kept, swap(given))
+    base = jnp.stack([group * members * rows, t, me, segment]).astype(jnp.int32)
+
+    def spread_heads(kept, given, *after):
+        pieces = route(base, kept, swap(given), *after)
         return [pieces[0]] + [
             lax.ppermute(pieces[d], "mem", [(i, i ^ d) for i in range(KV_HEADS)])
             for d in range(1, KV_HEADS)
         ]
 
-    wide, sent, spread = project(tp_index, patch_feats, proj_weight, count)
-    came = from_vision(sent)
-    pf_own = lax.all_to_all(spread, CTX, split_axis=0, concat_axis=0, tiled=True)
-
-    normed, kv = keyvals(tp_index, text_embed, swap(text_embed), gain, kv_weight, *text_kv, 1)
-    frame_embed = gelu_sum(kv, wide, came)
-    f_normed, f_kv = keyvals(tp_index, frame_embed, swap(frame_embed), gain, kv_weight, *frame_kv, 1)
-    f_kept, f_given = queries_of(tp_index, f_normed, q_weight, *frame_q)
-    packed = pack(base, pf_own, kv, f_kv, f_kept, swap(f_given), groups)
-    message = packed.reshape(count, *packed.shape[2:])
-    message = lax.all_to_all(message, CTX, split_axis=0, concat_axis=0, tiled=True)
-
-    part = pf_own.shape[1]
-    pf_own = pf_own.reshape(count * part, -1)
+    part = FRAME_TOK // 2
     offset = positions[:, None] - frame_start[None, :]
     inside = (offset >= 0) & (offset < FRAME_TOK)
-    is_frame = jnp.any(inside, axis=1, keepdims=True).astype(jnp.int32)
     frames = jnp.arange(frame_start.shape[0], dtype=jnp.int32)[None, :]
 
     def index_of(core):
@@ -624,36 +688,58 @@
         here = inside & (local >= 0) & (local < part)
         return jnp.max(jnp.where(here, frames * part + local, -1), axis=1, keepdims=True)
 
-    wide, *sent = project_placed(
-        packed, index_of(t), index_of(1 - t), pf_own, swap(pf_own), proj_weight
+    idx_own, idx_oth = index_of(t), index_of(1 - t)
+
+    wide, sent, spread = project(tp_index, patch_feats, proj_weight, count)
+    came = from_vision(sent)
+    pf_own = lax.all_to_all(spread, CTX, split_axis=0, concat_axis=0, tiled=True)
+
+    frame_embed = gelu_sum(wide, came, *kv_tables, *q_tables, idx_own, idx_oth)
+    packed, kept, given, f_kept, f_given = qkv(
+        tp_index,
+        text_embed,
+        swap(text_embed),
+        frame_embed,
+        swap(frame_embed),
+        gain,
+        kv_weight,
+        q_weight,
+        kv_tables,
+        q_tables,
+        groups,
     )
+    packed = pack(base, pf_own, packed, f_kept, swap(f_given))
+    message = packed.reshape(count, *packed.shape[2:])
+    message = lax.all_to_all(message, CTX, split_axis=0, concat_axis=0, tiled=True)
+
+    pf_own = pf_own.reshape(count * part, -1)
+    wide, *sent = project_placed(packed, idx_own, idx_oth, pf_own, swap(pf_own), proj_weight)
     placed = [from_vision(half) for half in sent]
-    pieces = spread_heads(*queries_of(tp_index, normed, q_weight, *text_q, *sent))
-    results = []
-    for tick in range(lax.axis_size("segment")):
-        if tick == 0:
-            at = jnp.concatenate([base, frame_start])
-            message = gate(message, *placed, *pieces[1:])
-            w_given = other_columns(tp_index, sent[0], out_weight)
-            w_oth = swap(w_given)
-            attended = attend(at, pieces, message, swap(message), frame_start.shape[0], w_given)
-            residual = (text_embed, wide, *placed, is_frame)
-        else:
-            h = lax.ppermute(h, "segment", [(tick - 1, tick)])
-            normed, kv = keyvals(tp_index, h, swap(h), gain, kv_weight, *text_kv, groups)
-            kv = kv.reshape(count, rows, HDIM)
-            kv = lax.all_to_all(kv, CTX, split_axis=0, concat_axis=0, tiled=True)
-            pieces = spread_heads(*queries_of(tp_index, normed, q_weight, *text_q))
-            kv = gate(kv, *pieces[1:])
-            attended = attend(base, pieces, kv, swap(kv), 0)
-            residual = (h,)
-        a_own = lax.all_to_all(attended, "mem", split_axis=0, concat_axis=0, tiled=True)
-        h = project_out(tp_index, a_own, swap(a_own), out_weight, w_oth, *residual)
-        results.append(h)
-    out = results[0]
-    for tick in range(1, len(results)):
-        out = jnp.where(segment == tick, results[tick], out)
-    return out[None]
+    pieces = spread_heads(kept, given, sent[0])
+    w_given = other_columns(tp_index, sent[0], out_weight)
+    w_oth = swap(w_given)
+
+    at = jnp.concatenate([base, frame_start])
+    message = gate(message, *placed, *pieces[1:])
+    attended = attend(at, pieces, message, swap(message), frame_start.shape[0], w_given)
+    a_own = lax.all_to_all(attended, "mem", split_axis=0, concat_axis=0, tiled=True)
+    a_oth = swap(a_own)
+    residual = (text_embed, wide, *placed, idx_own, idx_oth)
+    first = [
+        project_out(base, a_own, a_oth, out_weight, w_oth, residual, True, chunk, 2)
+        for chunk in range(2)
+    ]
+
+    h = [lax.ppermute(part, "segment", [(0, 1)]) for part in first]
+    h_oth = [swap(part) for part in h]
+    normed, kv = keyvals(tp_index, h, h_oth, gain, kv_weight, *kv_tables, groups)
+    kv = kv.reshape(count, rows, HDIM)
+    kv = lax.all_to_all(kv, CTX, split_axis=0, concat_axis=0, tiled=True)
+    pieces = spread_heads(*queries_of(tp_index, normed, q_weight, *q_tables))
+    kv = gate(kv, *pieces[1:])
+    attended = attend(base, pieces, kv, swap(kv), 0)
+    a_own = lax.all_to_all(attended, "mem", split_axis=0, concat_axis=0, tiled=True)
+    return project_out(base, a_own, swap(a_own), out_weight, w_oth, (*h, *first), False, 0, 1)
 
 
 def solution(mesh):

time: 212 us -> 204 us (0.962)
  Pallas kernels: 78.2 us -> 70.5 us
  starting transfers between devices: 39.6 us -> 46 us
  other arithmetic: 6.41 us -> 1.76 us
    pallas_call x3 -> x1, Pallas kernels: 16.7 us -> 5.86 us  [queries_of(): pl.pallas_call(q_kernel, grid_spec=pltpu.PrefetchScalarGridSpec(num_scala...]
    ppermute x1 -> x2, waiting for transfers between devices: 22.6 us -> 13.7 us  [per_device(): h = [lax.ppermute(part, 'segment', [(0, 1)]) for part in first]]
    ppermute x6, waiting for transfers between devices: 11.3 us -> 15.6 us  [spread_heads(): lax.ppermute(pieces[d], 'mem', [(i, i ^ d) for i in range(KV_HEADS)])]
    pallas_call x9, Pallas kernels: 33.3 us -> 37.2 us  [the longest x3 19.2 us: project_out(): pl.pallas_call(functools.partial(out_kernel, placing, block, chunk), grid...]
    ppermute x12 -> x13, starting transfers between devices: 11.3 us -> 14.2 us  [swap(): return lax.ppermute(value, 'tp', [(0, 1), (1, 0)])]
    ppermute x12 -> x13, waiting for transfers between devices: 10.8 us -> 13.6 us  [swap(): return lax.ppermute(value, 'tp', [(0, 1), (1, 0)])]
    ppermute x3, starting transfers between devices: 4.79 us -> 7.5 us  [from_vision(): return lax.ppermute(sent, 'segment', [(1, 0)])]
    broadcast_in_dim x1 -> x0, other arithmetic: 2.25 us -> none  [per_device(): return out[None]]
  transfers between devices with their start and end apart: 25 -> 27, of which waited for: 15 -> 18; matrix products, arithmetic and copies ran while one was open for 3% -> 1% of each run, Pallas kernels for 23% -> 21%
where the time goes in v4:
time: 204 us; the launch traced here: 203 us
  Pallas kernels  70.5 us (35%)
  waiting for transfers between devices  50.5 us (25%)
  starting transfers between devices  46 us (23%)
  blocking collectives  21.1 us (10%)
  local copies, waits for them, and re-layouts  12.7 us (6%)
    all_to_all x2, blocking collectives, per_device(): lax.all_to_all(attended, 'mem', split_axis=0, concat_axis=0, tiled=True)  21.1 us
    pallas_call x3, Pallas kernels, project_out(): pl.pallas_call(functools.partial(out_kernel, placing, block, chunk), grid...  19.2 us
    pallas_call x2, Pallas kernels, attend(): pl.pallas_call(functools.partial(attend_kernel, frames, len(after)), grid...  16.7 us
    ppermute x6, waiting for transfers between devices, spread_heads(): lax.ppermute(pieces[d], 'mem', [(i, i ^ d) for i in range(KV_HEADS)])  15.6 us
    ppermute x13, starting transfers between devices, swap(): return lax.ppermute(value, 'tp', [(0, 1), (1, 0)])  14.2 us
    ppermute x2, waiting for transfers between devices, per_device(): h = [lax.ppermute(part, 'segment', [(0, 1)]) for part in first]  13.7 us
    ppermute x13, waiting for transfers between devices, swap(): return lax.ppermute(value, 'tp', [(0, 1), (1, 0)])  13.6 us
    unnamed x70, local copies, waits for them, and re-layouts  11.7 us
  transfers between devices with their start and end apart: 27, of which 18 were waited for; matrix products, arithmetic and copies ran while one was open for 1% of the time, Pallas kernels for 21%

profile of v4, /device:TPU:19, one launch (start us, length us, event | category | flops | bytes accessed | tf_op | source)
XLA Modules:
  0.0 203.2 jit_solution(13000862996791151146)
XLA Ops:
  0.7 2.8 %shard_map.82 = (f32[96,1792]{1,0:T(8,128)}, bf16[96,1792]{1,0:T(8,128)(2,1)}, bf16[8,48,576]{2,1,0:T(8,128)(2,1)}) custom-call(s32[1]{0:T(128)} %bitcast.1.tp_ref, bf16[96,576]{1,0:T(8,128)(2,1)} %x_ref.1, bf16[576,1792]{1,0:T(8,128)(2,1)} %w_ref.3), custom_call_target="tpu_custom_call" | custom-call | tf_op jit(solution)/shard_map/pallas_call | solution.py:115
  3.5 5.7 %all-to-all-start = ((bf16[8,48,576]{2,1,0:T(8,128)(2,1)}), bf16[8,48,576]{2,1,0:T(8,128)(2,1)S(1)}, u32[]{:S(2)}, u32[]{:S(2)}) async-start(bf16[8,48,576]{2,1,0:T(8,128)(2,1)} %get-tuple-element.28), calls=%async_computation | async-start | bytes 983040 | tf_op jit(solution)/shard_map/all_to_all | solution.py:695
  14.1 4.4 %collective-permute-done.1.refs_7_ = bf16[96,1792]{1,0:T(8,128)(2,1)S(1)} collective-permute-done((bf16[96,1792]{1,0:T(8,128)(2,1)}, bf16[96,1792]{1,0:T(8,128)(2,1)S(1)}, u32[]{:S(2)}, u32[]{:S(2)}) %collective-permute-start.1) | collective-permute-done | bytes 344096 | tf_op jit(solution)/shard_map/ppermute | solution.py:670
  22.2 9.7 %shard_map.84 = (bf16[2,4,544,128]{3,2,1,0:T(8,128)(2,1)}, bf16[2,2,256,128]{3,2,1,0:T(8,128)(2,1)}, bf16[2,2,256,128]{3,2,1,0:T(8,128)(2,1)}, bf16[2,2,96,128]{3,2,1,0:T(8,128)(2,1)}, bf16[2,2,96,128]{3,2,1,0:T(8,128)(2,1)}) custom-call(s32[1]{0:T(128)} %bitcast.1.tp_ref, bf16[256,1792]{1,0:T(8,128)(2,1)} %refs_0_.5, ...), custom_call_target="tpu_custom_call" | custom-call | tf_op jit(solution)/shard_map/pallas_call | solution.py:256
  37.8 5.4 %all-to-all-start.1 = ((bf16[8,544,128]{2,1,0:T(8,128)(2,1)}), bf16[8,544,128]{2,1,0:T(8,128)(2,1)S(1)}, u32[]{:S(2)}, u32[]{:S(2)}) async-start(bf16[8,544,128]{2,1,0:T(8,128)(2,1)} %bitcast.13), calls=%async_computation.1 | async-start | bytes 2228224 | tf_op jit(solution)/shard_map/all_to_all | solution.py:713
  46.5 4.4 %shard_map.86 = (f32[256,1792]{1,0:T(8,128)}, bf16[128,1792]{1,0:T(8,128)(2,1)}, bf16[128,1792]{1,0:T(8,128)(2,1)}) custom-call(bf16[2,4,544,128]{3,2,1,0:T(8,128)(2,1)} %copy-done.2, s32[256,1]{1,0:T(8,128)} %copy-done.6, s32[256,1]{1,0:T(8,128)} %copy-done.7, bf16[384,576]{1,0:T(8,128)(2,1)} %bitcast.15, bf16[384,576]{1,0:T(8,128)(2,1)} %copy-done.28, ...), custom_call_target="tpu_custom_call" | custom-call | flops 1 | bytes 1 | tf_op jit(solution)/shard_map/pallas_call | solution.py:73
  50.9 3.6 %shard_map.87.refs_0_ = bf16[1024,1792]{1,0:T(8,128)(2,1)} custom-call(s32[1]{0:T(128)} %bitcast.1.tp_ref, bf16[128,1792]{1,0:T(8,128)(2,1)} %get-tuple-element.34.after.refs_0_, bf16[1024,3584]{1,0:T(8,128)(2,1)} %bitcast.16), custom_call_target="tpu_custom_call" | custom-call | flops 1 | bytes 1 | tf_op jit(solution)/shard_map/pallas_call | solution.py:404
  55.0 4.0 %collective-permute-start.10 = (bf16[128,1792]{1,0:T(8,128)(2,1)S(1)}, bf16[128,1792]{1,0:T(8,128)(2,1)S(1)}, u32[]{:S(2)}, u32[]{:S(2)}) collective-permute-start(bf16[128,1792]{1,0:T(8,128)(2,1)S(1)} %copy-done.33), channel_id=1, source_target_pairs={{16,0},{17,1},{18,2},{19,3},{20,4},{21,5},{22,6},{23,7},{24,8},{25... | collective-permute-start | bytes 1376264 | tf_op jit(solution)/shard_map/ppermute | solution.py:670
  64.0 5.5 %collective-permute-done.6.refs_3_.refs_2_ = bf16[2,256,128]{2,1,0:T(8,128)(2,1)S(1)} collective-permute-done((bf16[2,256,128]{2,1,0:T(8,128)(2,1)S(1)}, bf16[2,256,128]{2,1,0:T(8,128)(2,1)S(1)}, u32[]{:S(2)}, u32[]{:S(2)}) %collective-permute-start.6) | collective-permute-done | bytes 131104 | tf_op jit(solution)/shard_map/ppermute | solution.py:677
  71.1 4.0 %collective-permute-done.8.refs_5_.refs_4_ = bf16[2,256,128]{2,1,0:T(8,128)(2,1)S(1)} collective-permute-done((bf16[2,256,128]{2,1,0:T(8,128)(2,1)S(1)}, bf16[2,256,128]{2,1,0:T(8,128)(2,1)S(1)}, u32[]{:S(2)}, u32[]{:S(2)}) %collective-permute-start.8) | collective-permute-done | bytes 131104 | tf_op jit(solution)/shard_map/ppermute | solution.py:677
  75.0 3.3 %collective-permute-done.9.refs_1_.refs_2_ = bf16[128,1792]{1,0:T(8,128)(2,1)S(1)} collective-permute-done((bf16[128,1792]{1,0:T(8,128)(2,1)S(1)}, bf16[128,1792]{1,0:T(8,128)(2,1)S(1)}, u32[]{:S(2)}, u32[]{:S(2)}) %collective-permute-start.9) | collective-permute-done | bytes 458784 | tf_op jit(solution)/shard_map/ppermute | solution.py:670
  84.9 8.6 %shard_map.90 = bf16[4,2,256,128]{3,2,1,0:T(8,128)(2,1)S(1)} custom-call(s32[12]{0:T(128)S(1)} %concatenate.17.at_ref, bf16[1024,1792]{1,0:T(8,128)(2,1)S(1)} %copy-done, bf16[2,256,128]{2,1,0:T(8,128)(2,1)S(1)} %copy-done.18, bf16[2,256,128]{2,1,0:T(8,128)(2,1)S(1)} %collective-permute-done.6.refs_3_.refs_2_, ...), custom_call_target="tpu_custom_call" | custom-call | tf_op jit(solution)/shard_map/pallas_call | solution.py:534
  93.5 10.6 %all_to_all.25.a_own = bf16[4,2,256,128]{3,2,1,0:T(8,128)(2,1)S(1)} all-to-all(bf16[4,2,256,128]{3,2,1,0:T(8,128)(2,1)S(1)} %shard_map.90), channel_id=1, replica_groups=mesh['segment'=2,'grp'=2,'mem'=4,'tp'=2] {'mem'}, dimensions={0} | all-to-all | bytes 1048576 | tf_op jit(solution)/shard_map/all_to_all | solution.py:725
  108.5 5.9 %shard_map.91.refs_2_ = bf16[256,896]{1,0:T(8,128)(2,1)} custom-call(s32[4]{0:T(128)} %copy-done.20, bf16[4,2,256,128]{3,2,1,0:T(8,128)(2,1)} %copy-done.22, bf16[4,2,256,128]{3,2,1,0:T(8,128)(2,1)} %copy-done.23, bf16[1024,3584]{1,0:T(8,128)(2,1)} %bitcast.17, bf16[1024,1792]{1,0:T(8,128)(2,1)} %collective-permute-done.13.w_oth, bf16[256,1792]{1,0:T(8,128)(2,1)} %refs_0_.5, ...), custom_call_target="tpu_custom_call" | custom-call | tf_op jit(solution)/shard_map/pallas_call | solution.py:627
  115.7 5.9 %shard_map.92.refs_3_ = bf16[256,896]{1,0:T(8,128)(2,1)} custom-call(s32[4]{0:T(128)} %copy-done.20, bf16[4,2,256,128]{3,2,1,0:T(8,128)(2,1)} %copy-done.22, bf16[4,2,256,128]{3,2,1,0:T(8,128)(2,1)} %copy-done.23, bf16[1024,3584]{1,0:T(8,128)(2,1)} %bitcast.18, bf16[1024,1792]{1,0:T(8,128)(2,1)} %collective-permute-done.13.w_oth, bf16[256,1792]{1,0:T(8,128)(2,1)} %refs_0_.5, ...), custom_call_target="tpu_custom_call" | custom-call | tf_op jit(solution)/shard_map/pallas_call | solution.py:627
  122.9 5.6 %collective-permute-done.14.refs_0_ = bf16[256,896]{1,0:T(8,128)(2,1)S(1)} collective-permute-done((bf16[256,896]{1,0:T(8,128)(2,1)}, bf16[256,896]{1,0:T(8,128)(2,1)S(1)}, u32[]{:S(2)}, u32[]{:S(2)}) %collective-permute-start.14) | collective-permute-done | bytes 458784 | tf_op jit(solution)/shard_map/ppermute | solution.py:733
  130.2 8.1 %collective-permute-done.15.refs_1_ = bf16[256,896]{1,0:T(8,128)(2,1)S(1)} collective-permute-done((bf16[256,896]{1,0:T(8,128)(2,1)}, bf16[256,896]{1,0:T(8,128)(2,1)S(1)}, u32[]{:S(2)}, u32[]{:S(2)}) %collective-permute-start.15) | collective-permute-done | bytes 458784 | tf_op jit(solution)/shard_map/ppermute | solution.py:733
  141.7 5.6 %shard_map.93 = (bf16[256,3584]{1,0:T(8,128)(2,1)}, bf16[2,4,256,128]{3,2,1,0:T(8,128)(2,1)}) custom-call(s32[1]{0:T(128)} %bitcast.1.tp_ref, bf16[256,896]{1,0:T(8,128)(2,1)} %copy-done.25, bf16[256,896]{1,0:T(8,128)(2,1)} %copy-done.26, bf16[256,896]{1,0:T(8,128)(2,1)} %copy-done.29, bf16[256,896]{1,0:T(8,128)(2,1)} %copy-done.30, f32[1,3584]{1,0:T(1,128)} %refs_4_.3, ...), custom_call_target="tpu_custom_call" | custom-call | tf_op jit(solution)/shard_map/pallas_call | solution.py:199
  147.3 4.0 %all-to-all-start.3 = ((bf16[8,256,128]{2,1,0:T(8,128)(2,1)}), bf16[8,256,128]{2,1,0:T(8,128)(2,1)S(1)}, u32[]{:S(2)}, u32[]{:S(2)}) async-start(bf16[8,256,128]{2,1,0:T(8,128)(2,1)} %bitcast.24), calls=%async_computation.3 | async-start | bytes 1048576 | tf_op jit(solution)/shard_map/all_to_all | solution.py:737
  151.3 5.9 %shard_map.94 = (bf16[2,2,256,128]{3,2,1,0:T(8,128)(2,1)}, bf16[2,2,256,128]{3,2,1,0:T(8,128)(2,1)}) custom-call(s32[1]{0:T(128)} %bitcast.1.tp_ref, bf16[256,3584]{1,0:T(8,128)(2,1)} %get-tuple-element.43.refs_0_, bf16[3584,1024]{1,0:T(8,128)(2,1)} %bitcast.21, f32[352,128]{1,0:T(8,128)} %copy-done.10, f32[352,128]{1,0:T(8,128)} %copy-done.11), custom_call_target="tpu_custom_call" | custom-call | flops 1 | bytes 1 | tf_op jit(solution)/shard_map/pallas_call | solution.py:296
  166.7 3.2 %collective-permute-done.21.refs_3_ = bf16[2,256,128]{2,1,0:T(8,128)(2,1)S(1)} collective-permute-done((bf16[2,256,128]{2,1,0:T(8,128)(2,1)S(1)}, bf16[2,256,128]{2,1,0:T(8,128)(2,1)S(1)}, u32[]{:S(2)}, u32[]{:S(2)}) %collective-permute-start.21) | collective-permute-done | bytes 131104 | tf_op jit(solution)/shard_map/ppermute | solution.py:677
  172.6 8.1 %shard_map.97 = bf16[4,2,256,128]{3,2,1,0:T(8,128)(2,1)S(1)} custom-call(s32[4]{0:T(128)S(1)} %copy-done.21, bf16[2,256,128]{2,1,0:T(8,128)(2,1)S(1)} %get-tuple-element.46.refs_0_, bf16[2,256,128]{2,1,0:T(8,128)(2,1)S(1)} %collective-permute-done.19.refs_1_, bf16[2,256,128]{2,1,0:T(8,128)(2,1)S(1)} %collective-permute-done.20.refs_2_, ...), custom_call_target="tpu_custom_call" | custom-call | tf_op jit(solution)/shard_map/pallas_call | solution.py:534
  180.7 10.6 %all_to_all.26.a_own = bf16[4,2,256,128]{3,2,1,0:T(8,128)(2,1)S(1)} all-to-all(bf16[4,2,256,128]{3,2,1,0:T(8,128)(2,1)S(1)} %shard_map.97), channel_id=1, replica_groups=mesh['segment'=2,'grp'=2,'mem'=4,'tp'=2] {'mem'}, dimensions={0} | all-to-all | bytes 1048576 | tf_op jit(solution)/shard_map/all_to_all | solution.py:741
  195.7 7.4 %shard_map.98 = bf16[1,256,1792]{2,1,0:T(8,128)(2,1)} custom-call(s32[4]{0:T(128)} %copy-done.20, bf16[4,2,256,128]{3,2,1,0:T(8,128)(2,1)} %copy-done.24, bf16[4,2,256,128]{3,2,1,0:T(8,128)(2,1)} %copy-done.27, bf16[1024,3584]{1,0:T(8,128)(2,1)} %bitcast.19, bf16[1024,1792]{1,0:T(8,128)(2,1)} %collective-permute-done.13.w_oth, bf16[256,896]{1,0:T(8,128)(2,1)} %copy-done.25, ...), custom_call_target="tpu_custom_call" | custom-call | tf_op jit(solution)/shard_map/pallas_call | solution.py:627
  (132 shorter events, 60.4 us)
Async XLA Ops:
  0.0 21.5 %collective-permute-start = (bf16[256,1792]{1,0:T(8,128)(2,1)}, bf16[256,1792]{1,0:T(8,128)(2,1)}, u32[]{:S(2)}, u32[]{:S(2)}) collective-permute-start(bf16[256,1792]{1,0:T(8,128)(2,1)} %refs_0_.5), channel_id=1, source_target_pairs={{0,1},{1,0},{2,3},{3,2},{4,5},{5,4},{6,7},{7,6},{8,9},{9,8},{10,11... | collective-permute-start | bytes 2752520 | tf_op jit(solution)/shard_map/ppermute | solution.py:37
  3.5 28.9 %all-to-all-start = ((bf16[8,48,576]{2,1,0:T(8,128)(2,1)}), bf16[8,48,576]{2,1,0:T(8,128)(2,1)S(1)}, u32[]{:S(2)}, u32[]{:S(2)}) async-start(bf16[8,48,576]{2,1,0:T(8,128)(2,1)} %get-tuple-element.28), calls=%async_computation | async-start | bytes 983040 | tf_op jit(solution)/shard_map/all_to_all | solution.py:695
  9.2 9.3 %collective-permute-start.1 = (bf16[96,1792]{1,0:T(8,128)(2,1)}, bf16[96,1792]{1,0:T(8,128)(2,1)S(1)}, u32[]{:S(2)}, u32[]{:S(2)}) collective-permute-start(bf16[96,1792]{1,0:T(8,128)(2,1)} %get-tuple-element.30), channel_id=1, source_target_pairs={{16,0},{17,1},{18,2},{19,3},{20,4},{21,5},{22,6},{23,7},{24,8},{25... | collective-permute-start | bytes 1032200 | tf_op jit(solution)/shard_map/ppermute | solution.py:670
  18.7 2.8 %collective-permute-start.2 = (bf16[96,1792]{1,0:T(8,128)(2,1)S(1)}, bf16[96,1792]{1,0:T(8,128)(2,1)S(1)}, u32[]{:S(2)}, u32[]{:S(2)}) collective-permute-start(bf16[96,1792]{1,0:T(8,128)(2,1)S(1)} %shard_map.83.refs_2_), channel_id=1, source_target_pairs={{0,1},{1,0},{2,3},{3,2},{4,5},{5,4},{6,7},{7,6},{8,9},{9,8},{10,11... | collective-permute-start | bytes 1032200 | tf_op jit(solution)/shard_map/ppermute | solution.py:37
  37.8 40.5 %all-to-all-start.1 = ((bf16[8,544,128]{2,1,0:T(8,128)(2,1)}), bf16[8,544,128]{2,1,0:T(8,128)(2,1)S(1)}, u32[]{:S(2)}, u32[]{:S(2)}) async-start(bf16[8,544,128]{2,1,0:T(8,128)(2,1)} %bitcast.13), calls=%async_computation.1 | async-start | bytes 2228224 | tf_op jit(solution)/shard_map/all_to_all | solution.py:713
  54.5 51.7 %collective-permute-start.13 = (bf16[1024,1792]{1,0:T(8,128)(2,1)}, bf16[1024,1792]{1,0:T(8,128)(2,1)}, u32[]{:S(2)}, u32[]{:S(2)}) collective-permute-start(bf16[1024,1792]{1,0:T(8,128)(2,1)} %shard_map.87.refs_0_), channel_id=1, source_target_pairs={{0,1},{1,0},{2,3},{3,2},{4,5},{5,4},{6,7},{7,6},{8,9},{9,8},{10,11... | collective-permute-start | bytes 11010056 | tf_op jit(solution)/shard_map/ppermute | solution.py:37
  54.8 5.5 %collective-permute-start.5 = (bf16[2,2,256,128]{3,2,1,0:T(8,128)(2,1)S(1)}, bf16[2,2,256,128]{3,2,1,0:T(8,128)(2,1)S(1)}, u32[]{:S(2)}, u32[]{:S(2)}) collective-permute-start(bf16[2,2,256,128]{3,2,1,0:T(8,128)(2,1)S(1)} %copy-done.34), channel_id=1, source_target_pairs={{0,1},{1,0},{2,3},{3,2},{4,5},{5,4},{6,7},{7,6},{8,9},{9,8},{10,11... | collective-permute-start | bytes 786440 | tf_op jit(solution)/shard_map/ppermute | solution.py:37
  55.0 20.0 %collective-permute-start.10 = (bf16[128,1792]{1,0:T(8,128)(2,1)S(1)}, bf16[128,1792]{1,0:T(8,128)(2,1)S(1)}, u32[]{:S(2)}, u32[]{:S(2)}) collective-permute-start(bf16[128,1792]{1,0:T(8,128)(2,1)S(1)} %copy-done.33), channel_id=1, source_target_pairs={{16,0},{17,1},{18,2},{19,3},{20,4},{21,5},{22,6},{23,7},{24,8},{25... | collective-permute-start | bytes 1376264 | tf_op jit(solution)/shard_map/ppermute | solution.py:670
  59.0 19.3 %collective-permute-start.9 = (bf16[128,1792]{1,0:T(8,128)(2,1)S(1)}, bf16[128,1792]{1,0:T(8,128)(2,1)S(1)}, u32[]{:S(2)}, u32[]{:S(2)}) collective-permute-start(bf16[128,1792]{1,0:T(8,128)(2,1)S(1)} %copy-done.12), channel_id=1, source_target_pairs={{16,0},{17,1},{18,2},{19,3},{20,4},{21,5},{22,6},{23,7},{24,8},{25... | collective-permute-start | bytes 1376264 | tf_op jit(solution)/shard_map/ppermute | solution.py:670
  61.7 7.9 %collective-permute-start.6 = (bf16[2,256,128]{2,1,0:T(8,128)(2,1)S(1)}, bf16[2,256,128]{2,1,0:T(8,128)(2,1)S(1)}, u32[]{:S(2)}, u32[]{:S(2)}) collective-permute-start(bf16[2,256,128]{2,1,0:T(8,128)(2,1)S(1)} %get-tuple-element.38), channel_id=1, source_target_pairs={{0,2},{2,0},{4,6},{6,4},{1,3},{3,1},{5,7},{7,5},{8,10},{10,8},{12,... | collective-permute-start | bytes 393224 | tf_op jit(solution)/shard_map/ppermute | solution.py:677
  62.8 8.2 %collective-permute-start.7 = (bf16[2,256,128]{2,1,0:T(8,128)(2,1)S(1)}, bf16[2,256,128]{2,1,0:T(8,128)(2,1)S(1)}, u32[]{:S(2)}, u32[]{:S(2)}) collective-permute-start(bf16[2,256,128]{2,1,0:T(8,128)(2,1)S(1)} %get-tuple-element.39), channel_id=1, source_target_pairs={{0,4},{2,6},{4,0},{6,2},{1,5},{3,7},{5,1},{7,3},{8,12},{10,14},{12... | collective-permute-start | bytes 393224 | tf_op jit(solution)/shard_map/ppermute | solution.py:677
  69.6 5.5 %collective-permute-start.8 = (bf16[2,256,128]{2,1,0:T(8,128)(2,1)S(1)}, bf16[2,256,128]{2,1,0:T(8,128)(2,1)S(1)}, u32[]{:S(2)}, u32[]{:S(2)}) collective-permute-start(bf16[2,256,128]{2,1,0:T(8,128)(2,1)S(1)} %get-tuple-element.40), channel_id=1, source_target_pairs={{0,6},{2,4},{4,2},{6,0},{1,7},{3,5},{5,3},{7,1},{8,14},{10,12},{12... | collective-permute-start | bytes 393224 | tf_op jit(solution)/shard_map/ppermute | solution.py:677
  78.3 3.6 %collective-permute-start.11 = (bf16[8,544,128]{2,1,0:T(8,128)(2,1)S(1)}, bf16[8,544,128]{2,1,0:T(8,128)(2,1)S(1)}, u32[]{:S(2)}, u32[]{:S(2)}) collective-permute-start(bf16[8,544,128]{2,1,0:T(8,128)(2,1)S(1)} %shard_map.89.refs_5_), channel_id=1, source_target_pairs={{0,1},{1,0},{2,3},{3,2},{4,5},{5,4},{6,7},{7,6},{8,9},{9,8},{10,11... | collective-permute-start | bytes 3342344 | tf_op jit(solution)/shard_map/ppermute | solution.py:37
  104.1 3.6 %collective-permute-start.12 = (bf16[4,2,256,128]{3,2,1,0:T(8,128)(2,1)S(1)}, bf16[4,2,256,128]{3,2,1,0:T(8,128)(2,1)S(1)}, u32[]{:S(2)}, u32[]{:S(2)}) collective-permute-start(bf16[4,2,256,128]{3,2,1,0:T(8,128)(2,1)S(1)} %all_to_all.25.a_own), channel_id=1, source_target_pairs={{0,1},{1,0},{2,3},{3,2},{4,5},{5,4},{6,7},{7,6},{8,9},{9,8},{10,11... | collective-permute-start | bytes 1572872 | tf_op jit(solution)/shard_map/ppermute | solution.py:37
  114.4 14.1 %collective-permute-start.14 = (bf16[256,896]{1,0:T(8,128)(2,1)}, bf16[256,896]{1,0:T(8,128)(2,1)S(1)}, u32[]{:S(2)}, u32[]{:S(2)}) collective-permute-start(bf16[256,896]{1,0:T(8,128)(2,1)} %shard_map.91.refs_2_), channel_id=1, source_target_pairs={{0,16},{1,17},{2,18},{3,19},{4,20},{5,21},{6,22},{7,23},{8,24},{9,... | collective-permute-start | bytes 1376264 | tf_op jit(solution)/shard_map/ppermute | solution.py:733
  121.6 16.7 %collective-permute-start.15 = (bf16[256,896]{1,0:T(8,128)(2,1)}, bf16[256,896]{1,0:T(8,128)(2,1)S(1)}, u32[]{:S(2)}, u32[]{:S(2)}) collective-permute-start(bf16[256,896]{1,0:T(8,128)(2,1)} %shard_map.92.refs_3_), channel_id=1, source_target_pairs={{0,16},{1,17},{2,18},{3,19},{4,20},{5,21},{6,22},{7,23},{8,24},{9,... | collective-permute-start | bytes 1376264 | tf_op jit(solution)/shard_map/ppermute | solution.py:733
  128.5 10.9 %collective-permute-start.16 = (bf16[256,896]{1,0:T(8,128)(2,1)S(1)}, bf16[256,896]{1,0:T(8,128)(2,1)S(1)}, u32[]{:S(2)}, u32[]{:S(2)}) collective-permute-start(bf16[256,896]{1,0:T(8,128)(2,1)S(1)} %collective-permute-done.14.refs_0_), channel_id=1, source_target_pairs={{0,1},{1,0},{2,3},{3,2},{4,5},{5,4},{6,7},{7,6},{8,9},{9,8},{10,11... | collective-permute-start | bytes 1376264 | tf_op jit(solution)/shard_map/ppermute | solution.py:37
  138.3 2.5 %collective-permute-start.17 = (bf16[256,896]{1,0:T(8,128)(2,1)S(1)}, bf16[256,896]{1,0:T(8,128)(2,1)S(1)}, u32[]{:S(2)}, u32[]{:S(2)}) collective-permute-start(bf16[256,896]{1,0:T(8,128)(2,1)S(1)} %collective-permute-done.15.refs_1_), channel_id=1, source_target_pairs={{0,1},{1,0},{2,3},{3,2},{4,5},{5,4},{6,7},{7,6},{8,9},{9,8},{10,11... | collective-permute-start | bytes 1376264 | tf_op jit(solution)/shard_map/ppermute | solution.py:37
  147.3 22.6 %all-to-all-start.3 = ((bf16[8,256,128]{2,1,0:T(8,128)(2,1)}), bf16[8,256,128]{2,1,0:T(8,128)(2,1)S(1)}, u32[]{:S(2)}, u32[]{:S(2)}) async-start(bf16[8,256,128]{2,1,0:T(8,128)(2,1)} %bitcast.24), calls=%async_computation.3 | async-start | bytes 1048576 | tf_op jit(solution)/shard_map/all_to_all | solution.py:737
  161.1 4.8 %collective-permute-start.19 = (bf16[2,256,128]{2,1,0:T(8,128)(2,1)S(1)}, bf16[2,256,128]{2,1,0:T(8,128)(2,1)S(1)}, u32[]{:S(2)}, u32[]{:S(2)}) collective-permute-start(bf16[2,256,128]{2,1,0:T(8,128)(2,1)S(1)} %get-tuple-element.47), channel_id=1, source_target_pairs={{0,2},{2,0},{4,6},{6,4},{1,3},{3,1},{5,7},{7,5},{8,10},{10,8},{12,... | collective-permute-start | bytes 393224 | tf_op jit(solution)/shard_map/ppermute | solution.py:677
  162.3 4.4 %collective-permute-start.20 = (bf16[2,256,128]{2,1,0:T(8,128)(2,1)S(1)}, bf16[2,256,128]{2,1,0:T(8,128)(2,1)S(1)}, u32[]{:S(2)}, u32[]{:S(2)}) collective-permute-start(bf16[2,256,128]{2,1,0:T(8,128)(2,1)S(1)} %get-tuple-element.48), channel_id=1, source_target_pairs={{0,4},{2,6},{4,0},{6,2},{1,5},{3,7},{5,1},{7,3},{8,12},{10,14},{12... | collective-permute-start | bytes 393224 | tf_op jit(solution)/shard_map/ppermute | solution.py:677
  163.5 6.4 %collective-permute-start.21 = (bf16[2,256,128]{2,1,0:T(8,128)(2,1)S(1)}, bf16[2,256,128]{2,1,0:T(8,128)(2,1)S(1)}, u32[]{:S(2)}, u32[]{:S(2)}) collective-permute-start(bf16[2,256,128]{2,1,0:T(8,128)(2,1)S(1)} %get-tuple-element.49), channel_id=1, source_target_pairs={{0,6},{2,4},{4,2},{6,0},{1,7},{3,5},{5,3},{7,1},{8,14},{10,12},{12... | collective-permute-start | bytes 393224 | tf_op jit(solution)/shard_map/ppermute | solution.py:677
  169.9 2.7 %collective-permute-start.22 = (bf16[8,256,128]{2,1,0:T(8,128)(2,1)S(1)}, bf16[8,256,128]{2,1,0:T(8,128)(2,1)S(1)}, u32[]{:S(2)}, u32[]{:S(2)}) collective-permute-start(bf16[8,256,128]{2,1,0:T(8,128)(2,1)S(1)} %shard_map.96.refs_4_), channel_id=1, source_target_pairs={{0,1},{1,0},{2,3},{3,2},{4,5},{5,4},{6,7},{7,6},{8,9},{9,8},{10,11... | collective-permute-start | bytes 1572872 | tf_op jit(solution)/shard_map/ppermute | solution.py:37
  191.2 3.6 %collective-permute-start.23 = (bf16[4,2,256,128]{3,2,1,0:T(8,128)(2,1)S(1)}, bf16[4,2,256,128]{3,2,1,0:T(8,128)(2,1)S(1)}, u32[]{:S(2)}, u32[]{:S(2)}) collective-permute-start(bf16[4,2,256,128]{3,2,1,0:T(8,128)(2,1)S(1)} %all_to_all.26.a_own), channel_id=1, source_target_pairs={{0,1},{1,0},{2,3},{3,2},{4,5},{5,4},{6,7},{7,6},{8,9},{9,8},{10,11... | collective-permute-start | bytes 1572872 | tf_op jit(solution)/shard_map/ppermute | solution.py:37
  (38 other events, 219.2 us)

commit v5 on v4

--- a/solution.py
+++ b/solution.py
@@ -48,7 +48,7 @@
     )
 
 
-def place_kernel(after, idx_own, idx_oth, pf_own, pf_oth, w_ref, wide_ref, upper, lower, placed):
+def place_kernel(after, idx_own, idx_oth, pf_own, pf_oth, w_ref, wide_ref, left, right, placed):
     @pl.when(pl.program_id(0) == 0)
     def _():
         rows, count = idx_own.shape[0], pf_own.shape[0]
@@ -61,9 +61,14 @@
 
     term = jnp.dot(placed[...], w_ref[...], preferred_element_type=F32)
     wide_ref[...] = term
-    half = upper.shape[0]
-    upper[...] = term[:half].astype(BF16)
-    lower[...] = term[half:].astype(BF16)
+
+    @pl.when(pl.program_id(0) == 0)
+    def _():
+        left[...] = term.astype(BF16)
+
+    @pl.when(pl.program_id(0) == 1)
+    def _():
+        right[...] = term.astype(BF16)
 
 
 def project_placed(after, idx_own, idx_oth, pf_own, pf_oth, proj_weight):
@@ -83,57 +88,61 @@
         ],
         out_specs=[
             pl.BlockSpec((rows, block), lambda i: (0, i)),
-            *[pl.BlockSpec((rows // 2, block), lambda i: (0, i))] * 2,
+            *[pl.BlockSpec((rows, block), whole)] * 2,
         ],
         out_shape=[
             jax.ShapeDtypeStruct((rows, cols), F32),
-            *[jax.ShapeDtypeStruct((rows // 2, cols), BF16)] * 2,
+            *[jax.ShapeDtypeStruct((rows, block), BF16)] * 2,
         ],
         scratch_shapes=[pltpu.VMEM((rows, depth), BF16)],
         cost_estimate=LITTLE,
-        compiler_params=params(56),
+        compiler_params=params(60),
     )(after, idx_own, idx_oth, pf_own, pf_oth, proj_weight)
 
 
-def project_kernel(tp_ref, x_ref, w_ref, wide_ref, sent_ref, spread_ref):
-    @pl.when(pl.program_id(0) == 0)
-    def _():
-        part = spread_ref.shape[1]
-        mine = x_ref[pl.ds(pl.multiple_of(tp_ref[0] * part, part), part), :]
-        for c in range(spread_ref.shape[0]):
-            spread_ref[c] = mine
-
+def project_kernel(x_ref, w_ref, wide_ref, sent_ref):
     term = jnp.dot(x_ref[...], w_ref[...], preferred_element_type=F32)
     wide_ref[...] = term
     sent_ref[...] = term.astype(BF16)
 
 
-def project(tp_index, values, proj_weight, count):
+def project(values, proj_weight):
     rows, (depth, cols) = values.shape[0], proj_weight.shape
     block = cols // 2
-    part = rows // 2
     return pl.pallas_call(
         project_kernel,
-        grid_spec=pltpu.PrefetchScalarGridSpec(
-            num_scalar_prefetch=1,
-            grid=(cols // block,),
-            in_specs=[
-                pl.BlockSpec((rows, depth), lambda i, t: (0, 0)),
-                pl.BlockSpec((depth, block), lambda i, t: (0, i)),
-            ],
-            out_specs=[
-                pl.BlockSpec((rows, block), lambda i, t: (0, i)),
-                pl.BlockSpec((rows, block), lambda i, t: (0, i)),
-                pl.BlockSpec((count, part, depth), lambda i, t: (0, 0, 0)),
-            ],
-        ),
+        grid=(cols // block,),
+        in_specs=[
+            pl.BlockSpec((rows, depth), lambda i: (0, 0)),
+            pl.BlockSpec((depth, block), lambda i: (0, i)),
+        ],
+        out_specs=[pl.BlockSpec((rows, block), lambda i: (0, i))] * 2,
         out_shape=[
             jax.ShapeDtypeStruct((rows, cols), F32),
             jax.ShapeDtypeStruct((rows, cols), BF16),
-            jax.ShapeDtypeStruct((count, part, depth), BF16),
-        ],
-        compiler_params=params(56),
-    )(tp_index, values, proj_weight)
+        ],
+        compiler_params=params(60),
+    )(values, proj_weight)
+
+
+def spread_kernel(tp_ref, after, x_ref, o_ref):
+    part = o_ref.shape[1]
+    mine = x_ref[pl.ds(pl.multiple_of(tp_ref[0] * part, part), part), :]
+    for c in range(o_ref.shape[0]):
+        o_ref[c] = mine
+
+
+def spread(tp_index, after, values, count):
+    rows, depth = values.shape
+    shape = (count, rows // 2, depth)
+    return pl.pallas_call(
+        spread_kernel,
+        grid=(1,),
+        in_specs=[SMEM, ANY, pl.BlockSpec((rows, depth), lambda i: (0, 0))],
+        out_specs=pl.BlockSpec(shape, lambda i: (0, 0, 0)),
+        out_shape=jax.ShapeDtypeStruct(shape, BF16),
+        compiler_params=params(60),
+    )(tp_index, after, values)
 
 
 def gelu_kernel(*refs):
@@ -148,7 +157,7 @@
         in_specs=[*[ANY] * len(after), VMEM, VMEM],
         out_specs=VMEM,
         out_shape=jax.ShapeDtypeStruct(wide.shape, BF16),
-        compiler_params=params(16),
+        compiler_params=params(60),
     )(*after, wide, came)
 
 
@@ -205,7 +214,7 @@
             jax.ShapeDtypeStruct((groups, cols // HDIM, rows, HDIM), BF16),
         ],
         scratch_shapes=[pltpu.VMEM(kv_weight.shape, BF16), pltpu.SemaphoreType.DMA],
-        compiler_params=params(56),
+        compiler_params=params(60),
     )(tp_index, *own, *oth, gain, kv_weight, cosine, sine)
 
 
@@ -309,7 +318,7 @@
         ),
         out_shape=[jax.ShapeDtypeStruct((steps, 2, rows, HDIM), BF16)] * 2,
         cost_estimate=LITTLE,
-        compiler_params=params(56),
+        compiler_params=params(60),
     )(tp_index, *after, normed, q_weight, cosine, sine)
 
 
@@ -337,7 +346,7 @@
         out_specs=[VMEM] * KV_HEADS,
         out_shape=[jax.ShapeDtypeStruct(kept.shape[1:], BF16)] * KV_HEADS,
         cost_estimate=LITTLE,
-        compiler_params=params(16),
+        compiler_params=params(60),
     )(at, *after, kept, given)
 
 
@@ -375,7 +384,7 @@
         out_shape=jax.ShapeDtypeStruct(packed.shape, BF16),
         scratch_shapes=[pltpu.SemaphoreType.DMA((2 * KV_HEADS * packed.shape[0],))],
         input_output_aliases={2: 0},
-        compiler_params=params(16),
+        compiler_params=params(60),
     )(at, after, packed, f_kept, f_given)
 
 
@@ -390,7 +399,7 @@
         out_specs=ANY,
         out_shape=jax.ShapeDtypeStruct(value.shape, value.dtype),
         input_output_aliases={0: 0},
-        compiler_params=params(16),
+        compiler_params=params(60),
     )(value, *after)
 
 
@@ -411,7 +420,7 @@
         ),
         out_shape=jax.ShapeDtypeStruct((depth, cols // 2), BF16),
         cost_estimate=LITTLE,
-        compiler_params=params(56),
+        compiler_params=params(60),
     )(tp_index, after, weight)
 
 
@@ -439,8 +448,10 @@
 
 def attend_kernel(frames, skip, at_ref, *refs):
     refs = refs[skip:]
-    pieces, (own, oth, o_ref, keys, vals, qs) = refs[:-6], refs[-6:]
-    members, heads, rows, _ = o_ref.shape
+    members = KV_HEADS
+    pieces, (own, oth), outs = refs[:members], refs[members : members + 2], refs[members + 2 : -4]
+    keys, vals, qs, done = refs[-4:]
+    heads, rows, _ = outs[0].shape
     count = own.shape[0]
     base, core, me = at_ref[0], at_ref[1], at_ref[2]
     every, low, high = slice(None), slice(0, HDIM), slice(HDIM, 2 * HDIM)
@@ -522,7 +533,9 @@
                 state[i] = update(state[i], h, c, full + e, c * rows < (e + 1) * BK)
     for i, (h, c) in enumerate(chains):
         acc = state[i][1]
-        o_ref[c, h] = (acc[:, :HDIM] / acc[:, HDIM:]).astype(BF16)
+        done[c, h] = (acc[:, :HDIM] / acc[:, HDIM:]).astype(BF16)
+    for d in range(members):
+        outs[d][...] = done[jnp.bitwise_xor(me, d)]
 
 
 def attend(at, pieces, own, oth, frames, *after):
@@ -530,7 +543,8 @@
     members = KV_HEADS
     span = own.shape[0] * rows
     zeros = lambda value: pl.BlockSpec(value.shape, lambda i, t: (0,) * value.ndim)
-    shape = (members, heads, rows, HDIM)
+    shape = (heads, rows, HDIM)
+    done = (members, heads, rows, HDIM)
     return pl.pallas_call(
         functools.partial(attend_kernel, frames, len(after)),
         grid_spec=pltpu.PrefetchScalarGridSpec(
@@ -540,21 +554,23 @@
                 *[ANY] * len(after),
                 *[zeros(value) for value in (*pieces, own, oth)],
             ],
-            out_specs=pl.BlockSpec(shape, lambda i, t: (0, 0, 0, 0)),
+            out_specs=[pl.BlockSpec(shape, lambda i, t: (0, 0, 0))] * members,
             scratch_shapes=[
                 pltpu.VMEM((span + PAD, HDIM), BF16),
                 pltpu.VMEM((span + PAD, 2 * HDIM), BF16),
                 pltpu.VMEM((heads, members * rows + 3 * PAD, HDIM), BF16),
+                pltpu.VMEM(done, BF16),
             ],
         ),
-        out_shape=jax.ShapeDtypeStruct(shape, BF16),
-        compiler_params=params(40),
+        out_shape=[jax.ShapeDtypeStruct(shape, BF16)] * members,
+        compiler_params=params(60),
     )(at, *after, *pieces, own, oth)
 
 
-def out_kernel(placing, width, chunk, at_ref, a_own, a_oth, w_own, w_oth, *refs):
-    *residual, o_ref, near, far, own_w, oth_w, sems = refs
-    core, segment = at_ref[1], at_ref[3]
+def out_kernel(placing, width, chunk, at_ref, *refs):
+    a_own, a_oth, refs = refs[:KV_HEADS], refs[KV_HEADS : 2 * KV_HEADS], refs[2 * KV_HEADS :]
+    w_own, w_oth, *residual, o_ref, both, own_w, oth_w, sems = refs
+    core, me, segment = at_ref[1], at_ref[2], at_ref[3]
     half = o_ref.shape[-1]
     lanes = [slice(c, min(c + width, half)) for c in range(0, half, width)]
     start = pl.multiple_of(core * w_oth.shape[1], HDIM) + chunk * half
@@ -572,28 +588,26 @@
     for pair in copies:
         for copy in pair:
             copy.start()
-    for jj in range(2):
+    for d in range(KV_HEADS):
+        j = jnp.bitwise_xor(me, d)
+        away = jnp.where(jnp.right_shift(j, 1) == core, 0, 1)
+        low = jnp.bitwise_and(j, 1)
         for h in range(2):
-            mine = pl.multiple_of((2 * (2 * jj + core) + h) * HDIM, HDIM)
-            theirs = pl.multiple_of((2 * (2 * jj + 1 - core) + h) * HDIM, HDIM)
-            near[:, pl.ds(mine, HDIM)] = a_own[2 * core + jj, h]
-            near[:, pl.ds(theirs, HDIM)] = a_oth[2 * core + jj, h]
-            far[:, pl.ds(mine, HDIM)] = a_own[2 * (1 - core) + jj, h]
-            far[:, pl.ds(theirs, HDIM)] = a_oth[2 * (1 - core) + jj, h]
+            mine = pl.multiple_of((2 * (2 * low + core) + h) * HDIM, HDIM)
+            theirs = pl.multiple_of((2 * (2 * low + 1 - core) + h) * HDIM, HDIM)
+            both[away, :, pl.ds(mine, HDIM)] = a_own[d][h]
+            both[away, :, pl.ds(theirs, HDIM)] = a_oth[d][h]
     if placing:
-        text, wide, upper, lower, idx_own, idx_oth = residual
+        text, wide, came, idx_own, idx_oth = residual
         is_frame = jnp.maximum(idx_own[...], idx_oth[...]) >= 0
-        rows = upper.shape[0]
-        for r, came in enumerate((upper, lower)):
-            at = slice(r * rows, (r + 1) * rows)
-            total = wide[at, :] + came[...].astype(F32)
-            gelu = 0.5 * total * (1.0 + lax.erf(total * math.sqrt(0.5)))
-            o_ref[at, :] = jnp.where(is_frame[at], gelu, text[at, :].astype(F32)).astype(BF16)
+        total = wide[...] + came[...].astype(F32)
+        gelu = 0.5 * total * (1.0 + lax.erf(total * math.sqrt(0.5)))
+        o_ref[...] = jnp.where(is_frame, gelu, text[...].astype(F32)).astype(BF16)
     for i, at in enumerate(lanes):
         for copy in copies[i]:
             copy.wait()
-        term = jnp.dot(near[...], own_w[:, at], preferred_element_type=F32)
-        term += jnp.dot(far[...], oth_w[:, at], preferred_element_type=F32)
+        term = jnp.dot(both[0], own_w[:, at], preferred_element_type=F32)
+        term += jnp.dot(both[1], oth_w[:, at], preferred_element_type=F32)
         if placing:
             o_ref[:, at] = (o_ref[:, at].astype(F32) + term).astype(BF16)
         else:
@@ -610,7 +624,7 @@
 
 
 def project_out(at, a_own, a_oth, w_own, w_oth, residual, placing, chunk, chunks):
-    rows = a_own.shape[2]
+    rows = a_own[0].shape[1]
     depth, cols = w_oth.shape
     width = cols // chunks
     shape = (rows, width) if placing else (1, rows, width)
@@ -622,21 +636,21 @@
         else pl.BlockSpec(value.shape, whole)
         for value in residual
     ]
-    four = pl.BlockSpec(a_own.shape, lambda i: (0, 0, 0, 0))
+    piece = pl.BlockSpec(a_own[0].shape, lambda i: (0, 0, 0))
     block = 4 * HDIM
     return pl.pallas_call(
         functools.partial(out_kernel, placing, block, chunk),
         grid=(1,),
-        in_specs=[SMEM, four, four, ANY, ANY, *specs],
+        in_specs=[SMEM, *[piece] * (2 * KV_HEADS), ANY, ANY, *specs],
         out_specs=pl.BlockSpec(shape, lambda i: (0,) * len(shape)),
         out_shape=jax.ShapeDtypeStruct(shape, BF16),
         scratch_shapes=[
-            *[pltpu.VMEM((rows, depth), BF16)] * 2,
+            pltpu.VMEM((2, rows, depth), BF16),
             *[pltpu.VMEM((depth, width), BF16)] * 2,
             pltpu.SemaphoreType.DMA((2, -(-width // block))),
         ],
-        compiler_params=params(56),
-    )(at, a_own, a_oth, w_own, w_oth, *residual)
+        compiler_params=params(60),
+    )(at, *a_own, *a_oth, w_own, w_oth, *residual)
 
 
 def per_device(
@@ -678,6 +692,13 @@
             for d in range(1, KV_HEADS)
         ]
 
+    def returned(attended):
+        a_own = [attended[0]]
+        for d in range(1, KV_HEADS):
+            pairs = [(i, i ^ d) for i in range(KV_HEADS)]
+            a_own.append(lax.ppermute(attended[d], "mem", pairs))
+        return a_own, [swap(piece) for piece in a_own]
+
     part = FRAME_TOK // 2
     offset = positions[:, None] - frame_start[None, :]
     inside = (offset >= 0) & (offset < FRAME_TOK)
@@ -690,11 +711,14 @@
 
     idx_own, idx_oth = index_of(t), index_of(1 - t)
 
-    wide, sent, spread = project(tp_index, patch_feats, proj_weight, count)
+    wide, sent = project(patch_feats, proj_weight)
     came = from_vision(sent)
-    pf_own = lax.all_to_all(spread, CTX, split_axis=0, concat_axis=0, tiled=True)
-
-    frame_embed = gelu_sum(wide, came, *kv_tables, *q_tables, idx_own, idx_oth)
+    w_given = other_columns(tp_index, sent, out_weight)
+    w_oth = swap(w_given)
+    pf_own = spread(tp_index, sent, patch_feats, count)
+    pf_own = lax.all_to_all(pf_own, CTX, split_axis=0, concat_axis=0, tiled=True)
+
+    frame_embed = gelu_sum(wide, came, w_given, *kv_tables, *q_tables, idx_own, idx_oth)
     packed, kept, given, f_kept, f_given = qkv(
         tp_index,
         text_embed,
@@ -715,20 +739,18 @@
     pf_own = pf_own.reshape(count * part, -1)
     wide, *sent = project_placed(packed, idx_own, idx_oth, pf_own, swap(pf_own), proj_weight)
     placed = [from_vision(half) for half in sent]
-    pieces = spread_heads(kept, given, sent[0])
-    w_given = other_columns(tp_index, sent[0], out_weight)
-    w_oth = swap(w_given)
+    pieces = spread_heads(kept, given, packed)
 
     at = jnp.concatenate([base, frame_start])
-    message = gate(message, *placed, *pieces[1:])
-    attended = attend(at, pieces, message, swap(message), frame_start.shape[0], w_given)
-    a_own = lax.all_to_all(attended, "mem", split_axis=0, concat_axis=0, tiled=True)
-    a_oth = swap(a_own)
-    residual = (text_embed, wide, *placed, idx_own, idx_oth)
-    first = [
-        project_out(base, a_own, a_oth, out_weight, w_oth, residual, True, chunk, 2)
-        for chunk in range(2)
-    ]
+    message = gate(message, *sent, *pieces[1:])
+    attended = attend(at, pieces, message, swap(message), frame_start.shape[0])
+    a_own, a_oth = returned(attended)
+    first = []
+    for chunk in range(2):
+        residual = (text_embed, wide, placed[chunk], idx_own, idx_oth)
+        first.append(
+            project_out(base, a_own, a_oth, out_weight, w_oth, residual, True, chunk, 2)
+        )
 
     h = [lax.ppermute(part, "segment", [(0, 1)]) for part in first]
     h_oth = [swap(part) for part in h]
@@ -738,8 +760,8 @@
     pieces = spread_heads(*queries_of(tp_index, normed, q_weight, *q_tables))
     kv = gate(kv, *pieces[1:])
     attended = attend(base, pieces, kv, swap(kv), 0)
-    a_own = lax.all_to_all(attended, "mem", split_axis=0, concat_axis=0, tiled=True)
-    return project_out(base, a_own, swap(a_own), out_weight, w_oth, (*h, *first), False, 0, 1)
+    a_own, a_oth = returned(attended)
+    return project_out(base, a_own, a_oth, out_weight, w_oth, (*h, *first), False, 0, 1)
 
 
 def solution(mesh):

time: 204 us -> 202 us (level)
  blocking collectives: 21.1 us -> 0 us
  Pallas kernels: 70.5 us -> 83.2 us
  starting transfers between devices: 46 us -> 51.6 us
  waiting for transfers between devices: 50.5 us -> 47.8 us
    all_to_all x2 -> x0, blocking collectives: 21.1 us -> none  [per_device(): lax.all_to_all(attended, 'mem', split_axis=0, concat_axis=0, tiled=True)]
    ppermute x3, waiting for transfers between devices: 7.66 us -> 0.01 us  [from_vision(): return lax.ppermute(sent, 'segment', [(1, 0)])]
    ppermute x0 -> x6, waiting for transfers between devices: none -> 5.39 us  [returned(): a_own.append(lax.ppermute(attended[d], 'mem', pairs))]
    ppermute x0 -> x6, starting transfers between devices: none -> 5.3 us  [returned(): a_own.append(lax.ppermute(attended[d], 'mem', pairs))]
    pallas_call x2, Pallas kernels: 16.7 us -> 21.9 us  [attend(): pl.pallas_call(functools.partial(attend_kernel, frames, len(after)), grid...]
    ppermute x13 -> x19, starting transfers between devices: 14.2 us -> 18.5 us  [swap(): return lax.ppermute(value, 'tp', [(0, 1), (1, 0)])]
    ppermute x6, waiting for transfers between devices: 15.6 us -> 19.3 us  [spread_heads(): lax.ppermute(pieces[d], 'mem', [(i, i ^ d) for i in range(KV_HEADS)])]
    ppermute x13 -> x19, waiting for transfers between devices: 13.6 us -> 10.8 us  [swap(): return lax.ppermute(value, 'tp', [(0, 1), (1, 0)])]
  transfers between devices with their start and end apart: 27 -> 39, of which waited for: 18 -> 19; matrix products, arithmetic and copies ran while one was open for 1% -> 3% of each run, Pallas kernels for 21% -> 30%
where the time goes in v5:
time: 202 us; the launch traced here: 201 us
  Pallas kernels  83.2 us (41%)
  starting transfers between devices  51.6 us (26%)
  waiting for transfers between devices  47.8 us (24%)
  local copies, waits for them, and re-layouts  14.6 us (7%)
  other arithmetic  3.16 us (2%)
    pallas_call x2, Pallas kernels, attend(): pl.pallas_call(functools.partial(attend_kernel, frames, len(after)), grid...  21.9 us
    pallas_call x3, Pallas kernels, project_out(): pl.pallas_call(functools.partial(out_kernel, placing, block, chunk), grid...  19.7 us
    ppermute x6, waiting for transfers between devices, spread_heads(): lax.ppermute(pieces[d], 'mem', [(i, i ^ d) for i in range(KV_HEADS)])  19.3 us
    ppermute x19, starting transfers between devices, swap(): return lax.ppermute(value, 'tp', [(0, 1), (1, 0)])  18.5 us
    ppermute x2, waiting for transfers between devices, per_device(): h = [lax.ppermute(part, 'segment', [(0, 1)]) for part in first]  12.3 us
    unnamed x86, local copies, waits for them, and re-layouts  11.8 us
    ppermute x19, waiting for transfers between devices, swap(): return lax.ppermute(value, 'tp', [(0, 1), (1, 0)])  10.8 us
    pallas_call x1, Pallas kernels, qkv(): pl.pallas_call(qkv_kernel, in_specs=[SMEM, *[VMEM] * 5, ANY, ANY, *[VMEM]...  9.63 us
  transfers between devices with their start and end apart: 39, of which 19 were waited for; matrix products, arithmetic and copies ran while one was open for 3% of the time, Pallas kernels for 30%

profile of v5, /device:TPU:19, one launch (start us, length us, event | category | flops | bytes accessed | tf_op | source)
XLA Modules:
  0.0 201.0 jit_solution(15483938969908070999)
XLA Ops:
  0.7 2.7 %shard_map.82 = (f32[96,1792]{1,0:T(8,128)}, bf16[96,1792]{1,0:T(8,128)(2,1)}) custom-call(bf16[96,576]{1,0:T(8,128)(2,1)} %x_ref.3, bf16[576,1792]{1,0:T(8,128)(2,1)} %w_ref.3), custom_call_target="tpu_custom_call" | custom-call | tf_op jit(solution)/shard_map/pallas_call | solution.py:112
  3.4 2.2 %collective-permute-start.1 = (bf16[96,1792]{1,0:T(8,128)(2,1)}, bf16[96,1792]{1,0:T(8,128)(2,1)S(1)}, u32[]{:S(2)}, u32[]{:S(2)}) collective-permute-start(bf16[96,1792]{1,0:T(8,128)(2,1)} %get-tuple-element.35.after), channel_id=1, source_target_pairs={{16,0},{17,1},{18,2},{19,3},{20,4},{21,5},{22,6},{23,7},{24,8},{25... | collective-permute-start | bytes 1032200 | tf_op jit(solution)/shard_map/ppermute | solution.py:684
  7.4 5.6 %all-to-all-start = ((bf16[8,48,576]{2,1,0:T(8,128)(2,1)}), bf16[8,48,576]{2,1,0:T(8,128)(2,1)S(1)}, u32[]{:S(2)}, u32[]{:S(2)}) async-start(bf16[8,48,576]{2,1,0:T(8,128)(2,1)} %shard_map.83), calls=%async_computation | async-start | bytes 983040 | tf_op jit(solution)/shard_map/all_to_all | solution.py:719
  13.0 3.5 %shard_map.84.refs_0_ = bf16[1024,1792]{1,0:T(8,128)(2,1)} custom-call(s32[1]{0:T(128)} %bitcast.1.tp_ref, bf16[96,1792]{1,0:T(8,128)(2,1)} %get-tuple-element.35.after, bf16[1024,3584]{1,0:T(8,128)(2,1)} %bitcast.13), custom_call_target="tpu_custom_call" | custom-call | flops 1 | bytes 1 | tf_op jit(solution)/shard_map/pallas_call | solution.py:413
  22.8 2.1 %shard_map.85.refs_2_ = bf16[96,1792]{1,0:T(8,128)(2,1)} custom-call(bf16[1024,1792]{1,0:T(8,128)(2,1)} %shard_map.84.refs_0_, f32[352,128]{1,0:T(8,128)} %get-tuple-element.70.refs_1_.refs_7_.refs_6_, f32[352,128]{1,0:T(8,128)} %get-tuple-element.74.refs_2_.refs_8_.refs_7_, f32[352,128]{1,0:T(8,128)} %get-tuple-element.69.refs_3_.refs_9_.refs_2_, ...), custom_call_target="tpu_custom_call" | custom-call | tf_op jit(solution)/shard_map/pallas_call | solution.py:155
  27.8 9.6 %shard_map.86 = (bf16[2,4,544,128]{3,2,1,0:T(8,128)(2,1)}, bf16[2,2,256,128]{3,2,1,0:T(8,128)(2,1)}, bf16[2,2,256,128]{3,2,1,0:T(8,128)(2,1)}, bf16[2,2,96,128]{3,2,1,0:T(8,128)(2,1)}, bf16[2,2,96,128]{3,2,1,0:T(8,128)(2,1)}) custom-call(s32[1]{0:T(128)} %bitcast.1.tp_ref, bf16[256,1792]{1,0:T(8,128)(2,1)} %refs_10_.3, bf16[256,1792]{1,0:T(8,128)(2,1)} %copy-done.7, ...), custom_call_target="tpu_custom_call" | custom-call | tf_op jit(solution)/shard_map/pallas_call | solution.py:265
  41.6 5.6 %all-to-all-start.1 = ((bf16[8,544,128]{2,1,0:T(8,128)(2,1)}), bf16[8,544,128]{2,1,0:T(8,128)(2,1)S(1)}, u32[]{:S(2)}, u32[]{:S(2)}) async-start(bf16[8,544,128]{2,1,0:T(8,128)(2,1)} %bitcast.19), calls=%async_computation.1 | async-start | bytes 2228224 | tf_op jit(solution)/shard_map/all_to_all | solution.py:737
  55.8 4.7 %shard_map.89 = (f32[256,1792]{1,0:T(8,128)}, bf16[256,896]{1,0:T(8,128)(2,1)}, bf16[256,896]{1,0:T(8,128)(2,1)}) custom-call(bf16[2,4,544,128]{3,2,1,0:T(8,128)(2,1)} %shard_map.87.refs_0_.after, s32[256,1]{1,0:T(8,128)} %copy.20.refs_5_.idx_own.refs_13_, s32[256,1]{1,0:T(8,128)} %copy.21.refs_6_.idx_oth.refs_14_, bf16[384,576]{1,0:T(8,128)(2,1)} %bitcast.22, ...), custom_call_target="tpu_custom_call" | custom-call | flops 1 | bytes 1 | tf_op jit(solution)/shard_map/pallas_call | solution.py:78
  60.5 9.2 %collective-permute-done.6.refs_4_.refs_2_ = bf16[2,256,128]{2,1,0:T(8,128)(2,1)S(1)} collective-permute-done((bf16[2,256,128]{2,1,0:T(8,128)(2,1)}, bf16[2,256,128]{2,1,0:T(8,128)(2,1)S(1)}, u32[]{:S(2)}, u32[]{:S(2)}) %collective-permute-start.6) | collective-permute-done | bytes 131104 | tf_op jit(solution)/shard_map/ppermute | solution.py:691
  69.8 3.7 %collective-permute-done.7.refs_5_.refs_3_ = bf16[2,256,128]{2,1,0:T(8,128)(2,1)S(1)} collective-permute-done((bf16[2,256,128]{2,1,0:T(8,128)(2,1)}, bf16[2,256,128]{2,1,0:T(8,128)(2,1)S(1)}, u32[]{:S(2)}, u32[]{:S(2)}) %collective-permute-start.7) | collective-permute-done | bytes 131104 | tf_op jit(solution)/shard_map/ppermute | solution.py:691
  80.1 11.5 %shard_map.91 = (bf16[2,256,128]{2,1,0:T(8,128)(2,1)}, bf16[2,256,128]{2,1,0:T(8,128)(2,1)}, bf16[2,256,128]{2,1,0:T(8,128)(2,1)}, bf16[2,256,128]{2,1,0:T(8,128)(2,1)}) custom-call(s32[12]{0:T(128)} %concatenate.17.at_ref, bf16[2,256,128]{2,1,0:T(8,128)(2,1)} %get-tuple-element.42.refs_0_, bf16[2,256,128]{2,1,0:T(8,128)(2,1)} %copy-done.15, ...), custom_call_target="tpu_custom_call" | custom-call | tf_op jit(solution)/shard_map/pallas_call | solution.py:548
  103.3 6.0 %shard_map.92.refs_12_ = bf16[256,896]{1,0:T(8,128)(2,1)} custom-call(s32[4]{0:T(128)} %pad_add_fusion.at_ref, bf16[2,256,128]{2,1,0:T(8,128)(2,1)} %get-tuple-element.48.refs_0_, bf16[2,256,128]{2,1,0:T(8,128)(2,1)} %copy-done.8, bf16[2,256,128]{2,1,0:T(8,128)(2,1)} %copy-done.9, bf16[2,256,128]{2,1,0:T(8,128)(2,1)} %copy-done.10, ...), custom_call_target="tpu_custom_call" | custom-call | tf_op jit(solution)/shard_map/pallas_call | solution.py:641
  111.4 6.0 %shard_map.93.refs_13_ = bf16[256,896]{1,0:T(8,128)(2,1)} custom-call(s32[4]{0:T(128)} %pad_add_fusion.at_ref, bf16[2,256,128]{2,1,0:T(8,128)(2,1)} %get-tuple-element.48.refs_0_, bf16[2,256,128]{2,1,0:T(8,128)(2,1)} %copy-done.8, bf16[2,256,128]{2,1,0:T(8,128)(2,1)} %copy-done.9, bf16[2,256,128]{2,1,0:T(8,128)(2,1)} %copy-done.10, ...), custom_call_target="tpu_custom_call" | custom-call | tf_op jit(solution)/shard_map/pallas_call | solution.py:641
  118.7 4.5 %collective-permute-done.19.refs_0_.refs_10_ = bf16[256,896]{1,0:T(8,128)(2,1)S(1)} collective-permute-done((bf16[256,896]{1,0:T(8,128)(2,1)}, bf16[256,896]{1,0:T(8,128)(2,1)S(1)}, u32[]{:S(2)}, u32[]{:S(2)}) %collective-permute-start.19) | collective-permute-done | bytes 458784 | tf_op jit(solution)/shard_map/ppermute | solution.py:755
  123.2 2.0 collective-permute-start.22
  125.2 7.8 %collective-permute-done.21.refs_1_.refs_11_ = bf16[256,896]{1,0:T(8,128)(2,1)S(1)} collective-permute-done((bf16[256,896]{1,0:T(8,128)(2,1)}, bf16[256,896]{1,0:T(8,128)(2,1)S(1)}, u32[]{:S(2)}, u32[]{:S(2)}) %collective-permute-start.21) | collective-permute-done | bytes 458784 | tf_op jit(solution)/shard_map/ppermute | solution.py:755
  136.5 5.6 %shard_map.94 = (bf16[256,3584]{1,0:T(8,128)(2,1)}, bf16[2,4,256,128]{3,2,1,0:T(8,128)(2,1)}) custom-call(s32[1]{0:T(128)} %bitcast.1.tp_ref, bf16[256,896]{1,0:T(8,128)(2,1)} %copy-done.4, bf16[256,896]{1,0:T(8,128)(2,1)} %copy-done.5, bf16[256,896]{1,0:T(8,128)(2,1)} %copy-done.23, bf16[256,896]{1,0:T(8,128)(2,1)} %copy-done.24, f32[1,3584]{1,0:T(1,128)} %refs_4_.3, ...), custom_call_target="tpu_custom_call" | custom-call | tf_op jit(solution)/shard_map/pallas_call | solution.py:208
  142.1 3.9 %all-to-all-start.2 = ((bf16[8,256,128]{2,1,0:T(8,128)(2,1)}), bf16[8,256,128]{2,1,0:T(8,128)(2,1)S(1)}, u32[]{:S(2)}, u32[]{:S(2)}) async-start(bf16[8,256,128]{2,1,0:T(8,128)(2,1)} %bitcast.24), calls=%async_computation.2 | async-start | bytes 1048576 | tf_op jit(solution)/shard_map/all_to_all | solution.py:759
  146.0 5.9 %shard_map.95 = (bf16[2,2,256,128]{3,2,1,0:T(8,128)(2,1)}, bf16[2,2,256,128]{3,2,1,0:T(8,128)(2,1)}) custom-call(s32[1]{0:T(128)} %bitcast.1.tp_ref, bf16[256,3584]{1,0:T(8,128)(2,1)} %get-tuple-element.53.refs_0_, bf16[3584,1024]{1,0:T(8,128)(2,1)} %bitcast.18, f32[352,128]{1,0:T(8,128)} %get-tuple-element.69.refs_3_.refs_9_.refs_2_, ...), custom_call_target="tpu_custom_call" | custom-call | flops 1 | bytes 1 | tf_op jit(solution)/shard_map/pallas_call | solution.py:305
  159.5 2.3 %collective-permute-done.25.refs_1_ = bf16[2,256,128]{2,1,0:T(8,128)(2,1)S(1)} collective-permute-done((bf16[2,256,128]{2,1,0:T(8,128)(2,1)}, bf16[2,256,128]{2,1,0:T(8,128)(2,1)S(1)}, u32[]{:S(2)}, u32[]{:S(2)}) %collective-permute-start.25) | collective-permute-done | bytes 131104 | tf_op jit(solution)/shard_map/ppermute | solution.py:691
  162.6 3.2 %collective-permute-done.27.refs_3_ = bf16[2,256,128]{2,1,0:T(8,128)(2,1)S(1)} collective-permute-done((bf16[2,256,128]{2,1,0:T(8,128)(2,1)}, bf16[2,256,128]{2,1,0:T(8,128)(2,1)S(1)}, u32[]{:S(2)}, u32[]{:S(2)}) %collective-permute-start.27) | collective-permute-done | bytes 131104 | tf_op jit(solution)/shard_map/ppermute | solution.py:691
  170.9 10.5 %shard_map.98 = (bf16[2,256,128]{2,1,0:T(8,128)(2,1)}, bf16[2,256,128]{2,1,0:T(8,128)(2,1)}, bf16[2,256,128]{2,1,0:T(8,128)(2,1)}, bf16[2,256,128]{2,1,0:T(8,128)(2,1)}) custom-call(s32[4]{0:T(128)} %pad_add_fusion.at_ref, bf16[2,256,128]{2,1,0:T(8,128)(2,1)} %get-tuple-element.56.refs_0_, bf16[2,256,128]{2,1,0:T(8,128)(2,1)} %copy-done.19, ...), custom_call_target="tpu_custom_call" | custom-call | tf_op jit(solution)/shard_map/pallas_call | solution.py:548
  187.5 2.3 %collective-permute-start.34 = (bf16[2,256,128]{2,1,0:T(8,128)(2,1)S(1)}, bf16[2,256,128]{2,1,0:T(8,128)(2,1)S(1)}, u32[]{:S(2)}, u32[]{:S(2)}) collective-permute-start(bf16[2,256,128]{2,1,0:T(8,128)(2,1)S(1)} %collective-permute-done.30.refs_2_), channel_id=1, source_target_pairs={{0,1},{1,0},{2,3},{3,2},{4,5},{5,4},{6,7},{7,6},{8,9},{9,8},{10,11... | collective-permute-start | bytes 393224 | tf_op jit(solution)/shard_map/ppermute | solution.py:37
  193.2 7.7 %shard_map.99 = bf16[1,256,1792]{2,1,0:T(8,128)(2,1)} custom-call(s32[4]{0:T(128)} %pad_add_fusion.at_ref, bf16[2,256,128]{2,1,0:T(8,128)(2,1)} %get-tuple-element.61.refs_0_, bf16[2,256,128]{2,1,0:T(8,128)(2,1)} %copy-done.33, bf16[2,256,128]{2,1,0:T(8,128)(2,1)} %copy-done.34, bf16[2,256,128]{2,1,0:T(8,128)(2,1)} %copy-done.35, ...), custom_call_target="tpu_custom_call" | custom-call | tf_op jit(solution)/shard_map/pallas_call | solution.py:641
  (171 shorter events, 72.4 us)
Async XLA Ops:
  0.0 26.8 %collective-permute-start = (bf16[256,1792]{1,0:T(8,128)(2,1)}, bf16[256,1792]{1,0:T(8,128)(2,1)S(1)}, u32[]{:S(2)}, u32[]{:S(2)}) collective-permute-start(bf16[256,1792]{1,0:T(8,128)(2,1)} %refs_10_.3), channel_id=1, source_target_pairs={{0,1},{1,0},{2,3},{3,2},{4,5},{5,4},{6,7},{7,6},{8,9},{9,8},{10,11... | collective-permute-start | bytes 2752520 | tf_op jit(solution)/shard_map/ppermute | solution.py:37
  3.4 18.7 %collective-permute-start.1 = (bf16[96,1792]{1,0:T(8,128)(2,1)}, bf16[96,1792]{1,0:T(8,128)(2,1)S(1)}, u32[]{:S(2)}, u32[]{:S(2)}) collective-permute-start(bf16[96,1792]{1,0:T(8,128)(2,1)} %get-tuple-element.35.after), channel_id=1, source_target_pairs={{16,0},{17,1},{18,2},{19,3},{20,4},{21,5},{22,6},{23,7},{24,8},{25... | collective-permute-start | bytes 1032200 | tf_op jit(solution)/shard_map/ppermute | solution.py:684
  7.4 30.9 %all-to-all-start = ((bf16[8,48,576]{2,1,0:T(8,128)(2,1)}), bf16[8,48,576]{2,1,0:T(8,128)(2,1)S(1)}, u32[]{:S(2)}, u32[]{:S(2)}) async-start(bf16[8,48,576]{2,1,0:T(8,128)(2,1)} %shard_map.83), calls=%async_computation | async-start | bytes 983040 | tf_op jit(solution)/shard_map/all_to_all | solution.py:719
  16.5 77.8 %collective-permute-start.17 = (bf16[1024,1792]{1,0:T(8,128)(2,1)}, bf16[1024,1792]{1,0:T(8,128)(2,1)}, u32[]{:S(2)}, u32[]{:S(2)}) collective-permute-start(bf16[1024,1792]{1,0:T(8,128)(2,1)} %shard_map.84.refs_0_), channel_id=1, source_target_pairs={{0,1},{1,0},{2,3},{3,2},{4,5},{5,4},{6,7},{7,6},{8,9},{9,8},{10,11... | collective-permute-start | bytes 11010056 | tf_op jit(solution)/shard_map/ppermute | solution.py:37
  41.6 31.9 %all-to-all-start.1 = ((bf16[8,544,128]{2,1,0:T(8,128)(2,1)}), bf16[8,544,128]{2,1,0:T(8,128)(2,1)S(1)}, u32[]{:S(2)}, u32[]{:S(2)}) async-start(bf16[8,544,128]{2,1,0:T(8,128)(2,1)} %bitcast.19), calls=%async_computation.1 | async-start | bytes 2228224 | tf_op jit(solution)/shard_map/all_to_all | solution.py:737
  47.2 7.9 %collective-permute-start.8 = (bf16[384,576]{1,0:T(8,128)(2,1)S(1)}, bf16[384,576]{1,0:T(8,128)(2,1)S(1)}, u32[]{:S(2)}, u32[]{:S(2)}) collective-permute-start(bf16[384,576]{1,0:T(8,128)(2,1)S(1)} %bitcast.23), channel_id=1, source_target_pairs={{0,1},{1,0},{2,3},{3,2},{4,5},{5,4},{6,7},{7,6},{8,9},{9,8},{10,11... | collective-permute-start | bytes 1327112 | tf_op jit(solution)/shard_map/ppermute | solution.py:37
  52.4 8.2 %collective-permute-start.5 = (bf16[2,256,128]{2,1,0:T(8,128)(2,1)}, bf16[2,256,128]{2,1,0:T(8,128)(2,1)S(1)}, u32[]{:S(2)}, u32[]{:S(2)}) collective-permute-start(bf16[2,256,128]{2,1,0:T(8,128)(2,1)} %get-tuple-element.43), channel_id=1, source_target_pairs={{0,2},{2,0},{4,6},{6,4},{1,3},{3,1},{5,7},{7,5},{8,10},{10,8},{12,... | collective-permute-start | bytes 393224 | tf_op jit(solution)/shard_map/ppermute | solution.py:691
  53.5 16.2 %collective-permute-start.6 = (bf16[2,256,128]{2,1,0:T(8,128)(2,1)}, bf16[2,256,128]{2,1,0:T(8,128)(2,1)S(1)}, u32[]{:S(2)}, u32[]{:S(2)}) collective-permute-start(bf16[2,256,128]{2,1,0:T(8,128)(2,1)} %get-tuple-element.44), channel_id=1, source_target_pairs={{0,4},{2,6},{4,0},{6,2},{1,5},{3,7},{5,1},{7,3},{8,12},{10,14},{12... | collective-permute-start | bytes 393224 | tf_op jit(solution)/shard_map/ppermute | solution.py:691
  54.7 18.8 %collective-permute-start.7 = (bf16[2,256,128]{2,1,0:T(8,128)(2,1)}, bf16[2,256,128]{2,1,0:T(8,128)(2,1)S(1)}, u32[]{:S(2)}, u32[]{:S(2)}) collective-permute-start(bf16[2,256,128]{2,1,0:T(8,128)(2,1)} %get-tuple-element.45), channel_id=1, source_target_pairs={{0,6},{2,4},{4,2},{6,0},{1,7},{3,5},{5,3},{7,1},{8,14},{10,12},{12... | collective-permute-start | bytes 393224 | tf_op jit(solution)/shard_map/ppermute | solution.py:691
  75.8 16.6 %collective-permute-start.18 = (bf16[256,896]{1,0:T(8,128)(2,1)S(1)}, bf16[256,896]{1,0:T(8,128)(2,1)S(1)}, u32[]{:S(2)}, u32[]{:S(2)}) collective-permute-start(bf16[256,896]{1,0:T(8,128)(2,1)S(1)} %copy-done.26), channel_id=1, source_target_pairs={{16,0},{17,1},{18,2},{19,3},{20,4},{21,5},{22,6},{23,7},{24,8},{25... | collective-permute-start | bytes 1376264 | tf_op jit(solution)/shard_map/ppermute | solution.py:684
  77.2 33.5 %collective-permute-start.20 = (bf16[256,896]{1,0:T(8,128)(2,1)S(1)}, bf16[256,896]{1,0:T(8,128)(2,1)S(1)}, u32[]{:S(2)}, u32[]{:S(2)}) collective-permute-start(bf16[256,896]{1,0:T(8,128)(2,1)S(1)} %copy-done.25), channel_id=1, source_target_pairs={{16,0},{17,1},{18,2},{19,3},{20,4},{21,5},{22,6},{23,7},{24,8},{25... | collective-permute-start | bytes 1376264 | tf_op jit(solution)/shard_map/ppermute | solution.py:684
  91.6 5.3 %collective-permute-start.10 = (bf16[2,256,128]{2,1,0:T(8,128)(2,1)}, bf16[2,256,128]{2,1,0:T(8,128)(2,1)S(1)}, u32[]{:S(2)}, u32[]{:S(2)}) collective-permute-start(bf16[2,256,128]{2,1,0:T(8,128)(2,1)} %get-tuple-element.49), channel_id=1, source_target_pairs={{0,2},{2,0},{4,6},{6,4},{1,3},{3,1},{5,7},{7,5},{8,10},{10,8},{12,... | collective-permute-start | bytes 393224 | tf_op jit(solution)/shard_map/ppermute | solution.py:699
  91.9 5.8 %collective-permute-start.11 = (bf16[2,256,128]{2,1,0:T(8,128)(2,1)}, bf16[2,256,128]{2,1,0:T(8,128)(2,1)S(1)}, u32[]{:S(2)}, u32[]{:S(2)}) collective-permute-start(bf16[2,256,128]{2,1,0:T(8,128)(2,1)} %get-tuple-element.50), channel_id=1, source_target_pairs={{0,4},{2,6},{4,0},{6,2},{1,5},{3,7},{5,1},{7,3},{8,12},{10,14},{12... | collective-permute-start | bytes 393224 | tf_op jit(solution)/shard_map/ppermute | solution.py:699
  92.4 8.2 %collective-permute-start.12 = (bf16[2,256,128]{2,1,0:T(8,128)(2,1)}, bf16[2,256,128]{2,1,0:T(8,128)(2,1)S(1)}, u32[]{:S(2)}, u32[]{:S(2)}) collective-permute-start(bf16[2,256,128]{2,1,0:T(8,128)(2,1)} %get-tuple-element.51), channel_id=1, source_target_pairs={{0,6},{2,4},{4,2},{6,0},{1,7},{3,5},{5,3},{7,1},{8,14},{10,12},{12... | collective-permute-start | bytes 393224 | tf_op jit(solution)/shard_map/ppermute | solution.py:699
  94.3 7.5 %collective-permute-start.13 = (bf16[2,256,128]{2,1,0:T(8,128)(2,1)}, bf16[2,256,128]{2,1,0:T(8,128)(2,1)S(1)}, u32[]{:S(2)}, u32[]{:S(2)}) collective-permute-start(bf16[2,256,128]{2,1,0:T(8,128)(2,1)} %get-tuple-element.48.refs_0_), channel_id=1, source_target_pairs={{0,1},{1,0},{2,3},{3,2},{4,5},{5,4},{6,7},{7,6},{8,9},{9,8},{10,11... | collective-permute-start | bytes 393224 | tf_op jit(solution)/shard_map/ppermute | solution.py:37
  109.4 13.8 %collective-permute-start.19 = (bf16[256,896]{1,0:T(8,128)(2,1)}, bf16[256,896]{1,0:T(8,128)(2,1)S(1)}, u32[]{:S(2)}, u32[]{:S(2)}) collective-permute-start(bf16[256,896]{1,0:T(8,128)(2,1)} %shard_map.92.refs_12_), channel_id=1, source_target_pairs={{0,16},{1,17},{2,18},{3,19},{4,20},{5,21},{6,22},{7,23},{8,24},{9,... | collective-permute-start | bytes 1376264 | tf_op jit(solution)/shard_map/ppermute | solution.py:755
  117.4 15.6 %collective-permute-start.21 = (bf16[256,896]{1,0:T(8,128)(2,1)}, bf16[256,896]{1,0:T(8,128)(2,1)S(1)}, u32[]{:S(2)}, u32[]{:S(2)}) collective-permute-start(bf16[256,896]{1,0:T(8,128)(2,1)} %shard_map.93.refs_13_), channel_id=1, source_target_pairs={{0,16},{1,17},{2,18},{3,19},{4,20},{5,21},{6,22},{7,23},{8,24},{9,... | collective-permute-start | bytes 1376264 | tf_op jit(solution)/shard_map/ppermute | solution.py:755
  123.2 11.0 %collective-permute-start.22 = (bf16[256,896]{1,0:T(8,128)(2,1)S(1)}, bf16[256,896]{1,0:T(8,128)(2,1)S(1)}, u32[]{:S(2)}, u32[]{:S(2)}) collective-permute-start(bf16[256,896]{1,0:T(8,128)(2,1)S(1)} %collective-permute-done.19.refs_0_.refs_10_), channel_id=1, source_target_pairs={{0,1},{1,0},{2,3},{3,2},{4,5},{5,4},{6,7},{7,6},{8,9},{9,8},{10,11... | collective-permute-start | bytes 1376264 | tf_op jit(solution)/shard_map/ppermute | solution.py:37
  142.1 23.7 %all-to-all-start.2 = ((bf16[8,256,128]{2,1,0:T(8,128)(2,1)}), bf16[8,256,128]{2,1,0:T(8,128)(2,1)S(1)}, u32[]{:S(2)}, u32[]{:S(2)}) async-start(bf16[8,256,128]{2,1,0:T(8,128)(2,1)} %bitcast.24), calls=%async_computation.2 | async-start | bytes 1048576 | tf_op jit(solution)/shard_map/all_to_all | solution.py:759
  159.2 6.6 %collective-permute-start.27 = (bf16[2,256,128]{2,1,0:T(8,128)(2,1)}, bf16[2,256,128]{2,1,0:T(8,128)(2,1)S(1)}, u32[]{:S(2)}, u32[]{:S(2)}) collective-permute-start(bf16[2,256,128]{2,1,0:T(8,128)(2,1)} %get-tuple-element.59), channel_id=1, source_target_pairs={{0,6},{2,4},{4,2},{6,0},{1,7},{3,5},{5,3},{7,1},{8,14},{10,12},{12... | collective-permute-start | bytes 393224 | tf_op jit(solution)/shard_map/ppermute | solution.py:691
  182.6 4.9 %collective-permute-start.30 = (bf16[2,256,128]{2,1,0:T(8,128)(2,1)}, bf16[2,256,128]{2,1,0:T(8,128)(2,1)S(1)}, u32[]{:S(2)}, u32[]{:S(2)}) collective-permute-start(bf16[2,256,128]{2,1,0:T(8,128)(2,1)} %get-tuple-element.63), channel_id=1, source_target_pairs={{0,4},{2,6},{4,0},{6,2},{1,5},{3,7},{5,1},{7,3},{8,12},{10,14},{12... | collective-permute-start | bytes 393224 | tf_op jit(solution)/shard_map/ppermute | solution.py:699
  183.8 6.6 %collective-permute-start.31 = (bf16[2,256,128]{2,1,0:T(8,128)(2,1)}, bf16[2,256,128]{2,1,0:T(8,128)(2,1)S(1)}, u32[]{:S(2)}, u32[]{:S(2)}) collective-permute-start(bf16[2,256,128]{2,1,0:T(8,128)(2,1)} %get-tuple-element.64), channel_id=1, source_target_pairs={{0,6},{2,4},{4,2},{6,0},{1,7},{3,5},{5,3},{7,1},{8,14},{10,12},{12... | collective-permute-start | bytes 393224 | tf_op jit(solution)/shard_map/ppermute | solution.py:699
  184.0 7.5 %collective-permute-start.32 = (bf16[2,256,128]{2,1,0:T(8,128)(2,1)}, bf16[2,256,128]{2,1,0:T(8,128)(2,1)S(1)}, u32[]{:S(2)}, u32[]{:S(2)}) collective-permute-start(bf16[2,256,128]{2,1,0:T(8,128)(2,1)} %get-tuple-element.61.refs_0_), channel_id=1, source_target_pairs={{0,1},{1,0},{2,3},{3,2},{4,5},{5,4},{6,7},{7,6},{8,9},{9,8},{10,11... | collective-permute-start | bytes 393224 | tf_op jit(solution)/shard_map/ppermute | solution.py:37
  186.3 5.2 %collective-permute-start.33 = (bf16[2,256,128]{2,1,0:T(8,128)(2,1)S(1)}, bf16[2,256,128]{2,1,0:T(8,128)(2,1)S(1)}, u32[]{:S(2)}, u32[]{:S(2)}) collective-permute-start(bf16[2,256,128]{2,1,0:T(8,128)(2,1)S(1)} %collective-permute-done.29.refs_1_), channel_id=1, source_target_pairs={{0,1},{1,0},{2,3},{3,2},{4,5},{5,4},{6,7},{7,6},{8,9},{9,8},{10,11... | collective-permute-start | bytes 393224 | tf_op jit(solution)/shard_map/ppermute | solution.py:37
  (58 other events, 194.1 us)

commit v6 on v5

--- a/solution.py
+++ b/solution.py
@@ -48,56 +48,40 @@
     )
 
 
-def place_kernel(after, idx_own, idx_oth, pf_own, pf_oth, w_ref, wide_ref, left, right, placed):
-    @pl.when(pl.program_id(0) == 0)
-    def _():
-        rows, count = idx_own.shape[0], pf_own.shape[0]
-        at = lax.broadcasted_iota(jnp.int32, (rows, count), 1)
-        hot_own = jnp.where(at == idx_own[...], 1.0, 0.0).astype(BF16)
-        hot_oth = jnp.where(at == idx_oth[...], 1.0, 0.0).astype(BF16)
-        picked = jnp.dot(hot_own, pf_own[...], preferred_element_type=F32)
-        picked += jnp.dot(hot_oth, pf_oth[...], preferred_element_type=F32)
-        placed[...] = picked.astype(BF16)
-
-    term = jnp.dot(placed[...], w_ref[...], preferred_element_type=F32)
-    wide_ref[...] = term
-
-    @pl.when(pl.program_id(0) == 0)
-    def _():
-        left[...] = term.astype(BF16)
-
-    @pl.when(pl.program_id(0) == 1)
-    def _():
-        right[...] = term.astype(BF16)
-
-
-def project_placed(after, idx_own, idx_oth, pf_own, pf_oth, proj_weight):
+def place_kernel(after, idx_own, idx_oth, pf_own, pf_oth, w_ref, wide_ref, *pieces):
+    rows, count = idx_own.shape[0], pf_own.shape[0]
+    at = lax.broadcasted_iota(jnp.int32, (rows, count), 1)
+    hot_own = jnp.where(at == idx_own[...], 1.0, 0.0).astype(BF16)
+    hot_oth = jnp.where(at == idx_oth[...], 1.0, 0.0).astype(BF16)
+    picked = jnp.dot(hot_own, pf_own[...], preferred_element_type=F32)
+    picked += jnp.dot(hot_oth, pf_oth[...], preferred_element_type=F32)
+    placed = picked.astype(BF16)
+    begin = 0
+    for piece in pieces:
+        lanes = slice(begin, begin + piece.shape[1])
+        term = jnp.dot(placed, w_ref[:, lanes], preferred_element_type=F32)
+        wide_ref[:, lanes] = term
+        piece[...] = term.astype(BF16)
+        begin += piece.shape[1]
+
+
+def project_placed(after, idx_own, idx_oth, pf_own, pf_oth, proj_weight, widths):
     rows, (depth, cols) = idx_own.shape[0], proj_weight.shape
-    block = cols // 2
     whole = lambda i: (0, 0)
+    shapes = [(rows, cols), *[(rows, width) for width in widths]]
+    values = (idx_own, idx_oth, pf_own, pf_oth, proj_weight)
     return pl.pallas_call(
         place_kernel,
-        grid=(cols // block,),
-        in_specs=[
-            ANY,
-            pl.BlockSpec(idx_own.shape, whole),
-            pl.BlockSpec(idx_oth.shape, whole),
-            pl.BlockSpec(pf_own.shape, whole),
-            pl.BlockSpec(pf_oth.shape, whole),
-            pl.BlockSpec((depth, block), lambda i: (0, i)),
+        grid=(1,),
+        in_specs=[ANY, *[pl.BlockSpec(value.shape, whole) for value in values]],
+        out_specs=[pl.BlockSpec(shape, whole) for shape in shapes],
+        out_shape=[
+            jax.ShapeDtypeStruct(shapes[0], F32),
+            *[jax.ShapeDtypeStruct(shape, BF16) for shape in shapes[1:]],
         ],
-        out_specs=[
-            pl.BlockSpec((rows, block), lambda i: (0, i)),
-            *[pl.BlockSpec((rows, block), whole)] * 2,
-        ],
-        out_shape=[
-            jax.ShapeDtypeStruct((rows, cols), F32),
-            *[jax.ShapeDtypeStruct((rows, block), BF16)] * 2,
-        ],
-        scratch_shapes=[pltpu.VMEM((rows, depth), BF16)],
         cost_estimate=LITTLE,
         compiler_params=params(60),
-    )(after, idx_own, idx_oth, pf_own, pf_oth, proj_weight)
+    )(after, *values)
 
 
 def project_kernel(x_ref, w_ref, wide_ref, sent_ref):
@@ -121,7 +105,7 @@
             jax.ShapeDtypeStruct((rows, cols), F32),
             jax.ShapeDtypeStruct((rows, cols), BF16),
         ],
-        compiler_params=params(60),
+        compiler_params=params(32),
     )(values, proj_weight)
 
 
@@ -141,7 +125,7 @@
         in_specs=[SMEM, ANY, pl.BlockSpec((rows, depth), lambda i: (0, 0))],
         out_specs=pl.BlockSpec(shape, lambda i: (0, 0, 0)),
         out_shape=jax.ShapeDtypeStruct(shape, BF16),
-        compiler_params=params(60),
+        compiler_params=params(16),
     )(tp_index, after, values)
 
 
@@ -157,7 +141,7 @@
         in_specs=[*[ANY] * len(after), VMEM, VMEM],
         out_specs=VMEM,
         out_shape=jax.ShapeDtypeStruct(wide.shape, BF16),
-        compiler_params=params(60),
+        compiler_params=params(16),
     )(*after, wide, came)
 
 
@@ -166,12 +150,15 @@
 
 
 def norm_rows(t, own, oth, gain, scratch, first_row):
-    rows, width = own[0].shape
-    half = width * len(own)
+    rows = own[0].shape[0]
+    half = sum(ref.shape[1] for ref in own)
     places = []
     for refs, core in ((own, t), (oth, 1 - t)):
-        for i, ref in enumerate(refs):
-            places.append((ref, pl.ds(pl.multiple_of(core * half + i * width, HDIM), width)))
+        begin = 0
+        for ref in refs:
+            width = ref.shape[1]
+            places.append((ref, pl.ds(pl.multiple_of(core * half + begin, HDIM), width)))
+            begin += width
 
     def chunk(c, carry):
         at = pl.ds(pl.multiple_of(c * 32, 32), 32)
@@ -346,7 +333,7 @@
         out_specs=[VMEM] * KV_HEADS,
         out_shape=[jax.ShapeDtypeStruct(kept.shape[1:], BF16)] * KV_HEADS,
         cost_estimate=LITTLE,
-        compiler_params=params(60),
+        compiler_params=params(16),
     )(at, *after, kept, given)
 
 
@@ -384,7 +371,7 @@
         out_shape=jax.ShapeDtypeStruct(packed.shape, BF16),
         scratch_shapes=[pltpu.SemaphoreType.DMA((2 * KV_HEADS * packed.shape[0],))],
         input_output_aliases={2: 0},
-        compiler_params=params(60),
+        compiler_params=params(16),
     )(at, after, packed, f_kept, f_given)
 
 
@@ -399,26 +386,31 @@
         out_specs=ANY,
         out_shape=jax.ShapeDtypeStruct(value.shape, value.dtype),
         input_output_aliases={0: 0},
-        compiler_params=params(60),
+        compiler_params=params(16),
     )(value, *after)
 
 
-def half_kernel(tp_ref, after, w_ref, o_ref):
-    o_ref[...] = w_ref[...]
+def half_kernel(tp_ref, after, w_ref, *outs):
+    for i, out in enumerate(outs):
+
+        @pl.when(pl.program_id(0) == i)
+        def _():
+            out[...] = w_ref[...]
 
 
 def other_columns(tp_index, after, weight):
     depth, cols = weight.shape
-    block = depth // 2
+    block = depth // 4
+    shape = (block, cols // 2)
     return pl.pallas_call(
         half_kernel,
         grid_spec=pltpu.PrefetchScalarGridSpec(
             num_scalar_prefetch=1,
-            grid=(2,),
-            in_specs=[ANY, pl.BlockSpec((block, cols // 2), lambda i, t: (i, 1 - t[0]))],
-            out_specs=pl.BlockSpec((block, cols // 2), lambda i, t: (i, 0)),
+            grid=(4,),
+            in_specs=[ANY, pl.BlockSpec(shape, lambda i, t: (i, 1 - t[0]))],
+            out_specs=[pl.BlockSpec(shape, lambda i, t: (0, 0))] * 4,
         ),
-        out_shape=jax.ShapeDtypeStruct((depth, cols // 2), BF16),
+        out_shape=[jax.ShapeDtypeStruct(shape, BF16)] * 4,
         cost_estimate=LITTLE,
         compiler_params=params(60),
     )(tp_index, after, weight)
@@ -563,30 +555,30 @@
             ],
         ),
         out_shape=[jax.ShapeDtypeStruct(shape, BF16)] * members,
-        compiler_params=params(60),
+        compiler_params=params(40),
     )(at, *after, *pieces, own, oth)
 
 
-def out_kernel(placing, width, chunk, at_ref, *refs):
+def out_kernel(placing, begin, block, at_ref, *refs):
     a_own, a_oth, refs = refs[:KV_HEADS], refs[KV_HEADS : 2 * KV_HEADS], refs[2 * KV_HEADS :]
-    w_own, w_oth, *residual, o_ref, both, own_w, oth_w, sems = refs
+    w_own, *w_oth = refs[:5]
+    *residual, o_ref, both, own_w, oth_w, sems = refs[5:]
     core, me, segment = at_ref[1], at_ref[2], at_ref[3]
-    half = o_ref.shape[-1]
-    lanes = [slice(c, min(c + width, half)) for c in range(0, half, width)]
-    start = pl.multiple_of(core * w_oth.shape[1], HDIM) + chunk * half
+    width = o_ref.shape[-1]
+    lanes = [slice(c, min(c + block, width)) for c in range(0, width, block)]
+    start = pl.multiple_of(core * w_oth[0].shape[1], HDIM) + begin
+    piece = w_oth[0].shape[0]
     copies = []
     for i, at in enumerate(lanes):
-        size = at.stop - at.start
-        mine = w_own.at[:, pl.ds(pl.multiple_of(start + at.start, HDIM), size)]
-        theirs = w_oth.at[:, chunk * half + at.start : chunk * half + at.stop]
-        copies.append(
-            (
-                pltpu.make_async_copy(mine, own_w.at[:, at], sems.at[0, i]),
-                pltpu.make_async_copy(theirs, oth_w.at[:, at], sems.at[1, i]),
-            )
-        )
-    for pair in copies:
-        for copy in pair:
+        mine = w_own.at[:, pl.ds(pl.multiple_of(start + at.start, HDIM), at.stop - at.start)]
+        group = [pltpu.make_async_copy(mine, own_w.at[:, at], sems.at[4, i])]
+        for p, part in enumerate(w_oth):
+            source = part.at[:, begin + at.start : begin + at.stop]
+            target = oth_w.at[p * piece : (p + 1) * piece, at]
+            group.append(pltpu.make_async_copy(source, target, sems.at[p, i]))
+        copies.append(group)
+    for group in copies:
+        for copy in group:
             copy.start()
     for d in range(KV_HEADS):
         j = jnp.bitwise_xor(me, d)
@@ -611,46 +603,51 @@
         if placing:
             o_ref[:, at] = (o_ref[:, at].astype(F32) + term).astype(BF16)
         else:
-            pieces = len(residual) // 2
-            step = half // pieces
-            for p in range(pieces):
-                low, high = max(at.start, p * step), min(at.stop, (p + 1) * step)
+            count = len(residual) // 2
+            edge = 0
+            for p in range(count):
+                low, high = max(at.start, edge), min(at.stop, edge + residual[p].shape[1])
                 if low < high:
-                    inner = slice(low - p * step, high - p * step)
+                    inner = slice(low - edge, high - edge)
                     h = residual[p][:, inner].astype(F32)
                     h = (h + term[:, low - at.start : high - at.start]).astype(BF16)
-                    first = residual[pieces + p][:, inner]
+                    first = residual[count + p][:, inner]
                     o_ref[0, :, low:high] = jnp.where(segment == 0, first, h)
-
-
-def project_out(at, a_own, a_oth, w_own, w_oth, residual, placing, chunk, chunks):
+                edge += residual[p].shape[1]
+
+
+def project_out(at, a_own, a_oth, w_own, w_oth, residual, placing, begin, width):
     rows = a_own[0].shape[1]
-    depth, cols = w_oth.shape
-    width = cols // chunks
+    depth, cols = w_own.shape[0], w_oth[0].shape[1]
     shape = (rows, width) if placing else (1, rows, width)
-    whole = lambda i: (0, 0)
-    part = lambda i: (0, chunk)
-    specs = [
-        pl.BlockSpec((value.shape[0], width), part)
-        if value.shape[1] == cols
-        else pl.BlockSpec(value.shape, whole)
-        for value in residual
-    ]
+
+    def spec(value):
+        if value.shape[1] == cols and width < cols:
+            return pl.BlockSpec(
+                (pl.Element(rows), pl.Element(width)), lambda i: (0, begin)
+            )
+        return pl.BlockSpec(value.shape, lambda i: (0, 0))
+
     piece = pl.BlockSpec(a_own[0].shape, lambda i: (0, 0, 0))
     block = 4 * HDIM
     return pl.pallas_call(
-        functools.partial(out_kernel, placing, block, chunk),
+        functools.partial(out_kernel, placing, begin, block),
         grid=(1,),
-        in_specs=[SMEM, *[piece] * (2 * KV_HEADS), ANY, ANY, *specs],
+        in_specs=[
+            SMEM,
+            *[piece] * (2 * KV_HEADS),
+            *[ANY] * 5,
+            *[spec(value) for value in residual],
+        ],
         out_specs=pl.BlockSpec(shape, lambda i: (0,) * len(shape)),
         out_shape=jax.ShapeDtypeStruct(shape, BF16),
         scratch_shapes=[
             pltpu.VMEM((2, rows, depth), BF16),
             *[pltpu.VMEM((depth, width), BF16)] * 2,
-            pltpu.SemaphoreType.DMA((2, -(-width // block))),
+            pltpu.SemaphoreType.DMA((5, -(-width // block))),
         ],
-        compiler_params=params(60),
-    )(at, *a_own, *a_oth, w_own, w_oth, *residual)
+        compiler_params=params(56),
+    )(at, *a_own, *a_oth, w_own, *w_oth, *residual)
 
 
 def per_device(
@@ -684,9 +681,13 @@
         return lax.ppermute(sent, "segment", [(1, 0)])
 
     base = jnp.stack([group * members * rows, t, me, segment]).astype(jnp.int32)
+    at = jnp.concatenate([base, frame_start])
+    block = 4 * HDIM
+    widths = [block, cols - 2 * block, block]
+    begins = [0, block, cols - block]
 
     def spread_heads(kept, given, *after):
-        pieces = route(base, kept, swap(given), *after)
+        pieces = route(at, kept, swap(given), *after)
         return [pieces[0]] + [
             lax.ppermute(pieces[d], "mem", [(i, i ^ d) for i in range(KV_HEADS)])
             for d in range(1, KV_HEADS)
@@ -713,12 +714,10 @@
 
     wide, sent = project(patch_feats, proj_weight)
     came = from_vision(sent)
-    w_given = other_columns(tp_index, sent, out_weight)
-    w_oth = swap(w_given)
     pf_own = spread(tp_index, sent, patch_feats, count)
     pf_own = lax.all_to_all(pf_own, CTX, split_axis=0, concat_axis=0, tiled=True)
 
-    frame_embed = gelu_sum(wide, came, w_given, *kv_tables, *q_tables, idx_own, idx_oth)
+    frame_embed = gelu_sum(wide, came, *kv_tables, *q_tables, at)
     packed, kept, given, f_kept, f_given = qkv(
         tp_index,
         text_embed,
@@ -732,24 +731,27 @@
         q_tables,
         groups,
     )
-    packed = pack(base, pf_own, packed, f_kept, swap(f_given))
+    packed = pack(at, pf_own, packed, f_kept, swap(f_given))
     message = packed.reshape(count, *packed.shape[2:])
     message = lax.all_to_all(message, CTX, split_axis=0, concat_axis=0, tiled=True)
 
     pf_own = pf_own.reshape(count * part, -1)
-    wide, *sent = project_placed(packed, idx_own, idx_oth, pf_own, swap(pf_own), proj_weight)
+    wide, *sent = project_placed(
+        packed, idx_own, idx_oth, pf_own, swap(pf_own), proj_weight, widths
+    )
+    w_given = other_columns(tp_index, sent[0], out_weight)
+    w_oth = [swap(piece) for piece in w_given]
     placed = [from_vision(half) for half in sent]
     pieces = spread_heads(kept, given, packed)
 
-    at = jnp.concatenate([base, frame_start])
-    message = gate(message, *sent, *pieces[1:])
+    message = gate(message, w_given[0], *placed, *pieces[1:])
     attended = attend(at, pieces, message, swap(message), frame_start.shape[0])
     a_own, a_oth = returned(attended)
     first = []
-    for chunk in range(2):
-        residual = (text_embed, wide, placed[chunk], idx_own, idx_oth)
+    for came, begin, width in zip(placed, begins, widths):
+        residual = (text_embed, wide, came, idx_own, idx_oth)
         first.append(
-            project_out(base, a_own, a_oth, out_weight, w_oth, residual, True, chunk, 2)
+            project_out(at, a_own, a_oth, out_weight, w_oth, residual, True, begin, width)
         )
 
     h = [lax.ppermute(part, "segment", [(0, 1)]) for part in first]
@@ -759,9 +761,9 @@
     kv = lax.all_to_all(kv, CTX, split_axis=0, concat_axis=0, tiled=True)
     pieces = spread_heads(*queries_of(tp_index, normed, q_weight, *q_tables))
     kv = gate(kv, *pieces[1:])
-    attended = attend(base, pieces, kv, swap(kv), 0)
+    attended = attend(at, pieces, kv, swap(kv), 0)
     a_own, a_oth = returned(attended)
-    return project_out(base, a_own, a_oth, out_weight, w_oth, (*h, *first), False, 0, 1)
+    return project_out(at, a_own, a_oth, out_weight, w_oth, (*h, *first), False, 0, cols)
 
 
 def solution(mesh):

time: 202 us -> 189 us (0.936)
  waiting for transfers between devices: 47.8 us -> 33 us
  starting transfers between devices: 51.6 us -> 63.7 us
  Pallas kernels: 83.2 us -> 75.3 us
    ppermute x6, waiting for transfers between devices: 19.3 us -> 11.4 us  [spread_heads(): lax.ppermute(pieces[d], 'mem', [(i, i ^ d) for i in range(KV_HEADS)])]
    pallas_call x2, Pallas kernels: 21.9 us -> 16.8 us  [attend(): pl.pallas_call(functools.partial(attend_kernel, frames, len(after)), grid...]
    ppermute x2 -> x3, waiting for transfers between devices: 12.3 us -> 7.34 us  [per_device(): h = [lax.ppermute(part, 'segment', [(0, 1)]) for part in first]]
    ppermute x19 -> x23, starting transfers between devices: 18.5 us -> 23.3 us  [swap(): return lax.ppermute(value, 'tp', [(0, 1), (1, 0)])]
    pallas_call x4 -> x5, Pallas kernels: 24.3 us -> 28.3 us  [the longest x4 23.4 us: project_out(): pl.pallas_call(functools.partial(out_kernel, placing, begin, block), grid...]
    ppermute x3 -> x4, starting transfers between devices: 4.81 us -> 7.66 us  [from_vision(): return lax.ppermute(sent, 'segment', [(1, 0)])]
    pallas_call x2, Pallas kernels: 3.84 us -> 1.23 us  [route(): pl.pallas_call(functools.partial(route_kernel, len(after)), in_specs=[SME...]
    ppermute x6, waiting for transfers between devices: 5.39 us -> 2.82 us  [returned(): a_own.append(lax.ppermute(attended[d], 'mem', pairs))]
  transfers between devices with their start and end apart: 39 -> 45, of which waited for: 19 -> 20; matrix products, arithmetic and copies ran while one was open for 3% -> 2% of each run, Pallas kernels for 30% -> 25%
where the time goes in v6:
time: 189 us; the launch traced here: 188 us
  Pallas kernels  75.3 us (40%)
  starting transfers between devices  63.7 us (34%)
  waiting for transfers between devices  33 us (17%)
  local copies, waits for them, and re-layouts  13.4 us (7%)
    pallas_call x4, Pallas kernels, project_out(): pl.pallas_call(functools.partial(out_kernel, placing, begin, block), grid...  23.4 us
    ppermute x23, starting transfers between devices, swap(): return lax.ppermute(value, 'tp', [(0, 1), (1, 0)])  23.3 us
    pallas_call x2, Pallas kernels, attend(): pl.pallas_call(functools.partial(attend_kernel, frames, len(after)), grid...  16.8 us
    ppermute x6, waiting for transfers between devices, spread_heads(): lax.ppermute(pieces[d], 'mem', [(i, i ^ d) for i in range(KV_HEADS)])  11.4 us
    unnamed x104, local copies, waits for them, and re-layouts  11.1 us
    pallas_call x1, Pallas kernels, qkv(): pl.pallas_call(qkv_kernel, in_specs=[SMEM, *[VMEM] * 5, ANY, ANY, *[VMEM]...  9.64 us
    ppermute x23, waiting for transfers between devices, swap(): return lax.ppermute(value, 'tp', [(0, 1), (1, 0)])  9.4 us
    ppermute x4, starting transfers between devices, from_vision(): return lax.ppermute(sent, 'segment', [(1, 0)])  7.66 us
  transfers between devices with their start and end apart: 45, of which 20 were waited for; matrix products, arithmetic and copies ran while one was open for 2% of the time, Pallas kernels for 25%

profile of v6, /device:TPU:19, one launch (start us, length us, event | category | flops | bytes accessed | tf_op | source)
XLA Modules:
  0.0 187.9 jit_solution(16170778011067613902)
XLA Ops:
  4.1 2.2 %collective-permute-start.1 = (bf16[96,1792]{1,0:T(8,128)(2,1)S(1)}, bf16[96,1792]{1,0:T(8,128)(2,1)S(1)}, u32[]{:S(2)}, u32[]{:S(2)}) collective-permute-start(bf16[96,1792]{1,0:T(8,128)(2,1)S(1)} %get-tuple-element.40.after), channel_id=1, source_target_pairs={{16,0},{17,1},{18,2},{19,3},{20,4},{21,5},{22,6},{23,7},{24,8},{25... | collective-permute-start | bytes 1032200 | tf_op jit(solution)/shard_map/ppermute | solution.py:681
  7.2 5.6 %all-to-all-start = ((bf16[8,48,576]{2,1,0:T(8,128)(2,1)}), bf16[8,48,576]{2,1,0:T(8,128)(2,1)S(1)}, u32[]{:S(2)}, u32[]{:S(2)}) async-start(bf16[8,48,576]{2,1,0:T(8,128)(2,1)} %shard_map.83), calls=%async_computation | async-start | bytes 983040 | tf_op jit(solution)/shard_map/all_to_all | solution.py:718
  18.5 9.6 %shard_map.85 = (bf16[2,4,544,128]{3,2,1,0:T(8,128)(2,1)}, bf16[2,2,256,128]{3,2,1,0:T(8,128)(2,1)}, bf16[2,2,256,128]{3,2,1,0:T(8,128)(2,1)}, bf16[2,2,96,128]{3,2,1,0:T(8,128)(2,1)}, bf16[2,2,96,128]{3,2,1,0:T(8,128)(2,1)}) custom-call(s32[1]{0:T(128)} %bitcast.1.tp_ref, bf16[256,1792]{1,0:T(8,128)(2,1)} %refs_13_.5, bf16[256,1792]{1,0:T(8,128)(2,1)} %copy-done.36, ...), custom_call_target="tpu_custom_call" | custom-call | tf_op jit(solution)/shard_map/pallas_call | solution.py:252
  34.1 5.4 %all-to-all-start.1 = ((bf16[8,544,128]{2,1,0:T(8,128)(2,1)}), bf16[8,544,128]{2,1,0:T(8,128)(2,1)S(1)}, u32[]{:S(2)}, u32[]{:S(2)}) async-start(bf16[8,544,128]{2,1,0:T(8,128)(2,1)} %bitcast.13), calls=%async_computation.1 | async-start | bytes 2228224 | tf_op jit(solution)/shard_map/all_to_all | solution.py:736
  42.2 4.9 %shard_map.88 = (f32[256,1792]{1,0:T(8,128)}, bf16[256,512]{1,0:T(8,128)(2,1)}, bf16[256,768]{1,0:T(8,128)(2,1)}, bf16[256,512]{1,0:T(8,128)(2,1)}) custom-call(bf16[2,4,544,128]{3,2,1,0:T(8,128)(2,1)} %copy-done.1, s32[256,1]{1,0:T(8,128)} %copy.20.idx_own.refs_16_, s32[256,1]{1,0:T(8,128)} %copy.21.idx_oth.refs_17_, bf16[384,576]{1,0:T(8,128)(2,1)} %bitcast.15, ...), custom_call_target="tpu_custom_call" | custom-call | flops 1 | bytes 1 | tf_op jit(solution)/shard_map/pallas_call | solution.py:73
  47.1 2.9 %collective-permute-start.10 = (bf16[256,768]{1,0:T(8,128)(2,1)}, bf16[256,768]{1,0:T(8,128)(2,1)S(1)}, u32[]{:S(2)}, u32[]{:S(2)}) collective-permute-start(bf16[256,768]{1,0:T(8,128)(2,1)} %get-tuple-element.53), channel_id=1, source_target_pairs={{16,0},{17,1},{18,2},{19,3},{20,4},{21,5},{22,6},{23,7},{24,8},{25... | collective-permute-start | bytes 1179656 | tf_op jit(solution)/shard_map/ppermute | solution.py:681
  59.4 4.7 %shard_map.89 = (bf16[256,1792]{1,0:T(8,128)(2,1)}, bf16[256,1792]{1,0:T(8,128)(2,1)}, bf16[256,1792]{1,0:T(8,128)(2,1)}, bf16[256,1792]{1,0:T(8,128)(2,1)}) custom-call(s32[1]{0:T(128)} %bitcast.1.tp_ref, bf16[256,512]{1,0:T(8,128)(2,1)} %get-tuple-element.51.after, bf16[1024,3584]{1,0:T(8,128)(2,1)} %bitcast.16), custom_call_target="tpu_custom_call" | custom-call | flops 1 | bytes 1 | tf_op jit(solution)/shard_map/pallas_call | solution.py:405
  64.1 3.4 %collective-permute-done.7.refs_7_.refs_3_ = bf16[2,256,128]{2,1,0:T(8,128)(2,1)S(1)} collective-permute-done((bf16[2,256,128]{2,1,0:T(8,128)(2,1)S(1)}, bf16[2,256,128]{2,1,0:T(8,128)(2,1)S(1)}, u32[]{:S(2)}, u32[]{:S(2)}) %collective-permute-start.7) | collective-permute-done | bytes 131104 | tf_op jit(solution)/shard_map/ppermute | solution.py:692
  67.5 2.1 %collective-permute-done.9.refs_2_.refs_15_ = bf16[256,512]{1,0:T(8,128)(2,1)S(1)} collective-permute-done((bf16[256,512]{1,0:T(8,128)(2,1)}, bf16[256,512]{1,0:T(8,128)(2,1)S(1)}, u32[]{:S(2)}, u32[]{:S(2)}) %collective-permute-start.9) | collective-permute-done | bytes 262176 | tf_op jit(solution)/shard_map/ppermute | solution.py:681
  74.1 8.7 %shard_map.91 = (bf16[2,256,128]{2,1,0:T(8,128)(2,1)S(1)}, bf16[2,256,128]{2,1,0:T(8,128)(2,1)S(1)}, bf16[2,256,128]{2,1,0:T(8,128)(2,1)S(1)}, bf16[2,256,128]{2,1,0:T(8,128)(2,1)S(1)}) custom-call(s32[12]{0:T(128)S(1)} %concatenate.16.refs_4_.at_ref, bf16[2,256,128]{2,1,0:T(8,128)(2,1)S(1)} %get-tuple-element.47.refs_0_, ...), custom_call_target="tpu_custom_call" | custom-call | tf_op jit(solution)/shard_map/pallas_call | solution.py:540
  88.7 2.3 %collective-permute-start.18 = (bf16[2,256,128]{2,1,0:T(8,128)(2,1)S(1)}, bf16[2,256,128]{2,1,0:T(8,128)(2,1)S(1)}, u32[]{:S(2)}, u32[]{:S(2)}) collective-permute-start(bf16[2,256,128]{2,1,0:T(8,128)(2,1)S(1)} %collective-permute-done.14.refs_2_), channel_id=1, source_target_pairs={{0,1},{1,0},{2,3},{3,2},{4,5},{5,4},{6,7},{7,6},{8,9},{9,8},{10,11... | collective-permute-start | bytes 393224 | tf_op jit(solution)/shard_map/ppermute | solution.py:37
  94.3 6.1 %shard_map.93.refs_17_ = bf16[256,768]{1,0:T(8,128)(2,1)} custom-call(s32[12]{0:T(128)} %copy-done.20, bf16[2,256,128]{2,1,0:T(8,128)(2,1)} %copy-done.11, bf16[2,256,128]{2,1,0:T(8,128)(2,1)} %copy-done.27, bf16[2,256,128]{2,1,0:T(8,128)(2,1)} %copy-done.28, bf16[2,256,128]{2,1,0:T(8,128)(2,1)} %copy-done.29, bf16[2,256,128]{2,1,0:T(8,128)(2,1)} %copy-done.30, ...), custom_call_target="tpu_custom_call" | custom-call | tf_op jit(solution)/shard_map/pallas_call | solution.py:633
  101.8 4.9 %shard_map.92.refs_16_ = bf16[256,512]{1,0:T(8,128)(2,1)} custom-call(s32[12]{0:T(128)} %copy-done.20, bf16[2,256,128]{2,1,0:T(8,128)(2,1)} %copy-done.11, bf16[2,256,128]{2,1,0:T(8,128)(2,1)} %copy-done.27, bf16[2,256,128]{2,1,0:T(8,128)(2,1)} %copy-done.28, bf16[2,256,128]{2,1,0:T(8,128)(2,1)} %copy-done.29, bf16[2,256,128]{2,1,0:T(8,128)(2,1)} %copy-done.30, ...), custom_call_target="tpu_custom_call" | custom-call | tf_op jit(solution)/shard_map/pallas_call | solution.py:633
  108.0 4.8 %shard_map.94.refs_18_ = bf16[256,512]{1,0:T(8,128)(2,1)} custom-call(s32[12]{0:T(128)} %copy-done.20, bf16[2,256,128]{2,1,0:T(8,128)(2,1)} %copy-done.11, bf16[2,256,128]{2,1,0:T(8,128)(2,1)} %copy-done.27, bf16[2,256,128]{2,1,0:T(8,128)(2,1)} %copy-done.28, bf16[2,256,128]{2,1,0:T(8,128)(2,1)} %copy-done.29, bf16[2,256,128]{2,1,0:T(8,128)(2,1)} %copy-done.30, ...), custom_call_target="tpu_custom_call" | custom-call | tf_op jit(solution)/shard_map/pallas_call | solution.py:633
  114.9 3.7 %collective-permute-done.24.refs_0_.refs_13_ = bf16[256,512]{1,0:T(8,128)(2,1)S(1)} collective-permute-done((bf16[256,512]{1,0:T(8,128)(2,1)}, bf16[256,512]{1,0:T(8,128)(2,1)S(1)}, u32[]{:S(2)}, u32[]{:S(2)}) %collective-permute-start.24) | collective-permute-done | bytes 262176 | tf_op jit(solution)/shard_map/ppermute | solution.py:757
  120.5 3.7 %collective-permute-done.26.refs_2_.refs_15_ = bf16[256,512]{1,0:T(8,128)(2,1)S(1)} collective-permute-done((bf16[256,512]{1,0:T(8,128)(2,1)}, bf16[256,512]{1,0:T(8,128)(2,1)S(1)}, u32[]{:S(2)}, u32[]{:S(2)}) %collective-permute-start.26) | collective-permute-done | bytes 262176 | tf_op jit(solution)/shard_map/ppermute | solution.py:757
  128.0 5.6 %shard_map.95 = (bf16[256,3584]{1,0:T(8,128)(2,1)}, bf16[2,4,256,128]{3,2,1,0:T(8,128)(2,1)}) custom-call(s32[1]{0:T(128)} %bitcast.1.tp_ref, bf16[256,512]{1,0:T(8,128)(2,1)} %copy-done.34, bf16[256,768]{1,0:T(8,128)(2,1)} %copy-done.26, bf16[256,512]{1,0:T(8,128)(2,1)} %copy-done.35, bf16[256,512]{1,0:T(8,128)(2,1)} %copy-done.39, ...), custom_call_target="tpu_custom_call" | custom-call | tf_op jit(solution)/shard_map/pallas_call | solution.py:195
  133.7 5.5 %all-to-all-start.2 = ((bf16[8,256,128]{2,1,0:T(8,128)(2,1)}), bf16[8,256,128]{2,1,0:T(8,128)(2,1)S(1)}, u32[]{:S(2)}, u32[]{:S(2)}) async-start(bf16[8,256,128]{2,1,0:T(8,128)(2,1)} %bitcast.25), calls=%async_computation.2 | async-start | bytes 1048576 | tf_op jit(solution)/shard_map/all_to_all | solution.py:761
  139.1 5.9 %shard_map.96 = (bf16[2,2,256,128]{3,2,1,0:T(8,128)(2,1)}, bf16[2,2,256,128]{3,2,1,0:T(8,128)(2,1)}) custom-call(s32[1]{0:T(128)} %bitcast.1.tp_ref, bf16[256,3584]{1,0:T(8,128)(2,1)} %get-tuple-element.63.refs_0_, bf16[3584,1024]{1,0:T(8,128)(2,1)} %bitcast.22, f32[352,128]{1,0:T(8,128)} %copy-done.7, f32[352,128]{1,0:T(8,128)} %copy-done.8), custom_call_target="tpu_custom_call" | custom-call | flops 1 | bytes 1 | tf_op jit(solution)/shard_map/pallas_call | solution.py:292
  151.6 2.1 %collective-permute-done.31.refs_1_ = bf16[2,256,128]{2,1,0:T(8,128)(2,1)S(1)} collective-permute-done((bf16[2,256,128]{2,1,0:T(8,128)(2,1)S(1)}, bf16[2,256,128]{2,1,0:T(8,128)(2,1)S(1)}, u32[]{:S(2)}, u32[]{:S(2)}) %collective-permute-start.31) | collective-permute-done | bytes 131104 | tf_op jit(solution)/shard_map/ppermute | solution.py:692
  154.5 3.2 %collective-permute-done.33.refs_3_ = bf16[2,256,128]{2,1,0:T(8,128)(2,1)S(1)} collective-permute-done((bf16[2,256,128]{2,1,0:T(8,128)(2,1)S(1)}, bf16[2,256,128]{2,1,0:T(8,128)(2,1)S(1)}, u32[]{:S(2)}, u32[]{:S(2)}) %collective-permute-start.33) | collective-permute-done | bytes 131104 | tf_op jit(solution)/shard_map/ppermute | solution.py:692
  160.4 8.1 %shard_map.99 = (bf16[2,256,128]{2,1,0:T(8,128)(2,1)S(1)}, bf16[2,256,128]{2,1,0:T(8,128)(2,1)S(1)}, bf16[2,256,128]{2,1,0:T(8,128)(2,1)S(1)}, bf16[2,256,128]{2,1,0:T(8,128)(2,1)S(1)}) custom-call(s32[12]{0:T(128)S(1)} %copy-done.21, bf16[2,256,128]{2,1,0:T(8,128)(2,1)S(1)} %get-tuple-element.66.refs_0_, ...), custom_call_target="tpu_custom_call" | custom-call | tf_op jit(solution)/shard_map/pallas_call | solution.py:540
  174.5 2.3 %collective-permute-start.40 = (bf16[2,256,128]{2,1,0:T(8,128)(2,1)S(1)}, bf16[2,256,128]{2,1,0:T(8,128)(2,1)S(1)}, u32[]{:S(2)}, u32[]{:S(2)}) collective-permute-start(bf16[2,256,128]{2,1,0:T(8,128)(2,1)S(1)} %collective-permute-done.36.refs_2_), channel_id=1, source_target_pairs={{0,1},{1,0},{2,3},{3,2},{4,5},{5,4},{6,7},{7,6},{8,9},{9,8},{10,11... | collective-permute-start | bytes 393224 | tf_op jit(solution)/shard_map/ppermute | solution.py:37
  180.1 7.6 %shard_map.100 = bf16[1,256,1792]{2,1,0:T(8,128)(2,1)} custom-call(s32[12]{0:T(128)} %copy-done.20, bf16[2,256,128]{2,1,0:T(8,128)(2,1)} %copy-done.18, bf16[2,256,128]{2,1,0:T(8,128)(2,1)} %copy-done.41, bf16[2,256,128]{2,1,0:T(8,128)(2,1)} %copy-done.42, bf16[2,256,128]{2,1,0:T(8,128)(2,1)} %copy-done.43, bf16[2,256,128]{2,1,0:T(8,128)(2,1)} %copy-done.44, ...), custom_call_target="tpu_custom_call" | custom-call | tf_op jit(solution)/shard_map/pallas_call | solution.py:633
  (201 shorter events, 72.0 us)
Async XLA Ops:
  0.0 17.5 %collective-permute-start = (bf16[256,1792]{1,0:T(8,128)(2,1)}, bf16[256,1792]{1,0:T(8,128)(2,1)S(1)}, u32[]{:S(2)}, u32[]{:S(2)}) collective-permute-start(bf16[256,1792]{1,0:T(8,128)(2,1)} %refs_13_.5), channel_id=1, source_target_pairs={{0,1},{1,0},{2,3},{3,2},{4,5},{5,4},{6,7},{7,6},{8,9},{9,8},{10,11... | collective-permute-start | bytes 2752520 | tf_op jit(solution)/shard_map/ppermute | solution.py:37
  4.1 11.0 %collective-permute-start.1 = (bf16[96,1792]{1,0:T(8,128)(2,1)S(1)}, bf16[96,1792]{1,0:T(8,128)(2,1)S(1)}, u32[]{:S(2)}, u32[]{:S(2)}) collective-permute-start(bf16[96,1792]{1,0:T(8,128)(2,1)S(1)} %get-tuple-element.40.after), channel_id=1, source_target_pairs={{16,0},{17,1},{18,2},{19,3},{20,4},{21,5},{22,6},{23,7},{24,8},{25... | collective-permute-start | bytes 1032200 | tf_op jit(solution)/shard_map/ppermute | solution.py:681
  7.2 21.4 %all-to-all-start = ((bf16[8,48,576]{2,1,0:T(8,128)(2,1)}), bf16[8,48,576]{2,1,0:T(8,128)(2,1)S(1)}, u32[]{:S(2)}, u32[]{:S(2)}) async-start(bf16[8,48,576]{2,1,0:T(8,128)(2,1)} %shard_map.83), calls=%async_computation | async-start | bytes 983040 | tf_op jit(solution)/shard_map/all_to_all | solution.py:718
  34.1 35.4 %all-to-all-start.1 = ((bf16[8,544,128]{2,1,0:T(8,128)(2,1)}), bf16[8,544,128]{2,1,0:T(8,128)(2,1)S(1)}, u32[]{:S(2)}, u32[]{:S(2)}) async-start(bf16[8,544,128]{2,1,0:T(8,128)(2,1)} %bitcast.13), calls=%async_computation.1 | async-start | bytes 2228224 | tf_op jit(solution)/shard_map/all_to_all | solution.py:736
  40.5 9.5 %collective-permute-start.4 = (bf16[2,2,256,128]{3,2,1,0:T(8,128)(2,1)}, bf16[2,2,256,128]{3,2,1,0:T(8,128)(2,1)S(1)}, u32[]{:S(2)}, u32[]{:S(2)}) collective-permute-start(bf16[2,2,256,128]{3,2,1,0:T(8,128)(2,1)} %get-tuple-element.46), channel_id=1, source_target_pairs={{0,1},{1,0},{2,3},{3,2},{4,5},{5,4},{6,7},{7,6},{8,9},{9,8},{10,11... | collective-permute-start | bytes 786440 | tf_op jit(solution)/shard_map/ppermute | solution.py:37
  47.1 22.5 %collective-permute-start.10 = (bf16[256,768]{1,0:T(8,128)(2,1)}, bf16[256,768]{1,0:T(8,128)(2,1)S(1)}, u32[]{:S(2)}, u32[]{:S(2)}) collective-permute-start(bf16[256,768]{1,0:T(8,128)(2,1)} %get-tuple-element.53), channel_id=1, source_target_pairs={{16,0},{17,1},{18,2},{19,3},{20,4},{21,5},{22,6},{23,7},{24,8},{25... | collective-permute-start | bytes 1179656 | tf_op jit(solution)/shard_map/ppermute | solution.py:681
  50.6 7.0 %collective-permute-start.5 = (bf16[2,256,128]{2,1,0:T(8,128)(2,1)S(1)}, bf16[2,256,128]{2,1,0:T(8,128)(2,1)S(1)}, u32[]{:S(2)}, u32[]{:S(2)}) collective-permute-start(bf16[2,256,128]{2,1,0:T(8,128)(2,1)S(1)} %get-tuple-element.48), channel_id=1, source_target_pairs={{0,2},{2,0},{4,6},{6,4},{1,3},{3,1},{5,7},{7,5},{8,10},{10,8},{12,... | collective-permute-start | bytes 393224 | tf_op jit(solution)/shard_map/ppermute | solution.py:692
  51.9 15.6 %collective-permute-start.11 = (bf16[256,512]{1,0:T(8,128)(2,1)}, bf16[256,512]{1,0:T(8,128)(2,1)S(1)}, u32[]{:S(2)}, u32[]{:S(2)}) collective-permute-start(bf16[256,512]{1,0:T(8,128)(2,1)} %get-tuple-element.54), channel_id=1, source_target_pairs={{16,0},{17,1},{18,2},{19,3},{20,4},{21,5},{22,6},{23,7},{24,8},{25... | collective-permute-start | bytes 786440 | tf_op jit(solution)/shard_map/ppermute | solution.py:681
  53.2 16.4 %collective-permute-start.9 = (bf16[256,512]{1,0:T(8,128)(2,1)}, bf16[256,512]{1,0:T(8,128)(2,1)S(1)}, u32[]{:S(2)}, u32[]{:S(2)}) collective-permute-start(bf16[256,512]{1,0:T(8,128)(2,1)} %get-tuple-element.51.after), channel_id=1, source_target_pairs={{16,0},{17,1},{18,2},{19,3},{20,4},{21,5},{22,6},{23,7},{24,8},{25... | collective-permute-start | bytes 786440 | tf_op jit(solution)/shard_map/ppermute | solution.py:681
  54.5 9.6 %collective-permute-start.6 = (bf16[2,256,128]{2,1,0:T(8,128)(2,1)S(1)}, bf16[2,256,128]{2,1,0:T(8,128)(2,1)S(1)}, u32[]{:S(2)}, u32[]{:S(2)}) collective-permute-start(bf16[2,256,128]{2,1,0:T(8,128)(2,1)S(1)} %get-tuple-element.49), channel_id=1, source_target_pairs={{0,4},{2,6},{4,0},{6,2},{1,5},{3,7},{5,1},{7,3},{8,12},{10,14},{12... | collective-permute-start | bytes 393224 | tf_op jit(solution)/shard_map/ppermute | solution.py:692
  57.6 9.9 %collective-permute-start.7 = (bf16[2,256,128]{2,1,0:T(8,128)(2,1)S(1)}, bf16[2,256,128]{2,1,0:T(8,128)(2,1)S(1)}, u32[]{:S(2)}, u32[]{:S(2)}) collective-permute-start(bf16[2,256,128]{2,1,0:T(8,128)(2,1)S(1)} %get-tuple-element.50), channel_id=1, source_target_pairs={{0,6},{2,4},{4,2},{6,0},{1,7},{3,5},{5,3},{7,1},{8,14},{10,12},{12... | collective-permute-start | bytes 393224 | tf_op jit(solution)/shard_map/ppermute | solution.py:692
  71.7 12.3 %collective-permute-start.21 = (bf16[256,1792]{1,0:T(8,128)(2,1)S(1)}, bf16[256,1792]{1,0:T(8,128)(2,1)S(1)}, u32[]{:S(2)}, u32[]{:S(2)}) collective-permute-start(bf16[256,1792]{1,0:T(8,128)(2,1)S(1)} %copy-done.51), channel_id=1, source_target_pairs={{0,1},{1,0},{2,3},{3,2},{4,5},{5,4},{6,7},{7,6},{8,9},{9,8},{10,11... | collective-permute-start | bytes 2752520 | tf_op jit(solution)/shard_map/ppermute | solution.py:37
  72.3 12.9 %collective-permute-start.22 = (bf16[256,1792]{1,0:T(8,128)(2,1)S(1)}, bf16[256,1792]{1,0:T(8,128)(2,1)S(1)}, u32[]{:S(2)}, u32[]{:S(2)}) collective-permute-start(bf16[256,1792]{1,0:T(8,128)(2,1)S(1)} %copy-done.50), channel_id=1, source_target_pairs={{0,1},{1,0},{2,3},{3,2},{4,5},{5,4},{6,7},{7,6},{8,9},{9,8},{10,11... | collective-permute-start | bytes 2752520 | tf_op jit(solution)/shard_map/ppermute | solution.py:37
  72.5 12.9 %collective-permute-start.23 = (bf16[256,1792]{1,0:T(8,128)(2,1)S(1)}, bf16[256,1792]{1,0:T(8,128)(2,1)S(1)}, u32[]{:S(2)}, u32[]{:S(2)}) collective-permute-start(bf16[256,1792]{1,0:T(8,128)(2,1)S(1)} %copy-done.49), channel_id=1, source_target_pairs={{0,1},{1,0},{2,3},{3,2},{4,5},{5,4},{6,7},{7,6},{8,9},{9,8},{10,11... | collective-permute-start | bytes 2752520 | tf_op jit(solution)/shard_map/ppermute | solution.py:37
  72.8 19.9 %collective-permute-start.20 = (bf16[256,1792]{1,0:T(8,128)(2,1)}, bf16[256,1792]{1,0:T(8,128)(2,1)S(1)}, u32[]{:S(2)}, u32[]{:S(2)}) collective-permute-start(bf16[256,1792]{1,0:T(8,128)(2,1)} %get-tuple-element.52.refs_1_), channel_id=1, source_target_pairs={{0,1},{1,0},{2,3},{3,2},{4,5},{5,4},{6,7},{7,6},{8,9},{9,8},{10,11... | collective-permute-start | bytes 2752520 | tf_op jit(solution)/shard_map/ppermute | solution.py:37
  85.2 6.4 %collective-permute-start.15 = (bf16[2,256,128]{2,1,0:T(8,128)(2,1)S(1)}, bf16[2,256,128]{2,1,0:T(8,128)(2,1)S(1)}, u32[]{:S(2)}, u32[]{:S(2)}) collective-permute-start(bf16[2,256,128]{2,1,0:T(8,128)(2,1)S(1)} %get-tuple-element.58), channel_id=1, source_target_pairs={{0,6},{2,4},{4,2},{6,0},{1,7},{3,5},{5,3},{7,1},{8,14},{10,12},{12... | collective-permute-start | bytes 393224 | tf_op jit(solution)/shard_map/ppermute | solution.py:700
  85.5 7.3 %collective-permute-start.16 = (bf16[2,256,128]{2,1,0:T(8,128)(2,1)S(1)}, bf16[2,256,128]{2,1,0:T(8,128)(2,1)S(1)}, u32[]{:S(2)}, u32[]{:S(2)}) collective-permute-start(bf16[2,256,128]{2,1,0:T(8,128)(2,1)S(1)} %get-tuple-element.55.refs_0_), channel_id=1, source_target_pairs={{0,1},{1,0},{2,3},{3,2},{4,5},{5,4},{6,7},{7,6},{8,9},{9,8},{10,11... | collective-permute-start | bytes 393224 | tf_op jit(solution)/shard_map/ppermute | solution.py:37
  100.5 13.6 %collective-permute-start.25 = (bf16[256,768]{1,0:T(8,128)(2,1)}, bf16[256,768]{1,0:T(8,128)(2,1)S(1)}, u32[]{:S(2)}, u32[]{:S(2)}) collective-permute-start(bf16[256,768]{1,0:T(8,128)(2,1)} %shard_map.93.refs_17_), channel_id=1, source_target_pairs={{0,16},{1,17},{2,18},{3,19},{4,20},{5,21},{6,22},{7,23},{8,24},{9,... | collective-permute-start | bytes 1179656 | tf_op jit(solution)/shard_map/ppermute | solution.py:757
  106.7 11.9 %collective-permute-start.24 = (bf16[256,512]{1,0:T(8,128)(2,1)}, bf16[256,512]{1,0:T(8,128)(2,1)S(1)}, u32[]{:S(2)}, u32[]{:S(2)}) collective-permute-start(bf16[256,512]{1,0:T(8,128)(2,1)} %shard_map.92.refs_16_), channel_id=1, source_target_pairs={{0,16},{1,17},{2,18},{3,19},{4,20},{5,21},{6,22},{7,23},{8,24},{9,... | collective-permute-start | bytes 786440 | tf_op jit(solution)/shard_map/ppermute | solution.py:757
  112.8 11.4 %collective-permute-start.26 = (bf16[256,512]{1,0:T(8,128)(2,1)}, bf16[256,512]{1,0:T(8,128)(2,1)S(1)}, u32[]{:S(2)}, u32[]{:S(2)}) collective-permute-start(bf16[256,512]{1,0:T(8,128)(2,1)} %shard_map.94.refs_18_), channel_id=1, source_target_pairs={{0,16},{1,17},{2,18},{3,19},{4,20},{5,21},{6,22},{7,23},{8,24},{9,... | collective-permute-start | bytes 786440 | tf_op jit(solution)/shard_map/ppermute | solution.py:757
  114.1 12.4 %collective-permute-start.28 = (bf16[256,768]{1,0:T(8,128)(2,1)S(1)}, bf16[256,768]{1,0:T(8,128)(2,1)S(1)}, u32[]{:S(2)}, u32[]{:S(2)}) collective-permute-start(bf16[256,768]{1,0:T(8,128)(2,1)S(1)} %collective-permute-done.25.refs_1_.refs_14_), channel_id=1, source_target_pairs={{0,1},{1,0},{2,3},{3,2},{4,5},{5,4},{6,7},{7,6},{8,9},{9,8},{10,11... | collective-permute-start | bytes 1179656 | tf_op jit(solution)/shard_map/ppermute | solution.py:37
  118.6 6.8 %collective-permute-start.27 = (bf16[256,512]{1,0:T(8,128)(2,1)S(1)}, bf16[256,512]{1,0:T(8,128)(2,1)S(1)}, u32[]{:S(2)}, u32[]{:S(2)}) collective-permute-start(bf16[256,512]{1,0:T(8,128)(2,1)S(1)} %collective-permute-done.24.refs_0_.refs_13_), channel_id=1, source_target_pairs={{0,1},{1,0},{2,3},{3,2},{4,5},{5,4},{6,7},{7,6},{8,9},{9,8},{10,11... | collective-permute-start | bytes 786440 | tf_op jit(solution)/shard_map/ppermute | solution.py:37
  133.7 24.0 %all-to-all-start.2 = ((bf16[8,256,128]{2,1,0:T(8,128)(2,1)}), bf16[8,256,128]{2,1,0:T(8,128)(2,1)S(1)}, u32[]{:S(2)}, u32[]{:S(2)}) async-start(bf16[8,256,128]{2,1,0:T(8,128)(2,1)} %bitcast.25), calls=%async_computation.2 | async-start | bytes 1048576 | tf_op jit(solution)/shard_map/all_to_all | solution.py:761
  171.2 7.3 %collective-permute-start.38 = (bf16[2,256,128]{2,1,0:T(8,128)(2,1)S(1)}, bf16[2,256,128]{2,1,0:T(8,128)(2,1)S(1)}, u32[]{:S(2)}, u32[]{:S(2)}) collective-permute-start(bf16[2,256,128]{2,1,0:T(8,128)(2,1)S(1)} %get-tuple-element.71.refs_0_), channel_id=1, source_target_pairs={{0,1},{1,0},{2,3},{3,2},{4,5},{5,4},{6,7},{7,6},{8,9},{9,8},{10,11... | collective-permute-start | bytes 393224 | tf_op jit(solution)/shard_map/ppermute | solution.py:37
  (73 other events, 329.8 us)

commit v7 on v6

--- a/solution.py
+++ b/solution.py
@@ -105,7 +105,7 @@
             jax.ShapeDtypeStruct((rows, cols), F32),
             jax.ShapeDtypeStruct((rows, cols), BF16),
         ],
-        compiler_params=params(32),
+        compiler_params=params(60),
     )(values, proj_weight)
 
 
@@ -201,7 +201,7 @@
             jax.ShapeDtypeStruct((groups, cols // HDIM, rows, HDIM), BF16),
         ],
         scratch_shapes=[pltpu.VMEM(kv_weight.shape, BF16), pltpu.SemaphoreType.DMA],
-        compiler_params=params(60),
+        compiler_params=params(24),
     )(tp_index, *own, *oth, gain, kv_weight, cosine, sine)
 
 
@@ -305,7 +305,7 @@
         ),
         out_shape=[jax.ShapeDtypeStruct((steps, 2, rows, HDIM), BF16)] * 2,
         cost_estimate=LITTLE,
-        compiler_params=params(60),
+        compiler_params=params(24),
     )(tp_index, *after, normed, q_weight, cosine, sine)
 
 
@@ -371,7 +371,7 @@
         out_shape=jax.ShapeDtypeStruct(packed.shape, BF16),
         scratch_shapes=[pltpu.SemaphoreType.DMA((2 * KV_HEADS * packed.shape[0],))],
         input_output_aliases={2: 0},
-        compiler_params=params(16),
+        compiler_params=params(60),
     )(at, after, packed, f_kept, f_given)
 
 

time: 189 us -> 184 us (0.974)
  local copies, waits for them, and re-layouts: 13.4 us -> 10.2 us
  Pallas kernels: 75.3 us -> 73.4 us
    unnamed x104 -> x110, local copies, waits for them, and re-layouts: 11.1 us -> 7.94 us
    pallas_call x1, Pallas kernels: 5.85 us -> 3.02 us  [queries_of(): pl.pallas_call(q_kernel, grid_spec=pltpu.PrefetchScalarGridSpec(num_scala...]
    pallas_call x1, Pallas kernels: 0.95 us -> 2.99 us  [project(): pl.pallas_call(project_kernel, grid=(cols // block,), in_specs=[pl.BlockS...]
    pallas_call x1, Pallas kernels: 5.63 us -> 3.67 us  [keyvals(): pl.pallas_call(functools.partial(kv_kernel, len(own)), in_specs=[SMEM, *[...]
  transfers between devices with their start and end apart: 45 -> 45, of which waited for: 20 -> 19; matrix products, arithmetic and copies ran while one was open for 2% -> 2% of each run, Pallas kernels for 25% -> 25%
where the time goes in v7:
time: 184 us; the launch traced here: 183 us
  Pallas kernels  73.4 us (40%)
  starting transfers between devices  63.4 us (34%)
  waiting for transfers between devices  33.1 us (18%)
  local copies, waits for them, and re-layouts  10.2 us (6%)
    pallas_call x4, Pallas kernels, project_out(): pl.pallas_call(functools.partial(out_kernel, placing, begin, block), grid...  23.5 us
    ppermute x23, starting transfers between devices, swap(): return lax.ppermute(value, 'tp', [(0, 1), (1, 0)])  22.3 us
    pallas_call x2, Pallas kernels, attend(): pl.pallas_call(functools.partial(attend_kernel, frames, len(after)), grid...  16.7 us
    ppermute x6, waiting for transfers between devices, spread_heads(): lax.ppermute(pieces[d], 'mem', [(i, i ^ d) for i in range(KV_HEADS)])  11.5 us
    pallas_call x1, Pallas kernels, qkv(): pl.pallas_call(qkv_kernel, in_specs=[SMEM, *[VMEM] * 5, ANY, ANY, *[VMEM]...  9.63 us
    ppermute x23, waiting for transfers between devices, swap(): return lax.ppermute(value, 'tp', [(0, 1), (1, 0)])  9.24 us
    unnamed x110, local copies, waits for them, and re-layouts  7.94 us
    ppermute x6, starting transfers between devices, spread_heads(): lax.ppermute(pieces[d], 'mem', [(i, i ^ d) for i in range(KV_HEADS)])  7.33 us
  transfers between devices with their start and end apart: 45, of which 19 were waited for; matrix products, arithmetic and copies ran while one was open for 2% of the time, Pallas kernels for 25%

profile of v7, /device:TPU:19, one launch (start us, length us, event | category | flops | bytes accessed | tf_op | source)
XLA Modules:
  0.0 182.6 jit_solution(2936519119481530530)
XLA Ops:
  0.7 3.0 %shard_map.82 = (f32[96,1792]{1,0:T(8,128)}, bf16[96,1792]{1,0:T(8,128)(2,1)}) custom-call(bf16[96,576]{1,0:T(8,128)(2,1)} %x_ref.3, bf16[576,1792]{1,0:T(8,128)(2,1)} %w_ref.3), custom_call_target="tpu_custom_call" | custom-call | tf_op jit(solution)/shard_map/pallas_call | solution.py:96
  3.7 2.1 %collective-permute-start.1 = (bf16[96,1792]{1,0:T(8,128)(2,1)}, bf16[96,1792]{1,0:T(8,128)(2,1)S(1)}, u32[]{:S(2)}, u32[]{:S(2)}) collective-permute-start(bf16[96,1792]{1,0:T(8,128)(2,1)} %get-tuple-element.40.after), channel_id=1, source_target_pairs={{16,0},{17,1},{18,2},{19,3},{20,4},{21,5},{22,6},{23,7},{24,8},{25... | collective-permute-start | bytes 1032200 | tf_op jit(solution)/shard_map/ppermute | solution.py:681
  7.7 5.6 %all-to-all-start = ((bf16[8,48,576]{2,1,0:T(8,128)(2,1)}), bf16[8,48,576]{2,1,0:T(8,128)(2,1)S(1)}, u32[]{:S(2)}, u32[]{:S(2)}) async-start(bf16[8,48,576]{2,1,0:T(8,128)(2,1)} %shard_map.83), calls=%async_computation | async-start | bytes 983040 | tf_op jit(solution)/shard_map/all_to_all | solution.py:718
  19.0 9.6 %shard_map.85 = (bf16[2,4,544,128]{3,2,1,0:T(8,128)(2,1)}, bf16[2,2,256,128]{3,2,1,0:T(8,128)(2,1)}, bf16[2,2,256,128]{3,2,1,0:T(8,128)(2,1)}, bf16[2,2,96,128]{3,2,1,0:T(8,128)(2,1)}, bf16[2,2,96,128]{3,2,1,0:T(8,128)(2,1)}) custom-call(s32[1]{0:T(128)} %bitcast.1.tp_ref, bf16[256,1792]{1,0:T(8,128)(2,1)} %refs_13_.5, bf16[256,1792]{1,0:T(8,128)(2,1)} %copy-done.41, ...), custom_call_target="tpu_custom_call" | custom-call | tf_op jit(solution)/shard_map/pallas_call | solution.py:252
  32.8 5.6 %all-to-all-start.1 = ((bf16[8,544,128]{2,1,0:T(8,128)(2,1)}), bf16[8,544,128]{2,1,0:T(8,128)(2,1)S(1)}, u32[]{:S(2)}, u32[]{:S(2)}) async-start(bf16[8,544,128]{2,1,0:T(8,128)(2,1)} %bitcast.15), calls=%async_computation.1 | async-start | bytes 2228224 | tf_op jit(solution)/shard_map/all_to_all | solution.py:736
  41.0 4.9 %shard_map.88 = (f32[256,1792]{1,0:T(8,128)}, bf16[256,512]{1,0:T(8,128)(2,1)}, bf16[256,768]{1,0:T(8,128)(2,1)}, bf16[256,512]{1,0:T(8,128)(2,1)}) custom-call(bf16[2,4,544,128]{3,2,1,0:T(8,128)(2,1)} %shard_map.86.refs_0_.after, s32[256,1]{1,0:T(8,128)} %copy.20.idx_own.refs_16_, s32[256,1]{1,0:T(8,128)} %copy.21.idx_oth.refs_17_, ...), custom_call_target="tpu_custom_call" | custom-call | flops 1 | bytes 1 | tf_op jit(solution)/shard_map/pallas_call | solution.py:73
  53.9 2.3 %collective-permute-done.5.refs_5_.refs_1_ = bf16[2,256,128]{2,1,0:T(8,128)(2,1)S(1)} collective-permute-done((bf16[2,256,128]{2,1,0:T(8,128)(2,1)S(1)}, bf16[2,256,128]{2,1,0:T(8,128)(2,1)S(1)}, u32[]{:S(2)}, u32[]{:S(2)}) %collective-permute-start.5) | collective-permute-done | bytes 131104 | tf_op jit(solution)/shard_map/ppermute | solution.py:692
  58.3 4.7 %shard_map.89 = (bf16[256,1792]{1,0:T(8,128)(2,1)}, bf16[256,1792]{1,0:T(8,128)(2,1)}, bf16[256,1792]{1,0:T(8,128)(2,1)}, bf16[256,1792]{1,0:T(8,128)(2,1)}) custom-call(s32[1]{0:T(128)} %bitcast.1.tp_ref, bf16[256,512]{1,0:T(8,128)(2,1)} %get-tuple-element.51.after, bf16[1024,3584]{1,0:T(8,128)(2,1)} %bitcast.18), custom_call_target="tpu_custom_call" | custom-call | flops 1 | bytes 1 | tf_op jit(solution)/shard_map/pallas_call | solution.py:405
  63.0 3.0 %collective-permute-done.7.refs_7_.refs_3_ = bf16[2,256,128]{2,1,0:T(8,128)(2,1)S(1)} collective-permute-done((bf16[2,256,128]{2,1,0:T(8,128)(2,1)S(1)}, bf16[2,256,128]{2,1,0:T(8,128)(2,1)S(1)}, u32[]{:S(2)}, u32[]{:S(2)}) %collective-permute-start.7) | collective-permute-done | bytes 131104 | tf_op jit(solution)/shard_map/ppermute | solution.py:692
  72.2 8.6 %shard_map.91 = (bf16[2,256,128]{2,1,0:T(8,128)(2,1)S(1)}, bf16[2,256,128]{2,1,0:T(8,128)(2,1)S(1)}, bf16[2,256,128]{2,1,0:T(8,128)(2,1)S(1)}, bf16[2,256,128]{2,1,0:T(8,128)(2,1)S(1)}) custom-call(s32[12]{0:T(128)S(1)} %copy-done.25, bf16[2,256,128]{2,1,0:T(8,128)(2,1)S(1)} %get-tuple-element.47.refs_0_, ...), custom_call_target="tpu_custom_call" | custom-call | tf_op jit(solution)/shard_map/pallas_call | solution.py:540
  86.9 2.3 %collective-permute-start.18 = (bf16[2,256,128]{2,1,0:T(8,128)(2,1)S(1)}, bf16[2,256,128]{2,1,0:T(8,128)(2,1)S(1)}, u32[]{:S(2)}, u32[]{:S(2)}) collective-permute-start(bf16[2,256,128]{2,1,0:T(8,128)(2,1)S(1)} %collective-permute-done.14.refs_2_), channel_id=1, source_target_pairs={{0,1},{1,0},{2,3},{3,2},{4,5},{5,4},{6,7},{7,6},{8,9},{9,8},{10,11... | collective-permute-start | bytes 393224 | tf_op jit(solution)/shard_map/ppermute | solution.py:37
  92.5 6.1 %shard_map.93.refs_17_ = bf16[256,768]{1,0:T(8,128)(2,1)} custom-call(s32[12]{0:T(128)} %copy-done.24, bf16[2,256,128]{2,1,0:T(8,128)(2,1)} %copy-done.14, bf16[2,256,128]{2,1,0:T(8,128)(2,1)} %copy-done.34, bf16[2,256,128]{2,1,0:T(8,128)(2,1)} %copy-done.35, bf16[2,256,128]{2,1,0:T(8,128)(2,1)} %copy-done.36, bf16[2,256,128]{2,1,0:T(8,128)(2,1)} %copy-done.37, ...), custom_call_target="tpu_custom_call" | custom-call | tf_op jit(solution)/shard_map/pallas_call | solution.py:633
  100.0 4.8 %shard_map.92.refs_16_ = bf16[256,512]{1,0:T(8,128)(2,1)} custom-call(s32[12]{0:T(128)} %copy-done.24, bf16[2,256,128]{2,1,0:T(8,128)(2,1)} %copy-done.14, bf16[2,256,128]{2,1,0:T(8,128)(2,1)} %copy-done.34, bf16[2,256,128]{2,1,0:T(8,128)(2,1)} %copy-done.35, bf16[2,256,128]{2,1,0:T(8,128)(2,1)} %copy-done.36, bf16[2,256,128]{2,1,0:T(8,128)(2,1)} %copy-done.37, ...), custom_call_target="tpu_custom_call" | custom-call | tf_op jit(solution)/shard_map/pallas_call | solution.py:633
  106.3 5.0 %shard_map.94.refs_18_ = bf16[256,512]{1,0:T(8,128)(2,1)} custom-call(s32[12]{0:T(128)} %copy-done.24, bf16[2,256,128]{2,1,0:T(8,128)(2,1)} %copy-done.14, bf16[2,256,128]{2,1,0:T(8,128)(2,1)} %copy-done.34, bf16[2,256,128]{2,1,0:T(8,128)(2,1)} %copy-done.35, bf16[2,256,128]{2,1,0:T(8,128)(2,1)} %copy-done.36, bf16[2,256,128]{2,1,0:T(8,128)(2,1)} %copy-done.37, ...), custom_call_target="tpu_custom_call" | custom-call | tf_op jit(solution)/shard_map/pallas_call | solution.py:633
  113.2 3.6 %collective-permute-done.24.refs_0_.refs_13_ = bf16[256,512]{1,0:T(8,128)(2,1)S(1)} collective-permute-done((bf16[256,512]{1,0:T(8,128)(2,1)}, bf16[256,512]{1,0:T(8,128)(2,1)S(1)}, u32[]{:S(2)}, u32[]{:S(2)}) %collective-permute-start.24) | collective-permute-done | bytes 262176 | tf_op jit(solution)/shard_map/ppermute | solution.py:757
  118.7 3.7 %collective-permute-done.26.refs_2_.refs_15_ = bf16[256,512]{1,0:T(8,128)(2,1)S(1)} collective-permute-done((bf16[256,512]{1,0:T(8,128)(2,1)}, bf16[256,512]{1,0:T(8,128)(2,1)S(1)}, u32[]{:S(2)}, u32[]{:S(2)}) %collective-permute-start.26) | collective-permute-done | bytes 262176 | tf_op jit(solution)/shard_map/ppermute | solution.py:757
  124.7 3.7 %shard_map.95 = (bf16[256,3584]{1,0:T(8,128)(2,1)S(1)}, bf16[2,4,256,128]{3,2,1,0:T(8,128)(2,1)}) custom-call(s32[1]{0:T(128)} %bitcast.1.tp_ref, bf16[256,512]{1,0:T(8,128)(2,1)S(1)} %collective-permute-done.24.refs_0_.refs_13_, bf16[256,768]{1,0:T(8,128)(2,1)S(1)} %collective-permute-done.25.refs_1_.refs_14_, ...), custom_call_target="tpu_custom_call" | custom-call | tf_op jit(solution)/shard_map/pallas_call | solution.py:195
  128.4 5.4 %all-to-all-start.2 = ((bf16[8,256,128]{2,1,0:T(8,128)(2,1)}), bf16[8,256,128]{2,1,0:T(8,128)(2,1)S(1)}, u32[]{:S(2)}, u32[]{:S(2)}) async-start(bf16[8,256,128]{2,1,0:T(8,128)(2,1)} %bitcast.12), calls=%async_computation.2 | async-start | bytes 1048576 | tf_op jit(solution)/shard_map/all_to_all | solution.py:761
  133.9 3.1 %copy-done = bf16[1,3584,1024]{2,1,0:T(8,128)(2,1)S(1)} copy-done((bf16[1,3584,1024]{2,1,0:T(8,128)(2,1)S(1)}, bf16[1,3584,1024]{2,1,0:T(8,128)(2,1)}, u32[]{:S(2)}) %copy-start) | copy-done | bytes 7340056
  137.0 3.0 %shard_map.96 = (bf16[2,2,256,128]{3,2,1,0:T(8,128)(2,1)S(1)}, bf16[2,2,256,128]{3,2,1,0:T(8,128)(2,1)S(1)}) custom-call(s32[1]{0:T(128)} %bitcast.1.tp_ref, bf16[256,3584]{1,0:T(8,128)(2,1)S(1)} %get-tuple-element.63.refs_0_, bf16[3584,1024]{1,0:T(8,128)(2,1)S(1)} %bitcast.14, f32[352,128]{1,0:T(8,128)S(1)} %copy-done.8, f32[352,128]{1,0:T(8,128)S(1)} %copy-done.10), custom_call_target="tpu_custom_call" | custom-call | flops 1 | bytes 1 | tf_op jit(solution)/shard_map/pallas_call | solution.py:292
  145.5 3.8 %collective-permute-done.31.refs_1_ = bf16[2,256,128]{2,1,0:T(8,128)(2,1)S(1)} collective-permute-done((bf16[2,256,128]{2,1,0:T(8,128)(2,1)S(1)}, bf16[2,256,128]{2,1,0:T(8,128)(2,1)S(1)}, u32[]{:S(2)}, u32[]{:S(2)}) %collective-permute-start.31) | collective-permute-done | bytes 131104 | tf_op jit(solution)/shard_map/ppermute | solution.py:692
  149.3 2.4 %collective-permute-done.33.refs_3_ = bf16[2,256,128]{2,1,0:T(8,128)(2,1)S(1)} collective-permute-done((bf16[2,256,128]{2,1,0:T(8,128)(2,1)S(1)}, bf16[2,256,128]{2,1,0:T(8,128)(2,1)S(1)}, u32[]{:S(2)}, u32[]{:S(2)}) %collective-permute-start.33) | collective-permute-done | bytes 131104 | tf_op jit(solution)/shard_map/ppermute | solution.py:692
  154.3 8.1 %shard_map.99 = (bf16[2,256,128]{2,1,0:T(8,128)(2,1)S(1)}, bf16[2,256,128]{2,1,0:T(8,128)(2,1)S(1)}, bf16[2,256,128]{2,1,0:T(8,128)(2,1)S(1)}, bf16[2,256,128]{2,1,0:T(8,128)(2,1)S(1)}) custom-call(s32[12]{0:T(128)S(1)} %copy-done.26, bf16[2,256,128]{2,1,0:T(8,128)(2,1)S(1)} %get-tuple-element.66.refs_0_, ...), custom_call_target="tpu_custom_call" | custom-call | tf_op jit(solution)/shard_map/pallas_call | solution.py:540
  174.8 7.6 %shard_map.100 = bf16[1,256,1792]{2,1,0:T(8,128)(2,1)} custom-call(s32[12]{0:T(128)} %copy-done.24, bf16[2,256,128]{2,1,0:T(8,128)(2,1)} %copy-done.23, bf16[2,256,128]{2,1,0:T(8,128)(2,1)} %copy-done.43, bf16[2,256,128]{2,1,0:T(8,128)(2,1)} %copy-done.44, bf16[2,256,128]{2,1,0:T(8,128)(2,1)} %copy-done.45, bf16[2,256,128]{2,1,0:T(8,128)(2,1)} %copy-done.46, ...), custom_call_target="tpu_custom_call" | custom-call | tf_op jit(solution)/shard_map/pallas_call | solution.py:633
  (207 shorter events, 69.5 us)
Async XLA Ops:
  0.0 18.0 %collective-permute-start = (bf16[256,1792]{1,0:T(8,128)(2,1)}, bf16[256,1792]{1,0:T(8,128)(2,1)S(1)}, u32[]{:S(2)}, u32[]{:S(2)}) collective-permute-start(bf16[256,1792]{1,0:T(8,128)(2,1)} %refs_13_.5), channel_id=1, source_target_pairs={{0,1},{1,0},{2,3},{3,2},{4,5},{5,4},{6,7},{7,6},{8,9},{9,8},{10,11... | collective-permute-start | bytes 2752520 | tf_op jit(solution)/shard_map/ppermute | solution.py:37
  3.7 11.8 %collective-permute-start.1 = (bf16[96,1792]{1,0:T(8,128)(2,1)}, bf16[96,1792]{1,0:T(8,128)(2,1)S(1)}, u32[]{:S(2)}, u32[]{:S(2)}) collective-permute-start(bf16[96,1792]{1,0:T(8,128)(2,1)} %get-tuple-element.40.after), channel_id=1, source_target_pairs={{16,0},{17,1},{18,2},{19,3},{20,4},{21,5},{22,6},{23,7},{24,8},{25... | collective-permute-start | bytes 1032200 | tf_op jit(solution)/shard_map/ppermute | solution.py:681
  7.7 21.4 %all-to-all-start = ((bf16[8,48,576]{2,1,0:T(8,128)(2,1)}), bf16[8,48,576]{2,1,0:T(8,128)(2,1)S(1)}, u32[]{:S(2)}, u32[]{:S(2)}) async-start(bf16[8,48,576]{2,1,0:T(8,128)(2,1)} %shard_map.83), calls=%async_computation | async-start | bytes 983040 | tf_op jit(solution)/shard_map/all_to_all | solution.py:718
  32.8 34.9 %all-to-all-start.1 = ((bf16[8,544,128]{2,1,0:T(8,128)(2,1)}), bf16[8,544,128]{2,1,0:T(8,128)(2,1)S(1)}, u32[]{:S(2)}, u32[]{:S(2)}) async-start(bf16[8,544,128]{2,1,0:T(8,128)(2,1)} %bitcast.15), calls=%async_computation.1 | async-start | bytes 2228224 | tf_op jit(solution)/shard_map/all_to_all | solution.py:736
  39.3 8.9 %collective-permute-start.4 = (bf16[2,2,256,128]{3,2,1,0:T(8,128)(2,1)}, bf16[2,2,256,128]{3,2,1,0:T(8,128)(2,1)S(1)}, u32[]{:S(2)}, u32[]{:S(2)}) collective-permute-start(bf16[2,2,256,128]{3,2,1,0:T(8,128)(2,1)} %get-tuple-element.46), channel_id=1, source_target_pairs={{0,1},{1,0},{2,3},{3,2},{4,5},{5,4},{6,7},{7,6},{8,9},{9,8},{10,11... | collective-permute-start | bytes 786440 | tf_op jit(solution)/shard_map/ppermute | solution.py:37
  46.0 21.7 %collective-permute-start.10 = (bf16[256,768]{1,0:T(8,128)(2,1)}, bf16[256,768]{1,0:T(8,128)(2,1)S(1)}, u32[]{:S(2)}, u32[]{:S(2)}) collective-permute-start(bf16[256,768]{1,0:T(8,128)(2,1)} %get-tuple-element.53), channel_id=1, source_target_pairs={{16,0},{17,1},{18,2},{19,3},{20,4},{21,5},{22,6},{23,7},{24,8},{25... | collective-permute-start | bytes 1179656 | tf_op jit(solution)/shard_map/ppermute | solution.py:681
  48.8 7.4 %collective-permute-start.5 = (bf16[2,256,128]{2,1,0:T(8,128)(2,1)S(1)}, bf16[2,256,128]{2,1,0:T(8,128)(2,1)S(1)}, u32[]{:S(2)}, u32[]{:S(2)}) collective-permute-start(bf16[2,256,128]{2,1,0:T(8,128)(2,1)S(1)} %get-tuple-element.48), channel_id=1, source_target_pairs={{0,2},{2,0},{4,6},{6,4},{1,3},{3,1},{5,7},{7,5},{8,10},{10,8},{12,... | collective-permute-start | bytes 393224 | tf_op jit(solution)/shard_map/ppermute | solution.py:692
  50.0 16.0 %collective-permute-start.11 = (bf16[256,512]{1,0:T(8,128)(2,1)}, bf16[256,512]{1,0:T(8,128)(2,1)S(1)}, u32[]{:S(2)}, u32[]{:S(2)}) collective-permute-start(bf16[256,512]{1,0:T(8,128)(2,1)} %get-tuple-element.54), channel_id=1, source_target_pairs={{16,0},{17,1},{18,2},{19,3},{20,4},{21,5},{22,6},{23,7},{24,8},{25... | collective-permute-start | bytes 786440 | tf_op jit(solution)/shard_map/ppermute | solution.py:681
  51.3 16.3 %collective-permute-start.9 = (bf16[256,512]{1,0:T(8,128)(2,1)}, bf16[256,512]{1,0:T(8,128)(2,1)S(1)}, u32[]{:S(2)}, u32[]{:S(2)}) collective-permute-start(bf16[256,512]{1,0:T(8,128)(2,1)} %get-tuple-element.51.after), channel_id=1, source_target_pairs={{16,0},{17,1},{18,2},{19,3},{20,4},{21,5},{22,6},{23,7},{24,8},{25... | collective-permute-start | bytes 786440 | tf_op jit(solution)/shard_map/ppermute | solution.py:681
  52.6 10.4 %collective-permute-start.6 = (bf16[2,256,128]{2,1,0:T(8,128)(2,1)S(1)}, bf16[2,256,128]{2,1,0:T(8,128)(2,1)S(1)}, u32[]{:S(2)}, u32[]{:S(2)}) collective-permute-start(bf16[2,256,128]{2,1,0:T(8,128)(2,1)S(1)} %get-tuple-element.49), channel_id=1, source_target_pairs={{0,4},{2,6},{4,0},{6,2},{1,5},{3,7},{5,1},{7,3},{8,12},{10,14},{12... | collective-permute-start | bytes 393224 | tf_op jit(solution)/shard_map/ppermute | solution.py:692
  56.2 9.8 %collective-permute-start.7 = (bf16[2,256,128]{2,1,0:T(8,128)(2,1)S(1)}, bf16[2,256,128]{2,1,0:T(8,128)(2,1)S(1)}, u32[]{:S(2)}, u32[]{:S(2)}) collective-permute-start(bf16[2,256,128]{2,1,0:T(8,128)(2,1)S(1)} %get-tuple-element.50), channel_id=1, source_target_pairs={{0,6},{2,4},{4,2},{6,0},{1,7},{3,5},{5,3},{7,1},{8,14},{10,12},{12... | collective-permute-start | bytes 393224 | tf_op jit(solution)/shard_map/ppermute | solution.py:692
  69.8 12.3 %collective-permute-start.21 = (bf16[256,1792]{1,0:T(8,128)(2,1)S(1)}, bf16[256,1792]{1,0:T(8,128)(2,1)S(1)}, u32[]{:S(2)}, u32[]{:S(2)}) collective-permute-start(bf16[256,1792]{1,0:T(8,128)(2,1)S(1)} %copy-done.54), channel_id=1, source_target_pairs={{0,1},{1,0},{2,3},{3,2},{4,5},{5,4},{6,7},{7,6},{8,9},{9,8},{10,11... | collective-permute-start | bytes 2752520 | tf_op jit(solution)/shard_map/ppermute | solution.py:37
  70.4 12.9 %collective-permute-start.22 = (bf16[256,1792]{1,0:T(8,128)(2,1)S(1)}, bf16[256,1792]{1,0:T(8,128)(2,1)S(1)}, u32[]{:S(2)}, u32[]{:S(2)}) collective-permute-start(bf16[256,1792]{1,0:T(8,128)(2,1)S(1)} %copy-done.53), channel_id=1, source_target_pairs={{0,1},{1,0},{2,3},{3,2},{4,5},{5,4},{6,7},{7,6},{8,9},{9,8},{10,11... | collective-permute-start | bytes 2752520 | tf_op jit(solution)/shard_map/ppermute | solution.py:37
  70.7 13.0 %collective-permute-start.23 = (bf16[256,1792]{1,0:T(8,128)(2,1)S(1)}, bf16[256,1792]{1,0:T(8,128)(2,1)S(1)}, u32[]{:S(2)}, u32[]{:S(2)}) collective-permute-start(bf16[256,1792]{1,0:T(8,128)(2,1)S(1)} %copy-done.52), channel_id=1, source_target_pairs={{0,1},{1,0},{2,3},{3,2},{4,5},{5,4},{6,7},{7,6},{8,9},{9,8},{10,11... | collective-permute-start | bytes 2752520 | tf_op jit(solution)/shard_map/ppermute | solution.py:37
  70.9 19.9 %collective-permute-start.20 = (bf16[256,1792]{1,0:T(8,128)(2,1)}, bf16[256,1792]{1,0:T(8,128)(2,1)S(1)}, u32[]{:S(2)}, u32[]{:S(2)}) collective-permute-start(bf16[256,1792]{1,0:T(8,128)(2,1)} %get-tuple-element.52.refs_1_), channel_id=1, source_target_pairs={{0,1},{1,0},{2,3},{3,2},{4,5},{5,4},{6,7},{7,6},{8,9},{9,8},{10,11... | collective-permute-start | bytes 2752520 | tf_op jit(solution)/shard_map/ppermute | solution.py:37
  83.6 7.3 %collective-permute-start.16 = (bf16[2,256,128]{2,1,0:T(8,128)(2,1)S(1)}, bf16[2,256,128]{2,1,0:T(8,128)(2,1)S(1)}, u32[]{:S(2)}, u32[]{:S(2)}) collective-permute-start(bf16[2,256,128]{2,1,0:T(8,128)(2,1)S(1)} %get-tuple-element.55.refs_0_), channel_id=1, source_target_pairs={{0,1},{1,0},{2,3},{3,2},{4,5},{5,4},{6,7},{7,6},{8,9},{9,8},{10,11... | collective-permute-start | bytes 393224 | tf_op jit(solution)/shard_map/ppermute | solution.py:37
  98.7 14.1 %collective-permute-start.25 = (bf16[256,768]{1,0:T(8,128)(2,1)}, bf16[256,768]{1,0:T(8,128)(2,1)S(1)}, u32[]{:S(2)}, u32[]{:S(2)}) collective-permute-start(bf16[256,768]{1,0:T(8,128)(2,1)} %shard_map.93.refs_17_), channel_id=1, source_target_pairs={{0,16},{1,17},{2,18},{3,19},{4,20},{5,21},{6,22},{7,23},{8,24},{9,... | collective-permute-start | bytes 1179656 | tf_op jit(solution)/shard_map/ppermute | solution.py:757
  104.8 11.9 %collective-permute-start.24 = (bf16[256,512]{1,0:T(8,128)(2,1)}, bf16[256,512]{1,0:T(8,128)(2,1)S(1)}, u32[]{:S(2)}, u32[]{:S(2)}) collective-permute-start(bf16[256,512]{1,0:T(8,128)(2,1)} %shard_map.92.refs_16_), channel_id=1, source_target_pairs={{0,16},{1,17},{2,18},{3,19},{4,20},{5,21},{6,22},{7,23},{8,24},{9,... | collective-permute-start | bytes 786440 | tf_op jit(solution)/shard_map/ppermute | solution.py:757
  111.3 11.1 %collective-permute-start.26 = (bf16[256,512]{1,0:T(8,128)(2,1)}, bf16[256,512]{1,0:T(8,128)(2,1)S(1)}, u32[]{:S(2)}, u32[]{:S(2)}) collective-permute-start(bf16[256,512]{1,0:T(8,128)(2,1)} %shard_map.94.refs_18_), channel_id=1, source_target_pairs={{0,16},{1,17},{2,18},{3,19},{4,20},{5,21},{6,22},{7,23},{8,24},{9,... | collective-permute-start | bytes 786440 | tf_op jit(solution)/shard_map/ppermute | solution.py:757
  112.7 12.0 %collective-permute-start.28 = (bf16[256,768]{1,0:T(8,128)(2,1)S(1)}, bf16[256,768]{1,0:T(8,128)(2,1)S(1)}, u32[]{:S(2)}, u32[]{:S(2)}) collective-permute-start(bf16[256,768]{1,0:T(8,128)(2,1)S(1)} %collective-permute-done.25.refs_1_.refs_14_), channel_id=1, source_target_pairs={{0,1},{1,0},{2,3},{3,2},{4,5},{5,4},{6,7},{7,6},{8,9},{9,8},{10,11... | collective-permute-start | bytes 1179656 | tf_op jit(solution)/shard_map/ppermute | solution.py:37
  116.8 6.8 %collective-permute-start.27 = (bf16[256,512]{1,0:T(8,128)(2,1)S(1)}, bf16[256,512]{1,0:T(8,128)(2,1)S(1)}, u32[]{:S(2)}, u32[]{:S(2)}) collective-permute-start(bf16[256,512]{1,0:T(8,128)(2,1)S(1)} %collective-permute-done.24.refs_0_.refs_13_), channel_id=1, source_target_pairs={{0,1},{1,0},{2,3},{3,2},{4,5},{5,4},{6,7},{7,6},{8,9},{9,8},{10,11... | collective-permute-start | bytes 786440 | tf_op jit(solution)/shard_map/ppermute | solution.py:37
  128.4 23.2 %all-to-all-start.2 = ((bf16[8,256,128]{2,1,0:T(8,128)(2,1)}), bf16[8,256,128]{2,1,0:T(8,128)(2,1)S(1)}, u32[]{:S(2)}, u32[]{:S(2)}) async-start(bf16[8,256,128]{2,1,0:T(8,128)(2,1)} %bitcast.12), calls=%async_computation.2 | async-start | bytes 1048576 | tf_op jit(solution)/shard_map/all_to_all | solution.py:761
  164.9 7.0 %collective-permute-start.37 = (bf16[2,256,128]{2,1,0:T(8,128)(2,1)S(1)}, bf16[2,256,128]{2,1,0:T(8,128)(2,1)S(1)}, u32[]{:S(2)}, u32[]{:S(2)}) collective-permute-start(bf16[2,256,128]{2,1,0:T(8,128)(2,1)S(1)} %get-tuple-element.74), channel_id=1, source_target_pairs={{0,6},{2,4},{4,2},{6,0},{1,7},{3,5},{5,3},{7,1},{8,14},{10,12},{12... | collective-permute-start | bytes 393224 | tf_op jit(solution)/shard_map/ppermute | solution.py:700
  165.9 7.3 %collective-permute-start.38 = (bf16[2,256,128]{2,1,0:T(8,128)(2,1)S(1)}, bf16[2,256,128]{2,1,0:T(8,128)(2,1)S(1)}, u32[]{:S(2)}, u32[]{:S(2)}) collective-permute-start(bf16[2,256,128]{2,1,0:T(8,128)(2,1)S(1)} %get-tuple-element.71.refs_0_), channel_id=1, source_target_pairs={{0,1},{1,0},{2,3},{3,2},{4,5},{5,4},{6,7},{7,6},{8,9},{9,8},{10,11... | collective-permute-start | bytes 393224 | tf_op jit(solution)/shard_map/ppermute | solution.py:37
  (76 other events, 420.3 us)

commit v8 on v7

--- a/solution.py
+++ b/solution.py
@@ -80,7 +80,7 @@
             *[jax.ShapeDtypeStruct(shape, BF16) for shape in shapes[1:]],
         ],
         cost_estimate=LITTLE,
-        compiler_params=params(60),
+        compiler_params=params(32),
     )(after, *values)
 
 
@@ -744,7 +744,7 @@
     placed = [from_vision(half) for half in sent]
     pieces = spread_heads(kept, given, packed)
 
-    message = gate(message, w_given[0], *placed, *pieces[1:])
+    message = gate(message, w_given[0], *placed[:2], *pieces[1:])
     attended = attend(at, pieces, message, swap(message), frame_start.shape[0])
     a_own, a_oth = returned(attended)
     first = []

time: 184 us -> 181 us (0.984)
  starting transfers between devices: 63.4 us -> 60.3 us
  Pallas kernels: 73.4 us -> 70.9 us
  local copies, waits for them, and re-layouts: 10.2 us -> 12.5 us
    unnamed x110 -> x124, local copies, waits for them, and re-layouts: 7.94 us -> 11.5 us
    pallas_call x1, Pallas kernels: 4.9 us -> 2.01 us  [project_placed(): pl.pallas_call(place_kernel, grid=(1,), in_specs=[ANY, *[pl.BlockSpec(val...]
    ppermute x6, starting transfers between devices: 7.33 us -> 5.43 us  [spread_heads(): lax.ppermute(pieces[d], 'mem', [(i, i ^ d) for i in range(KV_HEADS)])]
  transfers between devices with their start and end apart: 45 -> 45, of which waited for: 19 -> 18; matrix products, arithmetic and copies ran while one was open for 2% -> 1% of each run, Pallas kernels for 25% -> 28%
where the time goes in v8:
time: 181 us; the launch traced here: 180 us
  Pallas kernels  70.9 us (39%)
  starting transfers between devices  60.3 us (33%)
  waiting for transfers between devices  33.8 us (19%)
  local copies, waits for them, and re-layouts  12.5 us (7%)
    pallas_call x4, Pallas kernels, project_out(): pl.pallas_call(functools.partial(out_kernel, placing, begin, block), grid...  23.5 us
    ppermute x23, starting transfers between devices, swap(): return lax.ppermute(value, 'tp', [(0, 1), (1, 0)])  21.2 us
    pallas_call x2, Pallas kernels, attend(): pl.pallas_call(functools.partial(attend_kernel, frames, len(after)), grid...  16.7 us
    ppermute x6, waiting for transfers between devices, spread_heads(): lax.ppermute(pieces[d], 'mem', [(i, i ^ d) for i in range(KV_HEADS)])  13.1 us
    unnamed x124, local copies, waits for them, and re-layouts  11.5 us
    pallas_call x1, Pallas kernels, qkv(): pl.pallas_call(qkv_kernel, in_specs=[SMEM, *[VMEM] * 5, ANY, ANY, *[VMEM]...  9.64 us
    ppermute x23, waiting for transfers between devices, swap(): return lax.ppermute(value, 'tp', [(0, 1), (1, 0)])  9.32 us
    ppermute x4, starting transfers between devices, from_vision(): return lax.ppermute(sent, 'segment', [(1, 0)])  7.66 us
  transfers between devices with their start and end apart: 45, of which 18 were waited for; matrix products, arithmetic and copies ran while one was open for 1% of the time, Pallas kernels for 28%

profile of v8, /device:TPU:19, one launch (start us, length us, event | category | flops | bytes accessed | tf_op | source)
XLA Modules:
  0.0 180.1 jit_solution(8365177627020326956)
XLA Ops:
  0.7 3.0 %shard_map.82 = (f32[96,1792]{1,0:T(8,128)}, bf16[96,1792]{1,0:T(8,128)(2,1)}) custom-call(bf16[96,576]{1,0:T(8,128)(2,1)} %x_ref.3, bf16[576,1792]{1,0:T(8,128)(2,1)} %w_ref.3), custom_call_target="tpu_custom_call" | custom-call | tf_op jit(solution)/shard_map/pallas_call | solution.py:96
  3.7 2.1 %collective-permute-start.1 = (bf16[96,1792]{1,0:T(8,128)(2,1)}, bf16[96,1792]{1,0:T(8,128)(2,1)S(1)}, u32[]{:S(2)}, u32[]{:S(2)}) collective-permute-start(bf16[96,1792]{1,0:T(8,128)(2,1)} %get-tuple-element.40.after), channel_id=1, source_target_pairs={{16,0},{17,1},{18,2},{19,3},{20,4},{21,5},{22,6},{23,7},{24,8},{25... | collective-permute-start | bytes 1032200 | tf_op jit(solution)/shard_map/ppermute | solution.py:681
  7.7 5.6 %all-to-all-start = ((bf16[8,48,576]{2,1,0:T(8,128)(2,1)}), bf16[8,48,576]{2,1,0:T(8,128)(2,1)S(1)}, u32[]{:S(2)}, u32[]{:S(2)}) async-start(bf16[8,48,576]{2,1,0:T(8,128)(2,1)} %shard_map.83), calls=%async_computation | async-start | bytes 983040 | tf_op jit(solution)/shard_map/all_to_all | solution.py:718
  19.0 9.6 %shard_map.85 = (bf16[2,4,544,128]{3,2,1,0:T(8,128)(2,1)}, bf16[2,2,256,128]{3,2,1,0:T(8,128)(2,1)}, bf16[2,2,256,128]{3,2,1,0:T(8,128)(2,1)}, bf16[2,2,96,128]{3,2,1,0:T(8,128)(2,1)}, bf16[2,2,96,128]{3,2,1,0:T(8,128)(2,1)}) custom-call(s32[1]{0:T(128)} %bitcast.1.tp_ref, bf16[256,1792]{1,0:T(8,128)(2,1)} %refs_13_.5, bf16[256,1792]{1,0:T(8,128)(2,1)} %copy-done.47, ...), custom_call_target="tpu_custom_call" | custom-call | tf_op jit(solution)/shard_map/pallas_call | solution.py:252
  32.9 5.6 %all-to-all-start.1 = ((bf16[8,544,128]{2,1,0:T(8,128)(2,1)}), bf16[8,544,128]{2,1,0:T(8,128)(2,1)S(1)}, u32[]{:S(2)}, u32[]{:S(2)}) async-start(bf16[8,544,128]{2,1,0:T(8,128)(2,1)} %bitcast.15), calls=%async_computation.1 | async-start | bytes 2228224 | tf_op jit(solution)/shard_map/all_to_all | solution.py:736
  45.7 2.1 %collective-permute-start.10 = (bf16[256,768]{1,0:T(8,128)(2,1)}, bf16[256,768]{1,0:T(8,128)(2,1)S(1)}, u32[]{:S(2)}, u32[]{:S(2)}) collective-permute-start(bf16[256,768]{1,0:T(8,128)(2,1)} %get-tuple-element.53), channel_id=1, source_target_pairs={{16,0},{17,1},{18,2},{19,3},{20,4},{21,5},{22,6},{23,7},{24,8},{25... | collective-permute-start | bytes 1179656 | tf_op jit(solution)/shard_map/ppermute | solution.py:681
  52.9 4.7 %shard_map.89 = (bf16[256,1792]{1,0:T(8,128)(2,1)}, bf16[256,1792]{1,0:T(8,128)(2,1)}, bf16[256,1792]{1,0:T(8,128)(2,1)}, bf16[256,1792]{1,0:T(8,128)(2,1)}) custom-call(s32[1]{0:T(128)} %bitcast.1.tp_ref, bf16[256,512]{1,0:T(8,128)(2,1)} %copy-done.27, bf16[1024,3584]{1,0:T(8,128)(2,1)} %bitcast.20), custom_call_target="tpu_custom_call" | custom-call | flops 1 | bytes 1 | tf_op jit(solution)/shard_map/pallas_call | solution.py:405
  57.6 3.4 %collective-permute-done.6.refs_5_.refs_2_ = bf16[2,256,128]{2,1,0:T(8,128)(2,1)S(1)} collective-permute-done((bf16[2,256,128]{2,1,0:T(8,128)(2,1)S(1)}, bf16[2,256,128]{2,1,0:T(8,128)(2,1)S(1)}, u32[]{:S(2)}, u32[]{:S(2)}) %collective-permute-start.6) | collective-permute-done | bytes 131104 | tf_op jit(solution)/shard_map/ppermute | solution.py:692
  60.9 3.6 %collective-permute-done.7.refs_6_.refs_3_ = bf16[2,256,128]{2,1,0:T(8,128)(2,1)S(1)} collective-permute-done((bf16[2,256,128]{2,1,0:T(8,128)(2,1)S(1)}, bf16[2,256,128]{2,1,0:T(8,128)(2,1)S(1)}, u32[]{:S(2)}, u32[]{:S(2)}) %collective-permute-start.7) | collective-permute-done | bytes 131104 | tf_op jit(solution)/shard_map/ppermute | solution.py:692
  69.3 8.6 %shard_map.91 = (bf16[2,256,128]{2,1,0:T(8,128)(2,1)S(1)}, bf16[2,256,128]{2,1,0:T(8,128)(2,1)S(1)}, bf16[2,256,128]{2,1,0:T(8,128)(2,1)S(1)}, bf16[2,256,128]{2,1,0:T(8,128)(2,1)S(1)}) custom-call(s32[12]{0:T(128)S(1)} %copy-done.31, bf16[2,256,128]{2,1,0:T(8,128)(2,1)S(1)} %get-tuple-element.47.refs_0_, ...), custom_call_target="tpu_custom_call" | custom-call | tf_op jit(solution)/shard_map/pallas_call | solution.py:540
  87.9 2.1 %collective-permute-start.25 = (bf16[256,512]{1,0:T(8,128)(2,1)S(1)}, bf16[256,512]{1,0:T(8,128)(2,1)S(1)}, u32[]{:S(2)}, u32[]{:S(2)}) collective-permute-start(bf16[256,512]{1,0:T(8,128)(2,1)S(1)} %copy-done.35), channel_id=1, source_target_pairs={{16,0},{17,1},{18,2},{19,3},{20,4},{21,5},{22,6},{23,7},{24,8},{25... | collective-permute-start | bytes 786440 | tf_op jit(solution)/shard_map/ppermute | solution.py:681
  90.8 6.1 %shard_map.93.refs_17_ = bf16[256,768]{1,0:T(8,128)(2,1)} custom-call(s32[12]{0:T(128)} %copy-done.30, bf16[2,256,128]{2,1,0:T(8,128)(2,1)} %copy-done.20, bf16[2,256,128]{2,1,0:T(8,128)(2,1)} %copy-done.40, bf16[2,256,128]{2,1,0:T(8,128)(2,1)} %copy-done.41, bf16[2,256,128]{2,1,0:T(8,128)(2,1)} %copy-done.42, bf16[2,256,128]{2,1,0:T(8,128)(2,1)} %copy-done.43, ...), custom_call_target="tpu_custom_call" | custom-call | tf_op jit(solution)/shard_map/pallas_call | solution.py:633
  98.3 4.8 %shard_map.92.refs_16_ = bf16[256,512]{1,0:T(8,128)(2,1)} custom-call(s32[12]{0:T(128)} %copy-done.30, bf16[2,256,128]{2,1,0:T(8,128)(2,1)} %copy-done.20, bf16[2,256,128]{2,1,0:T(8,128)(2,1)} %copy-done.40, bf16[2,256,128]{2,1,0:T(8,128)(2,1)} %copy-done.41, bf16[2,256,128]{2,1,0:T(8,128)(2,1)} %copy-done.42, bf16[2,256,128]{2,1,0:T(8,128)(2,1)} %copy-done.43, ...), custom_call_target="tpu_custom_call" | custom-call | tf_op jit(solution)/shard_map/pallas_call | solution.py:633
  105.3 5.0 %shard_map.94.refs_18_ = bf16[256,512]{1,0:T(8,128)(2,1)} custom-call(s32[12]{0:T(128)} %copy-done.30, bf16[2,256,128]{2,1,0:T(8,128)(2,1)} %copy-done.20, bf16[2,256,128]{2,1,0:T(8,128)(2,1)} %copy-done.40, bf16[2,256,128]{2,1,0:T(8,128)(2,1)} %copy-done.41, bf16[2,256,128]{2,1,0:T(8,128)(2,1)} %copy-done.42, bf16[2,256,128]{2,1,0:T(8,128)(2,1)} %copy-done.43, ...), custom_call_target="tpu_custom_call" | custom-call | tf_op jit(solution)/shard_map/pallas_call | solution.py:633
  112.1 3.0 %collective-permute-done.23.refs_0_.refs_13_ = bf16[256,512]{1,0:T(8,128)(2,1)S(1)} collective-permute-done((bf16[256,512]{1,0:T(8,128)(2,1)}, bf16[256,512]{1,0:T(8,128)(2,1)S(1)}, u32[]{:S(2)}, u32[]{:S(2)}) %collective-permute-start.23) | collective-permute-done | bytes 262176 | tf_op jit(solution)/shard_map/ppermute | solution.py:757
  116.7 4.3 %collective-permute-done.26.refs_2_.refs_15_ = bf16[256,512]{1,0:T(8,128)(2,1)S(1)} collective-permute-done((bf16[256,512]{1,0:T(8,128)(2,1)}, bf16[256,512]{1,0:T(8,128)(2,1)S(1)}, u32[]{:S(2)}, u32[]{:S(2)}) %collective-permute-start.26) | collective-permute-done | bytes 262176 | tf_op jit(solution)/shard_map/ppermute | solution.py:757
  123.0 3.7 %shard_map.95 = (bf16[256,3584]{1,0:T(8,128)(2,1)S(1)}, bf16[2,4,256,128]{3,2,1,0:T(8,128)(2,1)}) custom-call(s32[1]{0:T(128)} %bitcast.1.tp_ref, bf16[256,512]{1,0:T(8,128)(2,1)S(1)} %collective-permute-done.23.refs_0_.refs_13_, bf16[256,768]{1,0:T(8,128)(2,1)S(1)} %collective-permute-done.24.refs_1_.refs_14_, ...), custom_call_target="tpu_custom_call" | custom-call | tf_op jit(solution)/shard_map/pallas_call | solution.py:195
  126.7 4.6 %all-to-all-start.2 = ((bf16[8,256,128]{2,1,0:T(8,128)(2,1)}), bf16[8,256,128]{2,1,0:T(8,128)(2,1)S(1)}, u32[]{:S(2)}, u32[]{:S(2)}) async-start(bf16[8,256,128]{2,1,0:T(8,128)(2,1)} %bitcast.12), calls=%async_computation.2 | async-start | bytes 1048576 | tf_op jit(solution)/shard_map/all_to_all | solution.py:761
  131.4 3.1 %copy-done = bf16[1,3584,1024]{2,1,0:T(8,128)(2,1)S(1)} copy-done((bf16[1,3584,1024]{2,1,0:T(8,128)(2,1)S(1)}, bf16[1,3584,1024]{2,1,0:T(8,128)(2,1)}, u32[]{:S(2)}) %copy-start) | copy-done | bytes 7340056
  134.5 3.0 %shard_map.96 = (bf16[2,2,256,128]{3,2,1,0:T(8,128)(2,1)S(1)}, bf16[2,2,256,128]{3,2,1,0:T(8,128)(2,1)S(1)}) custom-call(s32[1]{0:T(128)} %bitcast.1.tp_ref, bf16[256,3584]{1,0:T(8,128)(2,1)S(1)} %get-tuple-element.63.refs_0_, bf16[3584,1024]{1,0:T(8,128)(2,1)S(1)} %bitcast.14, f32[352,128]{1,0:T(8,128)S(1)} %copy-done.14, f32[352,128]{1,0:T(8,128)S(1)} %copy-done.16), custom_call_target="tpu_custom_call" | custom-call | flops 1 | bytes 1 | tf_op jit(solution)/shard_map/pallas_call | solution.py:292
  143.0 3.8 %collective-permute-done.31.refs_1_ = bf16[2,256,128]{2,1,0:T(8,128)(2,1)S(1)} collective-permute-done((bf16[2,256,128]{2,1,0:T(8,128)(2,1)S(1)}, bf16[2,256,128]{2,1,0:T(8,128)(2,1)S(1)}, u32[]{:S(2)}, u32[]{:S(2)}) %collective-permute-start.31) | collective-permute-done | bytes 131104 | tf_op jit(solution)/shard_map/ppermute | solution.py:692
  146.8 2.3 %collective-permute-done.33.refs_3_ = bf16[2,256,128]{2,1,0:T(8,128)(2,1)S(1)} collective-permute-done((bf16[2,256,128]{2,1,0:T(8,128)(2,1)S(1)}, bf16[2,256,128]{2,1,0:T(8,128)(2,1)S(1)}, u32[]{:S(2)}, u32[]{:S(2)}) %collective-permute-start.33) | collective-permute-done | bytes 131104 | tf_op jit(solution)/shard_map/ppermute | solution.py:692
  151.8 8.1 %shard_map.99 = (bf16[2,256,128]{2,1,0:T(8,128)(2,1)S(1)}, bf16[2,256,128]{2,1,0:T(8,128)(2,1)S(1)}, bf16[2,256,128]{2,1,0:T(8,128)(2,1)S(1)}, bf16[2,256,128]{2,1,0:T(8,128)(2,1)S(1)}) custom-call(s32[12]{0:T(128)S(1)} %copy-done.32, bf16[2,256,128]{2,1,0:T(8,128)(2,1)S(1)} %get-tuple-element.66.refs_0_, ...), custom_call_target="tpu_custom_call" | custom-call | tf_op jit(solution)/shard_map/pallas_call | solution.py:540
  172.3 7.6 %shard_map.100 = bf16[1,256,1792]{2,1,0:T(8,128)(2,1)} custom-call(s32[12]{0:T(128)} %copy-done.30, bf16[2,256,128]{2,1,0:T(8,128)(2,1)} %copy-done.29, bf16[2,256,128]{2,1,0:T(8,128)(2,1)} %copy-done.50, bf16[2,256,128]{2,1,0:T(8,128)(2,1)} %copy-done.51, bf16[2,256,128]{2,1,0:T(8,128)(2,1)} %copy-done.52, bf16[2,256,128]{2,1,0:T(8,128)(2,1)} %copy-done.53, ...), custom_call_target="tpu_custom_call" | custom-call | tf_op jit(solution)/shard_map/pallas_call | solution.py:633
  (221 shorter events, 69.2 us)
Async XLA Ops:
  0.0 18.0 %collective-permute-start = (bf16[256,1792]{1,0:T(8,128)(2,1)}, bf16[256,1792]{1,0:T(8,128)(2,1)S(1)}, u32[]{:S(2)}, u32[]{:S(2)}) collective-permute-start(bf16[256,1792]{1,0:T(8,128)(2,1)} %refs_13_.5), channel_id=1, source_target_pairs={{0,1},{1,0},{2,3},{3,2},{4,5},{5,4},{6,7},{7,6},{8,9},{9,8},{10,11... | collective-permute-start | bytes 2752520 | tf_op jit(solution)/shard_map/ppermute | solution.py:37
  3.7 11.9 %collective-permute-start.1 = (bf16[96,1792]{1,0:T(8,128)(2,1)}, bf16[96,1792]{1,0:T(8,128)(2,1)S(1)}, u32[]{:S(2)}, u32[]{:S(2)}) collective-permute-start(bf16[96,1792]{1,0:T(8,128)(2,1)} %get-tuple-element.40.after), channel_id=1, source_target_pairs={{16,0},{17,1},{18,2},{19,3},{20,4},{21,5},{22,6},{23,7},{24,8},{25... | collective-permute-start | bytes 1032200 | tf_op jit(solution)/shard_map/ppermute | solution.py:681
  7.7 21.4 %all-to-all-start = ((bf16[8,48,576]{2,1,0:T(8,128)(2,1)}), bf16[8,48,576]{2,1,0:T(8,128)(2,1)S(1)}, u32[]{:S(2)}, u32[]{:S(2)}) async-start(bf16[8,48,576]{2,1,0:T(8,128)(2,1)} %shard_map.83), calls=%async_computation | async-start | bytes 983040 | tf_op jit(solution)/shard_map/all_to_all | solution.py:718
  32.9 31.7 %all-to-all-start.1 = ((bf16[8,544,128]{2,1,0:T(8,128)(2,1)}), bf16[8,544,128]{2,1,0:T(8,128)(2,1)S(1)}, u32[]{:S(2)}, u32[]{:S(2)}) async-start(bf16[8,544,128]{2,1,0:T(8,128)(2,1)} %bitcast.15), calls=%async_computation.1 | async-start | bytes 2228224 | tf_op jit(solution)/shard_map/all_to_all | solution.py:736
  39.4 9.7 %collective-permute-start.4 = (bf16[2,2,256,128]{3,2,1,0:T(8,128)(2,1)}, bf16[2,2,256,128]{3,2,1,0:T(8,128)(2,1)}, u32[]{:S(2)}, u32[]{:S(2)}) collective-permute-start(bf16[2,2,256,128]{3,2,1,0:T(8,128)(2,1)} %get-tuple-element.46), channel_id=1, source_target_pairs={{0,1},{1,0},{2,3},{3,2},{4,5},{5,4},{6,7},{7,6},{8,9},{9,8},{10,11... | collective-permute-start | bytes 786440 | tf_op jit(solution)/shard_map/ppermute | solution.py:37
  45.7 18.9 %collective-permute-start.10 = (bf16[256,768]{1,0:T(8,128)(2,1)}, bf16[256,768]{1,0:T(8,128)(2,1)S(1)}, u32[]{:S(2)}, u32[]{:S(2)}) collective-permute-start(bf16[256,768]{1,0:T(8,128)(2,1)} %get-tuple-element.53), channel_id=1, source_target_pairs={{16,0},{17,1},{18,2},{19,3},{20,4},{21,5},{22,6},{23,7},{24,8},{25... | collective-permute-start | bytes 1179656 | tf_op jit(solution)/shard_map/ppermute | solution.py:681
  47.8 16.8 %collective-permute-start.9 = (bf16[256,512]{1,0:T(8,128)(2,1)S(1)}, bf16[256,512]{1,0:T(8,128)(2,1)S(1)}, u32[]{:S(2)}, u32[]{:S(2)}) collective-permute-start(bf16[256,512]{1,0:T(8,128)(2,1)S(1)} %get-tuple-element.51.after), channel_id=1, source_target_pairs={{16,0},{17,1},{18,2},{19,3},{20,4},{21,5},{22,6},{23,7},{24,8},{25... | collective-permute-start | bytes 786440 | tf_op jit(solution)/shard_map/ppermute | solution.py:681
  50.2 7.4 %collective-permute-start.5 = (bf16[2,256,128]{2,1,0:T(8,128)(2,1)S(1)}, bf16[2,256,128]{2,1,0:T(8,128)(2,1)S(1)}, u32[]{:S(2)}, u32[]{:S(2)}) collective-permute-start(bf16[2,256,128]{2,1,0:T(8,128)(2,1)S(1)} %get-tuple-element.48), channel_id=1, source_target_pairs={{0,2},{2,0},{4,6},{6,4},{1,3},{3,1},{5,7},{7,5},{8,10},{10,8},{12,... | collective-permute-start | bytes 393224 | tf_op jit(solution)/shard_map/ppermute | solution.py:692
  51.4 9.5 %collective-permute-start.6 = (bf16[2,256,128]{2,1,0:T(8,128)(2,1)S(1)}, bf16[2,256,128]{2,1,0:T(8,128)(2,1)S(1)}, u32[]{:S(2)}, u32[]{:S(2)}) collective-permute-start(bf16[2,256,128]{2,1,0:T(8,128)(2,1)S(1)} %get-tuple-element.49), channel_id=1, source_target_pairs={{0,4},{2,6},{4,0},{6,2},{1,5},{3,7},{5,1},{7,3},{8,12},{10,14},{12... | collective-permute-start | bytes 393224 | tf_op jit(solution)/shard_map/ppermute | solution.py:692
  52.6 12.0 %collective-permute-start.7 = (bf16[2,256,128]{2,1,0:T(8,128)(2,1)S(1)}, bf16[2,256,128]{2,1,0:T(8,128)(2,1)S(1)}, u32[]{:S(2)}, u32[]{:S(2)}) collective-permute-start(bf16[2,256,128]{2,1,0:T(8,128)(2,1)S(1)} %get-tuple-element.50), channel_id=1, source_target_pairs={{0,6},{2,4},{4,2},{6,0},{1,7},{3,5},{5,3},{7,1},{8,14},{10,12},{12... | collective-permute-start | bytes 393224 | tf_op jit(solution)/shard_map/ppermute | solution.py:692
  66.9 11.4 %collective-permute-start.20 = (bf16[256,1792]{1,0:T(8,128)(2,1)S(1)}, bf16[256,1792]{1,0:T(8,128)(2,1)S(1)}, u32[]{:S(2)}, u32[]{:S(2)}) collective-permute-start(bf16[256,1792]{1,0:T(8,128)(2,1)S(1)} %copy-done.61), channel_id=1, source_target_pairs={{0,1},{1,0},{2,3},{3,2},{4,5},{5,4},{6,7},{7,6},{8,9},{9,8},{10,11... | collective-permute-start | bytes 2752520 | tf_op jit(solution)/shard_map/ppermute | solution.py:37
  67.4 12.8 %collective-permute-start.21 = (bf16[256,1792]{1,0:T(8,128)(2,1)S(1)}, bf16[256,1792]{1,0:T(8,128)(2,1)S(1)}, u32[]{:S(2)}, u32[]{:S(2)}) collective-permute-start(bf16[256,1792]{1,0:T(8,128)(2,1)S(1)} %copy-done.60), channel_id=1, source_target_pairs={{0,1},{1,0},{2,3},{3,2},{4,5},{5,4},{6,7},{7,6},{8,9},{9,8},{10,11... | collective-permute-start | bytes 2752520 | tf_op jit(solution)/shard_map/ppermute | solution.py:37
  67.7 12.9 %collective-permute-start.22 = (bf16[256,1792]{1,0:T(8,128)(2,1)S(1)}, bf16[256,1792]{1,0:T(8,128)(2,1)S(1)}, u32[]{:S(2)}, u32[]{:S(2)}) collective-permute-start(bf16[256,1792]{1,0:T(8,128)(2,1)S(1)} %copy-done.59), channel_id=1, source_target_pairs={{0,1},{1,0},{2,3},{3,2},{4,5},{5,4},{6,7},{7,6},{8,9},{9,8},{10,11... | collective-permute-start | bytes 2752520 | tf_op jit(solution)/shard_map/ppermute | solution.py:37
  68.0 19.9 %collective-permute-start.19 = (bf16[256,1792]{1,0:T(8,128)(2,1)}, bf16[256,1792]{1,0:T(8,128)(2,1)S(1)}, u32[]{:S(2)}, u32[]{:S(2)}) collective-permute-start(bf16[256,1792]{1,0:T(8,128)(2,1)} %get-tuple-element.52.refs_1_), channel_id=1, source_target_pairs={{0,1},{1,0},{2,3},{3,2},{4,5},{5,4},{6,7},{7,6},{8,9},{9,8},{10,11... | collective-permute-start | bytes 2752520 | tf_op jit(solution)/shard_map/ppermute | solution.py:37
  80.7 9.4 %collective-permute-start.15 = (bf16[2,256,128]{2,1,0:T(8,128)(2,1)S(1)}, bf16[2,256,128]{2,1,0:T(8,128)(2,1)S(1)}, u32[]{:S(2)}, u32[]{:S(2)}) collective-permute-start(bf16[2,256,128]{2,1,0:T(8,128)(2,1)S(1)} %get-tuple-element.54.refs_0_), channel_id=1, source_target_pairs={{0,1},{1,0},{2,3},{3,2},{4,5},{5,4},{6,7},{7,6},{8,9},{9,8},{10,11... | collective-permute-start | bytes 393224 | tf_op jit(solution)/shard_map/ppermute | solution.py:37
  82.7 7.3 %collective-permute-start.16 = (bf16[2,256,128]{2,1,0:T(8,128)(2,1)S(1)}, bf16[2,256,128]{2,1,0:T(8,128)(2,1)S(1)}, u32[]{:S(2)}, u32[]{:S(2)}) collective-permute-start(bf16[2,256,128]{2,1,0:T(8,128)(2,1)S(1)} %collective-permute-done.12.refs_1_), channel_id=1, source_target_pairs={{0,1},{1,0},{2,3},{3,2},{4,5},{5,4},{6,7},{7,6},{8,9},{9,8},{10,11... | collective-permute-start | bytes 393224 | tf_op jit(solution)/shard_map/ppermute | solution.py:37
  87.9 16.7 %collective-permute-start.25 = (bf16[256,512]{1,0:T(8,128)(2,1)S(1)}, bf16[256,512]{1,0:T(8,128)(2,1)S(1)}, u32[]{:S(2)}, u32[]{:S(2)}) collective-permute-start(bf16[256,512]{1,0:T(8,128)(2,1)S(1)} %copy-done.35), channel_id=1, source_target_pairs={{16,0},{17,1},{18,2},{19,3},{20,4},{21,5},{22,6},{23,7},{24,8},{25... | collective-permute-start | bytes 786440 | tf_op jit(solution)/shard_map/ppermute | solution.py:681
  97.0 14.8 %collective-permute-start.24 = (bf16[256,768]{1,0:T(8,128)(2,1)}, bf16[256,768]{1,0:T(8,128)(2,1)S(1)}, u32[]{:S(2)}, u32[]{:S(2)}) collective-permute-start(bf16[256,768]{1,0:T(8,128)(2,1)} %shard_map.93.refs_17_), channel_id=1, source_target_pairs={{0,16},{1,17},{2,18},{3,19},{4,20},{5,21},{6,22},{7,23},{8,24},{9,... | collective-permute-start | bytes 1179656 | tf_op jit(solution)/shard_map/ppermute | solution.py:757
  103.1 11.9 %collective-permute-start.23 = (bf16[256,512]{1,0:T(8,128)(2,1)}, bf16[256,512]{1,0:T(8,128)(2,1)S(1)}, u32[]{:S(2)}, u32[]{:S(2)}) collective-permute-start(bf16[256,512]{1,0:T(8,128)(2,1)} %shard_map.92.refs_16_), channel_id=1, source_target_pairs={{0,16},{1,17},{2,18},{3,19},{4,20},{5,21},{6,22},{7,23},{8,24},{9,... | collective-permute-start | bytes 786440 | tf_op jit(solution)/shard_map/ppermute | solution.py:757
  110.3 10.7 %collective-permute-start.26 = (bf16[256,512]{1,0:T(8,128)(2,1)}, bf16[256,512]{1,0:T(8,128)(2,1)S(1)}, u32[]{:S(2)}, u32[]{:S(2)}) collective-permute-start(bf16[256,512]{1,0:T(8,128)(2,1)} %shard_map.94.refs_18_), channel_id=1, source_target_pairs={{0,16},{1,17},{2,18},{3,19},{4,20},{5,21},{6,22},{7,23},{8,24},{9,... | collective-permute-start | bytes 786440 | tf_op jit(solution)/shard_map/ppermute | solution.py:757
  111.7 11.2 %collective-permute-start.28 = (bf16[256,768]{1,0:T(8,128)(2,1)S(1)}, bf16[256,768]{1,0:T(8,128)(2,1)S(1)}, u32[]{:S(2)}, u32[]{:S(2)}) collective-permute-start(bf16[256,768]{1,0:T(8,128)(2,1)S(1)} %collective-permute-done.24.refs_1_.refs_14_), channel_id=1, source_target_pairs={{0,1},{1,0},{2,3},{3,2},{4,5},{5,4},{6,7},{7,6},{8,9},{9,8},{10,11... | collective-permute-start | bytes 1179656 | tf_op jit(solution)/shard_map/ppermute | solution.py:37
  126.7 22.4 %all-to-all-start.2 = ((bf16[8,256,128]{2,1,0:T(8,128)(2,1)}), bf16[8,256,128]{2,1,0:T(8,128)(2,1)S(1)}, u32[]{:S(2)}, u32[]{:S(2)}) async-start(bf16[8,256,128]{2,1,0:T(8,128)(2,1)} %bitcast.12), calls=%async_computation.2 | async-start | bytes 1048576 | tf_op jit(solution)/shard_map/all_to_all | solution.py:761
  162.4 7.0 %collective-permute-start.37 = (bf16[2,256,128]{2,1,0:T(8,128)(2,1)S(1)}, bf16[2,256,128]{2,1,0:T(8,128)(2,1)S(1)}, u32[]{:S(2)}, u32[]{:S(2)}) collective-permute-start(bf16[2,256,128]{2,1,0:T(8,128)(2,1)S(1)} %get-tuple-element.74), channel_id=1, source_target_pairs={{0,6},{2,4},{4,2},{6,0},{1,7},{3,5},{5,3},{7,1},{8,14},{10,12},{12... | collective-permute-start | bytes 393224 | tf_op jit(solution)/shard_map/ppermute | solution.py:700
  163.3 7.3 %collective-permute-start.38 = (bf16[2,256,128]{2,1,0:T(8,128)(2,1)S(1)}, bf16[2,256,128]{2,1,0:T(8,128)(2,1)S(1)}, u32[]{:S(2)}, u32[]{:S(2)}) collective-permute-start(bf16[2,256,128]{2,1,0:T(8,128)(2,1)S(1)} %get-tuple-element.71.refs_0_), channel_id=1, source_target_pairs={{0,1},{1,0},{2,3},{3,2},{4,5},{5,4},{6,7},{7,6},{8,9},{9,8},{10,11... | collective-permute-start | bytes 393224 | tf_op jit(solution)/shard_map/ppermute | solution.py:37
  (83 other events, 484.0 us)
